TPU v7x, 256 devices: a whole 4x4x8 slice. The times are simulated.
256 devices in a mesh: ctx: 64 (over y, x_lo, z), grp: 4 (over x_hi, core).
Axes of the slice: x: 4 (x_hi: 2, x_lo: 2; x = x_hi * 2 + x_lo), y: 4, z: 8, core: 2. Of those that a mesh axis runs over, the one named last changes fastest.
Arguments:
- queries: bfloat16 [4096, 5120], P('ctx', 'grp')
- cache_codes: int32 [2, 8, 32768, 128], P(None, 'grp', 'ctx'), may hold values from 0 to 15
- cache_scales: float32 [2, 8, 4, 32768], P(None, 'grp', None, 'ctx'), may hold values from 0.03 to 0.3, as said below
- pattern: int32 [8, 64, 256], P('grp', None, 'ctx'), may hold values from 0 to 1, as said below
- out_weight: bfloat16 [5120, 5120], P('grp', 'ctx'), may hold values from -0.25 to 0.25
Outputs:
- mixed: bfloat16 [4096, 5120], P('ctx', 'grp')
Inputs may be any that keep to these rules, and one draw needn't show every extreme that they name: `cache_scales`: positive scales. `pattern`: for every key-value head and query block, page 0 is kept.
All inputs are finite; a program needn't handle non-finite values.
Results may differ from a plain program's by a relative error of at most 0.014.
Values may be sent and summed in bfloat16 or wider, within the bound.
No kernel may reach another device: no remote copies, remote signals or barrier semaphores. Data moves between devices by JAX's collectives and lax.ppermute only.
A program may use at most 64 MiB of HBM per device.

v0:
```python
import math

import jax
import jax.numpy as jnp
from jax import lax
from jax.sharding import PartitionSpec as P

NEG_FILL = -1e30


def passed_along(block, axis, distance):
    devices = range(lax.axis_size(axis))
    route = [((i - distance) % len(devices), i) for i in devices]
    return lax.ppermute(block, axis, route)


def hadamard(order):
    index = jnp.arange(order, dtype=jnp.int32)
    common = index[:, None] & index[None, :]
    parity = jnp.zeros((order, order), jnp.int32)
    for shift_bit in range(int(order).bit_length()):
        parity = parity ^ common >> shift_bit & 1
    return jnp.where(parity == 1, -1.0, 1.0).astype(jnp.float32)


def dequantize(codes, scales):
    width = codes.shape[-1]
    groups = scales.shape[1]
    spread = jnp.repeat(scales, width // groups, axis=1)
    spread = jnp.transpose(spread, (0, 2, 1))
    return ((codes.astype(jnp.float32) - 7.5) * spread).astype(jnp.bfloat16)


def tile_update(partial_value, rotated, keys, values, keep_cols, key_pos, query_pos, factor):
    running_max, running_sum, totals = partial_value
    scores = (
        jnp.einsum("hpqd,hkd->hpqk", rotated, keys, preferred_element_type=jnp.float32) * factor
    )
    allowed = (keep_cols[:, None, None, :] == 1) & (
        key_pos[None, None, None, :] <= query_pos[None, None, :, None]
    )
    scores = jnp.where(allowed, scores, NEG_FILL)
    new_max = jnp.maximum(running_max, jnp.max(scores, axis=-1))
    rescale = jnp.exp(running_max - new_max)
    weights = jnp.where(allowed, jnp.exp(scores - new_max[..., None]), 0.0)
    running_sum = running_sum * rescale + jnp.sum(weights, axis=-1)
    weighted = jnp.einsum(
        "hpqk,hkd->hpqd", weights.astype(jnp.bfloat16), values, preferred_element_type=jnp.float32
    )
    totals = totals * rescale[..., None] + weighted
    return (new_max, running_sum, totals)


def local_pass(partial_value, rotated, keys, values, keep_rows, first_key, query_pos, page, factor):
    shard_len = keys.shape[1]
    keep_cols = jnp.repeat(keep_rows, page, axis=1)
    key_pos = first_key + jnp.arange(shard_len, dtype=jnp.int32)
    return tile_update(partial_value, rotated, keys, values, keep_cols, key_pos, query_pos, factor)


def on_device(queries, cache_codes, cache_scales, pattern, out_weight):
    cycle_size = lax.axis_size("ctx")
    position = lax.axis_index("ctx")
    block_rows = queries.shape[0]
    groups = cache_codes.shape[1]
    shard_len = cache_codes.shape[2]
    width = cache_codes.shape[3]
    heads = queries.shape[1] // width
    per_group = heads // groups
    page = shard_len // pattern.shape[2]
    total_len = shard_len * cycle_size
    total_q = block_rows * cycle_size
    factor = 1.0 / math.sqrt(width)
    table = hadamard(width)
    turned = jnp.einsum(
        "qhd,de->hqe",
        queries.reshape(block_rows, heads, width),
        table.astype(jnp.bfloat16),
        preferred_element_type=jnp.float32,
    )
    rotated = (turned * factor).astype(jnp.bfloat16).reshape(groups, per_group, block_rows, width)
    keys = dequantize(cache_codes[0], cache_scales[0])
    values = dequantize(cache_codes[1], cache_scales[1])
    first_key = position * shard_len

    def advance(partial_value, moving, anchor, offset):
        keep_rows = lax.dynamic_index_in_dim(pattern, anchor, 1, keepdims=False)
        count = moving.shape[2]
        query_pos = (
            total_len - total_q + anchor * block_rows + offset + jnp.arange(count, dtype=jnp.int32)
        )
        return local_pass(
            partial_value, moving, keys, values, keep_rows, first_key, query_pos, page, factor
        )

    def forward_step(turn, carry):
        moving, partial_value = carry
        partial_value = advance(partial_value, moving, (position - turn) % cycle_size, 0)
        moving = passed_along(moving, "ctx", 1)
        partial_value = passed_along(
            (partial_value[0], partial_value[1], partial_value[2]), "ctx", 1
        )
        return (moving, tuple(partial_value))

    final = lax.fori_loop(
        0,
        cycle_size,
        forward_step,
        (
            rotated,
            (
                jnp.full((groups, per_group, block_rows), NEG_FILL, jnp.float32),
                jnp.zeros((groups, per_group, block_rows), jnp.float32),
                jnp.zeros((groups, per_group, block_rows, width), jnp.float32),
            ),
        ),
    )
    running_sum = final[1][1]
    totals = final[1][2]
    attended = totals / running_sum[..., None]
    restored = (
        jnp.einsum("hpqd,de->qhpe", attended, table, precision=lax.Precision.HIGHEST) * factor
    )
    restored = restored.astype(jnp.bfloat16).reshape(block_rows, heads * width)
    terms = jnp.dot(
        restored,
        lax.all_gather(out_weight, "ctx", axis=1, tiled=True),
        preferred_element_type=jnp.float32,
    )
    return lax.psum_scatter(terms, "grp", scatter_dimension=1, tiled=True).astype(jnp.bfloat16)


def solution(mesh):
    placed = (
        P("ctx", "grp"),
        P(None, "grp", "ctx", None),
        P(None, "grp", None, "ctx"),
        P("grp", None, "ctx"),
        P("grp", "ctx"),
    )
    return jax.shard_map(
        on_device, mesh=mesh, in_specs=placed, out_specs=P("ctx", "grp"), check_vma=False
    )
```

profile of v0, /device:TPU:6, one launch (start us, length us, event | category | flops | bytes accessed | tf_op | source)
XLA Modules:
  0.0 1237.4 jit_solution(6367652688822495973)
XLA Ops:
  10.3 1133.9 %while.21 = (s32[]{:T(128)}, bf16[2,5,64,128]{3,2,1,0:T(8,128)(2,1)S(1)}, f32[2,5,64]{2,1,0:T(8,128)S(1)}, f32[2,5,64]{2,1,0:T(8,128)S(1)}, f32[2,5,64,128]{3,2,...) while((s32[]{:T(128)}, ...), condition=%wide.region_3.4_spmd, body=%wide.region_0.3_spmd.sunk | while | flops 170985312 | bytes 7962652 | solution.py:105
  41.9 17.7 %collective-permute-done.1 = f32[2,5,64]{2,1,0:T(8,128)S(1)} collective-permute-done((f32[2,5,64]{2,1,0:T(8,128)S(1)}, f32[2,5,64]{2,1,0:T(8,128)S(1)}, u32[]{:S(2)}, u32[]{:S(2)}) %collective-permute-start.1) | collective-permute-done | bytes 2592 | tf_op jit(solution)/shard_map/while/body/eval_jaxpr/ppermute | solution.py:14
  67.4 16.2 %collective-permute-done.1 = f32[2,5,64]{2,1,0:T(8,128)S(1)} collective-permute-done((f32[2,5,64]{2,1,0:T(8,128)S(1)}, f32[2,5,64]{2,1,0:T(8,128)S(1)}, u32[]{:S(2)}, u32[]{:S(2)}) %collective-permute-start.1) | collective-permute-done | bytes 2592 | tf_op jit(solution)/shard_map/while/body/eval_jaxpr/ppermute | solution.py:14
  90.2 15.7 %collective-permute-done.1 = f32[2,5,64]{2,1,0:T(8,128)S(1)} collective-permute-done((f32[2,5,64]{2,1,0:T(8,128)S(1)}, f32[2,5,64]{2,1,0:T(8,128)S(1)}, u32[]{:S(2)}, u32[]{:S(2)}) %collective-permute-start.1) | collective-permute-done | bytes 2592 | tf_op jit(solution)/shard_map/while/body/eval_jaxpr/ppermute | solution.py:14
  112.0 15.3 %collective-permute-done.1 = f32[2,5,64]{2,1,0:T(8,128)S(1)} collective-permute-done((f32[2,5,64]{2,1,0:T(8,128)S(1)}, f32[2,5,64]{2,1,0:T(8,128)S(1)}, u32[]{:S(2)}, u32[]{:S(2)}) %collective-permute-start.1) | collective-permute-done | bytes 2592 | tf_op jit(solution)/shard_map/while/body/eval_jaxpr/ppermute | solution.py:14
  132.8 14.6 %collective-permute-done.1 = f32[2,5,64]{2,1,0:T(8,128)S(1)} collective-permute-done((f32[2,5,64]{2,1,0:T(8,128)S(1)}, f32[2,5,64]{2,1,0:T(8,128)S(1)}, u32[]{:S(2)}, u32[]{:S(2)}) %collective-permute-start.1) | collective-permute-done | bytes 2592 | tf_op jit(solution)/shard_map/while/body/eval_jaxpr/ppermute | solution.py:14
  152.5 16.6 %collective-permute-done.1 = f32[2,5,64]{2,1,0:T(8,128)S(1)} collective-permute-done((f32[2,5,64]{2,1,0:T(8,128)S(1)}, f32[2,5,64]{2,1,0:T(8,128)S(1)}, u32[]{:S(2)}, u32[]{:S(2)}) %collective-permute-start.1) | collective-permute-done | bytes 2592 | tf_op jit(solution)/shard_map/while/body/eval_jaxpr/ppermute | solution.py:14
  174.8 15.0 %collective-permute-done.1 = f32[2,5,64]{2,1,0:T(8,128)S(1)} collective-permute-done((f32[2,5,64]{2,1,0:T(8,128)S(1)}, f32[2,5,64]{2,1,0:T(8,128)S(1)}, u32[]{:S(2)}, u32[]{:S(2)}) %collective-permute-start.1) | collective-permute-done | bytes 2592 | tf_op jit(solution)/shard_map/while/body/eval_jaxpr/ppermute | solution.py:14
  242.2 16.6 %collective-permute-done.1 = f32[2,5,64]{2,1,0:T(8,128)S(1)} collective-permute-done((f32[2,5,64]{2,1,0:T(8,128)S(1)}, f32[2,5,64]{2,1,0:T(8,128)S(1)}, u32[]{:S(2)}, u32[]{:S(2)}) %collective-permute-start.1) | collective-permute-done | bytes 2592 | tf_op jit(solution)/shard_map/while/body/eval_jaxpr/ppermute | solution.py:14
  262.9 18.5 %collective-permute-done.1 = f32[2,5,64]{2,1,0:T(8,128)S(1)} collective-permute-done((f32[2,5,64]{2,1,0:T(8,128)S(1)}, f32[2,5,64]{2,1,0:T(8,128)S(1)}, u32[]{:S(2)}, u32[]{:S(2)}) %collective-permute-start.1) | collective-permute-done | bytes 2592 | tf_op jit(solution)/shard_map/while/body/eval_jaxpr/ppermute | solution.py:14
  283.5 25.6 %collective-permute-done.1 = f32[2,5,64]{2,1,0:T(8,128)S(1)} collective-permute-done((f32[2,5,64]{2,1,0:T(8,128)S(1)}, f32[2,5,64]{2,1,0:T(8,128)S(1)}, u32[]{:S(2)}, u32[]{:S(2)}) %collective-permute-start.1) | collective-permute-done | bytes 2592 | tf_op jit(solution)/shard_map/while/body/eval_jaxpr/ppermute | solution.py:14
  311.2 16.1 %collective-permute-done.1 = f32[2,5,64]{2,1,0:T(8,128)S(1)} collective-permute-done((f32[2,5,64]{2,1,0:T(8,128)S(1)}, f32[2,5,64]{2,1,0:T(8,128)S(1)}, u32[]{:S(2)}, u32[]{:S(2)}) %collective-permute-start.1) | collective-permute-done | bytes 2592 | tf_op jit(solution)/shard_map/while/body/eval_jaxpr/ppermute | solution.py:14
  329.4 12.9 %collective-permute-done.1 = f32[2,5,64]{2,1,0:T(8,128)S(1)} collective-permute-done((f32[2,5,64]{2,1,0:T(8,128)S(1)}, f32[2,5,64]{2,1,0:T(8,128)S(1)}, u32[]{:S(2)}, u32[]{:S(2)}) %collective-permute-start.1) | collective-permute-done | bytes 2592 | tf_op jit(solution)/shard_map/while/body/eval_jaxpr/ppermute | solution.py:14
  397.9 12.7 %collective-permute-done.1 = f32[2,5,64]{2,1,0:T(8,128)S(1)} collective-permute-done((f32[2,5,64]{2,1,0:T(8,128)S(1)}, f32[2,5,64]{2,1,0:T(8,128)S(1)}, u32[]{:S(2)}, u32[]{:S(2)}) %collective-permute-start.1) | collective-permute-done | bytes 2592 | tf_op jit(solution)/shard_map/while/body/eval_jaxpr/ppermute | solution.py:14
  412.7 13.8 %collective-permute-done.1 = f32[2,5,64]{2,1,0:T(8,128)S(1)} collective-permute-done((f32[2,5,64]{2,1,0:T(8,128)S(1)}, f32[2,5,64]{2,1,0:T(8,128)S(1)}, u32[]{:S(2)}, u32[]{:S(2)}) %collective-permute-start.1) | collective-permute-done | bytes 2592 | tf_op jit(solution)/shard_map/while/body/eval_jaxpr/ppermute | solution.py:14
  429.3 14.1 %collective-permute-done.1 = f32[2,5,64]{2,1,0:T(8,128)S(1)} collective-permute-done((f32[2,5,64]{2,1,0:T(8,128)S(1)}, f32[2,5,64]{2,1,0:T(8,128)S(1)}, u32[]{:S(2)}, u32[]{:S(2)}) %collective-permute-start.1) | collective-permute-done | bytes 2592 | tf_op jit(solution)/shard_map/while/body/eval_jaxpr/ppermute | solution.py:14
  447.6 14.0 %collective-permute-done.1 = f32[2,5,64]{2,1,0:T(8,128)S(1)} collective-permute-done((f32[2,5,64]{2,1,0:T(8,128)S(1)}, f32[2,5,64]{2,1,0:T(8,128)S(1)}, u32[]{:S(2)}, u32[]{:S(2)}) %collective-permute-start.1) | collective-permute-done | bytes 2592 | tf_op jit(solution)/shard_map/while/body/eval_jaxpr/ppermute | solution.py:14
  465.1 16.5 %collective-permute-done.1 = f32[2,5,64]{2,1,0:T(8,128)S(1)} collective-permute-done((f32[2,5,64]{2,1,0:T(8,128)S(1)}, f32[2,5,64]{2,1,0:T(8,128)S(1)}, u32[]{:S(2)}, u32[]{:S(2)}) %collective-permute-start.1) | collective-permute-done | bytes 2592 | tf_op jit(solution)/shard_map/while/body/eval_jaxpr/ppermute | solution.py:14
  483.6 17.9 %collective-permute-done.1 = f32[2,5,64]{2,1,0:T(8,128)S(1)} collective-permute-done((f32[2,5,64]{2,1,0:T(8,128)S(1)}, f32[2,5,64]{2,1,0:T(8,128)S(1)}, u32[]{:S(2)}, u32[]{:S(2)}) %collective-permute-start.1) | collective-permute-done | bytes 2592 | tf_op jit(solution)/shard_map/while/body/eval_jaxpr/ppermute | solution.py:14
  503.6 15.6 %collective-permute-done.1 = f32[2,5,64]{2,1,0:T(8,128)S(1)} collective-permute-done((f32[2,5,64]{2,1,0:T(8,128)S(1)}, f32[2,5,64]{2,1,0:T(8,128)S(1)}, u32[]{:S(2)}, u32[]{:S(2)}) %collective-permute-start.1) | collective-permute-done | bytes 2592 | tf_op jit(solution)/shard_map/while/body/eval_jaxpr/ppermute | solution.py:14
  521.2 14.8 %collective-permute-done.1 = f32[2,5,64]{2,1,0:T(8,128)S(1)} collective-permute-done((f32[2,5,64]{2,1,0:T(8,128)S(1)}, f32[2,5,64]{2,1,0:T(8,128)S(1)}, u32[]{:S(2)}, u32[]{:S(2)}) %collective-permute-start.1) | collective-permute-done | bytes 2592 | tf_op jit(solution)/shard_map/while/body/eval_jaxpr/ppermute | solution.py:14
  538.1 13.1 %collective-permute-done.1 = f32[2,5,64]{2,1,0:T(8,128)S(1)} collective-permute-done((f32[2,5,64]{2,1,0:T(8,128)S(1)}, f32[2,5,64]{2,1,0:T(8,128)S(1)}, u32[]{:S(2)}, u32[]{:S(2)}) %collective-permute-start.1) | collective-permute-done | bytes 2592 | tf_op jit(solution)/shard_map/while/body/eval_jaxpr/ppermute | solution.py:14
  593.1 12.6 %collective-permute-done.1 = f32[2,5,64]{2,1,0:T(8,128)S(1)} collective-permute-done((f32[2,5,64]{2,1,0:T(8,128)S(1)}, f32[2,5,64]{2,1,0:T(8,128)S(1)}, u32[]{:S(2)}, u32[]{:S(2)}) %collective-permute-start.1) | collective-permute-done | bytes 2592 | tf_op jit(solution)/shard_map/while/body/eval_jaxpr/ppermute | solution.py:14
  607.8 14.8 %collective-permute-done.1 = f32[2,5,64]{2,1,0:T(8,128)S(1)} collective-permute-done((f32[2,5,64]{2,1,0:T(8,128)S(1)}, f32[2,5,64]{2,1,0:T(8,128)S(1)}, u32[]{:S(2)}, u32[]{:S(2)}) %collective-permute-start.1) | collective-permute-done | bytes 2592 | tf_op jit(solution)/shard_map/while/body/eval_jaxpr/ppermute | solution.py:14
  624.7 14.4 %collective-permute-done.1 = f32[2,5,64]{2,1,0:T(8,128)S(1)} collective-permute-done((f32[2,5,64]{2,1,0:T(8,128)S(1)}, f32[2,5,64]{2,1,0:T(8,128)S(1)}, u32[]{:S(2)}, u32[]{:S(2)}) %collective-permute-start.1) | collective-permute-done | bytes 2592 | tf_op jit(solution)/shard_map/while/body/eval_jaxpr/ppermute | solution.py:14
  641.2 17.7 %collective-permute-done.1 = f32[2,5,64]{2,1,0:T(8,128)S(1)} collective-permute-done((f32[2,5,64]{2,1,0:T(8,128)S(1)}, f32[2,5,64]{2,1,0:T(8,128)S(1)}, u32[]{:S(2)}, u32[]{:S(2)}) %collective-permute-start.1) | collective-permute-done | bytes 2592 | tf_op jit(solution)/shard_map/while/body/eval_jaxpr/ppermute | solution.py:14
  661.0 19.2 %collective-permute-done.1 = f32[2,5,64]{2,1,0:T(8,128)S(1)} collective-permute-done((f32[2,5,64]{2,1,0:T(8,128)S(1)}, f32[2,5,64]{2,1,0:T(8,128)S(1)}, u32[]{:S(2)}, u32[]{:S(2)}) %collective-permute-start.1) | collective-permute-done | bytes 2592 | tf_op jit(solution)/shard_map/while/body/eval_jaxpr/ppermute | solution.py:14
  682.4 19.7 %collective-permute-done.1 = f32[2,5,64]{2,1,0:T(8,128)S(1)} collective-permute-done((f32[2,5,64]{2,1,0:T(8,128)S(1)}, f32[2,5,64]{2,1,0:T(8,128)S(1)}, u32[]{:S(2)}, u32[]{:S(2)}) %collective-permute-start.1) | collective-permute-done | bytes 2592 | tf_op jit(solution)/shard_map/while/body/eval_jaxpr/ppermute | solution.py:14
  704.2 18.1 %collective-permute-done.1 = f32[2,5,64]{2,1,0:T(8,128)S(1)} collective-permute-done((f32[2,5,64]{2,1,0:T(8,128)S(1)}, f32[2,5,64]{2,1,0:T(8,128)S(1)}, u32[]{:S(2)}, u32[]{:S(2)}) %collective-permute-start.1) | collective-permute-done | bytes 2592 | tf_op jit(solution)/shard_map/while/body/eval_jaxpr/ppermute | solution.py:14
  724.3 16.9 %collective-permute-done.1 = f32[2,5,64]{2,1,0:T(8,128)S(1)} collective-permute-done((f32[2,5,64]{2,1,0:T(8,128)S(1)}, f32[2,5,64]{2,1,0:T(8,128)S(1)}, u32[]{:S(2)}, u32[]{:S(2)}) %collective-permute-start.1) | collective-permute-done | bytes 2592 | tf_op jit(solution)/shard_map/while/body/eval_jaxpr/ppermute | solution.py:14
  743.2 15.8 %collective-permute-done.1 = f32[2,5,64]{2,1,0:T(8,128)S(1)} collective-permute-done((f32[2,5,64]{2,1,0:T(8,128)S(1)}, f32[2,5,64]{2,1,0:T(8,128)S(1)}, u32[]{:S(2)}, u32[]{:S(2)}) %collective-permute-start.1) | collective-permute-done | bytes 2592 | tf_op jit(solution)/shard_map/while/body/eval_jaxpr/ppermute | solution.py:14
  761.0 13.1 %collective-permute-done.1 = f32[2,5,64]{2,1,0:T(8,128)S(1)} collective-permute-done((f32[2,5,64]{2,1,0:T(8,128)S(1)}, f32[2,5,64]{2,1,0:T(8,128)S(1)}, u32[]{:S(2)}, u32[]{:S(2)}) %collective-permute-start.1) | collective-permute-done | bytes 2592 | tf_op jit(solution)/shard_map/while/body/eval_jaxpr/ppermute | solution.py:14
  776.1 12.5 %collective-permute-done.1 = f32[2,5,64]{2,1,0:T(8,128)S(1)} collective-permute-done((f32[2,5,64]{2,1,0:T(8,128)S(1)}, f32[2,5,64]{2,1,0:T(8,128)S(1)}, u32[]{:S(2)}, u32[]{:S(2)}) %collective-permute-start.1) | collective-permute-done | bytes 2592 | tf_op jit(solution)/shard_map/while/body/eval_jaxpr/ppermute | solution.py:14
  831.0 12.9 %collective-permute-done.1 = f32[2,5,64]{2,1,0:T(8,128)S(1)} collective-permute-done((f32[2,5,64]{2,1,0:T(8,128)S(1)}, f32[2,5,64]{2,1,0:T(8,128)S(1)}, u32[]{:S(2)}, u32[]{:S(2)}) %collective-permute-start.1) | collective-permute-done | bytes 2592 | tf_op jit(solution)/shard_map/while/body/eval_jaxpr/ppermute | solution.py:14
  846.0 14.7 %collective-permute-done.1 = f32[2,5,64]{2,1,0:T(8,128)S(1)} collective-permute-done((f32[2,5,64]{2,1,0:T(8,128)S(1)}, f32[2,5,64]{2,1,0:T(8,128)S(1)}, u32[]{:S(2)}, u32[]{:S(2)}) %collective-permute-start.1) | collective-permute-done | bytes 2592 | tf_op jit(solution)/shard_map/while/body/eval_jaxpr/ppermute | solution.py:14
  862.8 16.0 %collective-permute-done.1 = f32[2,5,64]{2,1,0:T(8,128)S(1)} collective-permute-done((f32[2,5,64]{2,1,0:T(8,128)S(1)}, f32[2,5,64]{2,1,0:T(8,128)S(1)}, u32[]{:S(2)}, u32[]{:S(2)}) %collective-permute-start.1) | collective-permute-done | bytes 2592 | tf_op jit(solution)/shard_map/while/body/eval_jaxpr/ppermute | solution.py:14
  880.9 18.8 %collective-permute-done.1 = f32[2,5,64]{2,1,0:T(8,128)S(1)} collective-permute-done((f32[2,5,64]{2,1,0:T(8,128)S(1)}, f32[2,5,64]{2,1,0:T(8,128)S(1)}, u32[]{:S(2)}, u32[]{:S(2)}) %collective-permute-start.1) | collective-permute-done | bytes 2592 | tf_op jit(solution)/shard_map/while/body/eval_jaxpr/ppermute | solution.py:14
  901.8 19.7 %collective-permute-done.1 = f32[2,5,64]{2,1,0:T(8,128)S(1)} collective-permute-done((f32[2,5,64]{2,1,0:T(8,128)S(1)}, f32[2,5,64]{2,1,0:T(8,128)S(1)}, u32[]{:S(2)}, u32[]{:S(2)}) %collective-permute-start.1) | collective-permute-done | bytes 2592 | tf_op jit(solution)/shard_map/while/body/eval_jaxpr/ppermute | solution.py:14
  923.5 18.6 %collective-permute-done.1 = f32[2,5,64]{2,1,0:T(8,128)S(1)} collective-permute-done((f32[2,5,64]{2,1,0:T(8,128)S(1)}, f32[2,5,64]{2,1,0:T(8,128)S(1)}, u32[]{:S(2)}, u32[]{:S(2)}) %collective-permute-start.1) | collective-permute-done | bytes 2592 | tf_op jit(solution)/shard_map/while/body/eval_jaxpr/ppermute | solution.py:14
  944.1 18.2 %collective-permute-done.1 = f32[2,5,64]{2,1,0:T(8,128)S(1)} collective-permute-done((f32[2,5,64]{2,1,0:T(8,128)S(1)}, f32[2,5,64]{2,1,0:T(8,128)S(1)}, u32[]{:S(2)}, u32[]{:S(2)}) %collective-permute-start.1) | collective-permute-done | bytes 2592 | tf_op jit(solution)/shard_map/while/body/eval_jaxpr/ppermute | solution.py:14
  964.4 15.2 %collective-permute-done.1 = f32[2,5,64]{2,1,0:T(8,128)S(1)} collective-permute-done((f32[2,5,64]{2,1,0:T(8,128)S(1)}, f32[2,5,64]{2,1,0:T(8,128)S(1)}, u32[]{:S(2)}, u32[]{:S(2)}) %collective-permute-start.1) | collective-permute-done | bytes 2592 | tf_op jit(solution)/shard_map/while/body/eval_jaxpr/ppermute | solution.py:14
  981.6 14.9 %collective-permute-done.1 = f32[2,5,64]{2,1,0:T(8,128)S(1)} collective-permute-done((f32[2,5,64]{2,1,0:T(8,128)S(1)}, f32[2,5,64]{2,1,0:T(8,128)S(1)}, u32[]{:S(2)}, u32[]{:S(2)}) %collective-permute-start.1) | collective-permute-done | bytes 2592 | tf_op jit(solution)/shard_map/while/body/eval_jaxpr/ppermute | solution.py:14
  998.5 13.8 %collective-permute-done.1 = f32[2,5,64]{2,1,0:T(8,128)S(1)} collective-permute-done((f32[2,5,64]{2,1,0:T(8,128)S(1)}, f32[2,5,64]{2,1,0:T(8,128)S(1)}, u32[]{:S(2)}, u32[]{:S(2)}) %collective-permute-start.1) | collective-permute-done | bytes 2592 | tf_op jit(solution)/shard_map/while/body/eval_jaxpr/ppermute | solution.py:14
  1068.2 14.6 %collective-permute-done.1 = f32[2,5,64]{2,1,0:T(8,128)S(1)} collective-permute-done((f32[2,5,64]{2,1,0:T(8,128)S(1)}, f32[2,5,64]{2,1,0:T(8,128)S(1)}, u32[]{:S(2)}, u32[]{:S(2)}) %collective-permute-start.1) | collective-permute-done | bytes 2592 | tf_op jit(solution)/shard_map/while/body/eval_jaxpr/ppermute | solution.py:14
  1098.6 13.5 %collective-permute-done.1 = f32[2,5,64]{2,1,0:T(8,128)S(1)} collective-permute-done((f32[2,5,64]{2,1,0:T(8,128)S(1)}, f32[2,5,64]{2,1,0:T(8,128)S(1)}, u32[]{:S(2)}, u32[]{:S(2)}) %collective-permute-start.1) | collective-permute-done | bytes 2592 | tf_op jit(solution)/shard_map/while/body/eval_jaxpr/ppermute | solution.py:14
  1114.1 13.9 %collective-permute-done.1 = f32[2,5,64]{2,1,0:T(8,128)S(1)} collective-permute-done((f32[2,5,64]{2,1,0:T(8,128)S(1)}, f32[2,5,64]{2,1,0:T(8,128)S(1)}, u32[]{:S(2)}, u32[]{:S(2)}) %collective-permute-start.1) | collective-permute-done | bytes 2592 | tf_op jit(solution)/shard_map/while/body/eval_jaxpr/ppermute | solution.py:14
  1130.1 14.0 %collective-permute-done.1 = f32[2,5,64]{2,1,0:T(8,128)S(1)} collective-permute-done((f32[2,5,64]{2,1,0:T(8,128)S(1)}, f32[2,5,64]{2,1,0:T(8,128)S(1)}, u32[]{:S(2)}, u32[]{:S(2)}) %collective-permute-start.1) | collective-permute-done | bytes 2592 | tf_op jit(solution)/shard_map/while/body/eval_jaxpr/ppermute | solution.py:14
  1154.9 74.0 %reduce-scatter.2.cloned.1.call-done = f32[64,1280]{1,0:T(8,128)} async-done(((f32[64,5120]{1,0:T(8,128)}), f32[64,1280]{1,0:T(8,128)}) %reduce-scatter.2.cloned.1.call-update) | async-done | bytes 327696 | tf_op jit(solution)/shard_map/reduce_scatter | solution.py:130
  (1326 shorter events, 417.0 us)
Async XLA Ops:
  6.5 1138.5 %all-gather.2.cloned.1.call-start = ((), (), s32[]{:S(2)}) async-start(), calls=%async_computation.1 | async-start | bytes 13312000 | tf_op jit(solution)/shard_map/all_gather | solution.py:127
  7.3 1221.6 %reduce-scatter.2.cloned.1.call-start = ((), (), s32[]{:S(2)}) async-start(), calls=%async_computation.2 | async-start | bytes 1638400 | tf_op jit(solution)/shard_map/reduce_scatter | solution.py:130
  11.9 20.8 %collective-permute-start.3 = (f32[2,5,64,128]{3,2,1,0:T(8,128)S(1)}, f32[2,5,64,128]{3,2,1,0:T(8,128)S(1)}, u32[]{:S(2)}, u32[]{:S(2)}) collective-permute-start(f32[2,5,64,128]{3,2,1,0:T(8,128)S(1)} %convolution_add_fusion.2), channel_id=1, source_target_pairs={{252,0},{0,4},{4,8},{8,12},{12,16},{16,20},{20,24},{24,28},{28,32}... | collective-permute-start | bytes 983048 | tf_op jit(solution)/shard_map/while/body/eval_jaxpr/ppermute | solution.py:14
  34.3 25.6 %collective-permute-start.3 = (f32[2,5,64,128]{3,2,1,0:T(8,128)S(1)}, f32[2,5,64,128]{3,2,1,0:T(8,128)S(1)}, u32[]{:S(2)}, u32[]{:S(2)}) collective-permute-start(f32[2,5,64,128]{3,2,1,0:T(8,128)S(1)} %convolution_add_fusion.2), channel_id=1, source_target_pairs={{252,0},{0,4},{4,8},{8,12},{12,16},{16,20},{20,24},{24,28},{28,32}... | collective-permute-start | bytes 983048 | tf_op jit(solution)/shard_map/while/body/eval_jaxpr/ppermute | solution.py:14
  34.4 25.5 %collective-permute-start = (bf16[2,5,64,128]{3,2,1,0:T(8,128)(2,1)S(1)}, bf16[2,5,64,128]{3,2,1,0:T(8,128)(2,1)S(1)}, u32[]{:S(2)}, u32[]{:S(2)}) collective-permute-start(bf16[2,5,64,128]{3,2,1,0:T(8,128)(2,1)S(1)} %copy.38), channel_id=1, source_target_pairs={{252,0},{0,4},{4,8},{8,12},{12,16},{16,20},{20,24},{24,28},{28,32}... | collective-permute-start | bytes 491528 | tf_op jit(solution)/shard_map/while/body/eval_jaxpr/ppermute | solution.py:14
  34.5 25.2 %collective-permute-start.1 = (f32[2,5,64]{2,1,0:T(8,128)S(1)}, f32[2,5,64]{2,1,0:T(8,128)S(1)}, u32[]{:S(2)}, u32[]{:S(2)}) collective-permute-start(f32[2,5,64]{2,1,0:T(8,128)S(1)} %max.11), channel_id=1, source_target_pairs={{252,0},{0,4},{4,8},{8,12},{12,16},{16,20},{20,24},{24,28},{28,32}... | collective-permute-start | bytes 7688 | tf_op jit(solution)/shard_map/while/body/eval_jaxpr/ppermute | solution.py:14
  38.2 21.6 %collective-permute-start.2 = (f32[2,5,64]{2,1,0:T(8,128)S(1)}, f32[2,5,64]{2,1,0:T(8,128)S(1)}, u32[]{:S(2)}, u32[]{:S(2)}) collective-permute-start(f32[2,5,64]{2,1,0:T(8,128)S(1)} %get-tuple-element.368), channel_id=1, source_target_pairs={{252,0},{0,4},{4,8},{8,12},{12,16},{16,20},{20,24},{24,28},{28,32}... | collective-permute-start | bytes 7688 | tf_op jit(solution)/shard_map/while/body/eval_jaxpr/ppermute | solution.py:14
  61.4 22.5 %collective-permute-start.3 = (f32[2,5,64,128]{3,2,1,0:T(8,128)S(1)}, f32[2,5,64,128]{3,2,1,0:T(8,128)S(1)}, u32[]{:S(2)}, u32[]{:S(2)}) collective-permute-start(f32[2,5,64,128]{3,2,1,0:T(8,128)S(1)} %convolution_add_fusion.2), channel_id=1, source_target_pairs={{252,0},{0,4},{4,8},{8,12},{12,16},{16,20},{20,24},{24,28},{28,32}... | collective-permute-start | bytes 983048 | tf_op jit(solution)/shard_map/while/body/eval_jaxpr/ppermute | solution.py:14
  61.5 22.4 %collective-permute-start = (bf16[2,5,64,128]{3,2,1,0:T(8,128)(2,1)S(1)}, bf16[2,5,64,128]{3,2,1,0:T(8,128)(2,1)S(1)}, u32[]{:S(2)}, u32[]{:S(2)}) collective-permute-start(bf16[2,5,64,128]{3,2,1,0:T(8,128)(2,1)S(1)} %copy.38), channel_id=1, source_target_pairs={{252,0},{0,4},{4,8},{8,12},{12,16},{16,20},{20,24},{24,28},{28,32}... | collective-permute-start | bytes 491528 | tf_op jit(solution)/shard_map/while/body/eval_jaxpr/ppermute | solution.py:14
  61.6 22.0 %collective-permute-start.1 = (f32[2,5,64]{2,1,0:T(8,128)S(1)}, f32[2,5,64]{2,1,0:T(8,128)S(1)}, u32[]{:S(2)}, u32[]{:S(2)}) collective-permute-start(f32[2,5,64]{2,1,0:T(8,128)S(1)} %max.11), channel_id=1, source_target_pairs={{252,0},{0,4},{4,8},{8,12},{12,16},{16,20},{20,24},{24,28},{28,32}... | collective-permute-start | bytes 7688 | tf_op jit(solution)/shard_map/while/body/eval_jaxpr/ppermute | solution.py:14
  63.7 20.2 %collective-permute-start.2 = (f32[2,5,64]{2,1,0:T(8,128)S(1)}, f32[2,5,64]{2,1,0:T(8,128)S(1)}, u32[]{:S(2)}, u32[]{:S(2)}) collective-permute-start(f32[2,5,64]{2,1,0:T(8,128)S(1)} %get-tuple-element.368), channel_id=1, source_target_pairs={{252,0},{0,4},{4,8},{8,12},{12,16},{16,20},{20,24},{24,28},{28,32}... | collective-permute-start | bytes 7688 | tf_op jit(solution)/shard_map/while/body/eval_jaxpr/ppermute | solution.py:14
  85.5 20.5 %collective-permute-start.3 = (f32[2,5,64,128]{3,2,1,0:T(8,128)S(1)}, f32[2,5,64,128]{3,2,1,0:T(8,128)S(1)}, u32[]{:S(2)}, u32[]{:S(2)}) collective-permute-start(f32[2,5,64,128]{3,2,1,0:T(8,128)S(1)} %convolution_add_fusion.2), channel_id=1, source_target_pairs={{252,0},{0,4},{4,8},{8,12},{12,16},{16,20},{20,24},{24,28},{28,32}... | collective-permute-start | bytes 983048 | tf_op jit(solution)/shard_map/while/body/eval_jaxpr/ppermute | solution.py:14
  85.6 20.4 %collective-permute-start = (bf16[2,5,64,128]{3,2,1,0:T(8,128)(2,1)S(1)}, bf16[2,5,64,128]{3,2,1,0:T(8,128)(2,1)S(1)}, u32[]{:S(2)}, u32[]{:S(2)}) collective-permute-start(bf16[2,5,64,128]{3,2,1,0:T(8,128)(2,1)S(1)} %copy.38), channel_id=1, source_target_pairs={{252,0},{0,4},{4,8},{8,12},{12,16},{16,20},{20,24},{24,28},{28,32}... | collective-permute-start | bytes 491528 | tf_op jit(solution)/shard_map/while/body/eval_jaxpr/ppermute | solution.py:14
  85.7 20.2 %collective-permute-start.1 = (f32[2,5,64]{2,1,0:T(8,128)S(1)}, f32[2,5,64]{2,1,0:T(8,128)S(1)}, u32[]{:S(2)}, u32[]{:S(2)}) collective-permute-start(f32[2,5,64]{2,1,0:T(8,128)S(1)} %max.11), channel_id=1, source_target_pairs={{252,0},{0,4},{4,8},{8,12},{12,16},{16,20},{20,24},{24,28},{28,32}... | collective-permute-start | bytes 7688 | tf_op jit(solution)/shard_map/while/body/eval_jaxpr/ppermute | solution.py:14
  86.5 19.5 %collective-permute-start.2 = (f32[2,5,64]{2,1,0:T(8,128)S(1)}, f32[2,5,64]{2,1,0:T(8,128)S(1)}, u32[]{:S(2)}, u32[]{:S(2)}) collective-permute-start(f32[2,5,64]{2,1,0:T(8,128)S(1)} %get-tuple-element.368), channel_id=1, source_target_pairs={{252,0},{0,4},{4,8},{8,12},{12,16},{16,20},{20,24},{24,28},{28,32}... | collective-permute-start | bytes 7688 | tf_op jit(solution)/shard_map/while/body/eval_jaxpr/ppermute | solution.py:14
  107.6 20.0 %collective-permute-start.3 = (f32[2,5,64,128]{3,2,1,0:T(8,128)S(1)}, f32[2,5,64,128]{3,2,1,0:T(8,128)S(1)}, u32[]{:S(2)}, u32[]{:S(2)}) collective-permute-start(f32[2,5,64,128]{3,2,1,0:T(8,128)S(1)} %convolution_add_fusion.2), channel_id=1, source_target_pairs={{252,0},{0,4},{4,8},{8,12},{12,16},{16,20},{20,24},{24,28},{28,32}... | collective-permute-start | bytes 983048 | tf_op jit(solution)/shard_map/while/body/eval_jaxpr/ppermute | solution.py:14
  107.7 19.9 %collective-permute-start = (bf16[2,5,64,128]{3,2,1,0:T(8,128)(2,1)S(1)}, bf16[2,5,64,128]{3,2,1,0:T(8,128)(2,1)S(1)}, u32[]{:S(2)}, u32[]{:S(2)}) collective-permute-start(bf16[2,5,64,128]{3,2,1,0:T(8,128)(2,1)S(1)} %copy.38), channel_id=1, source_target_pairs={{252,0},{0,4},{4,8},{8,12},{12,16},{16,20},{20,24},{24,28},{28,32}... | collective-permute-start | bytes 491528 | tf_op jit(solution)/shard_map/while/body/eval_jaxpr/ppermute | solution.py:14
  107.8 19.5 %collective-permute-start.1 = (f32[2,5,64]{2,1,0:T(8,128)S(1)}, f32[2,5,64]{2,1,0:T(8,128)S(1)}, u32[]{:S(2)}, u32[]{:S(2)}) collective-permute-start(f32[2,5,64]{2,1,0:T(8,128)S(1)} %max.11), channel_id=1, source_target_pairs={{252,0},{0,4},{4,8},{8,12},{12,16},{16,20},{20,24},{24,28},{28,32}... | collective-permute-start | bytes 7688 | tf_op jit(solution)/shard_map/while/body/eval_jaxpr/ppermute | solution.py:14
  149.4 20.1 %collective-permute-start.3 = (f32[2,5,64,128]{3,2,1,0:T(8,128)S(1)}, f32[2,5,64,128]{3,2,1,0:T(8,128)S(1)}, u32[]{:S(2)}, u32[]{:S(2)}) collective-permute-start(f32[2,5,64,128]{3,2,1,0:T(8,128)S(1)} %convolution_add_fusion.2), channel_id=1, source_target_pairs={{252,0},{0,4},{4,8},{8,12},{12,16},{16,20},{20,24},{24,28},{28,32}... | collective-permute-start | bytes 983048 | tf_op jit(solution)/shard_map/while/body/eval_jaxpr/ppermute | solution.py:14
  149.5 20.0 %collective-permute-start = (bf16[2,5,64,128]{3,2,1,0:T(8,128)(2,1)S(1)}, bf16[2,5,64,128]{3,2,1,0:T(8,128)(2,1)S(1)}, u32[]{:S(2)}, u32[]{:S(2)}) collective-permute-start(bf16[2,5,64,128]{3,2,1,0:T(8,128)(2,1)S(1)} %copy.38), channel_id=1, source_target_pairs={{252,0},{0,4},{4,8},{8,12},{12,16},{16,20},{20,24},{24,28},{28,32}... | collective-permute-start | bytes 491528 | tf_op jit(solution)/shard_map/while/body/eval_jaxpr/ppermute | solution.py:14
  150.2 19.3 %collective-permute-start.2 = (f32[2,5,64]{2,1,0:T(8,128)S(1)}, f32[2,5,64]{2,1,0:T(8,128)S(1)}, u32[]{:S(2)}, u32[]{:S(2)}) collective-permute-start(f32[2,5,64]{2,1,0:T(8,128)S(1)} %get-tuple-element.368), channel_id=1, source_target_pairs={{252,0},{0,4},{4,8},{8,12},{12,16},{16,20},{20,24},{24,28},{28,32}... | collective-permute-start | bytes 7688 | tf_op jit(solution)/shard_map/while/body/eval_jaxpr/ppermute | solution.py:14
  209.6 22.0 %collective-permute-start.3 = (f32[2,5,64,128]{3,2,1,0:T(8,128)S(1)}, f32[2,5,64,128]{3,2,1,0:T(8,128)S(1)}, u32[]{:S(2)}, u32[]{:S(2)}) collective-permute-start(f32[2,5,64,128]{3,2,1,0:T(8,128)S(1)} %convolution_add_fusion.2), channel_id=1, source_target_pairs={{252,0},{0,4},{4,8},{8,12},{12,16},{16,20},{20,24},{24,28},{28,32}... | collective-permute-start | bytes 983048 | tf_op jit(solution)/shard_map/while/body/eval_jaxpr/ppermute | solution.py:14
  212.0 19.5 %collective-permute-start = (bf16[2,5,64,128]{3,2,1,0:T(8,128)(2,1)S(1)}, bf16[2,5,64,128]{3,2,1,0:T(8,128)(2,1)S(1)}, u32[]{:S(2)}, u32[]{:S(2)}) collective-permute-start(bf16[2,5,64,128]{3,2,1,0:T(8,128)(2,1)S(1)} %copy.38), channel_id=1, source_target_pairs={{252,0},{0,4},{4,8},{8,12},{12,16},{16,20},{20,24},{24,28},{28,32}... | collective-permute-start | bytes 491528 | tf_op jit(solution)/shard_map/while/body/eval_jaxpr/ppermute | solution.py:14
  233.1 25.9 %collective-permute-start.3 = (f32[2,5,64,128]{3,2,1,0:T(8,128)S(1)}, f32[2,5,64,128]{3,2,1,0:T(8,128)S(1)}, u32[]{:S(2)}, u32[]{:S(2)}) collective-permute-start(f32[2,5,64,128]{3,2,1,0:T(8,128)S(1)} %convolution_add_fusion.2), channel_id=1, source_target_pairs={{252,0},{0,4},{4,8},{8,12},{12,16},{16,20},{20,24},{24,28},{28,32}... | collective-permute-start | bytes 983048 | tf_op jit(solution)/shard_map/while/body/eval_jaxpr/ppermute | solution.py:14
  233.8 25.2 %collective-permute-start = (bf16[2,5,64,128]{3,2,1,0:T(8,128)(2,1)S(1)}, bf16[2,5,64,128]{3,2,1,0:T(8,128)(2,1)S(1)}, u32[]{:S(2)}, u32[]{:S(2)}) collective-permute-start(bf16[2,5,64,128]{3,2,1,0:T(8,128)(2,1)S(1)} %copy.38), channel_id=1, source_target_pairs={{252,0},{0,4},{4,8},{8,12},{12,16},{16,20},{20,24},{24,28},{28,32}... | collective-permute-start | bytes 491528 | tf_op jit(solution)/shard_map/while/body/eval_jaxpr/ppermute | solution.py:14
  236.3 22.5 %collective-permute-start.1 = (f32[2,5,64]{2,1,0:T(8,128)S(1)}, f32[2,5,64]{2,1,0:T(8,128)S(1)}, u32[]{:S(2)}, u32[]{:S(2)}) collective-permute-start(f32[2,5,64]{2,1,0:T(8,128)S(1)} %max.11), channel_id=1, source_target_pairs={{252,0},{0,4},{4,8},{8,12},{12,16},{16,20},{20,24},{24,28},{28,32}... | collective-permute-start | bytes 7688 | tf_op jit(solution)/shard_map/while/body/eval_jaxpr/ppermute | solution.py:14
  236.7 22.4 %collective-permute-start.2 = (f32[2,5,64]{2,1,0:T(8,128)S(1)}, f32[2,5,64]{2,1,0:T(8,128)S(1)}, u32[]{:S(2)}, u32[]{:S(2)}) collective-permute-start(f32[2,5,64]{2,1,0:T(8,128)S(1)} %get-tuple-element.368), channel_id=1, source_target_pairs={{252,0},{0,4},{4,8},{8,12},{12,16},{16,20},{20,24},{24,28},{28,32}... | collective-permute-start | bytes 7688 | tf_op jit(solution)/shard_map/while/body/eval_jaxpr/ppermute | solution.py:14
  260.6 21.0 %collective-permute-start.3 = (f32[2,5,64,128]{3,2,1,0:T(8,128)S(1)}, f32[2,5,64,128]{3,2,1,0:T(8,128)S(1)}, u32[]{:S(2)}, u32[]{:S(2)}) collective-permute-start(f32[2,5,64,128]{3,2,1,0:T(8,128)S(1)} %convolution_add_fusion.2), channel_id=1, source_target_pairs={{252,0},{0,4},{4,8},{8,12},{12,16},{16,20},{20,24},{24,28},{28,32}... | collective-permute-start | bytes 983048 | tf_op jit(solution)/shard_map/while/body/eval_jaxpr/ppermute | solution.py:14
  260.7 20.9 %collective-permute-start = (bf16[2,5,64,128]{3,2,1,0:T(8,128)(2,1)S(1)}, bf16[2,5,64,128]{3,2,1,0:T(8,128)(2,1)S(1)}, u32[]{:S(2)}, u32[]{:S(2)}) collective-permute-start(bf16[2,5,64,128]{3,2,1,0:T(8,128)(2,1)S(1)} %copy.38), channel_id=1, source_target_pairs={{252,0},{0,4},{4,8},{8,12},{12,16},{16,20},{20,24},{24,28},{28,32}... | collective-permute-start | bytes 491528 | tf_op jit(solution)/shard_map/while/body/eval_jaxpr/ppermute | solution.py:14
  260.8 20.6 %collective-permute-start.1 = (f32[2,5,64]{2,1,0:T(8,128)S(1)}, f32[2,5,64]{2,1,0:T(8,128)S(1)}, u32[]{:S(2)}, u32[]{:S(2)}) collective-permute-start(f32[2,5,64]{2,1,0:T(8,128)S(1)} %max.11), channel_id=1, source_target_pairs={{252,0},{0,4},{4,8},{8,12},{12,16},{16,20},{20,24},{24,28},{28,32}... | collective-permute-start | bytes 7688 | tf_op jit(solution)/shard_map/while/body/eval_jaxpr/ppermute | solution.py:14
  260.9 20.7 %collective-permute-start.2 = (f32[2,5,64]{2,1,0:T(8,128)S(1)}, f32[2,5,64]{2,1,0:T(8,128)S(1)}, u32[]{:S(2)}, u32[]{:S(2)}) collective-permute-start(f32[2,5,64]{2,1,0:T(8,128)S(1)} %get-tuple-element.368), channel_id=1, source_target_pairs={{252,0},{0,4},{4,8},{8,12},{12,16},{16,20},{20,24},{24,28},{28,32}... | collective-permute-start | bytes 7688 | tf_op jit(solution)/shard_map/while/body/eval_jaxpr/ppermute | solution.py:14
  283.1 26.1 %collective-permute-start.3 = (f32[2,5,64,128]{3,2,1,0:T(8,128)S(1)}, f32[2,5,64,128]{3,2,1,0:T(8,128)S(1)}, u32[]{:S(2)}, u32[]{:S(2)}) collective-permute-start(f32[2,5,64,128]{3,2,1,0:T(8,128)S(1)} %convolution_add_fusion.2), channel_id=1, source_target_pairs={{252,0},{0,4},{4,8},{8,12},{12,16},{16,20},{20,24},{24,28},{28,32}... | collective-permute-start | bytes 983048 | tf_op jit(solution)/shard_map/while/body/eval_jaxpr/ppermute | solution.py:14
  283.2 26.0 %collective-permute-start = (bf16[2,5,64,128]{3,2,1,0:T(8,128)(2,1)S(1)}, bf16[2,5,64,128]{3,2,1,0:T(8,128)(2,1)S(1)}, u32[]{:S(2)}, u32[]{:S(2)}) collective-permute-start(bf16[2,5,64,128]{3,2,1,0:T(8,128)(2,1)S(1)} %copy.38), channel_id=1, source_target_pairs={{252,0},{0,4},{4,8},{8,12},{12,16},{16,20},{20,24},{24,28},{28,32}... | collective-permute-start | bytes 491528 | tf_op jit(solution)/shard_map/while/body/eval_jaxpr/ppermute | solution.py:14
  283.3 25.8 %collective-permute-start.1 = (f32[2,5,64]{2,1,0:T(8,128)S(1)}, f32[2,5,64]{2,1,0:T(8,128)S(1)}, u32[]{:S(2)}, u32[]{:S(2)}) collective-permute-start(f32[2,5,64]{2,1,0:T(8,128)S(1)} %max.11), channel_id=1, source_target_pairs={{252,0},{0,4},{4,8},{8,12},{12,16},{16,20},{20,24},{24,28},{28,32}... | collective-permute-start | bytes 7688 | tf_op jit(solution)/shard_map/while/body/eval_jaxpr/ppermute | solution.py:14
  283.4 25.9 %collective-permute-start.2 = (f32[2,5,64]{2,1,0:T(8,128)S(1)}, f32[2,5,64]{2,1,0:T(8,128)S(1)}, u32[]{:S(2)}, u32[]{:S(2)}) collective-permute-start(f32[2,5,64]{2,1,0:T(8,128)S(1)} %get-tuple-element.368), channel_id=1, source_target_pairs={{252,0},{0,4},{4,8},{8,12},{12,16},{16,20},{20,24},{24,28},{28,32}... | collective-permute-start | bytes 7688 | tf_op jit(solution)/shard_map/while/body/eval_jaxpr/ppermute | solution.py:14
  660.7 19.8 %collective-permute-start.3 = (f32[2,5,64,128]{3,2,1,0:T(8,128)S(1)}, f32[2,5,64,128]{3,2,1,0:T(8,128)S(1)}, u32[]{:S(2)}, u32[]{:S(2)}) collective-permute-start(f32[2,5,64,128]{3,2,1,0:T(8,128)S(1)} %convolution_add_fusion.2), channel_id=1, source_target_pairs={{252,0},{0,4},{4,8},{8,12},{12,16},{16,20},{20,24},{24,28},{28,32}... | collective-permute-start | bytes 983048 | tf_op jit(solution)/shard_map/while/body/eval_jaxpr/ppermute | solution.py:14
  660.8 19.7 %collective-permute-start = (bf16[2,5,64,128]{3,2,1,0:T(8,128)(2,1)S(1)}, bf16[2,5,64,128]{3,2,1,0:T(8,128)(2,1)S(1)}, u32[]{:S(2)}, u32[]{:S(2)}) collective-permute-start(bf16[2,5,64,128]{3,2,1,0:T(8,128)(2,1)S(1)} %copy.38), channel_id=1, source_target_pairs={{252,0},{0,4},{4,8},{8,12},{12,16},{16,20},{20,24},{24,28},{28,32}... | collective-permute-start | bytes 491528 | tf_op jit(solution)/shard_map/while/body/eval_jaxpr/ppermute | solution.py:14
  660.8 19.4 %collective-permute-start.1 = (f32[2,5,64]{2,1,0:T(8,128)S(1)}, f32[2,5,64]{2,1,0:T(8,128)S(1)}, u32[]{:S(2)}, u32[]{:S(2)}) collective-permute-start(f32[2,5,64]{2,1,0:T(8,128)S(1)} %max.11), channel_id=1, source_target_pairs={{252,0},{0,4},{4,8},{8,12},{12,16},{16,20},{20,24},{24,28},{28,32}... | collective-permute-start | bytes 7688 | tf_op jit(solution)/shard_map/while/body/eval_jaxpr/ppermute | solution.py:14
  660.9 19.5 %collective-permute-start.2 = (f32[2,5,64]{2,1,0:T(8,128)S(1)}, f32[2,5,64]{2,1,0:T(8,128)S(1)}, u32[]{:S(2)}, u32[]{:S(2)}) collective-permute-start(f32[2,5,64]{2,1,0:T(8,128)S(1)} %get-tuple-element.368), channel_id=1, source_target_pairs={{252,0},{0,4},{4,8},{8,12},{12,16},{16,20},{20,24},{24,28},{28,32}... | collective-permute-start | bytes 7688 | tf_op jit(solution)/shard_map/while/body/eval_jaxpr/ppermute | solution.py:14
  682.0 20.2 %collective-permute-start.3 = (f32[2,5,64,128]{3,2,1,0:T(8,128)S(1)}, f32[2,5,64,128]{3,2,1,0:T(8,128)S(1)}, u32[]{:S(2)}, u32[]{:S(2)}) collective-permute-start(f32[2,5,64,128]{3,2,1,0:T(8,128)S(1)} %convolution_add_fusion.2), channel_id=1, source_target_pairs={{252,0},{0,4},{4,8},{8,12},{12,16},{16,20},{20,24},{24,28},{28,32}... | collective-permute-start | bytes 983048 | tf_op jit(solution)/shard_map/while/body/eval_jaxpr/ppermute | solution.py:14
  682.1 20.1 %collective-permute-start = (bf16[2,5,64,128]{3,2,1,0:T(8,128)(2,1)S(1)}, bf16[2,5,64,128]{3,2,1,0:T(8,128)(2,1)S(1)}, u32[]{:S(2)}, u32[]{:S(2)}) collective-permute-start(bf16[2,5,64,128]{3,2,1,0:T(8,128)(2,1)S(1)} %copy.38), channel_id=1, source_target_pairs={{252,0},{0,4},{4,8},{8,12},{12,16},{16,20},{20,24},{24,28},{28,32}... | collective-permute-start | bytes 491528 | tf_op jit(solution)/shard_map/while/body/eval_jaxpr/ppermute | solution.py:14
  682.2 19.9 %collective-permute-start.1 = (f32[2,5,64]{2,1,0:T(8,128)S(1)}, f32[2,5,64]{2,1,0:T(8,128)S(1)}, u32[]{:S(2)}, u32[]{:S(2)}) collective-permute-start(f32[2,5,64]{2,1,0:T(8,128)S(1)} %max.11), channel_id=1, source_target_pairs={{252,0},{0,4},{4,8},{8,12},{12,16},{16,20},{20,24},{24,28},{28,32}... | collective-permute-start | bytes 7688 | tf_op jit(solution)/shard_map/while/body/eval_jaxpr/ppermute | solution.py:14
  682.3 19.9 %collective-permute-start.2 = (f32[2,5,64]{2,1,0:T(8,128)S(1)}, f32[2,5,64]{2,1,0:T(8,128)S(1)}, u32[]{:S(2)}, u32[]{:S(2)}) collective-permute-start(f32[2,5,64]{2,1,0:T(8,128)S(1)} %get-tuple-element.368), channel_id=1, source_target_pairs={{252,0},{0,4},{4,8},{8,12},{12,16},{16,20},{20,24},{24,28},{28,32}... | collective-permute-start | bytes 7688 | tf_op jit(solution)/shard_map/while/body/eval_jaxpr/ppermute | solution.py:14
  880.5 19.3 %collective-permute-start.3 = (f32[2,5,64,128]{3,2,1,0:T(8,128)S(1)}, f32[2,5,64,128]{3,2,1,0:T(8,128)S(1)}, u32[]{:S(2)}, u32[]{:S(2)}) collective-permute-start(f32[2,5,64,128]{3,2,1,0:T(8,128)S(1)} %convolution_add_fusion.2), channel_id=1, source_target_pairs={{252,0},{0,4},{4,8},{8,12},{12,16},{16,20},{20,24},{24,28},{28,32}... | collective-permute-start | bytes 983048 | tf_op jit(solution)/shard_map/while/body/eval_jaxpr/ppermute | solution.py:14
  901.4 20.1 %collective-permute-start.3 = (f32[2,5,64,128]{3,2,1,0:T(8,128)S(1)}, f32[2,5,64,128]{3,2,1,0:T(8,128)S(1)}, u32[]{:S(2)}, u32[]{:S(2)}) collective-permute-start(f32[2,5,64,128]{3,2,1,0:T(8,128)S(1)} %convolution_add_fusion.2), channel_id=1, source_target_pairs={{252,0},{0,4},{4,8},{8,12},{12,16},{16,20},{20,24},{24,28},{28,32}... | collective-permute-start | bytes 983048 | tf_op jit(solution)/shard_map/while/body/eval_jaxpr/ppermute | solution.py:14
  901.5 20.0 %collective-permute-start = (bf16[2,5,64,128]{3,2,1,0:T(8,128)(2,1)S(1)}, bf16[2,5,64,128]{3,2,1,0:T(8,128)(2,1)S(1)}, u32[]{:S(2)}, u32[]{:S(2)}) collective-permute-start(bf16[2,5,64,128]{3,2,1,0:T(8,128)(2,1)S(1)} %copy.38), channel_id=1, source_target_pairs={{252,0},{0,4},{4,8},{8,12},{12,16},{16,20},{20,24},{24,28},{28,32}... | collective-permute-start | bytes 491528 | tf_op jit(solution)/shard_map/while/body/eval_jaxpr/ppermute | solution.py:14
  901.6 19.9 %collective-permute-start.1 = (f32[2,5,64]{2,1,0:T(8,128)S(1)}, f32[2,5,64]{2,1,0:T(8,128)S(1)}, u32[]{:S(2)}, u32[]{:S(2)}) collective-permute-start(f32[2,5,64]{2,1,0:T(8,128)S(1)} %max.11), channel_id=1, source_target_pairs={{252,0},{0,4},{4,8},{8,12},{12,16},{16,20},{20,24},{24,28},{28,32}... | collective-permute-start | bytes 7688 | tf_op jit(solution)/shard_map/while/body/eval_jaxpr/ppermute | solution.py:14
  901.7 19.9 %collective-permute-start.2 = (f32[2,5,64]{2,1,0:T(8,128)S(1)}, f32[2,5,64]{2,1,0:T(8,128)S(1)}, u32[]{:S(2)}, u32[]{:S(2)}) collective-permute-start(f32[2,5,64]{2,1,0:T(8,128)S(1)} %get-tuple-element.368), channel_id=1, source_target_pairs={{252,0},{0,4},{4,8},{8,12},{12,16},{16,20},{20,24},{24,28},{28,32}... | collective-permute-start | bytes 7688 | tf_op jit(solution)/shard_map/while/body/eval_jaxpr/ppermute | solution.py:14
  (213 other events, 3063.5 us)
Sparse Core Ops, SparseCore 0:
  9.1 325.5 all-gather.1
  1155.0 73.8 reduce-scatter.1
where the time goes:
time: 1240 us
  waiting for transfers between devices  1010 us (81%)
  starting transfers between devices  93.3 us (8%)
  matrix products  63.8 us (5%)
  other arithmetic  39 us (3%)
  between operations  13.5 us (1%)
    ppermute x256, waiting for transfers between devices, passed_along(): return lax.ppermute(block, axis, route)  938 us
    ppermute x256, starting transfers between devices, passed_along(): return lax.ppermute(block, axis, route)  93.3 us
    reduce_scatter x1, waiting for transfers between devices, on_device(): lax.psum_scatter(terms, 'grp', scatter_dimension=1, tiled=True)  74 us
    reduce_sum x64, other arithmetic, tile_update(): running_sum = running_sum * rescale + jnp.sum(weights, axis=-1)  27.4 us
    dot_general x64, matrix products, tile_update(): jnp.einsum('hpqd,hkd->hpqk', rotated, keys, preferred_element_type=jnp.fl...  27.2 us
    dot_general x64, matrix products, tile_update(): jnp.einsum('hpqk,hkd->hpqd', weights.astype(jnp.bfloat16), values, prefer...  26.1 us
  transfers between devices with their start and end apart: 258, of which 129 were waited for; matrix products, arithmetic and copies ran while one was open for 8% of the time, Pallas kernels for 0%

commit v1 on v0

v1 whole, which is shorter than its diff:
```python
import functools
import math

import jax
import jax.numpy as jnp
from jax import lax
from jax.experimental import pallas as pl
from jax.experimental.pallas import tpu as pltpu
from jax.sharding import Mesh
from jax.sharding import PartitionSpec as P

NEG_FILL = -1e30
LOG2E = math.log2(math.e)
VMEM_LIMIT = 48 * 1024 * 1024

Y, X, Z = "y", "x_lo", "z"
PLANE = (Y, X)
GRP = ("x_hi", "core")


def hadamard(order):
    index = jnp.arange(order, dtype=jnp.int32)
    common = index[:, None] & index[None, :]
    parity = jnp.zeros((order, order), jnp.int32)
    for shift_bit in range(int(order).bit_length()):
        parity = parity ^ common >> shift_bit & 1
    return jnp.where(parity == 1, -1.0, 1.0).astype(jnp.float32)


def dequantize_kernel(codes_ref, scales_ref, tail_ref, out_ref):
    kinds, groups, length, width = codes_ref.shape
    parts = scales_ref.shape[2]
    for kind in range(kinds):
        for g in range(groups):
            scales = scales_ref[kind, g]
            spread = jnp.concatenate(
                [
                    jnp.broadcast_to(scales[i : i + 1], (width // parts, length))
                    for i in range(parts)
                ],
                axis=0,
            )
            values = (codes_ref[kind, g].astype(jnp.float32) - 7.5) * spread.T
            out_ref[pl.ds((kind * groups + g) * length, length), :] = values.astype(jnp.bfloat16)
    out_ref[pl.ds(kinds * groups * length, tail_ref.shape[0]), :] = tail_ref[...]


def dequantize(codes, scales, tail):
    kinds, groups, length, width = codes.shape
    rows = kinds * groups * length + tail.shape[0]
    return pl.pallas_call(
        dequantize_kernel,
        out_shape=jax.ShapeDtypeStruct((rows, width), jnp.bfloat16),
        compiler_params=pltpu.CompilerParams(vmem_limit_bytes=VMEM_LIMIT),
        name="dequantize",
    )(codes, scales, tail)


def rotate_kernel(queries_ref, table_ref, out_ref):
    copies, heads, _, width = out_ref.shape
    scale = LOG2E / width
    for h in range(heads):
        turned = jnp.dot(
            queries_ref[:, h * width : (h + 1) * width],
            table_ref[...],
            preferred_element_type=jnp.float32,
        )
        turned = (turned * scale).astype(jnp.bfloat16)
        for copy in range(copies):
            out_ref[copy, h] = turned


def rotate(queries, table, copies):
    rows, columns = queries.shape
    width = table.shape[0]
    return pl.pallas_call(
        rotate_kernel,
        out_shape=jax.ShapeDtypeStruct((copies, columns // width, rows, width), jnp.bfloat16),
        compiler_params=pltpu.CompilerParams(vmem_limit_bytes=VMEM_LIMIT),
        name="rotate",
    )(queries, table)


def attend_kernel(shards, per_group, carried, last, reach_ref, q_ref, *refs):
    kv = refs[: 2 * shards]
    refs = refs[2 * shards :]
    if carried:
        o_in, lse_in = refs[:2]
        refs = refs[2:]
    blocks, _, rows, width = q_ref.shape
    tokens = rows // per_group
    g, tile = pl.program_id(0), pl.program_id(1)
    length = kv[0].shape[0]
    page = 128
    pages = length // page
    groups = pl.num_programs(0)
    all_blocks = blocks * pl.num_programs(1)
    ahead = lax.broadcasted_iota(jnp.int32, (tokens, page), 1) - lax.broadcasted_iota(
        jnp.int32, (tokens, page), 0
    )

    def block(i, _):
        q = q_ref[i, 0]
        parts = []
        for s in range(shards):
            scores = lax.dot_general(
                q, kv[2 * s][...], (((1,), (1,)), ((), ())), preferred_element_type=jnp.float32
            )
            for p in range(pages):
                reach = reach_ref[((s * groups + g) * all_blocks + tile * blocks + i) * pages + p]
                x = scores[:, p * page : (p + 1) * page].reshape(per_group, tokens, page)
                x = jnp.where((ahead <= reach)[None], x, NEG_FILL)
                parts.append(x.reshape(rows, page))
        top = functools.reduce(jnp.maximum, parts)
        top = jnp.max(top, axis=1, keepdims=True)
        if carried:
            lse = lse_in[i, 0]
            top = jnp.maximum(lse, top)
        else:
            top = jnp.broadcast_to(top, (rows, page))
        total = jnp.zeros((rows, page), jnp.float32)
        out = jnp.zeros((rows, width), jnp.float32)
        for s in range(shards):
            weights = [jnp.exp2(x - top) for x in parts[s * pages : (s + 1) * pages]]
            total = total + functools.reduce(jnp.add, weights)
            weights = jnp.concatenate([w.astype(jnp.bfloat16) for w in weights], axis=1)
            out = out + jnp.dot(weights, kv[2 * s + 1][...], preferred_element_type=jnp.float32)
        total = jnp.sum(total, axis=1, keepdims=True)
        if carried:
            kept = jnp.exp2(lse - top)
            total = total + kept
            out = out + kept * o_in[i, 0]
        out = out / total
        lse = top + jnp.log2(total)
        if not last:
            o_out, lse_out = refs
            o_out[i, 0] = out
            lse_out[i, 0] = lse
        else:
            (packed,) = refs
            packed[i, 0, pl.ds(0, rows), :] = out.astype(jnp.bfloat16)
            across = []
            for h in range(per_group):
                column = lse[h * tokens : (h + 1) * tokens]
                across.append(
                    jnp.sum(jnp.where(ahead == 0, column, 0.0), axis=0, keepdims=True)
                )
            across.append(jnp.zeros((8 - per_group, page), jnp.float32))
            across = jnp.concatenate(across, axis=0)
            high = across.astype(jnp.bfloat16).astype(jnp.float32)
            middle = (across - high).astype(jnp.bfloat16).astype(jnp.float32)
            low = across - high - middle
            tail = jnp.concatenate([high, middle, low, jnp.zeros_like(low)], axis=0)
            packed[i, 0, pl.ds(rows, 32), :] = tail.astype(jnp.bfloat16)
        return 0

    lax.fori_loop(0, blocks, block, 0, unroll=2)


def attend(q, shards, reach, carry, per_group, last):
    all_blocks, groups, rows, width = q.shape
    length = 512
    n = 4
    tiles = all_blocks // n

    def per_block(height):
        return pl.BlockSpec((n, 1, height, width), lambda g, t, reach: (t, g, 0, 0))

    in_specs = [per_block(rows)]
    operands = [q]
    for (keys, k_at), (values, v_at) in shards:
        in_specs.append(pl.BlockSpec((length, width), lambda g, t, reach, k_at=k_at: (k_at + g, 0)))
        in_specs.append(pl.BlockSpec((length, width), lambda g, t, reach, v_at=v_at: (v_at + g, 0)))
        operands += [keys, values]
    if carry is not None:
        in_specs += [per_block(rows), per_block(rows)]
        operands += list(carry)
    if last:
        out_shape = jax.ShapeDtypeStruct((all_blocks, groups, rows + 32, width), jnp.bfloat16)
        out_specs = per_block(rows + 32)
    else:
        out_shape = [jax.ShapeDtypeStruct((all_blocks, groups, rows, width), jnp.float32)] * 2
        out_specs = [per_block(rows)] * 2
    scores = all_blocks * groups * rows * length * len(shards)
    return pl.pallas_call(
        functools.partial(attend_kernel, len(shards), per_group, carry is not None, last),
        grid_spec=pltpu.PrefetchScalarGridSpec(
            num_scalar_prefetch=1,
            grid=(groups, tiles),
            in_specs=in_specs,
            out_specs=out_specs,
        ),
        out_shape=out_shape,
        compiler_params=pltpu.CompilerParams(vmem_limit_bytes=VMEM_LIMIT),
        cost_estimate=pl.CostEstimate(
            flops=8 * scores * width, bytes_accessed=8 * 1024 * 1024, transcendentals=scores
        ),
        name="attend",
    )(reach, *operands)


def combine_kernel(per_group, packed_ref, table_ref, out_ref):
    sources, _, height, width = packed_ref.shape
    rows = height - 32
    tokens = rows // per_group
    tail = packed_ref[:, 0, pl.ds(rows, 32), :].astype(jnp.float32)
    lse = tail[:, 0:8] + tail[:, 8:16] + tail[:, 16:24]
    weights = jnp.exp2(lse - jnp.max(lse, axis=0, keepdims=True))
    weights = weights / jnp.sum(weights, axis=0, keepdims=True)
    weights = weights.reshape(sources * 8, width).T
    for h in range(per_group):
        attended = jnp.zeros((tokens, width), jnp.float32)
        for e in range(sources):
            part = packed_ref[e, 0, pl.ds(h * tokens, tokens), :].astype(jnp.float32)
            attended = attended + part * weights[:tokens, e * 8 + h : e * 8 + h + 1]
        restored = jnp.dot(
            attended,
            table_ref[...],
            preferred_element_type=jnp.float32,
            precision=lax.Precision.HIGHEST,
        )
        restored = (restored * (1.0 / math.sqrt(width))).astype(jnp.bfloat16)
        for copy in range(out_ref.shape[0]):
            out_ref[copy, :, h * width : (h + 1) * width] = restored


def combine(packed, table, per_group, copies):
    sources, groups, height, width = packed.shape
    tokens = (height - 32) // per_group
    return pl.pallas_call(
        functools.partial(combine_kernel, per_group),
        grid=(groups,),
        in_specs=[
            pl.BlockSpec((sources, 1, height, width), lambda g: (0, g, 0, 0)),
            pl.BlockSpec((width, width), lambda g: (0, 0)),
        ],
        out_specs=pl.BlockSpec((copies, tokens, per_group * width), lambda g: (0, 0, g)),
        out_shape=jax.ShapeDtypeStruct((copies, tokens, groups * per_group * width), jnp.bfloat16),
        compiler_params=pltpu.CompilerParams(vmem_limit_bytes=VMEM_LIMIT),
        name="combine",
    )(packed, table)


def on_device(queries, cache_codes, cache_scales, pattern, out_weight):
    ny, nx, nz = (lax.axis_size(a) for a in (Y, X, Z))
    y, x, z = (lax.axis_index(a) for a in (Y, X, Z))
    plane = ny * nx
    block_rows = queries.shape[0]
    _, groups, shard_len, width = cache_codes.shape
    heads = queries.shape[1] // width
    per_group = heads // groups
    pages = pattern.shape[2]
    page = shard_len // pages
    blocks = pattern.shape[1]
    total_len = shard_len * blocks
    total_q = block_rows * blocks
    table = hadamard(width)

    weight_rows = lax.all_gather(out_weight.T, Z, axis=0, tiled=True)

    tail = pattern.reshape(-1, width).astype(jnp.bfloat16)
    marks = tail.shape[0]
    tail = jnp.concatenate([tail, jnp.zeros((16 - marks, width), jnp.bfloat16)], axis=0)
    own = dequantize(cache_codes, cache_scales, tail)
    cut = groups * shard_len

    def moved(block, step):
        return lax.ppermute(block, Z, [(i, (i + step) % nz) for i in range(nz)])

    rotated = rotate(queries, table.astype(jnp.bfloat16), plane)
    gathered = lax.all_to_all(rotated, PLANE, 0, 0)
    q = gathered.reshape(plane, groups, per_group * block_rows, width)

    block_at = jnp.arange(plane, dtype=jnp.int32) * nz + z
    first_query = total_len - total_q + block_at * block_rows

    def reach_of(rows, distance):
        shard = (y * nx + x) * nz + (z - distance) % nz
        kept = rows.astype(jnp.float32).reshape(groups, plane, nz, pages)
        kept = lax.dynamic_index_in_dim(kept, z, 2, keepdims=False)
        first_key = shard * shard_len + jnp.arange(pages, dtype=jnp.int32) * page
        causal = first_query[:, None] - first_key[None, :]
        causal = jnp.clip(causal, -2 * page, 2 * page)
        return jnp.where(kept > 0.5, causal[None], -2 * page).reshape(-1)

    def whole(block):
        return ((block, 0), (block, groups))

    def marks_of(block):
        return block[2 * cut : 2 * cut + marks]

    ahead, behind = own, own
    carry = None
    for distance in range(1, nz // 2):
        ahead, behind = moved(ahead, 1), moved(behind, -1)
        shards = [whole(ahead), whole(behind)]
        reach = [reach_of(marks_of(ahead), distance), reach_of(marks_of(behind), -distance)]
        if carry is None:
            shards = [whole(own)] + shards
            reach = [reach_of(marks_of(own), 0)] + reach
        carry = attend(q, shards, jnp.concatenate(reach), carry, per_group, False)
    far_keys, far_values = moved(ahead[:cut], 1), moved(behind[cut:], -1)
    reach = reach_of(far_values[cut : cut + marks], nz // 2)
    packed = attend(q, [((far_keys, 0), (far_values, 0))], reach, carry, per_group, True)

    received = lax.all_to_all(packed, PLANE, 0, 0)
    restored = combine(received, table, per_group, plane)
    restored = lax.all_to_all(restored, PLANE, 0, 0)
    terms = lax.dot_general(
        restored.reshape(plane * block_rows, heads * width),
        weight_rows,
        (((1,), (1,)), ((), ())),
        preferred_element_type=jnp.float32,
    ).astype(jnp.bfloat16)
    columns = terms.shape[1]
    terms = lax.all_to_all(terms.reshape(ny, nx, block_rows, columns), GRP, 0, 0)
    share = jnp.sum(terms.astype(jnp.float32), axis=0).astype(jnp.bfloat16)

    same = lax.dynamic_index_in_dim(share, x, 0, keepdims=False)
    other = lax.dynamic_index_in_dim(share, 1 - x, 0, keepdims=False)
    where = [(a, b, c) for a in range(ny) for b in range(nx) for c in range(ny)]

    def flat(a, b, c):
        return (a * nx + b) * ny + c

    same = lax.ppermute(
        same, (Y, X) + GRP, [(flat(a, b, c), flat(c, b, a)) for a, b, c in where]
    )
    other = lax.ppermute(
        other, (Y, X) + GRP, [(flat(a, b, c), flat(c, 1 - b, a)) for a, b, c in where]
    )
    left = jnp.where(x == 0, same, other)
    right = jnp.where(x == 0, other, same)
    return jnp.concatenate([left, right], axis=1)


def solution(mesh):
    parts = Mesh(mesh.devices.reshape(4, 2, 8, 2, 2), (Y, X, Z) + GRP)
    ctx = (Y, X, Z)
    placed = (
        P(ctx, GRP),
        P(None, GRP, ctx, None),
        P(None, GRP, None, ctx),
        P(GRP, None, ctx),
        P(GRP, ctx),
    )
    return jax.shard_map(
        on_device, mesh=parts, in_specs=placed, out_specs=P(ctx, GRP), check_vma=False
    )
```

time: 1240 us -> 237 us (0.19)
  waiting for transfers between devices: 1010 us -> 65.9 us
  Pallas kernels: 0 us -> 62.7 us
  matrix products: 63.8 us -> 3.49 us
  starting transfers between devices: 93.3 us -> 45.6 us
  other arithmetic: 39 us -> 16.2 us
  local copies, waits for them, and re-layouts: 8.99 us -> 27.8 us
    ppermute x256 -> x10, waiting for transfers between devices: 938 us -> 23.8 us  [the longest x8 18 us: moved(): return lax.ppermute(block, Z, [(i, (i + step) % nz) for i in range(nz)])]
    reduce_scatter x1 -> x0, waiting for transfers between devices: 74 us -> none  [on_device(): lax.psum_scatter(terms, 'grp', scatter_dimension=1, tiled=True)]
    ppermute x256 -> x10, starting transfers between devices: 93.3 us -> 24.5 us  [the longest x8 16.2 us: moved(): return lax.ppermute(block, Z, [(i, (i + step) % nz) for i in range(nz)])]
    pallas_call x0 -> x7, Pallas kernels: none -> 62.7 us  [the longest x4 58.2 us: attend(): pl.pallas_call(functools.partial(attend_kernel, len(shards), per_group, c...]
    dot_general x131 -> x1, matrix products: 63.8 us -> 3.49 us  [on_device(): lax.dot_general(restored.reshape(plane * block_rows, heads * width), weig...]
    all_to_all x0 -> x4, waiting for transfers between devices: none -> 41.3 us  [the longest x1 17.1 us: on_device(): received = lax.all_to_all(packed, PLANE, 0, 0)]
    reduce_sum x64 -> x1, other arithmetic: 27.4 us -> 0.1 us  [on_device(): share = jnp.sum(terms.astype(jnp.float32), axis=0).astype(jnp.bfloat16)]
    all_to_all x0 -> x4, starting transfers between devices: none -> 21.2 us  [the longest x1 5.93 us: on_device(): gathered = lax.all_to_all(rotated, PLANE, 0, 0)]
  transfers between devices with their start and end apart: 258 -> 15, of which waited for: 129 -> 8; matrix products, arithmetic and copies ran while one was open for 8% -> 13% of each run, Pallas kernels for 0% -> 26%
where the time goes in v1:
time: 237 us; the launch traced here: 236 us
  waiting for transfers between devices  65.9 us (28%)
  Pallas kernels  62.7 us (26%)
  starting transfers between devices  45.6 us (19%)
  local copies, waits for them, and re-layouts  27.8 us (12%)
  other arithmetic  16.2 us (7%)
  between operations  13.9 us (6%)
  matrix products  3.49 us (1%)
    pallas_call x4, Pallas kernels, attend(): pl.pallas_call(functools.partial(attend_kernel, len(shards), per_group, c...  58.2 us
    ppermute x8, waiting for transfers between devices, moved(): return lax.ppermute(block, Z, [(i, (i + step) % nz) for i in range(nz)])  18 us
    all_to_all x1, waiting for transfers between devices, on_device(): received = lax.all_to_all(packed, PLANE, 0, 0)  17.1 us
    ppermute x8, starting transfers between devices, moved(): return lax.ppermute(block, Z, [(i, (i + step) % nz) for i in range(nz)])  16.2 us
    all_to_all x1, waiting for transfers between devices, on_device(): restored = lax.all_to_all(restored, PLANE, 0, 0)  15.7 us
    unnamed x28, local copies, waits for them, and re-layouts  12.6 us
    all_to_all x1, waiting for transfers between devices, on_device(): lax.all_to_all(terms.reshape(ny, nx, block_rows, columns), GRP, 0, 0)  8.59 us
    select_n x8, other arithmetic, reach_of(): return jnp.where(kept > 0.5, causal[None], -2 * page).reshape(-1)  6.25 us
  transfers between devices with their start and end apart: 15, of which 8 were waited for; matrix products, arithmetic and copies ran while one was open for 13% of the time, Pallas kernels for 26%

profile of v1, /device:TPU:6, one launch (start us, length us, event | category | flops | bytes accessed | tf_op | source)
XLA Modules:
  0.0 235.7 jit_solution(7810742574360353014)
XLA Ops:
  7.5 1.2 copy-done
  9.8 5.9 %collective-permute-start = (bf16[2064,128]{1,0:T(8,128)(2,1)S(1)}, bf16[2064,128]{1,0:T(8,128)(2,1)S(1)}, u32[]{:S(2)}, u32[]{:S(2)}) collective-permute-start(bf16[2064,128]{1,0:T(8,128)(2,1)S(1)} %dequantize.1.refs_0_.refs_1_), channel_id=1, source_target_pairs={{0,28},{4,0},{8,4},{12,8},{16,12},{20,16},{24,20},{28,24},{1,29},{... | collective-permute-start | bytes 1585160 | tf_op jit(solution)/shard_map/ppermute | solution.py:268
  15.8 1.3 rotate.1
  17.2 5.9 %all-to-all-start = ((bf16[8,10,64,128]{3,2,1,0:T(8,128)(2,1)}), bf16[8,10,64,128]{3,2,1,0:T(8,128)(2,1)S(1)}, u32[]{:S(2)}, u32[]{:S(2)}) async-start(bf16[8,10,64,128]{3,2,1,0:T(8,128)(2,1)} %rotate.1), calls=%async_computation | async-start | bytes 2621440 | tf_op jit(solution)/shard_map/all_to_all | solution.py:271
  29.6 3.2 %collective-permute-start.1 = (bf16[2064,128]{1,0:T(8,128)(2,1)S(1)}, bf16[2064,128]{1,0:T(8,128)(2,1)S(1)}, u32[]{:S(2)}, u32[]{:S(2)}) collective-permute-start(bf16[2064,128]{1,0:T(8,128)(2,1)S(1)} %collective-permute-done.refs_4_.refs_5_), channel_id=1, source_target_pairs={{0,28},{4,0},{8,4},{12,8},{16,12},{20,16},{24,20},{28,24},{1,29},{... | collective-permute-start | bytes 1585160 | tf_op jit(solution)/shard_map/ppermute | solution.py:268
  33.4 0.8 copy-done.3
  34.8 0.8 reshape.388
  35.6 1.4 reshape.390
  37.0 1.5 compare_reduce_fusion
  39.3 0.8 copy-done.5
  40.1 1.1 broadcast_select_fusion.2
  41.2 0.8 gt.69
  42.0 1.3 broadcast_select_fusion.3
  43.3 7.5 %collective-permute-done.1.refs_2_.refs_3_ = bf16[2064,128]{1,0:T(8,128)(2,1)S(1)} collective-permute-done((bf16[2064,128]{1,0:T(8,128)(2,1)S(1)}, bf16[2064,128]{1,0:T(8,128)(2,1)S(1)}, u32[]{:S(2)}, u32[]{:S(2)}) %collective-permute-start.1) | collective-permute-done | bytes 528416 | tf_op jit(solution)/shard_map/ppermute | solution.py:268
  50.8 3.7 %collective-permute-start.2 = (bf16[2064,128]{1,0:T(8,128)(2,1)S(1)}, bf16[2064,128]{1,0:T(8,128)(2,1)S(1)}, u32[]{:S(2)}, u32[]{:S(2)}) collective-permute-start(bf16[2064,128]{1,0:T(8,128)(2,1)S(1)} %collective-permute-done.1.refs_2_.refs_3_), channel_id=1, source_target_pairs={{0,28},{4,0},{8,4},{12,8},{16,12},{20,16},{24,20},{28,24},{1,29},{... | collective-permute-start | bytes 1585160 | tf_op jit(solution)/shard_map/ppermute | solution.py:268
  55.1 0.8 copy-done.7
  55.9 7.3 %collective-permute-done.5.refs_0_.refs_1_ = bf16[2064,128]{1,0:T(8,128)(2,1)} collective-permute-done((bf16[2064,128]{1,0:T(8,128)(2,1)S(1)}, bf16[2064,128]{1,0:T(8,128)(2,1)}, u32[]{:S(2)}, u32[]{:S(2)}) %collective-permute-start.5) | collective-permute-done | bytes 528416 | tf_op jit(solution)/shard_map/ppermute | solution.py:268
  63.2 1.2 slice_convert_fusion.4
  64.4 0.8 reshape.384
  65.9 0.8 gt.65
  66.6 1.1 broadcast_select_fusion.5
  67.8 0.8 reshape.382
  69.2 0.8 gt.63
  71.4 3.2 %collective-permute-start.3 = (bf16[1040,128]{1,0:T(8,128)(2,1)}, bf16[1040,128]{1,0:T(8,128)(2,1)S(1)}, u32[]{:S(2)}, u32[]{:S(2)}) collective-permute-start(bf16[1040,128]{1,0:T(8,128)(2,1)} %slice.40), channel_id=1, source_target_pairs={{0,28},{4,0},{8,4},{12,8},{16,12},{20,16},{24,20},{28,24},{1,29},{... | collective-permute-start | bytes 798728 | tf_op jit(solution)/shard_map/ppermute | solution.py:268
  74.6 3.1 %collective-permute-done.6.refs_0_.refs_1_ = bf16[2064,128]{1,0:T(8,128)(2,1)S(1)} collective-permute-done((bf16[2064,128]{1,0:T(8,128)(2,1)}, bf16[2064,128]{1,0:T(8,128)(2,1)S(1)}, u32[]{:S(2)}, u32[]{:S(2)}) %collective-permute-start.6) | collective-permute-done | bytes 528416 | tf_op jit(solution)/shard_map/ppermute | solution.py:268
  81.8 0.9 compare_reduce_fusion.2
  84.2 1.0 copy-done.4
  85.3 1.0 copy-done.6
  86.3 19.7 %attend.4 = (f32[8,2,320,128]{3,2,1,0:T(8,128)S(1)}, f32[8,2,320,128]{3,2,1,0:T(8,128)}) custom-call(s32[192]{0:T(256)S(1)} %pad_add_fusion.reach_ref, bf16[8,2,320,128]{3,2,1,0:T(8,128)(2,1)S(1)} %bitcast.10, bf16[2064,128]{1,0:T(8,128)(2,1)S(1)} %dequantize.1.refs_0_.refs_1_, bf16[2064,128]{1,0:T(8,128)(2,1)S(1)} %dequantize.1.refs_0_.refs_1_, ...), custom_call_target="tpu_custom_call" | custom-call | flops 8053063680 | bytes 8388608 | tf_op jit(solution)/shard_map/attend/pallas_call | solution.py:185
  106.1 1.5 copy-done.12
  107.5 14.4 %attend.5 = (f32[8,2,320,128]{3,2,1,0:T(8,128)S(1)}, f32[8,2,320,128]{3,2,1,0:T(8,128)}) custom-call(s32[128]{0:T(128)S(1)} %get-tuple-element.30.reach_ref, bf16[8,2,320,128]{3,2,1,0:T(8,128)(2,1)S(1)} %bitcast.11, bf16[2064,128]{1,0:T(8,128)(2,1)} %collective-permute-done.5.refs_0_.refs_1_, bf16[2064,128]{1,0:T(8,128)(2,1)} %collective-permute-done.5.refs_0_.refs_1_, ...), custom_call_target="tpu_custom_call" | custom-call | flops 5368709120 | bytes 8388608 | tf_op jit(solution)/shard_map/attend/pallas_call | solution.py:185
  121.9 1.5 copy-done.11
  123.4 14.2 %attend.6 = (f32[8,2,320,128]{3,2,1,0:T(8,128)S(1)}, f32[8,2,320,128]{3,2,1,0:T(8,128)}) custom-call(s32[128]{0:T(128)S(1)} %get-tuple-element.29.reach_ref, bf16[8,2,320,128]{3,2,1,0:T(8,128)(2,1)S(1)} %bitcast.12, bf16[2064,128]{1,0:T(8,128)(2,1)S(1)} %collective-permute-done.6.refs_0_.refs_1_, ...), custom_call_target="tpu_custom_call" | custom-call | flops 5368709120 | bytes 8388608 | tf_op jit(solution)/shard_map/attend/pallas_call | solution.py:185
  137.6 1.5 copy-done.9
  139.3 1.7 copy-done.10
  141.0 9.8 %attend.7 = bf16[8,2,352,128]{3,2,1,0:T(8,128)(2,1)} custom-call(s32[64]{0:T(128)S(1)} %broadcast_select_fusion.9.reach_ref, bf16[8,2,320,128]{3,2,1,0:T(8,128)(2,1)S(1)} %bitcast.13, bf16[1024,128]{1,0:T(8,128)(2,1)S(1)} %collective-permute-done.7.refs_0_, bf16[1040,128]{1,0:T(8,128)(2,1)S(1)} %collective-permute-done.3.refs_1_, ...), custom_call_target="tpu_custom_call" | custom-call | flops 2684354560 | bytes 8388608 | tf_op jit(solution)/shard_map/attend/pallas_call | solution.py:185
  150.8 5.8 %all-to-all-start.1 = ((bf16[8,2,352,128]{3,2,1,0:T(8,128)(2,1)}), bf16[8,2,352,128]{3,2,1,0:T(8,128)(2,1)S(1)}, u32[]{:S(2)}, u32[]{:S(2)}) async-start(bf16[8,2,352,128]{3,2,1,0:T(8,128)(2,1)} %attend.7), calls=%async_computation.1 | async-start | bytes 2883584 | tf_op jit(solution)/shard_map/all_to_all | solution.py:306
  156.6 17.1 %all-to-all-done.1.packed_ref = bf16[8,2,352,128]{3,2,1,0:T(8,128)(2,1)S(1)} async-done(((bf16[8,2,352,128]{3,2,1,0:T(8,128)(2,1)}), bf16[8,2,352,128]{3,2,1,0:T(8,128)(2,1)S(1)}, u32[]{:S(2)}, u32[]{:S(2)}) %all-to-all-start.1) | async-done | bytes 1441824 | tf_op jit(solution)/shard_map/all_to_all | solution.py:306
  173.7 2.9 %combine.1 = bf16[8,64,1280]{2,1,0:T(8,128)(2,1)} custom-call(bf16[8,2,352,128]{3,2,1,0:T(8,128)(2,1)S(1)} %all-to-all-done.1.packed_ref, f32[128,128]{1,0:T(8,128)S(1)} %fusion.table_ref), custom_call_target="tpu_custom_call" | custom-call | tf_op jit(solution)/shard_map/combine/pallas_call | solution.py:230
  176.6 4.7 %all-to-all-start.2 = ((bf16[8,64,1280]{2,1,0:T(8,128)(2,1)}), bf16[8,64,1280]{2,1,0:T(8,128)(2,1)S(1)}, u32[]{:S(2)}, u32[]{:S(2)}) async-start(bf16[8,64,1280]{2,1,0:T(8,128)(2,1)} %combine.1), calls=%async_computation.2 | async-start | bytes 2621440 | tf_op jit(solution)/shard_map/all_to_all | solution.py:308
  181.3 15.7 %all-to-all-done.2 = bf16[8,64,1280]{2,1,0:T(8,128)(2,1)S(1)} async-done(((bf16[8,64,1280]{2,1,0:T(8,128)(2,1)}), bf16[8,64,1280]{2,1,0:T(8,128)(2,1)S(1)}, u32[]{:S(2)}, u32[]{:S(2)}) %all-to-all-start.2) | async-done | bytes 1310752 | tf_op jit(solution)/shard_map/all_to_all | solution.py:308
  197.0 3.5 %convolution_convert_fusion = bf16[512,640]{1,0:T(8,128)(2,1)} fusion(bf16[512,1280]{1,0:T(8,128)(2,1)S(1)} %bitcast.14, bf16[640,1280]{1,0:T(8,128)(2,1)} %all-gather.2.cloned.1.call-done), kind=kOutput, calls=%fused_computation | convolution fusion | flops 839188480 | bytes 3604480 | tf_op jit(solution)/shard_map/dot_general | solution.py:309
  200.4 4.8 %all-to-all-start.3 = ((bf16[4,2,64,640]{3,2,1,0:T(8,128)(2,1)}), bf16[4,2,64,640]{3,2,1,0:T(8,128)(2,1)S(1)}, u32[]{:S(2)}, u32[]{:S(2)}) async-start(bf16[4,2,64,640]{3,2,1,0:T(8,128)(2,1)} %bitcast.3), calls=%async_computation.3 | async-start | bytes 1310720 | tf_op jit(solution)/shard_map/all_to_all | solution.py:316
  205.2 8.6 %all-to-all-done.3 = bf16[4,2,64,640]{3,2,1,0:T(8,128)(2,1)S(1)} async-done(((bf16[4,2,64,640]{3,2,1,0:T(8,128)(2,1)}), bf16[4,2,64,640]{3,2,1,0:T(8,128)(2,1)S(1)}, u32[]{:S(2)}, u32[]{:S(2)}) %all-to-all-start.3) | async-done | bytes 655392 | tf_op jit(solution)/shard_map/all_to_all | solution.py:316
  214.0 5.2 %collective-permute-start.8 = (bf16[64,640]{1,0:T(8,128)(2,1)S(1)}, bf16[64,640]{1,0:T(8,128)(2,1)S(1)}, u32[]{:S(2)}, u32[]{:S(2)}) collective-permute-start(bf16[64,640]{1,0:T(8,128)(2,1)S(1)} %get-tuple-element.19), channel_id=1, source_target_pairs={{0,0},{1,64},{2,128},{3,192},{32,32},{33,96},{34,160},{35,224},{64... | collective-permute-start | bytes 245768 | tf_op jit(solution)/shard_map/ppermute | solution.py:326
  219.1 3.1 %collective-permute-start.9 = (bf16[64,640]{1,0:T(8,128)(2,1)S(1)}, bf16[64,640]{1,0:T(8,128)(2,1)S(1)}, u32[]{:S(2)}, u32[]{:S(2)}) collective-permute-start(bf16[64,640]{1,0:T(8,128)(2,1)S(1)} %get-tuple-element.20), channel_id=1, source_target_pairs={{0,32},{1,96},{2,160},{3,224},{32,0},{33,64},{34,128},{35,192},{64... | collective-permute-start | bytes 245768 | tf_op jit(solution)/shard_map/ppermute | solution.py:329
  222.3 2.4 %collective-permute-done.8 = bf16[64,640]{1,0:T(8,128)(2,1)S(1)} collective-permute-done((bf16[64,640]{1,0:T(8,128)(2,1)S(1)}, bf16[64,640]{1,0:T(8,128)(2,1)S(1)}, u32[]{:S(2)}, u32[]{:S(2)}) %collective-permute-start.8) | collective-permute-done | bytes 81952 | tf_op jit(solution)/shard_map/ppermute | solution.py:326
  224.6 3.5 %collective-permute-done.9 = bf16[64,640]{1,0:T(8,128)(2,1)S(1)} collective-permute-done((bf16[64,640]{1,0:T(8,128)(2,1)S(1)}, bf16[64,640]{1,0:T(8,128)(2,1)S(1)}, u32[]{:S(2)}, u32[]{:S(2)}) %collective-permute-start.9) | collective-permute-done | bytes 81952 | tf_op jit(solution)/shard_map/ppermute | solution.py:329
  (97 shorter events, 20.1 us)
Async XLA Ops:
  7.5 1.2 copy-start
  8.7 0.8 copy-start.2
  9.5 6.3 %copy-start.1 = (bf16[64,1280]{1,0:T(8,128)(2,1)S(1)}, bf16[64,1280]{1,0:T(8,128)(2,1)}, u32[]{:S(2)}) copy-start(bf16[64,1280]{1,0:T(8,128)(2,1)} %queries_ref.1) | copy-start | bytes 491524
  9.8 19.7 %collective-permute-start = (bf16[2064,128]{1,0:T(8,128)(2,1)S(1)}, bf16[2064,128]{1,0:T(8,128)(2,1)S(1)}, u32[]{:S(2)}, u32[]{:S(2)}) collective-permute-start(bf16[2064,128]{1,0:T(8,128)(2,1)S(1)} %dequantize.1.refs_0_.refs_1_), channel_id=1, source_target_pairs={{0,28},{4,0},{8,4},{12,8},{16,12},{20,16},{24,20},{28,24},{1,29},{... | collective-permute-start | bytes 1585160 | tf_op jit(solution)/shard_map/ppermute | solution.py:268
  15.7 18.4 %collective-permute-start.4 = (bf16[2064,128]{1,0:T(8,128)(2,1)S(1)}, bf16[2064,128]{1,0:T(8,128)(2,1)S(1)}, u32[]{:S(2)}, u32[]{:S(2)}) collective-permute-start(bf16[2064,128]{1,0:T(8,128)(2,1)S(1)} %dequantize.1.refs_0_.refs_1_), channel_id=1, source_target_pairs={{0,4},{4,8},{8,12},{12,16},{16,20},{20,24},{24,28},{28,0},{1,5},{5... | collective-permute-start | bytes 1585160 | tf_op jit(solution)/shard_map/ppermute | solution.py:268
  17.2 67.0 %all-to-all-start = ((bf16[8,10,64,128]{3,2,1,0:T(8,128)(2,1)}), bf16[8,10,64,128]{3,2,1,0:T(8,128)(2,1)S(1)}, u32[]{:S(2)}, u32[]{:S(2)}) async-start(bf16[8,10,64,128]{3,2,1,0:T(8,128)(2,1)} %rotate.1), calls=%async_computation | async-start | bytes 2621440 | tf_op jit(solution)/shard_map/all_to_all | solution.py:271
  23.1 158.2 %all-gather.2.cloned.1.call-start = ((), (), s32[]{:S(2)}) async-start(), calls=%async_computation.4 | async-start | bytes 1843200 | tf_op jit(solution)/shard_map/all_gather | solution.py:259
  29.6 21.2 %collective-permute-start.1 = (bf16[2064,128]{1,0:T(8,128)(2,1)S(1)}, bf16[2064,128]{1,0:T(8,128)(2,1)S(1)}, u32[]{:S(2)}, u32[]{:S(2)}) collective-permute-start(bf16[2064,128]{1,0:T(8,128)(2,1)S(1)} %collective-permute-done.refs_4_.refs_5_), channel_id=1, source_target_pairs={{0,28},{4,0},{8,4},{12,8},{16,12},{20,16},{24,20},{28,24},{1,29},{... | collective-permute-start | bytes 1585160 | tf_op jit(solution)/shard_map/ppermute | solution.py:268
  33.4 0.8 copy-start.3
  39.2 24.0 %collective-permute-start.5 = (bf16[2064,128]{1,0:T(8,128)(2,1)S(1)}, bf16[2064,128]{1,0:T(8,128)(2,1)}, u32[]{:S(2)}, u32[]{:S(2)}) collective-permute-start(bf16[2064,128]{1,0:T(8,128)(2,1)S(1)} %collective-permute-done.4.refs_2_.refs_3_), channel_id=1, source_target_pairs={{0,4},{4,8},{8,12},{12,16},{16,20},{20,24},{24,28},{28,0},{1,5},{5... | collective-permute-start | bytes 1585160 | tf_op jit(solution)/shard_map/ppermute | solution.py:268
  39.3 0.8 copy-start.5
  50.8 19.8 %collective-permute-start.2 = (bf16[2064,128]{1,0:T(8,128)(2,1)S(1)}, bf16[2064,128]{1,0:T(8,128)(2,1)S(1)}, u32[]{:S(2)}, u32[]{:S(2)}) collective-permute-start(bf16[2064,128]{1,0:T(8,128)(2,1)S(1)} %collective-permute-done.1.refs_2_.refs_3_), channel_id=1, source_target_pairs={{0,28},{4,0},{8,4},{12,8},{16,12},{20,16},{24,20},{28,24},{1,29},{... | collective-permute-start | bytes 1585160 | tf_op jit(solution)/shard_map/ppermute | solution.py:268
  55.1 0.8 copy-start.7
  63.2 14.5 %collective-permute-start.6 = (bf16[2064,128]{1,0:T(8,128)(2,1)}, bf16[2064,128]{1,0:T(8,128)(2,1)S(1)}, u32[]{:S(2)}, u32[]{:S(2)}) collective-permute-start(bf16[2064,128]{1,0:T(8,128)(2,1)} %collective-permute-done.5.refs_0_.refs_1_), channel_id=1, source_target_pairs={{0,4},{4,8},{8,12},{12,16},{16,20},{20,24},{24,28},{28,0},{1,5},{5... | collective-permute-start | bytes 1585160 | tf_op jit(solution)/shard_map/ppermute | solution.py:268
  71.4 9.7 %collective-permute-start.3 = (bf16[1040,128]{1,0:T(8,128)(2,1)}, bf16[1040,128]{1,0:T(8,128)(2,1)S(1)}, u32[]{:S(2)}, u32[]{:S(2)}) collective-permute-start(bf16[1040,128]{1,0:T(8,128)(2,1)} %slice.40), channel_id=1, source_target_pairs={{0,28},{4,0},{8,4},{12,8},{16,12},{20,16},{24,20},{28,24},{1,29},{... | collective-permute-start | bytes 798728 | tf_op jit(solution)/shard_map/ppermute | solution.py:268
  79.0 60.3 %collective-permute-start.7 = (bf16[1024,128]{1,0:T(8,128)(2,1)}, bf16[1024,128]{1,0:T(8,128)(2,1)S(1)}, u32[]{:S(2)}, u32[]{:S(2)}) collective-permute-start(bf16[1024,128]{1,0:T(8,128)(2,1)} %slice.42), channel_id=1, source_target_pairs={{0,4},{4,8},{8,12},{12,16},{16,20},{20,24},{24,28},{28,0},{1,5},{5... | collective-permute-start | bytes 786440 | tf_op jit(solution)/shard_map/ppermute | solution.py:268
  84.2 1.0 copy-start.4
  85.3 1.0 copy-start.6
  86.3 21.2 %copy-start.8 = (bf16[2064,128]{1,0:T(8,128)(2,1)S(1)}, bf16[2064,128]{1,0:T(8,128)(2,1)}, u32[]{:S(2)}) copy-start(bf16[2064,128]{1,0:T(8,128)(2,1)} %copy-done.7) | copy-start | bytes 1585156
  106.0 1.5 copy-start.12
  121.9 1.5 copy-start.11
  123.4 15.8 %copy-start.13 = (s32[64]{0:T(128)S(1)}, s32[64]{0:T(128)}, u32[]{:S(2)}) copy-start(s32[64]{0:T(128)} %broadcast_in_dim.106) | copy-start | bytes 772
  137.6 1.5 copy-start.9
  139.3 1.7 copy-start.10
  150.8 22.9 %all-to-all-start.1 = ((bf16[8,2,352,128]{3,2,1,0:T(8,128)(2,1)}), bf16[8,2,352,128]{3,2,1,0:T(8,128)(2,1)S(1)}, u32[]{:S(2)}, u32[]{:S(2)}) async-start(bf16[8,2,352,128]{3,2,1,0:T(8,128)(2,1)} %attend.7), calls=%async_computation.1 | async-start | bytes 2883584 | tf_op jit(solution)/shard_map/all_to_all | solution.py:306
  176.6 20.4 %all-to-all-start.2 = ((bf16[8,64,1280]{2,1,0:T(8,128)(2,1)}), bf16[8,64,1280]{2,1,0:T(8,128)(2,1)S(1)}, u32[]{:S(2)}, u32[]{:S(2)}) async-start(bf16[8,64,1280]{2,1,0:T(8,128)(2,1)} %combine.1), calls=%async_computation.2 | async-start | bytes 2621440 | tf_op jit(solution)/shard_map/all_to_all | solution.py:308
  200.4 13.4 %all-to-all-start.3 = ((bf16[4,2,64,640]{3,2,1,0:T(8,128)(2,1)}), bf16[4,2,64,640]{3,2,1,0:T(8,128)(2,1)S(1)}, u32[]{:S(2)}, u32[]{:S(2)}) async-start(bf16[4,2,64,640]{3,2,1,0:T(8,128)(2,1)} %bitcast.3), calls=%async_computation.3 | async-start | bytes 1310720 | tf_op jit(solution)/shard_map/all_to_all | solution.py:316
  214.0 10.7 %collective-permute-start.8 = (bf16[64,640]{1,0:T(8,128)(2,1)S(1)}, bf16[64,640]{1,0:T(8,128)(2,1)S(1)}, u32[]{:S(2)}, u32[]{:S(2)}) collective-permute-start(bf16[64,640]{1,0:T(8,128)(2,1)S(1)} %get-tuple-element.19), channel_id=1, source_target_pairs={{0,0},{1,64},{2,128},{3,192},{32,32},{33,96},{34,160},{35,224},{64... | collective-permute-start | bytes 245768 | tf_op jit(solution)/shard_map/ppermute | solution.py:326
  219.1 9.0 %collective-permute-start.9 = (bf16[64,640]{1,0:T(8,128)(2,1)S(1)}, bf16[64,640]{1,0:T(8,128)(2,1)S(1)}, u32[]{:S(2)}, u32[]{:S(2)}) collective-permute-start(bf16[64,640]{1,0:T(8,128)(2,1)S(1)} %get-tuple-element.20), channel_id=1, source_target_pairs={{0,32},{1,96},{2,160},{3,224},{32,0},{33,64},{34,128},{35,192},{64... | collective-permute-start | bytes 245768 | tf_op jit(solution)/shard_map/ppermute | solution.py:329
Sparse Core Ops, SparseCore 0:
  25.7 43.6 all-gather.1

commit v2 on v1

v2 whole, which is shorter than its diff:
```python
import functools
import math

import jax
import jax.numpy as jnp
from jax import lax
from jax.experimental import pallas as pl
from jax.experimental.pallas import tpu as pltpu
from jax.sharding import Mesh
from jax.sharding import PartitionSpec as P

NEG_FILL = -1e30
LOG2E = math.log2(math.e)
VMEM_LIMIT = 58 * 1024 * 1024

Y, X, Z = "y", "x_lo", "z"
PLANE = (Y, X)
GRP = ("x_hi", "core")


def hadamard(order):
    index = jnp.arange(order, dtype=jnp.int32)
    common = index[:, None] & index[None, :]
    parity = jnp.zeros((order, order), jnp.int32)
    for shift_bit in range(int(order).bit_length()):
        parity = parity ^ common >> shift_bit & 1
    return jnp.where(parity == 1, -1.0, 1.0).astype(jnp.float32)


def dequantize_kernel(codes_ref, scales_ref, marks_ref, *outs):
    kinds, groups, length, width = codes_ref.shape
    parts = scales_ref.shape[2]
    for g in range(groups):
        out = outs[g]
        for kind in range(kinds):
            scales = scales_ref[kind, g]
            spread = jnp.concatenate(
                [
                    jnp.broadcast_to(scales[i : i + 1], (width // parts, length))
                    for i in range(parts)
                ],
                axis=0,
            )
            values = (codes_ref[kind, g].astype(jnp.float32) - 7.5) * spread.T
            values = values.astype(jnp.bfloat16)
            for copy in range(out.shape[0]):
                out[copy, pl.ds(kind * length, length), :] = values
        for copy in range(out.shape[0]):
            out[copy, pl.ds(kinds * length, 16), :] = marks_ref[g, copy]


def dequantize(codes, scales, marks):
    kinds, groups, length, width = codes.shape
    copies = marks.shape[1]
    out = jax.ShapeDtypeStruct((copies, kinds * length + 16, width), jnp.bfloat16)
    return pl.pallas_call(
        dequantize_kernel,
        out_shape=[out] * groups,
        compiler_params=pltpu.CompilerParams(vmem_limit_bytes=VMEM_LIMIT),
        name="dequantize",
    )(codes, scales, marks)


def rotate_kernel(queries_ref, table_ref, out_ref):
    groups, rows, width = out_ref.shape
    tokens = queries_ref.shape[0]
    per_group = rows // tokens
    scale = LOG2E / width
    for h in range(groups * per_group):
        turned = jnp.dot(
            queries_ref[:, h * width : (h + 1) * width],
            table_ref[...],
            preferred_element_type=jnp.float32,
        )
        at = pl.ds(h % per_group * tokens, tokens)
        out_ref[h // per_group, at, :] = (turned * scale).astype(jnp.bfloat16)


def rotate(queries, table, groups):
    tokens, columns = queries.shape
    width = table.shape[0]
    rows = columns // width // groups * tokens
    return pl.pallas_call(
        rotate_kernel,
        out_shape=jax.ShapeDtypeStruct((groups, rows, width), jnp.bfloat16),
        compiler_params=pltpu.CompilerParams(vmem_limit_bytes=VMEM_LIMIT),
        name="rotate",
    )(queries, table)


def attend_kernel(per_group, unit, page, blocks, ordered, *refs):
    if ordered:
        reach_ref, order_ref = refs[:2]
        refs = refs[2:]
    else:
        reach_ref = refs[0]
        refs = refs[1:]
    q_refs, kv_ref, refs = refs[:blocks], refs[blocks], refs[blocks + 1 :]
    outs, (pages_ref, s_ref, top_ref, sum_ref, acc_ref) = refs[:-5], refs[-5:]
    _, rows, width = q_refs[0].shape
    tokens = rows // per_group
    sources, height, _ = kv_ref.shape
    length = (height - 16) // 2
    shard_pages = length // page
    all_pages = sources * shard_pages
    masked_at = all_pages + unit

    def place(p, counts):
        full, some = counts
        reaches = [reach_ref[p * blocks + b] for b in range(blocks)]
        low = functools.reduce(jnp.minimum, reaches)
        high = functools.reduce(jnp.maximum, reaches)
        pages_ref[full] = p
        pages_ref[masked_at + some] = p
        whole = low >= page - 1
        part = jnp.logical_and(high > -tokens, low < page - 1)
        return full + whole.astype(jnp.int32), some + part.astype(jnp.int32)

    start = (jnp.int32(0), jnp.int32(0))
    full, some = lax.fori_loop(0, all_pages, place, start, unroll=4)
    whole = full // unit

    def leftover(i, some):
        pages_ref[masked_at + some] = pages_ref[whole * unit + i]
        return some + 1

    some = lax.fori_loop(0, full - whole * unit, leftover, some)
    rounds = (some + unit - 1) // unit

    def pad(i, _):
        pages_ref[masked_at + some + i] = -1
        return 0

    lax.fori_loop(0, rounds * unit - some, pad, 0)

    ahead = lax.broadcasted_iota(jnp.int32, (tokens, page), 1) - lax.broadcasted_iota(
        jnp.int32, (tokens, page), 0
    )
    top_ref[...] = jnp.full(top_ref.shape, NEG_FILL, jnp.float32)
    sum_ref[...] = jnp.zeros(sum_ref.shape, jnp.float32)
    acc_ref[...] = jnp.zeros(acc_ref.shape, jnp.float32)

    def fetch(p, at):
        first = pl.multiple_of(at + p % shard_pages * page, page)
        return kv_ref[p // shard_pages, pl.ds(first, page), :]

    def first_pass(i, base, slot, masked):
        ps = [pages_ref[base + i * unit + u] for u in range(unit)]
        held = [jnp.maximum(p, 0) for p in ps]
        k = jnp.concatenate([fetch(p, 0) for p in held], axis=0)
        for b in range(blocks):
            at = pl.ds(b * rows, rows)
            s = lax.dot_general(
                q_refs[b][0], k, (((1,), (1,)), ((), ())), preferred_element_type=jnp.float32
            )
            top = top_ref[at, :]
            for u in range(unit):
                x = s[:, u * page : (u + 1) * page]
                if masked:
                    reach = jnp.where(ps[u] < 0, -2 * page, reach_ref[held[u] * blocks + b])
                    x = x.reshape(per_group, tokens, page)
                    x = jnp.where((ahead <= reach)[None], x, NEG_FILL).reshape(rows, page)
                s_ref[slot, at, u * page : (u + 1) * page] = x
                top = jnp.maximum(top, x)
            top_ref[at, :] = top
        return 0

    def second_pass(i, base, slot):
        held = [jnp.maximum(pages_ref[base + i * unit + u], 0) for u in range(unit)]
        v = jnp.concatenate([fetch(p, length) for p in held], axis=0)
        for b in range(blocks):
            at = pl.ds(b * rows, rows)
            top = top_ref[at, :]
            weights = [
                jnp.exp2(s_ref[slot, at, u * page : (u + 1) * page] - top) for u in range(unit)
            ]
            sum_ref[at, :] = sum_ref[at, :] + functools.reduce(jnp.add, weights)
            weights = jnp.concatenate([w.astype(jnp.bfloat16) for w in weights], axis=1)
            acc_ref[at, :] = acc_ref[at, :] + jnp.dot(
                weights, v, preferred_element_type=jnp.float32
            )
        return 0

    lax.fori_loop(0, whole, lambda i, _: first_pass(i, 0, i, False), 0)
    lax.fori_loop(0, rounds, lambda i, _: first_pass(i, masked_at, whole + i, True), 0)
    for b in range(blocks):
        at = pl.ds(b * rows, rows)
        top = jnp.max(top_ref[at, :], axis=1, keepdims=True)
        top_ref[at, :] = jnp.broadcast_to(top, (rows, page))
    lax.fori_loop(0, whole, lambda i, _: second_pass(i, 0, i), 0)
    lax.fori_loop(0, rounds, lambda i, _: second_pass(i, masked_at, whole + i), 0)
    for b in range(blocks):
        at = pl.ds(b * rows, rows)
        total = jnp.sum(sum_ref[at, :], axis=1, keepdims=True)
        total = jnp.maximum(total, 1e-30)
        out = (acc_ref[at, :] / total).astype(jnp.bfloat16)
        lse = top_ref[at, :] + jnp.log2(total)
        across = [
            jnp.sum(
                jnp.where(ahead == 0, lse[h * tokens : (h + 1) * tokens], 0.0),
                axis=0,
                keepdims=True,
            )
            for h in range(per_group)
        ]
        across.append(jnp.zeros((8 - per_group, page), jnp.float32))
        across = jnp.concatenate(across, axis=0)
        high = across.astype(jnp.bfloat16).astype(jnp.float32)
        middle = (across - high).astype(jnp.bfloat16).astype(jnp.float32)
        low = across - high - middle
        tail = jnp.concatenate([high, middle, low, jnp.zeros_like(low)], axis=0)
        tail = tail.astype(jnp.bfloat16)
        if ordered:
            outs[0][order_ref[b], pl.ds(0, rows), :] = out
            outs[0][order_ref[b], pl.ds(rows, 32), :] = tail
        else:
            outs[b][pl.ds(0, rows), :] = out
            outs[b][pl.ds(rows, 32), :] = tail


def attend(q_blocks, kv, g, per_group, reach, order=None):
    blocks = len(q_blocks)
    _, rows, width = q_blocks[0].shape
    sources, height, _ = kv.shape
    page = 128
    pages = sources * ((height - 16) // 2 // page)
    unit = 4
    ordered = order is not None
    prefetched = (reach, order) if ordered else (reach,)
    part = (rows + 32, width)
    if ordered:
        out_shape = jax.ShapeDtypeStruct((blocks,) + part, jnp.bfloat16)
        out_specs = pl.BlockSpec((blocks,) + part, lambda t, *_: (0, 0, 0))
    else:
        out_shape = [jax.ShapeDtypeStruct(part, jnp.bfloat16)] * blocks
        out_specs = [pl.BlockSpec(part, lambda t, *_: (0, 0))] * blocks
    scores = blocks * rows * pages * page // 2
    once = pl.Buffered(1)
    return pl.pallas_call(
        functools.partial(attend_kernel, per_group, unit, page, blocks, ordered),
        grid_spec=pltpu.PrefetchScalarGridSpec(
            num_scalar_prefetch=len(prefetched),
            grid=(1,),
            in_specs=[
                pl.BlockSpec((1, rows, width), lambda t, *_: (g, 0, 0), pipeline_mode=once)
            ]
            * blocks
            + [pl.BlockSpec(kv.shape, lambda t, *_: (0, 0, 0), pipeline_mode=once)],
            out_specs=out_specs,
            scratch_shapes=[
                pltpu.SMEM((2 * (pages + unit),), jnp.int32),
                pltpu.VMEM((pages // unit + 1, blocks * rows, unit * page), jnp.float32),
                pltpu.VMEM((blocks * rows, page), jnp.float32),
                pltpu.VMEM((blocks * rows, page), jnp.float32),
                pltpu.VMEM((blocks * rows, width), jnp.float32),
            ],
        ),
        out_shape=out_shape,
        compiler_params=pltpu.CompilerParams(vmem_limit_bytes=VMEM_LIMIT),
        cost_estimate=pl.CostEstimate(
            flops=8 * scores * width, bytes_accessed=8 * 1024 * 1024, transcendentals=scores
        ),
        name="attend",
    )(*prefetched, *q_blocks, kv)


def combine_kernel(per_group, *refs):
    parts, table_ref, out_ref = refs[:-2], refs[-2], refs[-1]
    if len(parts) == 1:
        parts = [parts[0].at[e] for e in range(parts[0].shape[0])]
    height, width = parts[0].shape
    rows = height - 32
    tokens = rows // per_group
    lse = []
    for part in parts:
        tail = part[pl.ds(rows, 32), :].astype(jnp.float32)
        lse.append(tail[0:8] + tail[8:16] + tail[16:24])
    top = functools.reduce(jnp.maximum, lse)
    weights = [jnp.exp2(x - top) for x in lse]
    total = functools.reduce(jnp.add, weights)
    weights = jnp.concatenate([w / total for w in weights], axis=0).T
    for h in range(per_group):
        attended = jnp.zeros((tokens, width), jnp.float32)
        for e, part in enumerate(parts):
            value = part[pl.ds(h * tokens, tokens), :].astype(jnp.float32)
            attended = attended + value * weights[:tokens, e * 8 + h : e * 8 + h + 1]
        restored = jnp.dot(
            attended,
            table_ref[...],
            preferred_element_type=jnp.float32,
            precision=lax.Precision.HIGHEST,
        )
        restored = (restored * (1.0 / math.sqrt(width))).astype(jnp.bfloat16)
        for copy in range(out_ref.shape[0]):
            out_ref[copy, :, h * width : (h + 1) * width] = restored


def combine(parts, table, per_group, copies):
    height, width = parts[0].shape[-2:]
    tokens = (height - 32) // per_group
    return pl.pallas_call(
        functools.partial(combine_kernel, per_group),
        out_shape=jax.ShapeDtypeStruct((copies, tokens, per_group * width), jnp.bfloat16),
        compiler_params=pltpu.CompilerParams(vmem_limit_bytes=VMEM_LIMIT),
        name="combine",
    )(*parts, table)


def on_device(queries, cache_codes, cache_scales, pattern, out_weight):
    ny, nx, nz = (lax.axis_size(a) for a in (Y, X, Z))
    y, x, z = (lax.axis_index(a) for a in (Y, X, Z))
    plane = ny * nx
    block_rows = queries.shape[0]
    _, groups, shard_len, width = cache_codes.shape
    heads = queries.shape[1] // width
    per_group = heads // groups
    pages = pattern.shape[2]
    page = shard_len // pages
    blocks = pattern.shape[1]
    total_len = shard_len * blocks
    total_q = block_rows * blocks
    table = hadamard(width)

    marks = pattern.reshape(groups, plane, 1, nz * pages).astype(jnp.bfloat16)
    marks = jnp.pad(marks, ((0, 0), (0, 0), (0, 15), (0, width - nz * pages)))
    shards = dequantize(cache_codes, cache_scales, marks)
    gathered = [lax.all_to_all(shard, PLANE, 0, 0) for shard in shards]

    def moved(block, step):
        return lax.ppermute(block, Z, [(i, (i + step) % nz) for i in range(nz)])

    rotated = rotate(queries, table.astype(jnp.bfloat16), groups)
    q_blocks = [rotated] + [moved(rotated, i) for i in range(1, nz)]
    at = (z - jnp.arange(nz, dtype=jnp.int32)) % nz
    first_query = total_len - total_q + ((y * nx + x) * nz + at) * block_rows

    weight_rows, _ = lax.optimization_barrier((out_weight.T, q_blocks[-1]))
    weight_rows = lax.all_gather(weight_rows, Z, axis=0, tiled=True)

    def reach_of(kv):
        kept = kv[:, 2 * shard_len, : nz * pages].astype(jnp.float32).reshape(plane, nz, pages)
        kept = jnp.transpose(kept, (0, 2, 1))
        kept = jnp.flip(jnp.roll(kept, nz - 1 - z, axis=2), axis=2)
        shard = jnp.arange(plane, dtype=jnp.int32) * nz + z
        first_key = shard[:, None] * shard_len + jnp.arange(pages, dtype=jnp.int32) * page
        causal = jnp.clip(first_query[None, None, :] - first_key[:, :, None], -2 * page, 2 * page)
        return jnp.where(kept > 0.5, causal, -2 * page).reshape(-1)

    parts = attend(q_blocks, gathered[0], 0, per_group, reach_of(gathered[0]))
    received = [[parts[0]] + [moved(parts[i], -i) for i in range(1, nz)]]
    parts = attend(q_blocks, gathered[1], 1, per_group, reach_of(gathered[1]), at)
    received.append([lax.all_to_all(parts, Z, 0, 0)])
    restored = [combine(r, table, per_group, plane) for r in received]
    restored = jnp.concatenate(restored, axis=2)
    restored = lax.all_to_all(restored, PLANE, 0, 0)
    terms = lax.dot_general(
        restored.reshape(plane * block_rows, heads * width),
        weight_rows,
        (((1,), (1,)), ((), ())),
        preferred_element_type=jnp.float32,
    ).astype(jnp.bfloat16)
    columns = terms.shape[1]
    terms = lax.all_to_all(terms.reshape(ny, nx, block_rows, columns), GRP, 0, 0)
    share = jnp.sum(terms.astype(jnp.float32), axis=0).astype(jnp.bfloat16)

    same = lax.dynamic_index_in_dim(share, x, 0, keepdims=False)
    other = lax.dynamic_index_in_dim(share, 1 - x, 0, keepdims=False)
    where = [(a, b, c) for a in range(ny) for b in range(nx) for c in range(ny)]

    def flat(a, b, c):
        return (a * nx + b) * ny + c

    same = lax.ppermute(
        same, (Y, X) + GRP, [(flat(a, b, c), flat(c, b, a)) for a, b, c in where]
    )
    other = lax.ppermute(
        other, (Y, X) + GRP, [(flat(a, b, c), flat(c, 1 - b, a)) for a, b, c in where]
    )
    left = jnp.where(x == 0, same, other)
    right = jnp.where(x == 0, other, same)
    return jnp.concatenate([left, right], axis=1)


def solution(mesh):
    parts = Mesh(mesh.devices.reshape(4, 2, 8, 2, 2), (Y, X, Z) + GRP)
    ctx = (Y, X, Z)
    placed = (
        P(ctx, GRP),
        P(None, GRP, ctx, None),
        P(None, GRP, None, ctx),
        P(GRP, None, ctx),
        P(GRP, ctx),
    )
    return jax.shard_map(
        on_device, mesh=parts, in_specs=placed, out_specs=P(ctx, GRP), check_vma=False
    )
```

time: 237 us -> 224 us (0.945)
  blocking collectives: 0 us -> 32.3 us
  Pallas kernels: 62.7 us -> 33.3 us
  local copies, waits for them, and re-layouts: 27.8 us -> 4.77 us
  starting transfers between devices: 45.6 us -> 63.3 us
  other arithmetic: 16.2 us -> 6.58 us
    all_to_all x0 -> x1, blocking collectives: none -> 32.3 us  [on_device(): gathered = [lax.all_to_all(shard, PLANE, 0, 0) for shard in shards]]
    pallas_call x7 -> x6, Pallas kernels: 62.7 us -> 33.3 us  [the longest x2 22.1 us: attend(): pl.pallas_call(functools.partial(attend_kernel, per_group, unit, page, bl...]
    ppermute x8 -> x14, starting transfers between devices: 16.2 us -> 35.2 us  [moved(): return lax.ppermute(block, Z, [(i, (i + step) % nz) for i in range(nz)])]
    all_to_all x2, waiting for transfers between devices: 17.1 us -> 6.27 us  [the longest x1 6.27 us: on_device(): gathered = [lax.all_to_all(shard, PLANE, 0, 0) for shard in shards]]
    unnamed x28 -> x34, local copies, waits for them, and re-layouts: 12.6 us -> 2.19 us
    ppermute x8 -> x14, waiting for transfers between devices: 18 us -> 27.7 us  [moved(): return lax.ppermute(block, Z, [(i, (i + step) % nz) for i in range(nz)])]
    select_n x8 -> x2, other arithmetic: 6.25 us -> 0.57 us  [the longest x1 0.49 us: on_device(): at = (z - jnp.arange(nz, dtype=jnp.int32)) % nz]
    broadcast_in_dim x16 -> x0, local copies, waits for them, and re-layouts: 5.2 us -> none  [reach_of(): return jnp.where(kept > 0.5, causal[None], -2 * page).reshape(-1)]
  transfers between devices with their start and end apart: 15 -> 21, of which waited for: 8 -> 11; matrix products, arithmetic and copies ran while one was open for 13% -> 3% of each run, Pallas kernels for 26% -> 13%
where the time goes in v2:
time: 224 us; the launch traced here: 223 us
  waiting for transfers between devices  65.9 us (29%)
  starting transfers between devices  63.3 us (28%)
  Pallas kernels  33.3 us (15%)
  blocking collectives  32.3 us (14%)
  between operations  13.6 us (6%)
  other arithmetic  6.58 us (3%)
  local copies, waits for them, and re-layouts  4.77 us (2%)
  matrix products  3.5 us (2%)
    ppermute x14, starting transfers between devices, moved(): return lax.ppermute(block, Z, [(i, (i + step) % nz) for i in range(nz)])  35.2 us
    all_to_all x1, blocking collectives, on_device(): gathered = [lax.all_to_all(shard, PLANE, 0, 0) for shard in shards]  32.3 us
    ppermute x14, waiting for transfers between devices, moved(): return lax.ppermute(block, Z, [(i, (i + step) % nz) for i in range(nz)])  27.7 us
    pallas_call x2, Pallas kernels, attend(): pl.pallas_call(functools.partial(attend_kernel, per_group, unit, page, bl...  22.1 us
    all_to_all x1, waiting for transfers between devices, on_device(): restored = lax.all_to_all(restored, PLANE, 0, 0)  17.5 us
    all_to_all x1, waiting for transfers between devices, on_device(): lax.all_to_all(terms.reshape(ny, nx, block_rows, columns), GRP, 0, 0)  8.59 us
    all_to_all x1, waiting for transfers between devices, on_device(): gathered = [lax.all_to_all(shard, PLANE, 0, 0) for shard in shards]  6.27 us
    pallas_call x2, Pallas kernels, combine(): pl.pallas_call(functools.partial(combine_kernel, per_group), out_shape=ja...  5.85 us
  transfers between devices with their start and end apart: 21, of which 11 were waited for; matrix products, arithmetic and copies ran while one was open for 3% of the time, Pallas kernels for 13%

profile of v2, /device:TPU:6, one launch (start us, length us, event | category | flops | bytes accessed | tf_op | source)
XLA Modules:
  0.0 223.2 jit_solution(16860027827927524394)
XLA Ops:
  6.5 0.7 convert_element_type.34
  7.2 0.1 copy.13
  7.4 0.6 pad.4.marks_ref
  8.1 3.5 %dequantize.1 = (bf16[8,1040,128]{2,1,0:T(8,128)(2,1)}, bf16[8,1040,128]{2,1,0:T(8,128)(2,1)}) custom-call(s32[2,2,512,128]{3,2,1,0:T(8,128)} %codes_ref.1, f32[2,2,4,512]{3,2,1,0:T(4,128)} %scales_ref.1, bf16[2,8,16,128]{3,2,1,0:T(8,128)(2,1)} %pad.4.marks_ref), custom_call_target="tpu_custom_call" | custom-call | tf_op jit(solution)/shard_map/dequantize/pallas_call | solution.py:56
  11.6 32.3 %all_to_all.25.refs_9_ = bf16[8,1040,128]{2,1,0:T(8,128)(2,1)S(1)} all-to-all(bf16[8,1040,128]{2,1,0:T(8,128)(2,1)} %get-tuple-element.17), channel_id=1, replica_groups=mesh['y'=4,'x_lo'=2,'z'=8,'x_hi'=2,'core'=2] {'y','x_lo'}, dimensions={0} | all-to-all | bytes 4259840 | tf_op jit(solution)/shard_map/all_to_all | solution.py:327
  43.9 5.5 %all-to-all-start.1 = ((bf16[8,1040,128]{2,1,0:T(8,128)(2,1)}), bf16[8,1040,128]{2,1,0:T(8,128)(2,1)}, u32[]{:S(2)}, u32[]{:S(2)}) async-start(bf16[8,1040,128]{2,1,0:T(8,128)(2,1)} %get-tuple-element.26), calls=%async_computation.1 | async-start | bytes 4259840 | tf_op jit(solution)/shard_map/all_to_all | solution.py:327
  49.4 0.7 fusion.1.table_ref
  50.1 1.8 rotate.1.refs_1_.refs_2_
  51.9 5.9 %collective-permute-start.6 = (bf16[2,320,128]{2,1,0:T(8,128)(2,1)}, bf16[2,320,128]{2,1,0:T(8,128)(2,1)S(1)}, u32[]{:S(2)}, u32[]{:S(2)}) collective-permute-start(bf16[2,320,128]{2,1,0:T(8,128)(2,1)} %rotate.1.refs_1_.refs_2_), channel_id=1, source_target_pairs={{0,28},{4,0},{8,4},{12,8},{16,12},{20,16},{24,20},{28,24},{1,29},{... | collective-permute-start | bytes 491528 | tf_op jit(solution)/shard_map/ppermute | solution.py:330
  57.7 4.4 %collective-permute-start.2 = (bf16[2,320,128]{2,1,0:T(8,128)(2,1)}, bf16[2,320,128]{2,1,0:T(8,128)(2,1)S(1)}, u32[]{:S(2)}, u32[]{:S(2)}) collective-permute-start(bf16[2,320,128]{2,1,0:T(8,128)(2,1)} %rotate.1.refs_1_.refs_2_), channel_id=1, source_target_pairs={{0,12},{4,16},{8,20},{12,24},{16,28},{20,0},{24,4},{28,8},{1,13},{... | collective-permute-start | bytes 491528 | tf_op jit(solution)/shard_map/ppermute | solution.py:330
  62.1 2.1 collective-permute-start.3
  64.3 0.5 and_select_fusion.refs_1_
  64.8 3.4 %collective-permute-start.4 = (bf16[2,320,128]{2,1,0:T(8,128)(2,1)}, bf16[2,320,128]{2,1,0:T(8,128)(2,1)S(1)}, u32[]{:S(2)}, u32[]{:S(2)}) collective-permute-start(bf16[2,320,128]{2,1,0:T(8,128)(2,1)} %rotate.1.refs_1_.refs_2_), channel_id=1, source_target_pairs={{0,20},{4,24},{8,28},{12,0},{16,4},{20,8},{24,12},{28,16},{1,21},{... | collective-permute-start | bytes 491528 | tf_op jit(solution)/shard_map/ppermute | solution.py:330
  68.2 6.3 %all-to-all-done.1.refs_10_ = bf16[8,1040,128]{2,1,0:T(8,128)(2,1)} async-done(((bf16[8,1040,128]{2,1,0:T(8,128)(2,1)}), bf16[8,1040,128]{2,1,0:T(8,128)(2,1)}, u32[]{:S(2)}, u32[]{:S(2)}) %all-to-all-start.1) | async-done | bytes 2129952 | tf_op jit(solution)/shard_map/all_to_all | solution.py:327
  74.5 0.7 slice_convert_fusion
  75.4 6.4 %collective-permute-start.5 = (bf16[2,320,128]{2,1,0:T(8,128)(2,1)}, bf16[2,320,128]{2,1,0:T(8,128)(2,1)S(1)}, u32[]{:S(2)}, u32[]{:S(2)}) collective-permute-start(bf16[2,320,128]{2,1,0:T(8,128)(2,1)} %rotate.1.refs_1_.refs_2_), channel_id=1, source_target_pairs={{0,24},{4,28},{8,0},{12,4},{16,8},{20,12},{24,16},{28,20},{1,25},{... | collective-permute-start | bytes 491528 | tf_op jit(solution)/shard_map/ppermute | solution.py:330
  82.0 0.7 reshape.91.refs_0_
  82.7 4.8 %collective-permute-done.2.refs_4_.refs_5_ = bf16[2,320,128]{2,1,0:T(8,128)(2,1)S(1)} collective-permute-done((bf16[2,320,128]{2,1,0:T(8,128)(2,1)}, bf16[2,320,128]{2,1,0:T(8,128)(2,1)S(1)}, u32[]{:S(2)}, u32[]{:S(2)}) %collective-permute-start.2) | collective-permute-done | bytes 163872 | tf_op jit(solution)/shard_map/ppermute | solution.py:330
  87.5 8.0 %collective-permute-done.5.refs_7_.refs_8_ = bf16[2,320,128]{2,1,0:T(8,128)(2,1)S(1)} collective-permute-done((bf16[2,320,128]{2,1,0:T(8,128)(2,1)}, bf16[2,320,128]{2,1,0:T(8,128)(2,1)S(1)}, u32[]{:S(2)}, u32[]{:S(2)}) %collective-permute-start.5) | collective-permute-done | bytes 163872 | tf_op jit(solution)/shard_map/ppermute | solution.py:330
  95.6 0.7 copy-done.16
  96.3 10.1 %attend.3 = bf16[8,352,128]{2,1,0:T(8,128)(2,1)} custom-call(s32[256]{0:T(256)} %reshape.91.refs_0_, s32[8]{0:T(128)} %and_select_fusion.refs_1_, bf16[2,320,128]{2,1,0:T(8,128)(2,1)} %rotate.1.refs_1_.refs_2_, bf16[2,320,128]{2,1,0:T(8,128)(2,1)} %copy-done.11, bf16[2,320,128]{2,1,0:T(8,128)(2,1)} %copy-done.12, bf16[2,320,128]{2,1,0:T(8,128)(2,1)} %copy-done.13, ...), custom_call_target="tpu_custom_call" | custom-call | flops 5368709120 | bytes 8388608 | tf_op jit(solution)/shard_map/attend/pallas_call | solution.py:239
  106.4 4.6 %all-to-all-start.2 = ((bf16[8,352,128]{2,1,0:T(8,128)(2,1)}), bf16[8,352,128]{2,1,0:T(8,128)(2,1)S(1)}, u32[]{:S(2)}, u32[]{:S(2)}) async-start(bf16[8,352,128]{2,1,0:T(8,128)(2,1)} %attend.3), calls=%async_computation.2 | async-start | bytes 1441792 | tf_op jit(solution)/shard_map/all_to_all | solution.py:352
  111.1 0.7 reshape.90.refs_0_
  111.7 12.0 %attend.2 = (bf16[352,128]{1,0:T(8,128)(2,1)}, bf16[352,128]{1,0:T(8,128)(2,1)}, bf16[352,128]{1,0:T(8,128)(2,1)}, bf16[352,128]{1,0:T(8,128)(2,1)}, bf16[352,12...) custom-call(s32[256]{0:T(256)} %reshape.90.refs_0_, ...), custom_call_target="tpu_custom_call" | custom-call | flops 5368709120 | bytes 8388608 | tf_op jit(solution)/shard_map/attend/pallas_call | solution.py:239
  123.7 5.9 %collective-permute-start.10 = (bf16[352,128]{1,0:T(8,128)(2,1)}, bf16[352,128]{1,0:T(8,128)(2,1)S(1)}, u32[]{:S(2)}, u32[]{:S(2)}) collective-permute-start(bf16[352,128]{1,0:T(8,128)(2,1)} %get-tuple-element.22), channel_id=1, source_target_pairs={{0,16},{4,20},{8,24},{12,28},{16,0},{20,4},{24,8},{28,12},{1,17},{... | collective-permute-start | bytes 270344 | tf_op jit(solution)/shard_map/ppermute | solution.py:330
  129.6 3.8 %collective-permute-start.12 = (bf16[352,128]{1,0:T(8,128)(2,1)}, bf16[352,128]{1,0:T(8,128)(2,1)S(1)}, u32[]{:S(2)}, u32[]{:S(2)}) collective-permute-start(bf16[352,128]{1,0:T(8,128)(2,1)} %get-tuple-element.24), channel_id=1, source_target_pairs={{0,8},{4,12},{8,16},{12,20},{16,24},{20,28},{24,0},{28,4},{1,9},{5... | collective-permute-start | bytes 270344 | tf_op jit(solution)/shard_map/ppermute | solution.py:330
  133.5 3.2 %collective-permute-start.7 = (bf16[352,128]{1,0:T(8,128)(2,1)}, bf16[352,128]{1,0:T(8,128)(2,1)S(1)}, u32[]{:S(2)}, u32[]{:S(2)}) collective-permute-start(bf16[352,128]{1,0:T(8,128)(2,1)} %get-tuple-element.19), channel_id=1, source_target_pairs={{0,28},{4,0},{8,4},{12,8},{16,12},{20,16},{24,20},{28,24},{1,29},{... | collective-permute-start | bytes 270344 | tf_op jit(solution)/shard_map/ppermute | solution.py:330
  136.7 1.1 collective-permute-done.10.refs_4_
  137.8 5.9 %collective-permute-done.11.refs_5_ = bf16[352,128]{1,0:T(8,128)(2,1)S(1)} collective-permute-done((bf16[352,128]{1,0:T(8,128)(2,1)}, bf16[352,128]{1,0:T(8,128)(2,1)S(1)}, u32[]{:S(2)}, u32[]{:S(2)}) %collective-permute-start.11) | collective-permute-done | bytes 90144 | tf_op jit(solution)/shard_map/ppermute | solution.py:330
  143.7 0.2 collective-permute-start.9
  143.9 0.7 fusion.refs_8_.refs_1_
  144.6 1.4 collective-permute-done.13.refs_7_
  146.0 6.4 %collective-permute-done.9.refs_3_ = bf16[352,128]{1,0:T(8,128)(2,1)S(1)} collective-permute-done((bf16[352,128]{1,0:T(8,128)(2,1)}, bf16[352,128]{1,0:T(8,128)(2,1)S(1)}, u32[]{:S(2)}, u32[]{:S(2)}) %collective-permute-start.9) | collective-permute-done | bytes 90144 | tf_op jit(solution)/shard_map/ppermute | solution.py:330
  152.4 0.6 copy-done.9
  153.0 3.0 %combine.2 = bf16[8,64,640]{2,1,0:T(8,128)(2,1)} custom-call(bf16[352,128]{1,0:T(8,128)(2,1)} %get-tuple-element.18.refs_0_, bf16[352,128]{1,0:T(8,128)(2,1)} %copy-done.7, bf16[352,128]{1,0:T(8,128)(2,1)} %copy-done.8, bf16[352,128]{1,0:T(8,128)(2,1)} %copy-done.9, bf16[352,128]{1,0:T(8,128)(2,1)} %copy-done.3, bf16[352,128]{1,0:T(8,128)(2,1)} %copy-done.4, ...), custom_call_target="tpu_custom_call" | custom-call | tf_op jit(solution)/shard_map/combine/pallas_call | solution.py:301
  156.0 0.9 copy-done
  156.9 2.9 %combine.3 = bf16[8,64,640]{2,1,0:T(8,128)(2,1)} custom-call(bf16[8,352,128]{2,1,0:T(8,128)(2,1)} %copy-done, f32[128,128]{1,0:T(8,128)} %fusion.refs_8_.refs_1_), custom_call_target="tpu_custom_call" | custom-call | tf_op jit(solution)/shard_map/combine/pallas_call | solution.py:301
  159.8 2.3 %pad_maximum_fusion = bf16[8,64,1280]{2,1,0:T(8,128)(2,1)} fusion(bf16[8,64,640]{2,1,0:T(8,128)(2,1)} %combine.3, bf16[8,64,640]{2,1,0:T(8,128)(2,1)S(1)} %copy-done.1), kind=kLoop, calls=%fused_computation.1 | loop fusion | flops 2621440 | bytes 2621440 | tf_op jit(solution)/shard_map/concatenate | solution.py:354
  162.1 4.9 %all-to-all-start.3 = ((bf16[8,64,1280]{2,1,0:T(8,128)(2,1)}), bf16[8,64,1280]{2,1,0:T(8,128)(2,1)S(1)}, u32[]{:S(2)}, u32[]{:S(2)}) async-start(bf16[8,64,1280]{2,1,0:T(8,128)(2,1)} %pad_maximum_fusion), calls=%async_computation.3 | async-start | bytes 2621440 | tf_op jit(solution)/shard_map/all_to_all | solution.py:355
  167.0 17.5 %all-to-all-done.3 = bf16[8,64,1280]{2,1,0:T(8,128)(2,1)S(1)} async-done(((bf16[8,64,1280]{2,1,0:T(8,128)(2,1)}), bf16[8,64,1280]{2,1,0:T(8,128)(2,1)S(1)}, u32[]{:S(2)}, u32[]{:S(2)}) %all-to-all-start.3) | async-done | bytes 1310752 | tf_op jit(solution)/shard_map/all_to_all | solution.py:355
  184.5 3.5 %convolution_convert_fusion = bf16[512,640]{1,0:T(8,128)(2,1)} fusion(bf16[512,1280]{1,0:T(8,128)(2,1)S(1)} %bitcast.15, bf16[640,1280]{1,0:T(8,128)(2,1)} %all-gather.2.cloned.1.call-done), kind=kOutput, calls=%fused_computation | convolution fusion | flops 839188480 | bytes 3604480 | tf_op jit(solution)/shard_map/dot_general | solution.py:356
  188.0 4.8 %all-to-all-start.4 = ((bf16[4,2,64,640]{3,2,1,0:T(8,128)(2,1)}), bf16[4,2,64,640]{3,2,1,0:T(8,128)(2,1)S(1)}, u32[]{:S(2)}, u32[]{:S(2)}) async-start(bf16[4,2,64,640]{3,2,1,0:T(8,128)(2,1)} %bitcast.6), calls=%async_computation.4 | async-start | bytes 1310720 | tf_op jit(solution)/shard_map/all_to_all | solution.py:363
  192.8 8.6 %all-to-all-done.4 = bf16[4,2,64,640]{3,2,1,0:T(8,128)(2,1)S(1)} async-done(((bf16[4,2,64,640]{3,2,1,0:T(8,128)(2,1)}), bf16[4,2,64,640]{3,2,1,0:T(8,128)(2,1)S(1)}, u32[]{:S(2)}, u32[]{:S(2)}) %all-to-all-start.4) | async-done | bytes 655392 | tf_op jit(solution)/shard_map/all_to_all | solution.py:363
  201.5 5.3 %collective-permute-start.14 = (bf16[64,640]{1,0:T(8,128)(2,1)S(1)}, bf16[64,640]{1,0:T(8,128)(2,1)S(1)}, u32[]{:S(2)}, u32[]{:S(2)}) collective-permute-start(bf16[64,640]{1,0:T(8,128)(2,1)S(1)} %get-tuple-element.30), channel_id=1, source_target_pairs={{0,0},{1,64},{2,128},{3,192},{32,32},{33,96},{34,160},{35,224},{64... | collective-permute-start | bytes 245768 | tf_op jit(solution)/shard_map/ppermute | solution.py:373
  206.8 3.0 %collective-permute-start.15 = (bf16[64,640]{1,0:T(8,128)(2,1)S(1)}, bf16[64,640]{1,0:T(8,128)(2,1)S(1)}, u32[]{:S(2)}, u32[]{:S(2)}) collective-permute-start(bf16[64,640]{1,0:T(8,128)(2,1)S(1)} %get-tuple-element.31), channel_id=1, source_target_pairs={{0,32},{1,96},{2,160},{3,224},{32,0},{33,64},{34,128},{35,192},{64... | collective-permute-start | bytes 245768 | tf_op jit(solution)/shard_map/ppermute | solution.py:376
  209.8 2.4 %collective-permute-done.14 = bf16[64,640]{1,0:T(8,128)(2,1)S(1)} collective-permute-done((bf16[64,640]{1,0:T(8,128)(2,1)S(1)}, bf16[64,640]{1,0:T(8,128)(2,1)S(1)}, u32[]{:S(2)}, u32[]{:S(2)}) %collective-permute-start.14) | collective-permute-done | bytes 81952 | tf_op jit(solution)/shard_map/ppermute | solution.py:373
  212.2 3.5 %collective-permute-done.15 = bf16[64,640]{1,0:T(8,128)(2,1)S(1)} collective-permute-done((bf16[64,640]{1,0:T(8,128)(2,1)S(1)}, bf16[64,640]{1,0:T(8,128)(2,1)S(1)}, u32[]{:S(2)}, u32[]{:S(2)}) %collective-permute-start.15) | collective-permute-done | bytes 81952 | tf_op jit(solution)/shard_map/ppermute | solution.py:376
  215.7 0.7 pad_maximum_fusion.1
  (62 shorter events, 0.9 us)
Async XLA Ops:
  43.9 24.3 %copy-start.2 = (bf16[8,1040,128]{2,1,0:T(8,128)(2,1)}, bf16[8,1040,128]{2,1,0:T(8,128)(2,1)S(1)}, u32[]{:S(2)}) copy-start(bf16[8,1040,128]{2,1,0:T(8,128)(2,1)S(1)} %all_to_all.25.refs_9_) | copy-start | bytes 6389764
  43.9 30.6 %all-to-all-start.1 = ((bf16[8,1040,128]{2,1,0:T(8,128)(2,1)}), bf16[8,1040,128]{2,1,0:T(8,128)(2,1)}, u32[]{:S(2)}, u32[]{:S(2)}) async-start(bf16[8,1040,128]{2,1,0:T(8,128)(2,1)} %get-tuple-element.26), calls=%async_computation.1 | async-start | bytes 4259840 | tf_op jit(solution)/shard_map/all_to_all | solution.py:327
  49.4 117.6 %all-gather.2.cloned.1.call-start = ((), (), s32[]{:S(2)}) async-start(), calls=%async_computation.5 | async-start | bytes 1843200 | tf_op jit(solution)/shard_map/all_gather | solution.py:338
  51.9 12.9 %collective-permute-start.6 = (bf16[2,320,128]{2,1,0:T(8,128)(2,1)}, bf16[2,320,128]{2,1,0:T(8,128)(2,1)S(1)}, u32[]{:S(2)}, u32[]{:S(2)}) collective-permute-start(bf16[2,320,128]{2,1,0:T(8,128)(2,1)} %rotate.1.refs_1_.refs_2_), channel_id=1, source_target_pairs={{0,28},{4,0},{8,4},{12,8},{16,12},{20,16},{24,20},{28,24},{1,29},{... | collective-permute-start | bytes 491528 | tf_op jit(solution)/shard_map/ppermute | solution.py:330
  57.7 17.7 %collective-permute-start = (bf16[2,320,128]{2,1,0:T(8,128)(2,1)}, bf16[2,320,128]{2,1,0:T(8,128)(2,1)S(1)}, u32[]{:S(2)}, u32[]{:S(2)}) collective-permute-start(bf16[2,320,128]{2,1,0:T(8,128)(2,1)} %rotate.1.refs_1_.refs_2_), channel_id=1, source_target_pairs={{0,4},{4,8},{8,12},{12,16},{16,20},{20,24},{24,28},{28,0},{1,5},{5... | collective-permute-start | bytes 491528 | tf_op jit(solution)/shard_map/ppermute | solution.py:330
  57.7 24.9 %collective-permute-start.1 = (bf16[2,320,128]{2,1,0:T(8,128)(2,1)}, bf16[2,320,128]{2,1,0:T(8,128)(2,1)S(1)}, u32[]{:S(2)}, u32[]{:S(2)}) collective-permute-start(bf16[2,320,128]{2,1,0:T(8,128)(2,1)} %rotate.1.refs_1_.refs_2_), channel_id=1, source_target_pairs={{0,8},{4,12},{8,16},{12,20},{16,24},{20,28},{24,0},{28,4},{1,9},{5... | collective-permute-start | bytes 491528 | tf_op jit(solution)/shard_map/ppermute | solution.py:330
  57.7 29.8 %collective-permute-start.2 = (bf16[2,320,128]{2,1,0:T(8,128)(2,1)}, bf16[2,320,128]{2,1,0:T(8,128)(2,1)S(1)}, u32[]{:S(2)}, u32[]{:S(2)}) collective-permute-start(bf16[2,320,128]{2,1,0:T(8,128)(2,1)} %rotate.1.refs_1_.refs_2_), channel_id=1, source_target_pairs={{0,12},{4,16},{8,20},{12,24},{16,28},{20,0},{24,4},{28,8},{1,13},{... | collective-permute-start | bytes 491528 | tf_op jit(solution)/shard_map/ppermute | solution.py:330
  62.1 25.4 %collective-permute-start.3 = (bf16[2,320,128]{2,1,0:T(8,128)(2,1)}, bf16[2,320,128]{2,1,0:T(8,128)(2,1)S(1)}, u32[]{:S(2)}, u32[]{:S(2)}) collective-permute-start(bf16[2,320,128]{2,1,0:T(8,128)(2,1)} %rotate.1.refs_1_.refs_2_), channel_id=1, source_target_pairs={{0,16},{4,20},{8,24},{12,28},{16,0},{20,4},{24,8},{28,12},{1,17},{... | collective-permute-start | bytes 491528 | tf_op jit(solution)/shard_map/ppermute | solution.py:330
  64.8 30.7 %copy-start.10 = (bf16[2,320,128]{2,1,0:T(8,128)(2,1)}, bf16[2,320,128]{2,1,0:T(8,128)(2,1)S(1)}, u32[]{:S(2)}) copy-start(bf16[2,320,128]{2,1,0:T(8,128)(2,1)S(1)} %collective-permute-done.6.refs_8_.refs_9_) | copy-start | bytes 491524
  64.8 22.7 %collective-permute-start.4 = (bf16[2,320,128]{2,1,0:T(8,128)(2,1)}, bf16[2,320,128]{2,1,0:T(8,128)(2,1)S(1)}, u32[]{:S(2)}, u32[]{:S(2)}) collective-permute-start(bf16[2,320,128]{2,1,0:T(8,128)(2,1)} %rotate.1.refs_1_.refs_2_), channel_id=1, source_target_pairs={{0,20},{4,24},{8,28},{12,0},{16,4},{20,8},{24,12},{28,16},{1,21},{... | collective-permute-start | bytes 491528 | tf_op jit(solution)/shard_map/ppermute | solution.py:330
  75.4 20.1 %copy-start.11 = (bf16[2,320,128]{2,1,0:T(8,128)(2,1)}, bf16[2,320,128]{2,1,0:T(8,128)(2,1)S(1)}, u32[]{:S(2)}) copy-start(bf16[2,320,128]{2,1,0:T(8,128)(2,1)S(1)} %collective-permute-done.refs_2_.refs_3_) | copy-start | bytes 491524
  75.4 20.1 %collective-permute-start.5 = (bf16[2,320,128]{2,1,0:T(8,128)(2,1)}, bf16[2,320,128]{2,1,0:T(8,128)(2,1)S(1)}, u32[]{:S(2)}, u32[]{:S(2)}) collective-permute-start(bf16[2,320,128]{2,1,0:T(8,128)(2,1)} %rotate.1.refs_1_.refs_2_), channel_id=1, source_target_pairs={{0,24},{4,28},{8,0},{12,4},{16,8},{20,12},{24,16},{28,20},{1,25},{... | collective-permute-start | bytes 491528 | tf_op jit(solution)/shard_map/ppermute | solution.py:330
  82.7 12.9 %copy-start.12 = (bf16[2,320,128]{2,1,0:T(8,128)(2,1)}, bf16[2,320,128]{2,1,0:T(8,128)(2,1)S(1)}, u32[]{:S(2)}) copy-start(bf16[2,320,128]{2,1,0:T(8,128)(2,1)S(1)} %collective-permute-done.1.refs_3_.refs_4_) | copy-start | bytes 491524
  87.5 8.1 %copy-start.13 = (bf16[2,320,128]{2,1,0:T(8,128)(2,1)}, bf16[2,320,128]{2,1,0:T(8,128)(2,1)S(1)}, u32[]{:S(2)}) copy-start(bf16[2,320,128]{2,1,0:T(8,128)(2,1)S(1)} %collective-permute-done.2.refs_4_.refs_5_) | copy-start | bytes 491524
  87.5 8.1 %copy-start.14 = (bf16[2,320,128]{2,1,0:T(8,128)(2,1)}, bf16[2,320,128]{2,1,0:T(8,128)(2,1)S(1)}, u32[]{:S(2)}) copy-start(bf16[2,320,128]{2,1,0:T(8,128)(2,1)S(1)} %collective-permute-done.3.refs_5_.refs_6_) | copy-start | bytes 491524
  87.5 8.1 %copy-start.15 = (bf16[2,320,128]{2,1,0:T(8,128)(2,1)}, bf16[2,320,128]{2,1,0:T(8,128)(2,1)S(1)}, u32[]{:S(2)}) copy-start(bf16[2,320,128]{2,1,0:T(8,128)(2,1)S(1)} %collective-permute-done.4.refs_6_.refs_7_) | copy-start | bytes 491524
  95.6 0.7 copy-start.16
  106.4 49.6 %all-to-all-start.2 = ((bf16[8,352,128]{2,1,0:T(8,128)(2,1)}), bf16[8,352,128]{2,1,0:T(8,128)(2,1)S(1)}, u32[]{:S(2)}, u32[]{:S(2)}) async-start(bf16[8,352,128]{2,1,0:T(8,128)(2,1)} %attend.3), calls=%async_computation.2 | async-start | bytes 1441792 | tf_op jit(solution)/shard_map/all_to_all | solution.py:352
  123.7 14.1 %collective-permute-start.10 = (bf16[352,128]{1,0:T(8,128)(2,1)}, bf16[352,128]{1,0:T(8,128)(2,1)S(1)}, u32[]{:S(2)}, u32[]{:S(2)}) collective-permute-start(bf16[352,128]{1,0:T(8,128)(2,1)} %get-tuple-element.22), channel_id=1, source_target_pairs={{0,16},{4,20},{8,24},{12,28},{16,0},{20,4},{24,8},{28,12},{1,17},{... | collective-permute-start | bytes 270344 | tf_op jit(solution)/shard_map/ppermute | solution.py:330
  129.6 14.1 %collective-permute-start.11 = (bf16[352,128]{1,0:T(8,128)(2,1)}, bf16[352,128]{1,0:T(8,128)(2,1)S(1)}, u32[]{:S(2)}, u32[]{:S(2)}) collective-permute-start(bf16[352,128]{1,0:T(8,128)(2,1)} %get-tuple-element.23), channel_id=1, source_target_pairs={{0,12},{4,16},{8,20},{12,24},{16,28},{20,0},{24,4},{28,8},{1,13},{... | collective-permute-start | bytes 270344 | tf_op jit(solution)/shard_map/ppermute | solution.py:330
  129.6 14.9 %collective-permute-start.12 = (bf16[352,128]{1,0:T(8,128)(2,1)}, bf16[352,128]{1,0:T(8,128)(2,1)S(1)}, u32[]{:S(2)}, u32[]{:S(2)}) collective-permute-start(bf16[352,128]{1,0:T(8,128)(2,1)} %get-tuple-element.24), channel_id=1, source_target_pairs={{0,8},{4,12},{8,16},{12,20},{16,24},{20,28},{24,0},{28,4},{1,9},{5... | collective-permute-start | bytes 270344 | tf_op jit(solution)/shard_map/ppermute | solution.py:330
  133.5 12.5 %collective-permute-start.13 = (bf16[352,128]{1,0:T(8,128)(2,1)}, bf16[352,128]{1,0:T(8,128)(2,1)S(1)}, u32[]{:S(2)}, u32[]{:S(2)}) collective-permute-start(bf16[352,128]{1,0:T(8,128)(2,1)} %get-tuple-element.25), channel_id=1, source_target_pairs={{0,4},{4,8},{8,12},{12,16},{16,20},{20,24},{24,28},{28,0},{1,5},{5... | collective-permute-start | bytes 270344 | tf_op jit(solution)/shard_map/ppermute | solution.py:330
  133.5 12.5 %collective-permute-start.7 = (bf16[352,128]{1,0:T(8,128)(2,1)}, bf16[352,128]{1,0:T(8,128)(2,1)S(1)}, u32[]{:S(2)}, u32[]{:S(2)}) collective-permute-start(bf16[352,128]{1,0:T(8,128)(2,1)} %get-tuple-element.19), channel_id=1, source_target_pairs={{0,28},{4,0},{8,4},{12,8},{16,12},{20,16},{24,20},{28,24},{1,29},{... | collective-permute-start | bytes 270344 | tf_op jit(solution)/shard_map/ppermute | solution.py:330
  137.8 14.6 %copy-start.3 = (bf16[352,128]{1,0:T(8,128)(2,1)}, bf16[352,128]{1,0:T(8,128)(2,1)S(1)}, u32[]{:S(2)}) copy-start(bf16[352,128]{1,0:T(8,128)(2,1)S(1)} %collective-permute-done.10.refs_4_) | copy-start | bytes 270340
  137.8 8.2 %collective-permute-start.8 = (bf16[352,128]{1,0:T(8,128)(2,1)}, bf16[352,128]{1,0:T(8,128)(2,1)S(1)}, u32[]{:S(2)}, u32[]{:S(2)}) collective-permute-start(bf16[352,128]{1,0:T(8,128)(2,1)} %get-tuple-element.20), channel_id=1, source_target_pairs={{0,24},{4,28},{8,0},{12,4},{16,8},{20,12},{24,16},{28,20},{1,25},{... | collective-permute-start | bytes 270344 | tf_op jit(solution)/shard_map/ppermute | solution.py:330
  143.7 8.7 %copy-start.4 = (bf16[352,128]{1,0:T(8,128)(2,1)}, bf16[352,128]{1,0:T(8,128)(2,1)S(1)}, u32[]{:S(2)}) copy-start(bf16[352,128]{1,0:T(8,128)(2,1)S(1)} %collective-permute-done.11.refs_5_) | copy-start | bytes 270340
  143.7 8.7 %collective-permute-start.9 = (bf16[352,128]{1,0:T(8,128)(2,1)}, bf16[352,128]{1,0:T(8,128)(2,1)S(1)}, u32[]{:S(2)}, u32[]{:S(2)}) collective-permute-start(bf16[352,128]{1,0:T(8,128)(2,1)} %get-tuple-element.21), channel_id=1, source_target_pairs={{0,20},{4,24},{8,28},{12,0},{16,4},{20,8},{24,12},{28,16},{1,21},{... | collective-permute-start | bytes 270344 | tf_op jit(solution)/shard_map/ppermute | solution.py:330
  144.6 7.8 %copy-start.5 = (bf16[352,128]{1,0:T(8,128)(2,1)}, bf16[352,128]{1,0:T(8,128)(2,1)S(1)}, u32[]{:S(2)}) copy-start(bf16[352,128]{1,0:T(8,128)(2,1)S(1)} %collective-permute-done.12.refs_6_) | copy-start | bytes 270340
  146.0 6.4 %copy-start.6 = (bf16[352,128]{1,0:T(8,128)(2,1)}, bf16[352,128]{1,0:T(8,128)(2,1)S(1)}, u32[]{:S(2)}) copy-start(bf16[352,128]{1,0:T(8,128)(2,1)S(1)} %collective-permute-done.13.refs_7_) | copy-start | bytes 270340
  146.0 6.4 %copy-start.7 = (bf16[352,128]{1,0:T(8,128)(2,1)}, bf16[352,128]{1,0:T(8,128)(2,1)S(1)}, u32[]{:S(2)}) copy-start(bf16[352,128]{1,0:T(8,128)(2,1)S(1)} %collective-permute-done.7.refs_1_) | copy-start | bytes 270340
  146.0 6.4 %copy-start.8 = (bf16[352,128]{1,0:T(8,128)(2,1)}, bf16[352,128]{1,0:T(8,128)(2,1)S(1)}, u32[]{:S(2)}) copy-start(bf16[352,128]{1,0:T(8,128)(2,1)S(1)} %collective-permute-done.8.refs_2_) | copy-start | bytes 270340
  152.4 0.6 copy-start.9
  156.0 3.8 %copy-start.1 = (bf16[8,64,640]{2,1,0:T(8,128)(2,1)S(1)}, bf16[8,64,640]{2,1,0:T(8,128)(2,1)}, u32[]{:S(2)}) copy-start(bf16[8,64,640]{2,1,0:T(8,128)(2,1)} %combine.2) | copy-start | bytes 1966084
  156.0 0.9 copy-start
  162.1 22.4 %all-to-all-start.3 = ((bf16[8,64,1280]{2,1,0:T(8,128)(2,1)}), bf16[8,64,1280]{2,1,0:T(8,128)(2,1)S(1)}, u32[]{:S(2)}, u32[]{:S(2)}) async-start(bf16[8,64,1280]{2,1,0:T(8,128)(2,1)} %pad_maximum_fusion), calls=%async_computation.3 | async-start | bytes 2621440 | tf_op jit(solution)/shard_map/all_to_all | solution.py:355
  188.0 13.4 %all-to-all-start.4 = ((bf16[4,2,64,640]{3,2,1,0:T(8,128)(2,1)}), bf16[4,2,64,640]{3,2,1,0:T(8,128)(2,1)S(1)}, u32[]{:S(2)}, u32[]{:S(2)}) async-start(bf16[4,2,64,640]{3,2,1,0:T(8,128)(2,1)} %bitcast.6), calls=%async_computation.4 | async-start | bytes 1310720 | tf_op jit(solution)/shard_map/all_to_all | solution.py:363
  201.5 10.7 %collective-permute-start.14 = (bf16[64,640]{1,0:T(8,128)(2,1)S(1)}, bf16[64,640]{1,0:T(8,128)(2,1)S(1)}, u32[]{:S(2)}, u32[]{:S(2)}) collective-permute-start(bf16[64,640]{1,0:T(8,128)(2,1)S(1)} %get-tuple-element.30), channel_id=1, source_target_pairs={{0,0},{1,64},{2,128},{3,192},{32,32},{33,96},{34,160},{35,224},{64... | collective-permute-start | bytes 245768 | tf_op jit(solution)/shard_map/ppermute | solution.py:373
  206.8 8.8 %collective-permute-start.15 = (bf16[64,640]{1,0:T(8,128)(2,1)S(1)}, bf16[64,640]{1,0:T(8,128)(2,1)S(1)}, u32[]{:S(2)}, u32[]{:S(2)}) collective-permute-start(bf16[64,640]{1,0:T(8,128)(2,1)S(1)} %get-tuple-element.31), channel_id=1, source_target_pairs={{0,32},{1,96},{2,160},{3,224},{32,0},{33,64},{34,128},{35,192},{64... | collective-permute-start | bytes 245768 | tf_op jit(solution)/shard_map/ppermute | solution.py:376
Sparse Core Ops, SparseCore 0:
  68.3 42.8 all-gather.1

commit v3 on v2

--- a/solution.py
+++ b/solution.py
@@ -27,38 +27,74 @@
     return jnp.where(parity == 1, -1.0, 1.0).astype(jnp.float32)
 
 
-def dequantize_kernel(codes_ref, scales_ref, marks_ref, *outs):
-    kinds, groups, length, width = codes_ref.shape
+def dequantize_kernel(g, codes_ref, scales_ref, marks_ref, after_ref, out):
+    kinds, _, length, width = codes_ref.shape
     parts = scales_ref.shape[2]
-    for g in range(groups):
-        out = outs[g]
-        for kind in range(kinds):
-            scales = scales_ref[kind, g]
-            spread = jnp.concatenate(
-                [
-                    jnp.broadcast_to(scales[i : i + 1], (width // parts, length))
-                    for i in range(parts)
-                ],
-                axis=0,
-            )
-            values = (codes_ref[kind, g].astype(jnp.float32) - 7.5) * spread.T
-            values = values.astype(jnp.bfloat16)
-            for copy in range(out.shape[0]):
-                out[copy, pl.ds(kind * length, length), :] = values
+    for kind in range(kinds):
+        scales = scales_ref[kind, g]
+        spread = jnp.concatenate(
+            [
+                jnp.broadcast_to(scales[i : i + 1], (width // parts, length))
+                for i in range(parts)
+            ],
+            axis=0,
+        )
+        values = (codes_ref[kind, 0].astype(jnp.float32) - 7.5) * spread.T
+        values = values.astype(jnp.bfloat16)
         for copy in range(out.shape[0]):
-            out[copy, pl.ds(kinds * length, 16), :] = marks_ref[g, copy]
-
-
-def dequantize(codes, scales, marks):
+            out[copy, pl.ds(kind * length, length), :] = values
+    if g == 0:
+        for copy in range(out.shape[0]):
+            out[copy, pl.ds(kinds * length, 16), :] = marks_ref[copy]
+
+
+def dequantize(g, codes, scales, marks, after):
     kinds, groups, length, width = codes.shape
-    copies = marks.shape[1]
-    out = jax.ShapeDtypeStruct((copies, kinds * length + 16, width), jnp.bfloat16)
-    return pl.pallas_call(
-        dequantize_kernel,
-        out_shape=[out] * groups,
+    copies = marks.shape[0]
+    height = kinds * length + (16 if g == 0 else 0)
+    return pl.pallas_call(
+        functools.partial(dequantize_kernel, g),
+        grid=(1,),
+        in_specs=[
+            pl.BlockSpec((kinds, 1, length, width), lambda i: (0, g, 0, 0)),
+            pl.BlockSpec(scales.shape, lambda i: (0, 0, 0, 0)),
+            pl.BlockSpec(marks.shape, lambda i: (0, 0, 0)),
+            pl.BlockSpec(memory_space=pl.ANY),
+        ],
+        out_specs=pl.BlockSpec((copies, height, width), lambda i: (0, 0, 0)),
+        out_shape=jax.ShapeDtypeStruct((copies, height, width), jnp.bfloat16),
         compiler_params=pltpu.CompilerParams(vmem_limit_bytes=VMEM_LIMIT),
         name="dequantize",
-    )(codes, scales, marks)
+    )(codes, scales, marks, after)
+
+
+def pass_kernel(block_ref, after_ref, out_ref):
+    out_ref[...] = block_ref[...]
+
+
+def tie_kernel(block_ref, after_ref, out_ref):
+    pass
+
+
+def tied(block, after):
+    anywhere = pl.BlockSpec(memory_space=pl.ANY)
+    return pl.pallas_call(
+        tie_kernel,
+        in_specs=[anywhere, anywhere],
+        out_specs=anywhere,
+        out_shape=jax.ShapeDtypeStruct(block.shape, block.dtype),
+        input_output_aliases={0: 0},
+        name="tie",
+    )(block, after)
+
+
+def passed_after(block, after):
+    return pl.pallas_call(
+        pass_kernel,
+        in_specs=[pl.BlockSpec(memory_space=pltpu.VMEM), pl.BlockSpec(memory_space=pl.ANY)],
+        out_shape=jax.ShapeDtypeStruct(block.shape, block.dtype),
+        name="pass",
+    )(block, after)
 
 
 def rotate_kernel(queries_ref, table_ref, out_ref):
@@ -88,19 +124,14 @@
     )(queries, table)
 
 
-def attend_kernel(per_group, unit, page, blocks, ordered, *refs):
-    if ordered:
-        reach_ref, order_ref = refs[:2]
-        refs = refs[2:]
-    else:
-        reach_ref = refs[0]
-        refs = refs[1:]
-    q_refs, kv_ref, refs = refs[:blocks], refs[blocks], refs[blocks + 1 :]
+def attend_kernel(
+    per_group, unit, page, ordered, reach_ref, order_ref, q_ref, kv_ref, after_ref, *refs
+):
     outs, (pages_ref, s_ref, top_ref, sum_ref, acc_ref) = refs[:-5], refs[-5:]
-    _, rows, width = q_refs[0].shape
+    blocks, _, rows, width = q_ref.shape
     tokens = rows // per_group
     sources, height, _ = kv_ref.shape
-    length = (height - 16) // 2
+    length = height // 2 // page * page
     shard_pages = length // page
     all_pages = sources * shard_pages
     masked_at = all_pages + unit
@@ -151,7 +182,7 @@
         for b in range(blocks):
             at = pl.ds(b * rows, rows)
             s = lax.dot_general(
-                q_refs[b][0], k, (((1,), (1,)), ((), ())), preferred_element_type=jnp.float32
+                q_ref[order_ref[b], 0], k, (((1,), (1,)), ((), ())), preferred_element_type=jnp.float32
             )
             top = top_ref[at, :]
             for u in range(unit):
@@ -218,15 +249,12 @@
             outs[b][pl.ds(rows, 32), :] = tail
 
 
-def attend(q_blocks, kv, g, per_group, reach, order=None):
-    blocks = len(q_blocks)
-    _, rows, width = q_blocks[0].shape
+def attend(q, kv, g, per_group, reach, order, ordered, after):
+    blocks, _, rows, width = q.shape
     sources, height, _ = kv.shape
     page = 128
-    pages = sources * ((height - 16) // 2 // page)
+    pages = sources * (height // 2 // page)
     unit = 4
-    ordered = order is not None
-    prefetched = (reach, order) if ordered else (reach,)
     part = (rows + 32, width)
     if ordered:
         out_shape = jax.ShapeDtypeStruct((blocks,) + part, jnp.bfloat16)
@@ -237,15 +265,17 @@
     scores = blocks * rows * pages * page // 2
     once = pl.Buffered(1)
     return pl.pallas_call(
-        functools.partial(attend_kernel, per_group, unit, page, blocks, ordered),
+        functools.partial(attend_kernel, per_group, unit, page, ordered),
         grid_spec=pltpu.PrefetchScalarGridSpec(
-            num_scalar_prefetch=len(prefetched),
+            num_scalar_prefetch=2,
             grid=(1,),
             in_specs=[
-                pl.BlockSpec((1, rows, width), lambda t, *_: (g, 0, 0), pipeline_mode=once)
-            ]
-            * blocks
-            + [pl.BlockSpec(kv.shape, lambda t, *_: (0, 0, 0), pipeline_mode=once)],
+                pl.BlockSpec(
+                    (blocks, 1, rows, width), lambda t, *_: (0, g, 0, 0), pipeline_mode=once
+                ),
+                pl.BlockSpec(kv.shape, lambda t, *_: (0, 0, 0), pipeline_mode=once),
+                pl.BlockSpec(memory_space=pl.ANY),
+            ],
             out_specs=out_specs,
             scratch_shapes=[
                 pltpu.SMEM((2 * (pages + unit),), jnp.int32),
@@ -261,7 +291,7 @@
             flops=8 * scores * width, bytes_accessed=8 * 1024 * 1024, transcendentals=scores
         ),
         name="attend",
-    )(*prefetched, *q_blocks, kv)
+    )(reach, order, q, kv, after)
 
 
 def combine_kernel(per_group, *refs):
@@ -279,28 +309,29 @@
     weights = [jnp.exp2(x - top) for x in lse]
     total = functools.reduce(jnp.add, weights)
     weights = jnp.concatenate([w / total for w in weights], axis=0).T
+    attended = []
     for h in range(per_group):
-        attended = jnp.zeros((tokens, width), jnp.float32)
+        one = jnp.zeros((tokens, width), jnp.float32)
         for e, part in enumerate(parts):
             value = part[pl.ds(h * tokens, tokens), :].astype(jnp.float32)
-            attended = attended + value * weights[:tokens, e * 8 + h : e * 8 + h + 1]
-        restored = jnp.dot(
-            attended,
-            table_ref[...],
-            preferred_element_type=jnp.float32,
-            precision=lax.Precision.HIGHEST,
-        )
-        restored = (restored * (1.0 / math.sqrt(width))).astype(jnp.bfloat16)
-        for copy in range(out_ref.shape[0]):
-            out_ref[copy, :, h * width : (h + 1) * width] = restored
-
-
-def combine(parts, table, per_group, copies):
+            one = one + value * weights[:tokens, e * 8 + h : e * 8 + h + 1]
+        attended.append(one)
+    attended = jnp.concatenate(attended, axis=0)
+    high = attended.astype(jnp.bfloat16)
+    low = (attended - high.astype(jnp.float32)).astype(jnp.bfloat16)
+    restored = jnp.dot(high, table_ref[...], preferred_element_type=jnp.float32)
+    restored = restored + jnp.dot(low, table_ref[...], preferred_element_type=jnp.float32)
+    restored = (restored * (1.0 / math.sqrt(width))).astype(jnp.bfloat16)
+    for h in range(per_group):
+        out_ref[:, h * width : (h + 1) * width] = restored[h * tokens : (h + 1) * tokens]
+
+
+def combine(parts, table, per_group):
     height, width = parts[0].shape[-2:]
     tokens = (height - 32) // per_group
     return pl.pallas_call(
         functools.partial(combine_kernel, per_group),
-        out_shape=jax.ShapeDtypeStruct((copies, tokens, per_group * width), jnp.bfloat16),
+        out_shape=jax.ShapeDtypeStruct((tokens, per_group * width), jnp.bfloat16),
         compiler_params=pltpu.CompilerParams(vmem_limit_bytes=VMEM_LIMIT),
         name="combine",
     )(*parts, table)
@@ -322,36 +353,41 @@
     table = hadamard(width)
 
     marks = pattern.reshape(groups, plane, 1, nz * pages).astype(jnp.bfloat16)
-    marks = jnp.pad(marks, ((0, 0), (0, 0), (0, 15), (0, width - nz * pages)))
-    shards = dequantize(cache_codes, cache_scales, marks)
-    gathered = [lax.all_to_all(shard, PLANE, 0, 0) for shard in shards]
+    marks = jnp.transpose(marks, (1, 2, 0, 3)).reshape(plane, 1, -1)
+    marks = jnp.pad(marks, ((0, 0), (0, 15), (0, width - marks.shape[2])))
+
+    rotated = rotate(queries, table.astype(jnp.bfloat16), groups)
+    q = lax.all_gather(rotated, Z, axis=0, tiled=False)
+    weight_rows = lax.all_gather(passed_after(out_weight.T, q), Z, axis=0, tiled=True)
+
+    shards = [dequantize(g, cache_codes, cache_scales, marks, rotated) for g in range(groups)]
+    gathered = [lax.all_to_all(shards[0], PLANE, 0, 0)]
 
     def moved(block, step):
         return lax.ppermute(block, Z, [(i, (i + step) % nz) for i in range(nz)])
 
-    rotated = rotate(queries, table.astype(jnp.bfloat16), groups)
-    q_blocks = [rotated] + [moved(rotated, i) for i in range(1, nz)]
     at = (z - jnp.arange(nz, dtype=jnp.int32)) % nz
     first_query = total_len - total_q + ((y * nx + x) * nz + at) * block_rows
 
-    weight_rows, _ = lax.optimization_barrier((out_weight.T, q_blocks[-1]))
-    weight_rows = lax.all_gather(weight_rows, Z, axis=0, tiled=True)
-
-    def reach_of(kv):
-        kept = kv[:, 2 * shard_len, : nz * pages].astype(jnp.float32).reshape(plane, nz, pages)
-        kept = jnp.transpose(kept, (0, 2, 1))
-        kept = jnp.flip(jnp.roll(kept, nz - 1 - z, axis=2), axis=2)
-        shard = jnp.arange(plane, dtype=jnp.int32) * nz + z
-        first_key = shard[:, None] * shard_len + jnp.arange(pages, dtype=jnp.int32) * page
-        causal = jnp.clip(first_query[None, None, :] - first_key[:, :, None], -2 * page, 2 * page)
-        return jnp.where(kept > 0.5, causal, -2 * page).reshape(-1)
-
-    parts = attend(q_blocks, gathered[0], 0, per_group, reach_of(gathered[0]))
-    received = [[parts[0]] + [moved(parts[i], -i) for i in range(1, nz)]]
-    parts = attend(q_blocks, gathered[1], 1, per_group, reach_of(gathered[1]), at)
-    received.append([lax.all_to_all(parts, Z, 0, 0)])
-    restored = [combine(r, table, per_group, plane) for r in received]
-    restored = jnp.concatenate(restored, axis=2)
+    kept = gathered[0][:, 2 * shard_len, : groups * nz * pages].astype(jnp.float32)
+    kept = kept.reshape(plane, groups, nz, pages)
+    kept = jnp.transpose(kept, (1, 0, 3, 2))
+    kept = jnp.flip(jnp.roll(kept, nz - 1 - z, axis=3), axis=3)
+    shard = jnp.arange(plane, dtype=jnp.int32) * nz + z
+    first_key = shard[:, None] * shard_len + jnp.arange(pages, dtype=jnp.int32) * page
+    causal = jnp.clip(first_query[None, None, :] - first_key[:, :, None], -2 * page, 2 * page)
+    reach = jnp.where(kept > 0.5, causal[None], -2 * page).reshape(groups, -1)
+
+    gathered.append(lax.all_to_all(tied(shards[1], reach), PLANE, 0, 0))
+
+    parts = attend(q, gathered[0], 0, per_group, reach[0], at, False, q)
+    received = [parts[0]] + [moved(parts[i], -i) for i in range(1, nz)]
+    packed = attend(q, gathered[1], 1, per_group, reach[1], at, True, parts[0])
+    packed = lax.all_to_all(packed, Z, 0, 0)
+    signs = table.astype(jnp.bfloat16)
+    restored = [combine(received, signs, per_group), combine([packed], signs, per_group)]
+    restored = jnp.concatenate(restored, axis=1)
+    restored = jnp.broadcast_to(restored[None], (plane,) + restored.shape)
     restored = lax.all_to_all(restored, PLANE, 0, 0)
     terms = lax.dot_general(
         restored.reshape(plane * block_rows, heads * width),

time: 224 us -> 205 us (0.915); the launches traced: 223 us -> 202 us
  blocking collectives: 32.3 us -> 0 us
  waiting for transfers between devices: 65.9 us -> 84.7 us
  starting transfers between devices: 63.3 us -> 50.8 us
  Pallas kernels: 33.3 us -> 37.5 us
  local copies, waits for them, and re-layouts: 4.77 us -> 7.84 us
  other arithmetic: 6.58 us -> 3.93 us
    all_to_all x1 -> x0, blocking collectives: 32.3 us -> none  [on_device(): gathered = [lax.all_to_all(shard, PLANE, 0, 0) for shard in shards]]
    ppermute x14 -> x7, starting transfers between devices: 35.2 us -> 13.7 us  [moved(): return lax.ppermute(block, Z, [(i, (i + step) % nz) for i in range(nz)])]
    all_to_all x2 -> x3, waiting for transfers between devices: 6.27 us -> 22.6 us  [the longest x1 22.6 us: on_device(): gathered = [lax.all_to_all(shards[0], PLANE, 0, 0)]]
    all_gather x1 -> x2, waiting for transfers between devices: 0.01 us -> 10.1 us  [the longest x1 10.1 us: on_device(): q = lax.all_gather(rotated, Z, axis=0, tiled=False)]
    all_to_all x2 -> x3, starting transfers between devices: 10 us -> 18.2 us  [the longest x1 7.58 us: on_device(): packed = lax.all_to_all(packed, Z, 0, 0)]
    ppermute x14 -> x7, waiting for transfers between devices: 27.7 us -> 20 us  [moved(): return lax.ppermute(block, Z, [(i, (i + step) % nz) for i in range(nz)])]
    pallas_call x3 -> x6, Pallas kernels: 25.6 us -> 30.6 us  [the longest x2 23.7 us: attend(): pl.pallas_call(functools.partial(attend_kernel, per_group, unit, page, or...]
  transfers between devices with their start and end apart: 21 -> 16, of which waited for: 11 -> 12; matrix products, arithmetic and copies ran while one was open for 3% -> 3% of each run, Pallas kernels for 13% -> 16%
where the time goes in v3:
time: 205 us; the launch traced here: 202 us
  waiting for transfers between devices  84.7 us (41%)
  starting transfers between devices  50.8 us (25%)
  Pallas kernels  37.5 us (18%)
  between operations  13.6 us (7%)
  local copies, waits for them, and re-layouts  7.84 us (4%)
  other arithmetic  3.93 us (2%)
  matrix products  3.48 us (2%)
    pallas_call x2, Pallas kernels, attend(): pl.pallas_call(functools.partial(attend_kernel, per_group, unit, page, or...  23.7 us
    all_to_all x1, waiting for transfers between devices, on_device(): gathered = [lax.all_to_all(shards[0], PLANE, 0, 0)]  22.6 us
    ppermute x7, waiting for transfers between devices, moved(): return lax.ppermute(block, Z, [(i, (i + step) % nz) for i in range(nz)])  20 us
    all_to_all x1, waiting for transfers between devices, on_device(): restored = lax.all_to_all(restored, PLANE, 0, 0)  16.4 us
    ppermute x7, starting transfers between devices, moved(): return lax.ppermute(block, Z, [(i, (i + step) % nz) for i in range(nz)])  13.7 us
    all_gather x1, waiting for transfers between devices, on_device(): q = lax.all_gather(rotated, Z, axis=0, tiled=False)  10.1 us
    all_to_all x1, waiting for transfers between devices, on_device(): lax.all_to_all(terms.reshape(ny, nx, block_rows, columns), GRP, 0, 0)  8.59 us
    all_to_all x1, starting transfers between devices, on_device(): packed = lax.all_to_all(packed, Z, 0, 0)  7.58 us
  transfers between devices with their start and end apart: 16, of which 12 were waited for; matrix products, arithmetic and copies ran while one was open for 3% of the time, Pallas kernels for 16%

profile of v3, /device:TPU:6, one launch (start us, length us, event | category | flops | bytes accessed | tf_op | source)
XLA Modules:
  0.0 201.8 jit_solution(12536393515692556092)
XLA Ops:
  6.5 0.7 select_convert_fusion.table_ref.refs_8_.refs_1_
  7.2 0.7 convert_element_type.34
  8.2 1.8 rotate.1.after_ref
  10.0 0.6 pad.4.marks_ref
  10.6 2.6 %dequantize.2 = bf16[8,1040,128]{2,1,0:T(8,128)(2,1)} custom-call(s32[2,2,512,128]{3,2,1,0:T(8,128)} %codes_ref.3, f32[2,2,4,512]{3,2,1,0:T(4,128)} %scales_ref.3, bf16[8,16,128]{2,1,0:T(8,128)(2,1)} %pad.4.marks_ref, bf16[2,320,128]{2,1,0:T(8,128)(2,1)} %rotate.1.after_ref), custom_call_target="tpu_custom_call" | custom-call | tf_op jit(solution)/shard_map/dequantize/pallas_call | solution.py:55
  13.2 5.9 %all-to-all-start = ((bf16[8,1040,128]{2,1,0:T(8,128)(2,1)}), bf16[8,1040,128]{2,1,0:T(8,128)(2,1)S(1)}, u32[]{:S(2)}, u32[]{:S(2)}) async-start(bf16[8,1040,128]{2,1,0:T(8,128)(2,1)} %dequantize.2), calls=%async_computation | async-start | bytes 4259840 | tf_op jit(solution)/shard_map/all_to_all | solution.py:364
  19.2 0.7 all-gather.6.cloned.1.call-update
  19.9 2.7 %dequantize.3.block_ref = bf16[8,1024,128]{2,1,0:T(8,128)(2,1)} custom-call(s32[2,2,512,128]{3,2,1,0:T(8,128)} %codes_ref.3, f32[2,2,4,512]{3,2,1,0:T(4,128)} %scales_ref.3, bf16[8,16,128]{2,1,0:T(8,128)(2,1)} %pad.4.marks_ref, bf16[2,320,128]{2,1,0:T(8,128)(2,1)} %rotate.1.after_ref), custom_call_target="tpu_custom_call" | custom-call | tf_op jit(solution)/shard_map/dequantize/pallas_call | solution.py:55
  22.7 22.6 %all-to-all-done.kv_ref = bf16[8,1040,128]{2,1,0:T(8,128)(2,1)S(1)} async-done(((bf16[8,1040,128]{2,1,0:T(8,128)(2,1)}), bf16[8,1040,128]{2,1,0:T(8,128)(2,1)S(1)}, u32[]{:S(2)}, u32[]{:S(2)}) %all-to-all-start) | async-done | bytes 2129952 | tf_op jit(solution)/shard_map/all_to_all | solution.py:364
  45.6 1.1 reshape.94.after_ref
  46.6 4.7 %all-to-all-start.1 = ((bf16[8,1024,128]{2,1,0:T(8,128)(2,1)}), bf16[8,1024,128]{2,1,0:T(8,128)(2,1)S(1)}, u32[]{:S(2)}, u32[]{:S(2)}) async-start(bf16[8,1024,128]{2,1,0:T(8,128)(2,1)} %tie.1), calls=%async_computation.1 | async-start | bytes 4194304 | tf_op jit(solution)/shard_map/all_to_all | solution.py:381
  51.4 0.6 and_select_fusion.order_ref
  52.1 0.7 squeeze.14.reach_ref
  52.8 0.7 squeeze.15.reach_ref
  53.5 10.1 %all-gather.6.cloned.1.call-done = bf16[16,320,128]{2,1,0:T(8,128)(2,1)} async-done(((bf16[2,320,128]{2,1,0:T(8,128)(2,1)}), bf16[16,320,128]{2,1,0:T(8,128)(2,1)}) %all-gather.6.cloned.1.call-update) | async-done | bytes 1310736 | tf_op jit(solution)/shard_map/all_gather | solution.py:360
  63.6 1.6 pass.1
  65.3 11.7 %attend.2 = (bf16[352,128]{1,0:T(8,128)(2,1)}, bf16[352,128]{1,0:T(8,128)(2,1)}, bf16[352,128]{1,0:T(8,128)(2,1)}, bf16[352,128]{1,0:T(8,128)(2,1)}, bf16[352,12...) custom-call(s32[256]{0:T(256)} %squeeze.14.reach_ref, ...), custom_call_target="tpu_custom_call" | custom-call | flops 5368709120 | bytes 8388608 | tf_op jit(solution)/shard_map/attend/pallas_call | solution.py:267
  77.0 1.4 copy-done.2
  78.4 12.0 %attend.3 = bf16[8,352,128]{2,1,0:T(8,128)(2,1)} custom-call(s32[256]{0:T(256)} %squeeze.15.reach_ref, s32[8]{0:T(128)} %and_select_fusion.order_ref, bf16[8,2,320,128]{3,2,1,0:T(8,128)(2,1)} %bitcast.20, bf16[8,1024,128]{2,1,0:T(8,128)(2,1)} %copy-done.2, bf16[352,128]{1,0:T(8,128)(2,1)} %get-tuple-element.13.refs_0_.after_ref), custom_call_target="tpu_custom_call" | custom-call | flops 5368709120 | bytes 8388608 | tf_op jit(solution)/shard_map/attend/pallas_call | solution.py:267
  90.3 7.6 %all-to-all-start.2 = ((bf16[8,352,128]{2,1,0:T(8,128)(2,1)}), bf16[8,352,128]{2,1,0:T(8,128)(2,1)S(1)}, u32[]{:S(2)}, u32[]{:S(2)}) async-start(bf16[8,352,128]{2,1,0:T(8,128)(2,1)} %attend.3), calls=%async_computation.2 | async-start | bytes 1441792 | tf_op jit(solution)/shard_map/all_to_all | solution.py:386
  97.9 3.2 %collective-permute-start = (bf16[352,128]{1,0:T(8,128)(2,1)S(1)}, bf16[352,128]{1,0:T(8,128)(2,1)S(1)}, u32[]{:S(2)}, u32[]{:S(2)}) collective-permute-start(bf16[352,128]{1,0:T(8,128)(2,1)S(1)} %copy-done.16), channel_id=1, source_target_pairs={{0,28},{4,0},{8,4},{12,8},{16,12},{20,16},{24,20},{28,24},{1,29},{... | collective-permute-start | bytes 270344 | tf_op jit(solution)/shard_map/ppermute | solution.py:367
  101.2 2.4 %collective-permute-start.1 = (bf16[352,128]{1,0:T(8,128)(2,1)S(1)}, bf16[352,128]{1,0:T(8,128)(2,1)S(1)}, u32[]{:S(2)}, u32[]{:S(2)}) collective-permute-start(bf16[352,128]{1,0:T(8,128)(2,1)S(1)} %copy-done.15), channel_id=1, source_target_pairs={{0,24},{4,28},{8,0},{12,4},{16,8},{20,12},{24,16},{28,20},{1,25},{... | collective-permute-start | bytes 270344 | tf_op jit(solution)/shard_map/ppermute | solution.py:367
  103.5 1.5 collective-permute-start.2
  105.0 3.6 %collective-permute-start.3 = (bf16[352,128]{1,0:T(8,128)(2,1)S(1)}, bf16[352,128]{1,0:T(8,128)(2,1)S(1)}, u32[]{:S(2)}, u32[]{:S(2)}) collective-permute-start(bf16[352,128]{1,0:T(8,128)(2,1)S(1)} %copy-done.13), channel_id=1, source_target_pairs={{0,16},{4,20},{8,24},{12,28},{16,0},{20,4},{24,8},{28,12},{1,17},{... | collective-permute-start | bytes 270344 | tf_op jit(solution)/shard_map/ppermute | solution.py:367
  108.8 13.5 %collective-permute-done.refs_1_ = bf16[352,128]{1,0:T(8,128)(2,1)S(1)} collective-permute-done((bf16[352,128]{1,0:T(8,128)(2,1)S(1)}, bf16[352,128]{1,0:T(8,128)(2,1)S(1)}, u32[]{:S(2)}, u32[]{:S(2)}) %collective-permute-start) | collective-permute-done | bytes 90144 | tf_op jit(solution)/shard_map/ppermute | solution.py:367
  122.3 1.2 collective-permute-start.5
  123.5 1.9 collective-permute-done.1.refs_2_
  125.4 1.6 collective-permute-start.6
  127.1 1.2 collective-permute-done.2.refs_3_
  128.3 0.5 collective-permute-done.4.refs_5_
  128.8 1.3 collective-permute-done.5.refs_6_
  130.1 1.6 collective-permute-done.6.refs_7_
  131.8 0.6 copy-done.9
  132.4 2.6 %combine.2 = bf16[64,640]{1,0:T(8,128)(2,1)} custom-call(bf16[352,128]{1,0:T(8,128)(2,1)} %get-tuple-element.13.refs_0_.after_ref, bf16[352,128]{1,0:T(8,128)(2,1)} %copy-done.3, bf16[352,128]{1,0:T(8,128)(2,1)} %copy-done.4, bf16[352,128]{1,0:T(8,128)(2,1)} %copy-done.5, bf16[352,128]{1,0:T(8,128)(2,1)} %copy-done.6, bf16[352,128]{1,0:T(8,128)(2,1)} %copy-done.7, ...), custom_call_target="tpu_custom_call" | custom-call | tf_op jit(solution)/shard_map/combine/pallas_call | solution.py:332
  135.0 0.9 copy-done
  135.9 2.5 %combine.3 = bf16[64,640]{1,0:T(8,128)(2,1)} custom-call(bf16[8,352,128]{2,1,0:T(8,128)(2,1)} %copy-done, bf16[128,128]{1,0:T(8,128)(2,1)} %select_convert_fusion.table_ref.refs_8_.refs_1_), custom_call_target="tpu_custom_call" | custom-call | tf_op jit(solution)/shard_map/combine/pallas_call | solution.py:332
  138.4 0.9 pad_maximum_fusion
  139.3 1.2 broadcast_in_dim.37
  140.5 5.8 %all-to-all-start.3 = ((bf16[8,64,1280]{2,1,0:T(8,128)(2,1)}), bf16[8,64,1280]{2,1,0:T(8,128)(2,1)S(1)}, u32[]{:S(2)}, u32[]{:S(2)}) async-start(bf16[8,64,1280]{2,1,0:T(8,128)(2,1)} %broadcast_in_dim.37), calls=%async_computation.3 | async-start | bytes 2621440 | tf_op jit(solution)/shard_map/all_to_all | solution.py:391
  146.4 16.4 %all-to-all-done.3 = bf16[8,64,1280]{2,1,0:T(8,128)(2,1)S(1)} async-done(((bf16[8,64,1280]{2,1,0:T(8,128)(2,1)}), bf16[8,64,1280]{2,1,0:T(8,128)(2,1)S(1)}, u32[]{:S(2)}, u32[]{:S(2)}) %all-to-all-start.3) | async-done | bytes 1310752 | tf_op jit(solution)/shard_map/all_to_all | solution.py:391
  162.8 3.5 %convolution_convert_fusion = bf16[512,640]{1,0:T(8,128)(2,1)} fusion(bf16[512,1280]{1,0:T(8,128)(2,1)S(1)} %bitcast.16, bf16[640,1280]{1,0:T(8,128)(2,1)} %all-gather.4.cloned.1.call-done), kind=kOutput, calls=%fused_computation | convolution fusion | flops 839188480 | bytes 3604480 | tf_op jit(solution)/shard_map/dot_general | solution.py:392
  166.3 5.2 %all-to-all-start.4 = ((bf16[4,2,64,640]{3,2,1,0:T(8,128)(2,1)}), bf16[4,2,64,640]{3,2,1,0:T(8,128)(2,1)S(1)}, u32[]{:S(2)}, u32[]{:S(2)}) async-start(bf16[4,2,64,640]{3,2,1,0:T(8,128)(2,1)} %bitcast.6), calls=%async_computation.4 | async-start | bytes 1310720 | tf_op jit(solution)/shard_map/all_to_all | solution.py:399
  171.5 8.6 %all-to-all-done.4 = bf16[4,2,64,640]{3,2,1,0:T(8,128)(2,1)S(1)} async-done(((bf16[4,2,64,640]{3,2,1,0:T(8,128)(2,1)}), bf16[4,2,64,640]{3,2,1,0:T(8,128)(2,1)S(1)}, u32[]{:S(2)}, u32[]{:S(2)}) %all-to-all-start.4) | async-done | bytes 655392 | tf_op jit(solution)/shard_map/all_to_all | solution.py:399
  180.2 5.1 %collective-permute-start.7 = (bf16[64,640]{1,0:T(8,128)(2,1)S(1)}, bf16[64,640]{1,0:T(8,128)(2,1)S(1)}, u32[]{:S(2)}, u32[]{:S(2)}) collective-permute-start(bf16[64,640]{1,0:T(8,128)(2,1)S(1)} %get-tuple-element.23), channel_id=1, source_target_pairs={{0,0},{1,64},{2,128},{3,192},{32,32},{33,96},{34,160},{35,224},{64... | collective-permute-start | bytes 245768 | tf_op jit(solution)/shard_map/ppermute | solution.py:409
  185.3 2.7 %collective-permute-start.8 = (bf16[64,640]{1,0:T(8,128)(2,1)S(1)}, bf16[64,640]{1,0:T(8,128)(2,1)S(1)}, u32[]{:S(2)}, u32[]{:S(2)}) collective-permute-start(bf16[64,640]{1,0:T(8,128)(2,1)S(1)} %get-tuple-element.24), channel_id=1, source_target_pairs={{0,32},{1,96},{2,160},{3,224},{32,0},{33,64},{34,128},{35,192},{64... | collective-permute-start | bytes 245768 | tf_op jit(solution)/shard_map/ppermute | solution.py:412
  188.0 2.8 %collective-permute-done.7 = bf16[64,640]{1,0:T(8,128)(2,1)S(1)} collective-permute-done((bf16[64,640]{1,0:T(8,128)(2,1)S(1)}, bf16[64,640]{1,0:T(8,128)(2,1)S(1)}, u32[]{:S(2)}, u32[]{:S(2)}) %collective-permute-start.7) | collective-permute-done | bytes 81952 | tf_op jit(solution)/shard_map/ppermute | solution.py:409
  190.8 3.5 %collective-permute-done.8 = bf16[64,640]{1,0:T(8,128)(2,1)S(1)} collective-permute-done((bf16[64,640]{1,0:T(8,128)(2,1)S(1)}, bf16[64,640]{1,0:T(8,128)(2,1)S(1)}, u32[]{:S(2)}, u32[]{:S(2)}) %collective-permute-start.8) | collective-permute-done | bytes 81952 | tf_op jit(solution)/shard_map/ppermute | solution.py:412
  194.3 0.7 pad_maximum_fusion.1
  (59 shorter events, 1.4 us)
Async XLA Ops:
  13.2 32.0 %all-to-all-start = ((bf16[8,1040,128]{2,1,0:T(8,128)(2,1)}), bf16[8,1040,128]{2,1,0:T(8,128)(2,1)S(1)}, u32[]{:S(2)}, u32[]{:S(2)}) async-start(bf16[8,1040,128]{2,1,0:T(8,128)(2,1)} %dequantize.2), calls=%async_computation | async-start | bytes 4259840 | tf_op jit(solution)/shard_map/all_to_all | solution.py:364
  19.2 44.4 %all-gather.6.cloned.1.call-start = ((), (), s32[]{:S(2)}) async-start(), calls=%async_computation.6 | async-start | bytes 1474560 | tf_op jit(solution)/shard_map/all_gather | solution.py:360
  45.3 1.4 copy-start.1
  46.6 30.3 %all-to-all-start.1 = ((bf16[8,1024,128]{2,1,0:T(8,128)(2,1)}), bf16[8,1024,128]{2,1,0:T(8,128)(2,1)S(1)}, u32[]{:S(2)}, u32[]{:S(2)}) async-start(bf16[8,1024,128]{2,1,0:T(8,128)(2,1)} %tie.1), calls=%async_computation.1 | async-start | bytes 4194304 | tf_op jit(solution)/shard_map/all_to_all | solution.py:381
  51.4 95.0 %all-gather.4.cloned.1.call-start = ((), (), s32[]{:S(2)}) async-start(), calls=%async_computation.5 | async-start | bytes 1843200 | tf_op jit(solution)/shard_map/all_gather | solution.py:361
  77.0 1.4 copy-start.2
  78.3 19.6 %copy-start.16 = (bf16[352,128]{1,0:T(8,128)(2,1)S(1)}, bf16[352,128]{1,0:T(8,128)(2,1)}, u32[]{:S(2)}) copy-start(bf16[352,128]{1,0:T(8,128)(2,1)} %get-tuple-element.14) | copy-start | bytes 270340
  78.3 22.8 %copy-start.15 = (bf16[352,128]{1,0:T(8,128)(2,1)S(1)}, bf16[352,128]{1,0:T(8,128)(2,1)}, u32[]{:S(2)}) copy-start(bf16[352,128]{1,0:T(8,128)(2,1)} %get-tuple-element.15) | copy-start | bytes 270340
  78.3 25.2 %copy-start.14 = (bf16[352,128]{1,0:T(8,128)(2,1)S(1)}, bf16[352,128]{1,0:T(8,128)(2,1)}, u32[]{:S(2)}) copy-start(bf16[352,128]{1,0:T(8,128)(2,1)} %get-tuple-element.16) | copy-start | bytes 270340
  78.3 26.7 %copy-start.13 = (bf16[352,128]{1,0:T(8,128)(2,1)S(1)}, bf16[352,128]{1,0:T(8,128)(2,1)}, u32[]{:S(2)}) copy-start(bf16[352,128]{1,0:T(8,128)(2,1)} %get-tuple-element.17) | copy-start | bytes 270340
  78.3 30.2 %copy-start.12 = (bf16[352,128]{1,0:T(8,128)(2,1)S(1)}, bf16[352,128]{1,0:T(8,128)(2,1)}, u32[]{:S(2)}) copy-start(bf16[352,128]{1,0:T(8,128)(2,1)} %get-tuple-element.18) | copy-start | bytes 270340
  78.3 44.0 %copy-start.11 = (bf16[352,128]{1,0:T(8,128)(2,1)S(1)}, bf16[352,128]{1,0:T(8,128)(2,1)}, u32[]{:S(2)}) copy-start(bf16[352,128]{1,0:T(8,128)(2,1)} %get-tuple-element.19) | copy-start | bytes 270340
  78.3 47.1 %copy-start.10 = (bf16[352,128]{1,0:T(8,128)(2,1)S(1)}, bf16[352,128]{1,0:T(8,128)(2,1)}, u32[]{:S(2)}) copy-start(bf16[352,128]{1,0:T(8,128)(2,1)} %get-tuple-element.20) | copy-start | bytes 270340
  90.3 44.7 %all-to-all-start.2 = ((bf16[8,352,128]{2,1,0:T(8,128)(2,1)}), bf16[8,352,128]{2,1,0:T(8,128)(2,1)S(1)}, u32[]{:S(2)}, u32[]{:S(2)}) async-start(bf16[8,352,128]{2,1,0:T(8,128)(2,1)} %attend.3), calls=%async_computation.2 | async-start | bytes 1441792 | tf_op jit(solution)/shard_map/all_to_all | solution.py:386
  97.9 24.4 %collective-permute-start = (bf16[352,128]{1,0:T(8,128)(2,1)S(1)}, bf16[352,128]{1,0:T(8,128)(2,1)S(1)}, u32[]{:S(2)}, u32[]{:S(2)}) collective-permute-start(bf16[352,128]{1,0:T(8,128)(2,1)S(1)} %copy-done.16), channel_id=1, source_target_pairs={{0,28},{4,0},{8,4},{12,8},{16,12},{20,16},{24,20},{28,24},{1,29},{... | collective-permute-start | bytes 270344 | tf_op jit(solution)/shard_map/ppermute | solution.py:367
  101.2 24.3 %collective-permute-start.1 = (bf16[352,128]{1,0:T(8,128)(2,1)S(1)}, bf16[352,128]{1,0:T(8,128)(2,1)S(1)}, u32[]{:S(2)}, u32[]{:S(2)}) collective-permute-start(bf16[352,128]{1,0:T(8,128)(2,1)S(1)} %copy-done.15), channel_id=1, source_target_pairs={{0,24},{4,28},{8,0},{12,4},{16,8},{20,12},{24,16},{28,20},{1,25},{... | collective-permute-start | bytes 270344 | tf_op jit(solution)/shard_map/ppermute | solution.py:367
  103.5 24.8 %collective-permute-start.2 = (bf16[352,128]{1,0:T(8,128)(2,1)S(1)}, bf16[352,128]{1,0:T(8,128)(2,1)S(1)}, u32[]{:S(2)}, u32[]{:S(2)}) collective-permute-start(bf16[352,128]{1,0:T(8,128)(2,1)S(1)} %copy-done.14), channel_id=1, source_target_pairs={{0,20},{4,24},{8,28},{12,0},{16,4},{20,8},{24,12},{28,16},{1,21},{... | collective-permute-start | bytes 270344 | tf_op jit(solution)/shard_map/ppermute | solution.py:367
  105.0 23.3 %collective-permute-start.3 = (bf16[352,128]{1,0:T(8,128)(2,1)S(1)}, bf16[352,128]{1,0:T(8,128)(2,1)S(1)}, u32[]{:S(2)}, u32[]{:S(2)}) collective-permute-start(bf16[352,128]{1,0:T(8,128)(2,1)S(1)} %copy-done.13), channel_id=1, source_target_pairs={{0,16},{4,20},{8,24},{12,28},{16,0},{20,4},{24,8},{28,12},{1,17},{... | collective-permute-start | bytes 270344 | tf_op jit(solution)/shard_map/ppermute | solution.py:367
  108.6 20.3 %collective-permute-start.4 = (bf16[352,128]{1,0:T(8,128)(2,1)S(1)}, bf16[352,128]{1,0:T(8,128)(2,1)S(1)}, u32[]{:S(2)}, u32[]{:S(2)}) collective-permute-start(bf16[352,128]{1,0:T(8,128)(2,1)S(1)} %copy-done.12), channel_id=1, source_target_pairs={{0,12},{4,16},{8,20},{12,24},{16,28},{20,0},{24,4},{28,8},{1,13},{... | collective-permute-start | bytes 270344 | tf_op jit(solution)/shard_map/ppermute | solution.py:367
  122.3 9.4 %copy-start.3 = (bf16[352,128]{1,0:T(8,128)(2,1)}, bf16[352,128]{1,0:T(8,128)(2,1)S(1)}, u32[]{:S(2)}) copy-start(bf16[352,128]{1,0:T(8,128)(2,1)S(1)} %collective-permute-done.refs_1_) | copy-start | bytes 270340
  122.3 7.8 %collective-permute-start.5 = (bf16[352,128]{1,0:T(8,128)(2,1)S(1)}, bf16[352,128]{1,0:T(8,128)(2,1)S(1)}, u32[]{:S(2)}, u32[]{:S(2)}) collective-permute-start(bf16[352,128]{1,0:T(8,128)(2,1)S(1)} %copy-done.11), channel_id=1, source_target_pairs={{0,8},{4,12},{8,16},{12,20},{16,24},{20,28},{24,0},{28,4},{1,9},{5... | collective-permute-start | bytes 270344 | tf_op jit(solution)/shard_map/ppermute | solution.py:367
  125.4 6.3 %copy-start.4 = (bf16[352,128]{1,0:T(8,128)(2,1)}, bf16[352,128]{1,0:T(8,128)(2,1)S(1)}, u32[]{:S(2)}) copy-start(bf16[352,128]{1,0:T(8,128)(2,1)S(1)} %collective-permute-done.1.refs_2_) | copy-start | bytes 270340
  125.4 6.3 %collective-permute-start.6 = (bf16[352,128]{1,0:T(8,128)(2,1)S(1)}, bf16[352,128]{1,0:T(8,128)(2,1)S(1)}, u32[]{:S(2)}, u32[]{:S(2)}) collective-permute-start(bf16[352,128]{1,0:T(8,128)(2,1)S(1)} %copy-done.10), channel_id=1, source_target_pairs={{0,4},{4,8},{8,12},{12,16},{16,20},{20,24},{24,28},{28,0},{1,5},{5... | collective-permute-start | bytes 270344 | tf_op jit(solution)/shard_map/ppermute | solution.py:367
  128.3 3.4 %copy-start.5 = (bf16[352,128]{1,0:T(8,128)(2,1)}, bf16[352,128]{1,0:T(8,128)(2,1)S(1)}, u32[]{:S(2)}) copy-start(bf16[352,128]{1,0:T(8,128)(2,1)S(1)} %collective-permute-done.2.refs_3_) | copy-start | bytes 270340
  128.3 3.4 %copy-start.6 = (bf16[352,128]{1,0:T(8,128)(2,1)}, bf16[352,128]{1,0:T(8,128)(2,1)S(1)}, u32[]{:S(2)}) copy-start(bf16[352,128]{1,0:T(8,128)(2,1)S(1)} %collective-permute-done.3.refs_4_) | copy-start | bytes 270340
  128.8 2.9 %copy-start.7 = (bf16[352,128]{1,0:T(8,128)(2,1)}, bf16[352,128]{1,0:T(8,128)(2,1)S(1)}, u32[]{:S(2)}) copy-start(bf16[352,128]{1,0:T(8,128)(2,1)S(1)} %collective-permute-done.4.refs_5_) | copy-start | bytes 270340
  130.1 1.6 copy-start.8
  131.8 0.7 copy-start.9
  135.0 0.9 copy-start
  140.5 22.3 %all-to-all-start.3 = ((bf16[8,64,1280]{2,1,0:T(8,128)(2,1)}), bf16[8,64,1280]{2,1,0:T(8,128)(2,1)S(1)}, u32[]{:S(2)}, u32[]{:S(2)}) async-start(bf16[8,64,1280]{2,1,0:T(8,128)(2,1)} %broadcast_in_dim.37), calls=%async_computation.3 | async-start | bytes 2621440 | tf_op jit(solution)/shard_map/all_to_all | solution.py:391
  166.3 13.8 %all-to-all-start.4 = ((bf16[4,2,64,640]{3,2,1,0:T(8,128)(2,1)}), bf16[4,2,64,640]{3,2,1,0:T(8,128)(2,1)S(1)}, u32[]{:S(2)}, u32[]{:S(2)}) async-start(bf16[4,2,64,640]{3,2,1,0:T(8,128)(2,1)} %bitcast.6), calls=%async_computation.4 | async-start | bytes 1310720 | tf_op jit(solution)/shard_map/all_to_all | solution.py:399
  180.2 10.6 %collective-permute-start.7 = (bf16[64,640]{1,0:T(8,128)(2,1)S(1)}, bf16[64,640]{1,0:T(8,128)(2,1)S(1)}, u32[]{:S(2)}, u32[]{:S(2)}) collective-permute-start(bf16[64,640]{1,0:T(8,128)(2,1)S(1)} %get-tuple-element.23), channel_id=1, source_target_pairs={{0,0},{1,64},{2,128},{3,192},{32,32},{33,96},{34,160},{35,224},{64... | collective-permute-start | bytes 245768 | tf_op jit(solution)/shard_map/ppermute | solution.py:409
  185.3 9.0 %collective-permute-start.8 = (bf16[64,640]{1,0:T(8,128)(2,1)S(1)}, bf16[64,640]{1,0:T(8,128)(2,1)S(1)}, u32[]{:S(2)}, u32[]{:S(2)}) collective-permute-start(bf16[64,640]{1,0:T(8,128)(2,1)S(1)} %get-tuple-element.24), channel_id=1, source_target_pairs={{0,32},{1,96},{2,160},{3,224},{32,0},{33,64},{34,128},{35,192},{64... | collective-permute-start | bytes 245768 | tf_op jit(solution)/shard_map/ppermute | solution.py:412
Sparse Core Ops, SparseCore 0:
  21.8 41.7 all-gather.5
  65.4 43.2 all-gather.3

commit v4 on v2

--- a/solution.py
+++ b/solution.py
@@ -27,11 +27,10 @@
     return jnp.where(parity == 1, -1.0, 1.0).astype(jnp.float32)
 
 
-def dequantize_kernel(codes_ref, scales_ref, marks_ref, *outs):
+def dequantize_kernel(codes_ref, scales_ref, marks_ref, after_ref, out):
     kinds, groups, length, width = codes_ref.shape
     parts = scales_ref.shape[2]
     for g in range(groups):
-        out = outs[g]
         for kind in range(kinds):
             scales = scales_ref[kind, g]
             spread = jnp.concatenate(
@@ -44,21 +43,22 @@
             values = (codes_ref[kind, g].astype(jnp.float32) - 7.5) * spread.T
             values = values.astype(jnp.bfloat16)
             for copy in range(out.shape[0]):
-                out[copy, pl.ds(kind * length, length), :] = values
-        for copy in range(out.shape[0]):
-            out[copy, pl.ds(kinds * length, 16), :] = marks_ref[g, copy]
-
-
-def dequantize(codes, scales, marks):
+                out[copy, pl.ds((g * kinds + kind) * length, length), :] = values
+    for copy in range(out.shape[0]):
+        out[copy, pl.ds(groups * kinds * length, 16), :] = marks_ref[copy]
+
+
+def dequantize(codes, scales, marks, after):
     kinds, groups, length, width = codes.shape
-    copies = marks.shape[1]
-    out = jax.ShapeDtypeStruct((copies, kinds * length + 16, width), jnp.bfloat16)
+    shape = (marks.shape[0], groups * kinds * length + 16, width)
+    whole = pl.BlockSpec(memory_space=pltpu.VMEM)
     return pl.pallas_call(
         dequantize_kernel,
-        out_shape=[out] * groups,
+        in_specs=[whole, whole, whole, pl.BlockSpec(memory_space=pl.ANY)],
+        out_shape=jax.ShapeDtypeStruct(shape, jnp.bfloat16),
         compiler_params=pltpu.CompilerParams(vmem_limit_bytes=VMEM_LIMIT),
         name="dequantize",
-    )(codes, scales, marks)
+    )(codes, scales, marks, after)
 
 
 def rotate_kernel(queries_ref, table_ref, out_ref):
@@ -88,19 +88,13 @@
     )(queries, table)
 
 
-def attend_kernel(per_group, unit, page, blocks, ordered, *refs):
-    if ordered:
-        reach_ref, order_ref = refs[:2]
-        refs = refs[2:]
-    else:
-        reach_ref = refs[0]
-        refs = refs[1:]
-    q_refs, kv_ref, refs = refs[:blocks], refs[blocks], refs[blocks + 1 :]
-    outs, (pages_ref, s_ref, top_ref, sum_ref, acc_ref) = refs[:-5], refs[-5:]
-    _, rows, width = q_refs[0].shape
+def attend_kernel(per_group, unit, page, blocks, reach_ref, order_ref, *refs):
+    q_refs, kv_ref, after_ref, packed_ref = refs[: blocks // 2], *refs[blocks // 2 : blocks // 2 + 3]
+    pages_ref, s_ref, top_ref, sum_ref, acc_ref = refs[blocks // 2 + 3 :]
+    _, _, rows, width = q_refs[0].shape
     tokens = rows // per_group
     sources, height, _ = kv_ref.shape
-    length = (height - 16) // 2
+    length = height // 2
     shard_pages = length // page
     all_pages = sources * shard_pages
     masked_at = all_pages + unit
@@ -151,7 +145,7 @@
         for b in range(blocks):
             at = pl.ds(b * rows, rows)
             s = lax.dot_general(
-                q_refs[b][0], k, (((1,), (1,)), ((), ())), preferred_element_type=jnp.float32
+                q_refs[b // 2][b % 2, 0], k, (((1,), (1,)), ((), ())), preferred_element_type=jnp.float32
             )
             top = top_ref[at, :]
             for u in range(unit):
@@ -210,43 +204,39 @@
         low = across - high - middle
         tail = jnp.concatenate([high, middle, low, jnp.zeros_like(low)], axis=0)
         tail = tail.astype(jnp.bfloat16)
-        if ordered:
-            outs[0][order_ref[b], pl.ds(0, rows), :] = out
-            outs[0][order_ref[b], pl.ds(rows, 32), :] = tail
-        else:
-            outs[b][pl.ds(0, rows), :] = out
-            outs[b][pl.ds(rows, 32), :] = tail
-
-
-def attend(q_blocks, kv, g, per_group, reach, order=None):
-    blocks = len(q_blocks)
-    _, rows, width = q_blocks[0].shape
+        packed_ref[order_ref[b], pl.ds(0, rows), :] = out
+        packed_ref[order_ref[b], pl.ds(rows, 32), :] = tail
+
+
+def attend(q_pairs, kv, g, per_group, reach, order, after):
+    blocks = 2 * len(q_pairs)
+    _, groups, rows, width = q_pairs[0].shape
     sources, height, _ = kv.shape
+    height = (height - 16) // groups
     page = 128
-    pages = sources * ((height - 16) // 2 // page)
+    pages = sources * (height // 2 // page)
     unit = 4
-    ordered = order is not None
-    prefetched = (reach, order) if ordered else (reach,)
-    part = (rows + 32, width)
-    if ordered:
-        out_shape = jax.ShapeDtypeStruct((blocks,) + part, jnp.bfloat16)
-        out_specs = pl.BlockSpec((blocks,) + part, lambda t, *_: (0, 0, 0))
-    else:
-        out_shape = [jax.ShapeDtypeStruct(part, jnp.bfloat16)] * blocks
-        out_specs = [pl.BlockSpec(part, lambda t, *_: (0, 0))] * blocks
+    packed = (blocks, rows + 32, width)
     scores = blocks * rows * pages * page // 2
     once = pl.Buffered(1)
     return pl.pallas_call(
-        functools.partial(attend_kernel, per_group, unit, page, blocks, ordered),
+        functools.partial(attend_kernel, per_group, unit, page, blocks),
         grid_spec=pltpu.PrefetchScalarGridSpec(
-            num_scalar_prefetch=len(prefetched),
+            num_scalar_prefetch=2,
             grid=(1,),
             in_specs=[
-                pl.BlockSpec((1, rows, width), lambda t, *_: (g, 0, 0), pipeline_mode=once)
+                pl.BlockSpec(
+                    (2, 1, rows, width), lambda t, *_: (0, g, 0, 0), pipeline_mode=once
+                )
             ]
-            * blocks
-            + [pl.BlockSpec(kv.shape, lambda t, *_: (0, 0, 0), pipeline_mode=once)],
-            out_specs=out_specs,
+            * len(q_pairs)
+            + [
+                pl.BlockSpec(
+                    (sources, height, width), lambda t, *_: (0, g, 0), pipeline_mode=once
+                ),
+                pl.BlockSpec(memory_space=pl.ANY),
+            ],
+            out_specs=pl.BlockSpec(packed, lambda t, *_: (0, 0, 0)),
             scratch_shapes=[
                 pltpu.SMEM((2 * (pages + unit),), jnp.int32),
                 pltpu.VMEM((pages // unit + 1, blocks * rows, unit * page), jnp.float32),
@@ -255,20 +245,18 @@
                 pltpu.VMEM((blocks * rows, width), jnp.float32),
             ],
         ),
-        out_shape=out_shape,
+        out_shape=jax.ShapeDtypeStruct(packed, jnp.bfloat16),
         compiler_params=pltpu.CompilerParams(vmem_limit_bytes=VMEM_LIMIT),
         cost_estimate=pl.CostEstimate(
             flops=8 * scores * width, bytes_accessed=8 * 1024 * 1024, transcendentals=scores
         ),
         name="attend",
-    )(*prefetched, *q_blocks, kv)
-
-
-def combine_kernel(per_group, *refs):
-    parts, table_ref, out_ref = refs[:-2], refs[-2], refs[-1]
-    if len(parts) == 1:
-        parts = [parts[0].at[e] for e in range(parts[0].shape[0])]
-    height, width = parts[0].shape
+    )(reach, order, *q_pairs, kv, after)
+
+
+def combine_kernel(per_group, parts_ref, table_ref, after_ref, out_ref):
+    sources, height, width = parts_ref.shape
+    parts = [parts_ref.at[e] for e in range(sources)]
     rows = height - 32
     tokens = rows // per_group
     lse = []
@@ -279,31 +267,65 @@
     weights = [jnp.exp2(x - top) for x in lse]
     total = functools.reduce(jnp.add, weights)
     weights = jnp.concatenate([w / total for w in weights], axis=0).T
+    attended = []
     for h in range(per_group):
-        attended = jnp.zeros((tokens, width), jnp.float32)
+        one = jnp.zeros((tokens, width), jnp.float32)
         for e, part in enumerate(parts):
             value = part[pl.ds(h * tokens, tokens), :].astype(jnp.float32)
-            attended = attended + value * weights[:tokens, e * 8 + h : e * 8 + h + 1]
-        restored = jnp.dot(
-            attended,
-            table_ref[...],
-            preferred_element_type=jnp.float32,
-            precision=lax.Precision.HIGHEST,
-        )
-        restored = (restored * (1.0 / math.sqrt(width))).astype(jnp.bfloat16)
-        for copy in range(out_ref.shape[0]):
-            out_ref[copy, :, h * width : (h + 1) * width] = restored
-
-
-def combine(parts, table, per_group, copies):
-    height, width = parts[0].shape[-2:]
+            one = one + value * weights[:tokens, e * 8 + h : e * 8 + h + 1]
+        attended.append(one)
+    attended = jnp.concatenate(attended, axis=0)
+    high = attended.astype(jnp.bfloat16)
+    low = (attended - high.astype(jnp.float32)).astype(jnp.bfloat16)
+    restored = jnp.dot(high, table_ref[...], preferred_element_type=jnp.float32)
+    restored = restored + jnp.dot(low, table_ref[...], preferred_element_type=jnp.float32)
+    restored = (restored * (1.0 / math.sqrt(width))).astype(jnp.bfloat16)
+    for copy in range(out_ref.shape[0]):
+        for h in range(per_group):
+            part = restored[h * tokens : (h + 1) * tokens]
+            out_ref[copy, :, h * width : (h + 1) * width] = part
+
+
+def combine(parts, table, per_group, copies, after):
+    _, height, width = parts.shape
     tokens = (height - 32) // per_group
+    whole = pl.BlockSpec(memory_space=pltpu.VMEM)
     return pl.pallas_call(
         functools.partial(combine_kernel, per_group),
+        in_specs=[whole, whole, pl.BlockSpec(memory_space=pl.ANY)],
         out_shape=jax.ShapeDtypeStruct((copies, tokens, per_group * width), jnp.bfloat16),
         compiler_params=pltpu.CompilerParams(vmem_limit_bytes=VMEM_LIMIT),
         name="combine",
-    )(*parts, table)
+    )(parts, table, after)
+
+
+def project_kernel(plane, place_ref, *refs):
+    firsts, second_ref, weights_ref, out_ref, rows_ref = refs[: plane // 2], *refs[plane // 2 :]
+    tokens, half = firsts[0].shape[-2:]
+    for d in range(plane):
+        source = place_ref[0] ^ d
+        at = pl.ds(pl.multiple_of(source * tokens, tokens), tokens)
+        rows_ref[at, pl.ds(0, half)] = firsts[d // 2][d % 2]
+    for e in range(plane):
+        rows_ref[pl.ds(e * tokens, tokens), pl.ds(half, half)] = second_ref[e]
+    terms = lax.dot_general(
+        rows_ref[...], weights_ref[...], (((1,), (1,)), ((), ())), preferred_element_type=jnp.float32
+    )
+    out_ref[...] = terms.astype(jnp.bfloat16).reshape(out_ref.shape)
+
+
+def project(firsts, second, weights, place):
+    plane, tokens, half = second.shape
+    columns = weights.shape[0]
+    whole = pl.BlockSpec(memory_space=pltpu.VMEM)
+    return pl.pallas_call(
+        functools.partial(project_kernel, plane),
+        in_specs=[pl.BlockSpec(memory_space=pltpu.SMEM)] + [whole] * (len(firsts) + 2),
+        out_shape=jax.ShapeDtypeStruct((plane, tokens, columns), jnp.bfloat16),
+        scratch_shapes=[pltpu.VMEM((plane * tokens, 2 * half), jnp.bfloat16)],
+        compiler_params=pltpu.CompilerParams(vmem_limit_bytes=VMEM_LIMIT),
+        name="project",
+    )(place, *firsts, second, weights)
 
 
 def on_device(queries, cache_codes, cache_scales, pattern, out_weight):
@@ -322,44 +344,51 @@
     table = hadamard(width)
 
     marks = pattern.reshape(groups, plane, 1, nz * pages).astype(jnp.bfloat16)
-    marks = jnp.pad(marks, ((0, 0), (0, 0), (0, 15), (0, width - nz * pages)))
-    shards = dequantize(cache_codes, cache_scales, marks)
-    gathered = [lax.all_to_all(shard, PLANE, 0, 0) for shard in shards]
+    marks = jnp.transpose(marks, (1, 2, 0, 3)).reshape(plane, 1, -1)
+    marks = jnp.pad(marks, ((0, 0), (0, 15), (0, width - marks.shape[2])))
+
+    weight_rows = lax.all_gather(out_weight.T, Z, axis=0, tiled=True)
+    rotated = rotate(queries, table.astype(jnp.bfloat16), groups)
+    shards = dequantize(cache_codes, cache_scales, marks, rotated)
+    kv = lax.all_to_all(shards, PLANE, 0, 0)
 
     def moved(block, step):
         return lax.ppermute(block, Z, [(i, (i + step) % nz) for i in range(nz)])
 
-    rotated = rotate(queries, table.astype(jnp.bfloat16), groups)
-    q_blocks = [rotated] + [moved(rotated, i) for i in range(1, nz)]
-    at = (z - jnp.arange(nz, dtype=jnp.int32)) % nz
+    pair = jnp.stack([rotated, moved(rotated, nz // 2)])
+    steps = [0, 1, -1, 2]
+    q_pairs = [pair] + [moved(pair, step) for step in steps[1:]]
+    back = jnp.array([s + far for s in steps for far in (0, nz // 2)], jnp.int32)
+    at = (z - back) % nz
     first_query = total_len - total_q + ((y * nx + x) * nz + at) * block_rows
 
-    weight_rows, _ = lax.optimization_barrier((out_weight.T, q_blocks[-1]))
-    weight_rows = lax.all_gather(weight_rows, Z, axis=0, tiled=True)
-
-    def reach_of(kv):
-        kept = kv[:, 2 * shard_len, : nz * pages].astype(jnp.float32).reshape(plane, nz, pages)
-        kept = jnp.transpose(kept, (0, 2, 1))
-        kept = jnp.flip(jnp.roll(kept, nz - 1 - z, axis=2), axis=2)
-        shard = jnp.arange(plane, dtype=jnp.int32) * nz + z
-        first_key = shard[:, None] * shard_len + jnp.arange(pages, dtype=jnp.int32) * page
-        causal = jnp.clip(first_query[None, None, :] - first_key[:, :, None], -2 * page, 2 * page)
-        return jnp.where(kept > 0.5, causal, -2 * page).reshape(-1)
-
-    parts = attend(q_blocks, gathered[0], 0, per_group, reach_of(gathered[0]))
-    received = [[parts[0]] + [moved(parts[i], -i) for i in range(1, nz)]]
-    parts = attend(q_blocks, gathered[1], 1, per_group, reach_of(gathered[1]), at)
-    received.append([lax.all_to_all(parts, Z, 0, 0)])
-    restored = [combine(r, table, per_group, plane) for r in received]
-    restored = jnp.concatenate(restored, axis=2)
-    restored = lax.all_to_all(restored, PLANE, 0, 0)
-    terms = lax.dot_general(
-        restored.reshape(plane * block_rows, heads * width),
-        weight_rows,
-        (((1,), (1,)), ((), ())),
-        preferred_element_type=jnp.float32,
-    ).astype(jnp.bfloat16)
-    columns = terms.shape[1]
+    kept = kv[:, 2 * groups * shard_len, : groups * nz * pages].astype(jnp.float32)
+    kept = kept.reshape(plane, groups, nz, pages)
+    kept = jnp.transpose(kept, (1, 0, 3, 2))
+    kept = sum(
+        jnp.where(at == i, kept[..., i : i + 1], 0.0) for i in range(nz)
+    )
+    shard = jnp.arange(plane, dtype=jnp.int32) * nz + z
+    first_key = shard[:, None] * shard_len + jnp.arange(pages, dtype=jnp.int32) * page
+    causal = jnp.clip(first_query[None, None, :] - first_key[:, :, None], -2 * page, 2 * page)
+    reach = jnp.where(kept > 0.5, causal[None], -2 * page).reshape(groups, -1)
+
+    signs = table.astype(jnp.bfloat16)
+    packed = attend(q_pairs, kv, 0, per_group, reach[0], at, kv)
+    first = lax.all_to_all(packed, Z, 0, 0)
+    packed = attend(q_pairs, kv, 1, per_group, reach[1], at, weight_rows)
+    second = lax.all_to_all(packed, Z, 0, 0)
+    first = combine(first, signs, per_group, 1, first)
+    beside = lax.ppermute(first, PLANE, [(e, e ^ 1) for e in range(plane)])
+    first = jnp.concatenate([first, beside], axis=0)
+    firsts = [first]
+    for d in range(2, plane, 2):
+        firsts.append(lax.ppermute(first, PLANE, [(e, e ^ d) for e in range(plane)]))
+    second = combine(second, signs, per_group, plane, sum(f[0, 0, :1] for f in firsts))
+    second = lax.all_to_all(second, PLANE, 0, 0)
+    place = (y * nx + x).astype(jnp.int32).reshape(1)
+    terms = project(firsts, second, weight_rows, place)
+    columns = terms.shape[2]
     terms = lax.all_to_all(terms.reshape(ny, nx, block_rows, columns), GRP, 0, 0)
     share = jnp.sum(terms.astype(jnp.float32), axis=0).astype(jnp.bfloat16)
 

time: 224 us -> 199 us (0.89)
  blocking collectives: 32.3 us -> 15.7 us
  starting transfers between devices: 63.3 us -> 50.6 us
  Pallas kernels: 33.3 us -> 40.7 us
  local copies, waits for them, and re-layouts: 4.77 us -> 8.32 us
  matrix products: 3.5 us -> 0 us
  waiting for transfers between devices: 65.9 us -> 63 us
  between operations: 13.6 us -> 16 us
  other arithmetic: 6.58 us -> 4.21 us
    ppermute x14 -> x4, waiting for transfers between devices: 27.7 us -> 3.47 us  [moved(): return lax.ppermute(block, Z, [(i, (i + step) % nz) for i in range(nz)])]
    ppermute x14 -> x4, starting transfers between devices: 35.2 us -> 14.7 us  [moved(): return lax.ppermute(block, Z, [(i, (i + step) % nz) for i in range(nz)])]
    all_to_all x1, blocking collectives: 32.3 us -> 15.7 us  [on_device(): second = lax.all_to_all(second, PLANE, 0, 0)]
    all_to_all x3, waiting for transfers between devices: 23.8 us -> 37.5 us  [the longest x1 30.2 us: on_device(): kv = lax.all_to_all(shards, PLANE, 0, 0)]
    ppermute x0 -> x4, waiting for transfers between devices: none -> 7.58 us  [the longest x3 4.15 us: on_device(): lax.ppermute(first, PLANE, [(e, e ^ d) for e in range(plane)])]
    ppermute x0 -> x4, starting transfers between devices: none -> 6.02 us  [the longest x3 4.8 us: on_device(): lax.ppermute(first, PLANE, [(e, e ^ d) for e in range(plane)])]
    pallas_call x2, Pallas kernels: 22.1 us -> 25.9 us  [attend(): pl.pallas_call(functools.partial(attend_kernel, per_group, unit, page, bl...]
    pallas_call x3 -> x4, Pallas kernels: 9.37 us -> 13 us  [the longest x2 5.28 us: combine(): pl.pallas_call(functools.partial(combine_kernel, per_group), in_specs=[wh...]
  transfers between devices with their start and end apart: 21 -> 15, of which waited for: 11 -> 10; matrix products, arithmetic and copies ran while one was open for 3% -> 4% of each run, Pallas kernels for 13% -> 14%
where the time goes in v4:
time: 199 us; the launch traced here: 198 us
  waiting for transfers between devices  63 us (32%)
  starting transfers between devices  50.6 us (25%)
  Pallas kernels  40.7 us (20%)
  between operations  16 us (8%)
  blocking collectives  15.7 us (8%)
  local copies, waits for them, and re-layouts  8.32 us (4%)
  other arithmetic  4.21 us (2%)
    all_to_all x1, waiting for transfers between devices, on_device(): kv = lax.all_to_all(shards, PLANE, 0, 0)  30.2 us
    pallas_call x2, Pallas kernels, attend(): pl.pallas_call(functools.partial(attend_kernel, per_group, unit, page, bl...  25.9 us
    all_to_all x1, blocking collectives, on_device(): second = lax.all_to_all(second, PLANE, 0, 0)  15.7 us
    ppermute x4, starting transfers between devices, moved(): return lax.ppermute(block, Z, [(i, (i + step) % nz) for i in range(nz)])  14.7 us
    all_to_all x1, waiting for transfers between devices, on_device(): lax.all_to_all(terms.reshape(ny, nx, block_rows, columns), GRP, 0, 0)  8.59 us
    all_to_all x1, waiting for transfers between devices, on_device(): first = lax.all_to_all(packed, Z, 0, 0)  7.23 us
    all_to_all x1, starting transfers between devices, on_device(): first = lax.all_to_all(packed, Z, 0, 0)  7.12 us
    all_to_all x1, starting transfers between devices, on_device(): kv = lax.all_to_all(shards, PLANE, 0, 0)  6.06 us
  transfers between devices with their start and end apart: 15, of which 10 were waited for; matrix products, arithmetic and copies ran while one was open for 4% of the time, Pallas kernels for 14%

profile of v4, /device:TPU:6, one launch (start us, length us, event | category | flops | bytes accessed | tf_op | source)
XLA Modules:
  0.0 198.4 jit_solution(8679916541625268222)
XLA Ops:
  6.5 0.7 select_convert_fusion.table_ref
  7.2 0.7 convert_element_type.31
  8.2 1.8 rotate.1.after_ref
  10.0 0.6 pad.4.marks_ref
  10.6 3.6 %dequantize.1 = bf16[8,2064,128]{2,1,0:T(8,128)(2,1)} custom-call(s32[2,2,512,128]{3,2,1,0:T(8,128)} %codes_ref.1, f32[2,2,4,512]{3,2,1,0:T(4,128)} %scales_ref.1, bf16[8,16,128]{2,1,0:T(8,128)(2,1)} %pad.4.marks_ref, bf16[2,320,128]{2,1,0:T(8,128)(2,1)} %rotate.1.after_ref), custom_call_target="tpu_custom_call" | custom-call | tf_op jit(solution)/shard_map/dequantize/pallas_call | solution.py:55
  14.3 6.1 %all-to-all-start = ((bf16[8,2064,128]{2,1,0:T(8,128)(2,1)}), bf16[8,2064,128]{2,1,0:T(8,128)(2,1)}, u32[]{:S(2)}, u32[]{:S(2)}) async-start(bf16[8,2064,128]{2,1,0:T(8,128)(2,1)} %dequantize.1), calls=%async_computation | async-start | bytes 8454144 | tf_op jit(solution)/shard_map/all_to_all | solution.py:353
  20.3 7.3 %collective-permute-start = (bf16[2,320,128]{2,1,0:T(8,128)(2,1)S(1)}, bf16[2,320,128]{2,1,0:T(8,128)(2,1)S(1)}, u32[]{:S(2)}, u32[]{:S(2)}) collective-permute-start(bf16[2,320,128]{2,1,0:T(8,128)(2,1)S(1)} %copy-done.2), channel_id=1, source_target_pairs={{0,16},{4,20},{8,24},{12,28},{16,0},{20,4},{24,8},{28,12},{1,17},{... | collective-permute-start | bytes 491528 | tf_op jit(solution)/shard_map/ppermute | solution.py:356
  27.9 3.5 %collective-permute-done = bf16[2,320,128]{2,1,0:T(8,128)(2,1)S(1)} collective-permute-done((bf16[2,320,128]{2,1,0:T(8,128)(2,1)S(1)}, bf16[2,320,128]{2,1,0:T(8,128)(2,1)S(1)}, u32[]{:S(2)}, u32[]{:S(2)}) %collective-permute-start) | collective-permute-done | bytes 163872 | tf_op jit(solution)/shard_map/ppermute | solution.py:356
  31.4 4.3 %collective-permute-start.1 = (bf16[2,2,320,128]{3,2,1,0:T(8,128)(2,1)S(1)}, bf16[2,2,320,128]{3,2,1,0:T(8,128)(2,1)S(1)}, u32[]{:S(2)}, u32[]{:S(2)}) collective-permute-start(bf16[2,2,320,128]{3,2,1,0:T(8,128)(2,1)S(1)} %pad_maximum_fusion.refs_0_), channel_id=1, source_target_pairs={{0,4},{4,8},{8,12},{12,16},{16,20},{20,24},{24,28},{28,0},{1,5},{5... | collective-permute-start | bytes 983048 | tf_op jit(solution)/shard_map/ppermute | solution.py:356
  35.7 2.6 %collective-permute-start.2 = (bf16[2,2,320,128]{3,2,1,0:T(8,128)(2,1)S(1)}, bf16[2,2,320,128]{3,2,1,0:T(8,128)(2,1)S(1)}, u32[]{:S(2)}, u32[]{:S(2)}) collective-permute-start(bf16[2,2,320,128]{3,2,1,0:T(8,128)(2,1)S(1)} %pad_maximum_fusion.refs_0_), channel_id=1, source_target_pairs={{0,28},{4,0},{8,4},{12,8},{16,12},{20,16},{24,20},{28,24},{1,29},{... | collective-permute-start | bytes 983048 | tf_op jit(solution)/shard_map/ppermute | solution.py:356
  38.3 0.5 collective-permute-start.3
  38.8 30.2 %all-to-all-done.refs_4_.refs_5_ = bf16[8,2064,128]{2,1,0:T(8,128)(2,1)} async-done(((bf16[8,2064,128]{2,1,0:T(8,128)(2,1)}), bf16[8,2064,128]{2,1,0:T(8,128)(2,1)}, u32[]{:S(2)}, u32[]{:S(2)}) %all-to-all-start) | async-done | bytes 4227104 | tf_op jit(solution)/shard_map/all_to_all | solution.py:353
  69.0 0.7 slice_convert_fusion
  70.6 0.2 fusion
  70.8 0.7 squeeze.18.reach_ref
  71.5 0.7 copy-done.10
  72.3 0.7 copy-done.12
  73.0 12.0 %attend.2 = bf16[8,352,128]{2,1,0:T(8,128)(2,1)} custom-call(s32[256]{0:T(256)} %squeeze.18.reach_ref, s32[8]{0:T(128)} %copy-done.8, bf16[2,2,320,128]{3,2,1,0:T(8,128)(2,1)} %copy-done.4, bf16[2,2,320,128]{3,2,1,0:T(8,128)(2,1)} %copy-done.10, bf16[2,2,320,128]{3,2,1,0:T(8,128)(2,1)} %copy-done.11, bf16[2,2,320,128]{3,2,1,0:T(8,128)(2,1)} %copy-done.12, ...), custom_call_target="tpu_custom_call" | custom-call | flops 5368709120 | bytes 8388608 | tf_op jit(solution)/shard_map/attend/pallas_call | solution.py:222
  85.0 7.1 %all-to-all-start.1 = ((bf16[8,352,128]{2,1,0:T(8,128)(2,1)}), bf16[8,352,128]{2,1,0:T(8,128)(2,1)S(1)}, u32[]{:S(2)}, u32[]{:S(2)}) async-start(bf16[8,352,128]{2,1,0:T(8,128)(2,1)} %attend.2), calls=%async_computation.1 | async-start | bytes 1441792 | tf_op jit(solution)/shard_map/all_to_all | solution.py:378
  92.1 0.7 squeeze.19.reach_ref
  92.8 14.0 %attend.3 = bf16[8,352,128]{2,1,0:T(8,128)(2,1)} custom-call(s32[256]{0:T(256)} %squeeze.19.reach_ref, s32[8]{0:T(128)} %copy-done.8, bf16[2,2,320,128]{3,2,1,0:T(8,128)(2,1)} %copy-done.4, bf16[2,2,320,128]{3,2,1,0:T(8,128)(2,1)} %copy-done.10, bf16[2,2,320,128]{3,2,1,0:T(8,128)(2,1)} %copy-done.11, bf16[2,2,320,128]{3,2,1,0:T(8,128)(2,1)} %copy-done.12, ...), custom_call_target="tpu_custom_call" | custom-call | flops 5368709120 | bytes 8388608 | tf_op jit(solution)/shard_map/attend/pallas_call | solution.py:222
  106.8 7.2 %all-to-all-done.1.parts_ref.after_ref = bf16[8,352,128]{2,1,0:T(8,128)(2,1)S(1)} async-done(((bf16[8,352,128]{2,1,0:T(8,128)(2,1)}), bf16[8,352,128]{2,1,0:T(8,128)(2,1)S(1)}, u32[]{:S(2)}, u32[]{:S(2)}) %all-to-all-start.1) | async-done | bytes 720928 | tf_op jit(solution)/shard_map/all_to_all | solution.py:378
  114.0 3.5 %all-to-all-start.2 = ((bf16[8,352,128]{2,1,0:T(8,128)(2,1)}), bf16[8,352,128]{2,1,0:T(8,128)(2,1)S(1)}, u32[]{:S(2)}, u32[]{:S(2)}) async-start(bf16[8,352,128]{2,1,0:T(8,128)(2,1)} %attend.3), calls=%async_computation.2 | async-start | bytes 1441792 | tf_op jit(solution)/shard_map/all_to_all | solution.py:380
  117.6 2.5 %combine.2 = bf16[1,64,640]{2,1,0:T(8,128)(2,1)} custom-call(bf16[8,352,128]{2,1,0:T(8,128)(2,1)} %copy-done, bf16[128,128]{1,0:T(8,128)(2,1)} %select_convert_fusion.table_ref, bf16[8,352,128]{2,1,0:T(8,128)(2,1)} %copy-done), custom_call_target="tpu_custom_call" | custom-call | tf_op jit(solution)/shard_map/combine/pallas_call | solution.py:293
  120.1 1.2 collective-permute-start.4
  121.3 3.4 %collective-permute-done.4 = bf16[1,64,640]{2,1,0:T(8,128)(2,1)S(1)} collective-permute-done((bf16[1,64,640]{2,1,0:T(8,128)(2,1)}, bf16[1,64,640]{2,1,0:T(8,128)(2,1)S(1)}, u32[]{:S(2)}, u32[]{:S(2)}) %collective-permute-start.4) | collective-permute-done | bytes 81952 | tf_op jit(solution)/shard_map/ppermute | solution.py:382
  124.7 0.9 pad_maximum_fusion.1.refs_0_
  125.6 2.0 %collective-permute-start.5 = (bf16[2,64,640]{2,1,0:T(8,128)(2,1)S(1)}, bf16[2,64,640]{2,1,0:T(8,128)(2,1)S(1)}, u32[]{:S(2)}, u32[]{:S(2)}) collective-permute-start(bf16[2,64,640]{2,1,0:T(8,128)(2,1)S(1)} %pad_maximum_fusion.1.refs_0_), channel_id=1, source_target_pairs={{0,64},{32,96},{64,0},{96,32},{128,192},{160,224},{192,128},{224,1... | collective-permute-start | bytes 491528 | tf_op jit(solution)/shard_map/ppermute | solution.py:386
  127.7 2.1 %collective-permute-start.6 = (bf16[2,64,640]{2,1,0:T(8,128)(2,1)S(1)}, bf16[2,64,640]{2,1,0:T(8,128)(2,1)S(1)}, u32[]{:S(2)}, u32[]{:S(2)}) collective-permute-start(bf16[2,64,640]{2,1,0:T(8,128)(2,1)S(1)} %pad_maximum_fusion.1.refs_0_), channel_id=1, source_target_pairs={{0,128},{32,160},{64,192},{96,224},{128,0},{160,32},{192,64},{224,... | collective-permute-start | bytes 491528 | tf_op jit(solution)/shard_map/ppermute | solution.py:386
  129.7 0.7 collective-permute-start.7
  130.4 1.2 slice.73
  131.6 1.2 collective-permute-done.5.refs_1_
  132.9 0.5 slice.74
  134.6 2.0 collective-permute-done.6.refs_2_
  136.6 0.5 slice.75
  137.7 1.0 collective-permute-done.7.refs_3_
  138.6 0.5 slice.76
  139.7 0.9 copy-done.1
  140.6 2.8 %combine.3 = bf16[8,64,640]{2,1,0:T(8,128)(2,1)} custom-call(bf16[8,352,128]{2,1,0:T(8,128)(2,1)} %copy-done.1, bf16[128,128]{1,0:T(8,128)(2,1)} %select_convert_fusion.table_ref, bf16[1]{0:T(256)(128)(2,1)} %bitcast.16.after_ref), custom_call_target="tpu_custom_call" | custom-call | tf_op jit(solution)/shard_map/combine/pallas_call | solution.py:293
  143.4 15.7 %all_to_all.25.refs_4_ = bf16[8,64,640]{2,1,0:T(8,128)(2,1)} all-to-all(bf16[8,64,640]{2,1,0:T(8,128)(2,1)} %combine.3), channel_id=1, replica_groups=mesh['y'=4,'x_lo'=2,'z'=8,'x_hi'=2,'core'=2] {'y','x_lo'}, dimensions={0} | all-to-all | bytes 1310720 | tf_op jit(solution)/shard_map/all_to_all | solution.py:388
  159.1 4.1 %project.1 = bf16[8,64,640]{2,1,0:T(8,128)(2,1)} custom-call(s32[1]{0:T(128)} %bitcast.place_ref, bf16[2,64,640]{2,1,0:T(8,128)(2,1)} %copy-done.3, bf16[2,64,640]{2,1,0:T(8,128)(2,1)} %copy-done.5, bf16[2,64,640]{2,1,0:T(8,128)(2,1)} %copy-done.6, bf16[2,64,640]{2,1,0:T(8,128)(2,1)} %copy-done.7, bf16[8,64,640]{2,1,0:T(8,128)(2,1)} %all_to_all.25.refs_4_, ...), custom_call_target="tpu_custom_call" | custom-call | tf_op jit(solution)/shard_map/project/pallas_call | solution.py:321
  163.2 4.8 %all-to-all-start.4 = ((bf16[4,2,64,640]{3,2,1,0:T(8,128)(2,1)}), bf16[4,2,64,640]{3,2,1,0:T(8,128)(2,1)S(1)}, u32[]{:S(2)}, u32[]{:S(2)}) async-start(bf16[4,2,64,640]{3,2,1,0:T(8,128)(2,1)} %bitcast.32), calls=%async_computation.4 | async-start | bytes 1310720 | tf_op jit(solution)/shard_map/all_to_all | solution.py:392
  168.0 8.6 %all-to-all-done.4 = bf16[4,2,64,640]{3,2,1,0:T(8,128)(2,1)S(1)} async-done(((bf16[4,2,64,640]{3,2,1,0:T(8,128)(2,1)}), bf16[4,2,64,640]{3,2,1,0:T(8,128)(2,1)S(1)}, u32[]{:S(2)}, u32[]{:S(2)}) %all-to-all-start.4) | async-done | bytes 655392 | tf_op jit(solution)/shard_map/all_to_all | solution.py:392
  176.7 5.5 %collective-permute-start.8 = (bf16[64,640]{1,0:T(8,128)(2,1)S(1)}, bf16[64,640]{1,0:T(8,128)(2,1)S(1)}, u32[]{:S(2)}, u32[]{:S(2)}) collective-permute-start(bf16[64,640]{1,0:T(8,128)(2,1)S(1)} %get-tuple-element.9), channel_id=1, source_target_pairs={{0,0},{1,64},{2,128},{3,192},{32,32},{33,96},{34,160},{35,224},{64... | collective-permute-start | bytes 245768 | tf_op jit(solution)/shard_map/ppermute | solution.py:402
  182.2 2.8 %collective-permute-start.9 = (bf16[64,640]{1,0:T(8,128)(2,1)S(1)}, bf16[64,640]{1,0:T(8,128)(2,1)S(1)}, u32[]{:S(2)}, u32[]{:S(2)}) collective-permute-start(bf16[64,640]{1,0:T(8,128)(2,1)S(1)} %get-tuple-element.10), channel_id=1, source_target_pairs={{0,32},{1,96},{2,160},{3,224},{32,0},{33,64},{34,128},{35,192},{64... | collective-permute-start | bytes 245768 | tf_op jit(solution)/shard_map/ppermute | solution.py:405
  185.0 2.3 %collective-permute-done.8 = bf16[64,640]{1,0:T(8,128)(2,1)S(1)} collective-permute-done((bf16[64,640]{1,0:T(8,128)(2,1)S(1)}, bf16[64,640]{1,0:T(8,128)(2,1)S(1)}, u32[]{:S(2)}, u32[]{:S(2)}) %collective-permute-start.8) | collective-permute-done | bytes 81952 | tf_op jit(solution)/shard_map/ppermute | solution.py:402
  187.4 3.5 %collective-permute-done.9 = bf16[64,640]{1,0:T(8,128)(2,1)S(1)} collective-permute-done((bf16[64,640]{1,0:T(8,128)(2,1)S(1)}, bf16[64,640]{1,0:T(8,128)(2,1)S(1)}, u32[]{:S(2)}, u32[]{:S(2)}) %collective-permute-start.9) | collective-permute-done | bytes 81952 | tf_op jit(solution)/shard_map/ppermute | solution.py:405
  190.9 0.7 pad_maximum_fusion.2
  (56 shorter events, 1.7 us)
Async XLA Ops:
  14.3 6.1 %copy-start.2 = (bf16[2,320,128]{2,1,0:T(8,128)(2,1)S(1)}, bf16[2,320,128]{2,1,0:T(8,128)(2,1)}, u32[]{:S(2)}) copy-start(bf16[2,320,128]{2,1,0:T(8,128)(2,1)} %rotate.1.after_ref) | copy-start | bytes 491524
  14.3 13.4 %copy-start.9 = (s32[8]{0:T(128)S(1)}, s32[8]{0:T(128)}, u32[]{:S(2)}) copy-start(s32[8]{0:T(128)} %constant.97) | copy-start | bytes 100
  14.3 54.8 %all-to-all-start = ((bf16[8,2064,128]{2,1,0:T(8,128)(2,1)}), bf16[8,2064,128]{2,1,0:T(8,128)(2,1)}, u32[]{:S(2)}, u32[]{:S(2)}) async-start(bf16[8,2064,128]{2,1,0:T(8,128)(2,1)} %dequantize.1), calls=%async_computation | async-start | bytes 8454144 | tf_op jit(solution)/shard_map/all_to_all | solution.py:353
  20.3 72.5 %all-gather.2.cloned.1.call-start = ((), (), s32[]{:S(2)}) async-start(), calls=%async_computation.5 | async-start | bytes 1843200 | tf_op jit(solution)/shard_map/all_gather | solution.py:350
  20.3 11.0 %collective-permute-start = (bf16[2,320,128]{2,1,0:T(8,128)(2,1)S(1)}, bf16[2,320,128]{2,1,0:T(8,128)(2,1)S(1)}, u32[]{:S(2)}, u32[]{:S(2)}) collective-permute-start(bf16[2,320,128]{2,1,0:T(8,128)(2,1)S(1)} %copy-done.2), channel_id=1, source_target_pairs={{0,16},{4,20},{8,24},{12,28},{16,0},{20,4},{24,8},{28,12},{1,17},{... | collective-permute-start | bytes 491528 | tf_op jit(solution)/shard_map/ppermute | solution.py:356
  27.7 43.7 %copy-start.8 = (s32[8]{0:T(128)}, s32[8]{0:T(128)S(1)}, u32[]{:S(2)}) copy-start(s32[8]{0:T(128)S(1)} %get-tuple-element.6.order_ref) | copy-start | bytes 100
  31.4 40.1 %copy-start.4 = (bf16[2,2,320,128]{3,2,1,0:T(8,128)(2,1)}, bf16[2,2,320,128]{3,2,1,0:T(8,128)(2,1)S(1)}, u32[]{:S(2)}) copy-start(bf16[2,2,320,128]{3,2,1,0:T(8,128)(2,1)S(1)} %pad_maximum_fusion.refs_0_) | copy-start | bytes 983044
  31.4 40.0 %collective-permute-start.1 = (bf16[2,2,320,128]{3,2,1,0:T(8,128)(2,1)S(1)}, bf16[2,2,320,128]{3,2,1,0:T(8,128)(2,1)S(1)}, u32[]{:S(2)}, u32[]{:S(2)}) collective-permute-start(bf16[2,2,320,128]{3,2,1,0:T(8,128)(2,1)S(1)} %pad_maximum_fusion.refs_0_), channel_id=1, source_target_pairs={{0,4},{4,8},{8,12},{12,16},{16,20},{20,24},{24,28},{28,0},{1,5},{5... | collective-permute-start | bytes 983048 | tf_op jit(solution)/shard_map/ppermute | solution.py:356
  35.7 35.8 %collective-permute-start.2 = (bf16[2,2,320,128]{3,2,1,0:T(8,128)(2,1)S(1)}, bf16[2,2,320,128]{3,2,1,0:T(8,128)(2,1)S(1)}, u32[]{:S(2)}, u32[]{:S(2)}) collective-permute-start(bf16[2,2,320,128]{3,2,1,0:T(8,128)(2,1)S(1)} %pad_maximum_fusion.refs_0_), channel_id=1, source_target_pairs={{0,28},{4,0},{8,4},{12,8},{16,12},{20,16},{24,20},{28,24},{1,29},{... | collective-permute-start | bytes 983048 | tf_op jit(solution)/shard_map/ppermute | solution.py:356
  38.3 33.2 %collective-permute-start.3 = (bf16[2,2,320,128]{3,2,1,0:T(8,128)(2,1)S(1)}, bf16[2,2,320,128]{3,2,1,0:T(8,128)(2,1)S(1)}, u32[]{:S(2)}, u32[]{:S(2)}) collective-permute-start(bf16[2,2,320,128]{3,2,1,0:T(8,128)(2,1)S(1)} %pad_maximum_fusion.refs_0_), channel_id=1, source_target_pairs={{0,8},{4,12},{8,16},{12,20},{16,24},{20,28},{24,0},{28,4},{1,9},{5... | collective-permute-start | bytes 983048 | tf_op jit(solution)/shard_map/ppermute | solution.py:356
  71.4 0.7 copy-start.10
  71.4 0.8 copy-start.11
  72.3 0.7 copy-start.12
  85.0 29.0 %all-to-all-start.1 = ((bf16[8,352,128]{2,1,0:T(8,128)(2,1)}), bf16[8,352,128]{2,1,0:T(8,128)(2,1)S(1)}, u32[]{:S(2)}, u32[]{:S(2)}) async-start(bf16[8,352,128]{2,1,0:T(8,128)(2,1)} %attend.2), calls=%async_computation.1 | async-start | bytes 1441792 | tf_op jit(solution)/shard_map/all_to_all | solution.py:378
  114.0 3.6 %copy-start = (bf16[8,352,128]{2,1,0:T(8,128)(2,1)}, bf16[8,352,128]{2,1,0:T(8,128)(2,1)S(1)}, u32[]{:S(2)}) copy-start(bf16[8,352,128]{2,1,0:T(8,128)(2,1)S(1)} %all-to-all-done.1.parts_ref.after_ref) | copy-start | bytes 2162692
  114.0 25.7 %all-to-all-start.2 = ((bf16[8,352,128]{2,1,0:T(8,128)(2,1)}), bf16[8,352,128]{2,1,0:T(8,128)(2,1)S(1)}, u32[]{:S(2)}, u32[]{:S(2)}) async-start(bf16[8,352,128]{2,1,0:T(8,128)(2,1)} %attend.3), calls=%async_computation.2 | async-start | bytes 1441792 | tf_op jit(solution)/shard_map/all_to_all | solution.py:380
  120.1 4.7 %collective-permute-start.4 = (bf16[1,64,640]{2,1,0:T(8,128)(2,1)}, bf16[1,64,640]{2,1,0:T(8,128)(2,1)S(1)}, u32[]{:S(2)}, u32[]{:S(2)}) collective-permute-start(bf16[1,64,640]{2,1,0:T(8,128)(2,1)} %combine.2), channel_id=1, source_target_pairs={{0,32},{32,0},{64,96},{96,64},{128,160},{160,128},{192,224},{224,1... | collective-permute-start | bytes 245768 | tf_op jit(solution)/shard_map/ppermute | solution.py:382
  125.6 33.5 %copy-start.3 = (bf16[2,64,640]{2,1,0:T(8,128)(2,1)}, bf16[2,64,640]{2,1,0:T(8,128)(2,1)S(1)}, u32[]{:S(2)}) copy-start(bf16[2,64,640]{2,1,0:T(8,128)(2,1)S(1)} %pad_maximum_fusion.1.refs_0_) | copy-start | bytes 491524
  125.6 7.2 %collective-permute-start.5 = (bf16[2,64,640]{2,1,0:T(8,128)(2,1)S(1)}, bf16[2,64,640]{2,1,0:T(8,128)(2,1)S(1)}, u32[]{:S(2)}, u32[]{:S(2)}) collective-permute-start(bf16[2,64,640]{2,1,0:T(8,128)(2,1)S(1)} %pad_maximum_fusion.1.refs_0_), channel_id=1, source_target_pairs={{0,64},{32,96},{64,0},{96,32},{128,192},{160,224},{192,128},{224,1... | collective-permute-start | bytes 491528 | tf_op jit(solution)/shard_map/ppermute | solution.py:386
  127.7 8.9 %collective-permute-start.6 = (bf16[2,64,640]{2,1,0:T(8,128)(2,1)S(1)}, bf16[2,64,640]{2,1,0:T(8,128)(2,1)S(1)}, u32[]{:S(2)}, u32[]{:S(2)}) collective-permute-start(bf16[2,64,640]{2,1,0:T(8,128)(2,1)S(1)} %pad_maximum_fusion.1.refs_0_), channel_id=1, source_target_pairs={{0,128},{32,160},{64,192},{96,224},{128,0},{160,32},{192,64},{224,... | collective-permute-start | bytes 491528 | tf_op jit(solution)/shard_map/ppermute | solution.py:386
  129.7 8.9 %collective-permute-start.7 = (bf16[2,64,640]{2,1,0:T(8,128)(2,1)S(1)}, bf16[2,64,640]{2,1,0:T(8,128)(2,1)S(1)}, u32[]{:S(2)}, u32[]{:S(2)}) collective-permute-start(bf16[2,64,640]{2,1,0:T(8,128)(2,1)S(1)} %pad_maximum_fusion.1.refs_0_), channel_id=1, source_target_pairs={{0,192},{32,224},{64,128},{96,160},{128,64},{160,96},{192,0},{224,... | collective-permute-start | bytes 491528 | tf_op jit(solution)/shard_map/ppermute | solution.py:386
  132.9 26.2 %copy-start.5 = (bf16[2,64,640]{2,1,0:T(8,128)(2,1)}, bf16[2,64,640]{2,1,0:T(8,128)(2,1)S(1)}, u32[]{:S(2)}) copy-start(bf16[2,64,640]{2,1,0:T(8,128)(2,1)S(1)} %collective-permute-done.5.refs_1_) | copy-start | bytes 491524
  136.6 22.5 %copy-start.6 = (bf16[2,64,640]{2,1,0:T(8,128)(2,1)}, bf16[2,64,640]{2,1,0:T(8,128)(2,1)S(1)}, u32[]{:S(2)}) copy-start(bf16[2,64,640]{2,1,0:T(8,128)(2,1)S(1)} %collective-permute-done.6.refs_2_) | copy-start | bytes 491524
  138.6 20.5 %copy-start.7 = (bf16[2,64,640]{2,1,0:T(8,128)(2,1)}, bf16[2,64,640]{2,1,0:T(8,128)(2,1)S(1)}, u32[]{:S(2)}) copy-start(bf16[2,64,640]{2,1,0:T(8,128)(2,1)S(1)} %collective-permute-done.7.refs_3_) | copy-start | bytes 491524
  139.7 0.9 copy-start.1
  163.2 13.4 %all-to-all-start.4 = ((bf16[4,2,64,640]{3,2,1,0:T(8,128)(2,1)}), bf16[4,2,64,640]{3,2,1,0:T(8,128)(2,1)S(1)}, u32[]{:S(2)}, u32[]{:S(2)}) async-start(bf16[4,2,64,640]{3,2,1,0:T(8,128)(2,1)} %bitcast.32), calls=%async_computation.4 | async-start | bytes 1310720 | tf_op jit(solution)/shard_map/all_to_all | solution.py:392
  176.7 10.7 %collective-permute-start.8 = (bf16[64,640]{1,0:T(8,128)(2,1)S(1)}, bf16[64,640]{1,0:T(8,128)(2,1)S(1)}, u32[]{:S(2)}, u32[]{:S(2)}) collective-permute-start(bf16[64,640]{1,0:T(8,128)(2,1)S(1)} %get-tuple-element.9), channel_id=1, source_target_pairs={{0,0},{1,64},{2,128},{3,192},{32,32},{33,96},{34,160},{35,224},{64... | collective-permute-start | bytes 245768 | tf_op jit(solution)/shard_map/ppermute | solution.py:402
  182.2 8.7 %collective-permute-start.9 = (bf16[64,640]{1,0:T(8,128)(2,1)S(1)}, bf16[64,640]{1,0:T(8,128)(2,1)S(1)}, u32[]{:S(2)}, u32[]{:S(2)}) collective-permute-start(bf16[64,640]{1,0:T(8,128)(2,1)S(1)} %get-tuple-element.10), channel_id=1, source_target_pairs={{0,32},{1,96},{2,160},{3,224},{32,0},{33,64},{34,128},{35,192},{64... | collective-permute-start | bytes 245768 | tf_op jit(solution)/shard_map/ppermute | solution.py:405
Sparse Core Ops, SparseCore 0:
  27.8 48.6 all-gather.1

commit v5 on v2

v5 whole, which is shorter than its diff:
```python
import functools
import math

import jax
import jax.numpy as jnp
from jax import lax
from jax.experimental import pallas as pl
from jax.experimental.pallas import tpu as pltpu
from jax.sharding import Mesh
from jax.sharding import PartitionSpec as P

NEG_FILL = -1e30
LOG2E = math.log2(math.e)
VMEM_LIMIT = 60 * 1024 * 1024

Y, X, Z = "y", "x_lo", "z"
PLANE = (Y, X)
GRP = ("x_hi", "core")


def hadamard(order):
    index = jnp.arange(order, dtype=jnp.int32)
    common = index[:, None] & index[None, :]
    parity = jnp.zeros((order, order), jnp.int32)
    for shift_bit in range(int(order).bit_length()):
        parity = parity ^ common >> shift_bit & 1
    return jnp.where(parity == 1, -1.0, 1.0).astype(jnp.float32)


def dequantize_kernel(codes_ref, scales_ref, out):
    kinds, groups, length, width = codes_ref.shape
    parts = scales_ref.shape[2]
    for g in range(groups):
        for kind in range(kinds):
            scales = scales_ref[kind, g]
            spread = jnp.concatenate(
                [
                    jnp.broadcast_to(scales[i : i + 1], (width // parts, length))
                    for i in range(parts)
                ],
                axis=0,
            )
            values = (codes_ref[kind, g].astype(jnp.float32) - 7.5) * spread.T
            values = values.astype(jnp.bfloat16)
            for copy in range(out.shape[0]):
                out[copy, pl.ds((g * kinds + kind) * length, length), :] = values


def dequantize(codes, scales, copies):
    kinds, groups, length, width = codes.shape
    shape = (copies, groups * kinds * length, width)
    return pl.pallas_call(
        dequantize_kernel,
        out_shape=jax.ShapeDtypeStruct(shape, jnp.bfloat16),
        compiler_params=pltpu.CompilerParams(vmem_limit_bytes=VMEM_LIMIT),
        name="dequantize",
    )(codes, scales)


def tie_kernel(block_ref, after_ref, out_ref):
    pass


def tied(block, after):
    anywhere = pl.BlockSpec(memory_space=pl.ANY)
    return pl.pallas_call(
        tie_kernel,
        in_specs=[anywhere, anywhere],
        out_specs=anywhere,
        out_shape=jax.ShapeDtypeStruct(block.shape, block.dtype),
        input_output_aliases={0: 0},
        name="tie",
    )(block, after)


def rotate_kernel(queries_ref, table_ref, out_ref):
    groups, rows, width = out_ref.shape
    tokens = queries_ref.shape[0]
    per_group = rows // tokens
    scale = LOG2E / width
    for h in range(groups * per_group):
        turned = jnp.dot(
            queries_ref[:, h * width : (h + 1) * width],
            table_ref[...],
            preferred_element_type=jnp.float32,
        )
        at = pl.ds(h % per_group * tokens, tokens)
        out_ref[h // per_group, at, :] = (turned * scale).astype(jnp.bfloat16)


def rotate(queries, table, groups):
    tokens, columns = queries.shape
    width = table.shape[0]
    rows = columns // width // groups * tokens
    return pl.pallas_call(
        rotate_kernel,
        out_shape=jax.ShapeDtypeStruct((groups, rows, width), jnp.bfloat16),
        compiler_params=pltpu.CompilerParams(vmem_limit_bytes=VMEM_LIMIT),
        name="rotate",
    )(queries, table)


def attend_kernel(per_group, unit, page, held, reach_ref, order_ref, *refs):
    q_refs, kv_ref, packed_ref = refs[: len(held)], *refs[len(held) : len(held) + 2]
    pages_ref, s_ref, top_ref, sum_ref, acc_ref = refs[len(held) + 2 :]
    queries = [ref.at[i, 0] for ref, n in zip(q_refs, held) for i in range(n)]
    blocks = len(queries)
    rows, width = queries[0].shape
    tokens = rows // per_group
    sources, height, _ = kv_ref.shape
    length = height // 2
    shard_pages = length // page
    all_pages = sources * shard_pages
    masked_at = all_pages + unit
    group_at = pl.program_id(0) * all_pages

    def place(p, counts):
        full, some = counts
        reaches = [reach_ref[(group_at + p) * blocks + b] for b in range(blocks)]
        low = functools.reduce(jnp.minimum, reaches)
        high = functools.reduce(jnp.maximum, reaches)
        pages_ref[full] = p
        pages_ref[masked_at + some] = p
        whole = low >= page - 1
        part = jnp.logical_and(high > -tokens, low < page - 1)
        return full + whole.astype(jnp.int32), some + part.astype(jnp.int32)

    start = (jnp.int32(0), jnp.int32(0))
    full, some = lax.fori_loop(0, all_pages, place, start, unroll=4)
    whole = full // unit

    def leftover(i, some):
        pages_ref[masked_at + some] = pages_ref[whole * unit + i]
        return some + 1

    some = lax.fori_loop(0, full - whole * unit, leftover, some)
    rounds = (some + unit - 1) // unit

    def pad(i, _):
        pages_ref[masked_at + some + i] = -1
        return 0

    lax.fori_loop(0, rounds * unit - some, pad, 0)

    ahead = lax.broadcasted_iota(jnp.int32, (tokens, page), 1) - lax.broadcasted_iota(
        jnp.int32, (tokens, page), 0
    )
    top_ref[...] = jnp.full(top_ref.shape, NEG_FILL, jnp.float32)
    sum_ref[...] = jnp.zeros(sum_ref.shape, jnp.float32)
    acc_ref[...] = jnp.zeros(acc_ref.shape, jnp.float32)

    def fetch(p, at):
        first = pl.multiple_of(at + p % shard_pages * page, page)
        return kv_ref[p // shard_pages, pl.ds(first, page), :]

    def first_pass(i, base, slot, masked):
        ps = [pages_ref[base + i * unit + u] for u in range(unit)]
        pages_at = [jnp.maximum(p, 0) for p in ps]
        k = jnp.concatenate([fetch(p, 0) for p in pages_at], axis=0)
        for b in range(blocks):
            at = pl.ds(b * rows, rows)
            s = lax.dot_general(
                queries[b][...], k, (((1,), (1,)), ((), ())), preferred_element_type=jnp.float32
            )
            top = top_ref[at, :]
            for u in range(unit):
                x = s[:, u * page : (u + 1) * page]
                if masked:
                    reach = jnp.where(ps[u] < 0, -2 * page, reach_ref[(group_at + pages_at[u]) * blocks + b])
                    x = x.reshape(per_group, tokens, page)
                    x = jnp.where((ahead <= reach)[None], x, NEG_FILL).reshape(rows, page)
                s_ref[slot, at, u * page : (u + 1) * page] = x
                top = jnp.maximum(top, x)
            top_ref[at, :] = top
        return 0

    def second_pass(i, base, slot):
        pages_at = [jnp.maximum(pages_ref[base + i * unit + u], 0) for u in range(unit)]
        v = jnp.concatenate([fetch(p, length) for p in pages_at], axis=0)
        for b in range(blocks):
            at = pl.ds(b * rows, rows)
            top = top_ref[at, :]
            weights = [
                jnp.exp2(s_ref[slot, at, u * page : (u + 1) * page] - top) for u in range(unit)
            ]
            sum_ref[at, :] = sum_ref[at, :] + functools.reduce(jnp.add, weights)
            weights = jnp.concatenate([w.astype(jnp.bfloat16) for w in weights], axis=1)
            acc_ref[at, :] = acc_ref[at, :] + jnp.dot(
                weights, v, preferred_element_type=jnp.float32
            )
        return 0

    lax.fori_loop(0, whole, lambda i, _: first_pass(i, 0, i, False), 0)
    lax.fori_loop(0, rounds, lambda i, _: first_pass(i, masked_at, whole + i, True), 0)
    for b in range(blocks):
        at = pl.ds(b * rows, rows)
        top = jnp.max(top_ref[at, :], axis=1, keepdims=True)
        top_ref[at, :] = jnp.broadcast_to(top, (rows, page))
    lax.fori_loop(0, whole, lambda i, _: second_pass(i, 0, i), 0)
    lax.fori_loop(0, rounds, lambda i, _: second_pass(i, masked_at, whole + i), 0)
    for b in range(blocks):
        at = pl.ds(b * rows, rows)
        total = jnp.sum(sum_ref[at, :], axis=1, keepdims=True)
        total = jnp.maximum(total, 1e-30)
        out = (acc_ref[at, :] / total).astype(jnp.bfloat16)
        lse = top_ref[at, :] + jnp.log2(total)
        across = [
            jnp.sum(
                jnp.where(ahead == 0, lse[h * tokens : (h + 1) * tokens], 0.0),
                axis=0,
                keepdims=True,
            )
            for h in range(per_group)
        ]
        across.append(jnp.zeros((8 - per_group, page), jnp.float32))
        across = jnp.concatenate(across, axis=0)
        high = across.astype(jnp.bfloat16).astype(jnp.float32)
        middle = (across - high).astype(jnp.bfloat16).astype(jnp.float32)
        low = across - high - middle
        tail = jnp.concatenate([high, middle, low, jnp.zeros_like(low)], axis=0)
        tail = tail.astype(jnp.bfloat16)
        packed_ref[order_ref[b], 0, pl.ds(0, rows), :] = out
        packed_ref[order_ref[b], 0, pl.ds(rows, 32), :] = tail


def attend(queries, kv, per_group, reach, order):
    held = [q.shape[0] for q in queries]
    blocks = sum(held)
    _, groups, rows, width = queries[0].shape
    sources, height, _ = kv.shape
    height = height // groups
    page = 128
    pages = sources * (height // 2 // page)
    unit = 4
    packed = (blocks, groups, rows + 32, width)
    scores = blocks * groups * rows * pages * page // 2
    return pl.pallas_call(
        functools.partial(attend_kernel, per_group, unit, page, held),
        grid_spec=pltpu.PrefetchScalarGridSpec(
            num_scalar_prefetch=2,
            grid=(groups,),
            in_specs=[pl.BlockSpec((n, 1, rows, width), lambda g, *_: (0, g, 0, 0)) for n in held]
            + [pl.BlockSpec((sources, height, width), lambda g, *_: (0, g, 0))],
            out_specs=pl.BlockSpec((blocks, 1, rows + 32, width), lambda g, *_: (0, g, 0, 0)),
            scratch_shapes=[
                pltpu.SMEM((2 * (pages + unit),), jnp.int32),
                pltpu.VMEM((pages // unit + 1, blocks * rows, unit * page), jnp.float32),
                pltpu.VMEM((blocks * rows, page), jnp.float32),
                pltpu.VMEM((blocks * rows, page), jnp.float32),
                pltpu.VMEM((blocks * rows, width), jnp.float32),
            ],
        ),
        out_shape=jax.ShapeDtypeStruct(packed, jnp.bfloat16),
        compiler_params=pltpu.CompilerParams(vmem_limit_bytes=VMEM_LIMIT),
        cost_estimate=pl.CostEstimate(
            flops=8 * scores * width, bytes_accessed=8 * 1024 * 1024, transcendentals=scores
        ),
        name="attend",
    )(reach, order, *queries, kv)


def combine_kernel(per_group, parts_ref, table_ref, out_ref):
    sources, groups, height, width = parts_ref.shape
    rows = height - 32
    tokens = rows // per_group
    for g in range(groups):
        tails = parts_ref[:, g, pl.ds(rows, 32), :].astype(jnp.float32)
        lse = tails[:, 0:8] + tails[:, 8:16] + tails[:, 16:24]
        weights = jnp.exp2(lse - jnp.max(lse, axis=0, keepdims=True))
        weights = weights / jnp.sum(weights, axis=0, keepdims=True)
        weights = weights.reshape(sources * 8, width).T
        attended = []
        for h in range(per_group):
            one = jnp.zeros((tokens, width), jnp.float32)
            for e in range(sources):
                value = parts_ref[e, g, pl.ds(h * tokens, tokens), :].astype(jnp.float32)
                one = one + value * weights[:tokens, e * 8 + h : e * 8 + h + 1]
            attended.append(one)
        attended = jnp.concatenate(attended, axis=0)
        high = attended.astype(jnp.bfloat16)
        low = (attended - high.astype(jnp.float32)).astype(jnp.bfloat16)
        restored = jnp.dot(high, table_ref[...], preferred_element_type=jnp.float32)
        restored = restored + jnp.dot(low, table_ref[...], preferred_element_type=jnp.float32)
        restored = (restored * (1.0 / math.sqrt(width))).astype(jnp.bfloat16)
        for copy in range(out_ref.shape[0]):
            for h in range(per_group):
                at = (g * per_group + h) * width
                out_ref[copy, :, at : at + width] = restored[h * tokens : (h + 1) * tokens]


def combine(parts, table, per_group, copies):
    _, groups, height, width = parts.shape
    tokens = (height - 32) // per_group
    return pl.pallas_call(
        functools.partial(combine_kernel, per_group),
        out_shape=jax.ShapeDtypeStruct((copies, tokens, groups * per_group * width), jnp.bfloat16),
        compiler_params=pltpu.CompilerParams(vmem_limit_bytes=VMEM_LIMIT),
        name="combine",
    )(parts, table)


def project_kernel(place_ref, rows_ref, own_ref, other_ref, keep_ref, send_ref):
    _, tokens, _ = rows_ref.shape
    columns = own_ref.shape[0]
    x, x_hi, core = place_ref[0], place_ref[1], place_ref[2]
    wanted = [2 * hi + c for c in (core, 1 - core) for hi in (x_hi, 1 - x_hi)]
    rows = jnp.concatenate([rows_ref[i] for i in wanted], axis=0)
    for side, weights_ref in ((x, own_ref), (1 - x, other_ref)):
        at = pl.ds(pl.multiple_of(side * columns, columns), columns)
        terms = lax.dot_general(
            rows, weights_ref[...], (((1,), (1,)), ((), ())), preferred_element_type=jnp.float32
        ).astype(jnp.bfloat16)
        for i in range(2):
            keep_ref[i, :, at] = terms[i * tokens : (i + 1) * tokens]
            send_ref[i, :, at] = terms[(2 + i) * tokens : (3 + i) * tokens]


def project(rows, own, other, place):
    _, tokens, _ = rows.shape
    columns = own.shape[0]
    whole = pl.BlockSpec(memory_space=pltpu.VMEM)
    return pl.pallas_call(
        project_kernel,
        in_specs=[pl.BlockSpec(memory_space=pltpu.SMEM), whole, whole, whole],
        out_shape=[jax.ShapeDtypeStruct((2, tokens, 2 * columns), jnp.bfloat16)] * 2,
        compiler_params=pltpu.CompilerParams(vmem_limit_bytes=VMEM_LIMIT),
        name="project",
    )(place, rows, own, other)


def on_device(queries, cache_codes, cache_scales, pattern, out_weight):
    ny, nx, nz = (lax.axis_size(a) for a in (Y, X, Z))
    y, x, z = (lax.axis_index(a) for a in (Y, X, Z))
    x_hi, core = (lax.axis_index(a) for a in GRP)
    plane = ny * nx
    place = y * nx + x
    block_rows = queries.shape[0]
    _, groups, shard_len, width = cache_codes.shape
    heads = queries.shape[1] // width
    per_group = heads // groups
    pages = pattern.shape[2]
    page = shard_len // pages
    blocks = pattern.shape[1]
    total_len = shard_len * blocks
    total_q = block_rows * blocks
    table = hadamard(width)

    def along(block, step):
        return lax.ppermute(block, Z, [(i, (i + step) % nz) for i in range(nz)])

    def across(block, step):
        return lax.ppermute(block, PLANE, [(e, e ^ step) for e in range(plane)])

    kv = lax.all_to_all(dequantize(cache_codes, cache_scales, plane), PLANE, 0, 0)

    rotated = rotate(queries, table.astype(jnp.bfloat16), groups)
    pair = jnp.stack([rotated, along(rotated, nz // 2)])
    held = [pair, along(pair, 1), along(pair, -1)]
    held += [along(rotated, 2)[None], along(rotated, -2)[None]]
    back = [s + far for s in (0, 1, -1) for far in (0, nz // 2)] + [2, -2]
    at = (z - jnp.array(back, jnp.int32)) % nz
    first_query = total_len - total_q + (place * nz + at) * block_rows

    kept = jnp.stack([pattern, across(pattern, 1)])
    kept = jnp.concatenate([kept] + [across(kept, d) for d in range(2, plane, 2)])
    kept = lax.dynamic_slice_in_dim(kept, place * nz, nz, axis=2)
    shard = jnp.arange(plane, dtype=jnp.int32)
    kept = sum(
        jnp.where((shard ^ place == d)[:, None, None, None], kept[d][None], 0)
        for d in range(plane)
    )
    kept = jnp.transpose(kept, (1, 0, 3, 2))
    kept = sum(jnp.where(at == i, kept[..., i : i + 1], 0) for i in range(nz))
    first_key = (shard * nz + z)[:, None] * shard_len + jnp.arange(pages, dtype=jnp.int32) * page
    causal = jnp.clip(first_query[None, None, :] - first_key[:, :, None], -2 * page, 2 * page)
    reach = jnp.where(kept == 1, causal[None], -2 * page).reshape(-1)

    own = lax.all_gather(out_weight.T, Z, axis=0, tiled=True)
    other = across(own, 1)

    packed = attend(held, kv, per_group, reach, at)
    parts = lax.all_to_all(tied(packed, own[:16, :width]), Z, 0, 0)
    restored = combine(parts, table.astype(jnp.bfloat16), per_group, ny)
    restored = lax.all_to_all(restored, Y, 0, 0)
    here = jnp.stack([x, x_hi, core]).astype(jnp.int32)
    keep, send = project(restored, own, other, here)

    send = lax.ppermute(send, GRP[1], [(0, 1), (1, 0)])
    share = (keep.astype(jnp.float32) + send.astype(jnp.float32)).astype(jnp.bfloat16)
    cores = ny // 2
    where = [(a, b, c) for a in range(ny) for b in range(cores) for c in range(2)]
    mixed = jnp.zeros(share.shape[1:], jnp.float32)
    for i in range(2):
        route = [
            ((a * cores + b) * 2 + c, ((2 * (b ^ i) + c) * cores + a // 2) * 2 + a % 2)
            for a, b, c in where
        ]
        mixed = mixed + lax.ppermute(share[i], (Y,) + GRP, route).astype(jnp.float32)
    return mixed.astype(jnp.bfloat16)


def solution(mesh):
    parts = Mesh(mesh.devices.reshape(4, 2, 8, 2, 2), (Y, X, Z) + GRP)
    ctx = (Y, X, Z)
    placed = (
        P(ctx, GRP),
        P(None, GRP, ctx, None),
        P(None, GRP, None, ctx),
        P(GRP, None, ctx),
        P(GRP, ctx),
    )
    return jax.shard_map(
        on_device, mesh=parts, in_specs=placed, out_specs=P(ctx, GRP), check_vma=False
    )
```

time: 224 us -> 196 us (0.88); the launches traced: 223 us -> 192 us
  blocking collectives: 32.3 us -> 0 us
  waiting for transfers between devices: 65.9 us -> 84.7 us
  starting transfers between devices: 63.3 us -> 46.6 us
  matrix products: 3.5 us -> 0 us
  Pallas kernels: 33.3 us -> 36 us
    all_to_all x1 -> x0, blocking collectives: 32.3 us -> none  [on_device(): gathered = [lax.all_to_all(shard, PLANE, 0, 0) for shard in shards]]
    ppermute x16 -> x13, waiting for transfers between devices: 33.5 us -> 47.8 us  [the longest x5 34.5 us: across(): return lax.ppermute(block, PLANE, [(e, e ^ step) for e in range(plane)])]
    ppermute x16 -> x13, starting transfers between devices: 43.5 us -> 31.9 us  [the longest x5 17.5 us: along(): return lax.ppermute(block, Z, [(i, (i + step) % nz) for i in range(nz)])]
    pallas_call x3 -> x4, Pallas kernels: 25.6 us -> 30.8 us  [the longest x1 22.9 us: attend(): pl.pallas_call(functools.partial(attend_kernel, per_group, unit, page, he...]
    all_to_all x4 -> x3, starting transfers between devices: 19.7 us -> 14.7 us  [the longest x1 6.06 us: on_device(): lax.all_to_all(dequantize(cache_codes, cache_scales, plane), PLANE, 0, 0)]
    all_to_all x4 -> x3, waiting for transfers between devices: 32.4 us -> 36.9 us  [the longest x1 28.8 us: on_device(): parts = lax.all_to_all(tied(packed, own[:16, :width]), Z, 0, 0)]
    dot_general x1 -> x0, matrix products: 3.5 us -> none  [on_device(): lax.dot_general(restored.reshape(plane * block_rows, heads * width), weig...]
    concatenate x3 -> x0, other arithmetic: 3.02 us -> none  [the longest x1 2.31 us: on_device(): restored = jnp.concatenate(restored, axis=2)]
  transfers between devices with their start and end apart: 21 -> 17, of which waited for: 11 -> 9; matrix products, arithmetic and copies ran while one was open for 3% -> 4% of each run, Pallas kernels for 13% -> 3%
where the time goes in v5:
time: 196 us; the launch traced here: 192 us
  waiting for transfers between devices  84.7 us (43%)
  starting transfers between devices  46.6 us (24%)
  Pallas kernels  36 us (18%)
  between operations  13.6 us (7%)
  local copies, waits for them, and re-layouts  6.74 us (3%)
  other arithmetic  4.65 us (2%)
    ppermute x5, waiting for transfers between devices, across(): return lax.ppermute(block, PLANE, [(e, e ^ step) for e in range(plane)])  34.5 us
    all_to_all x1, waiting for transfers between devices, on_device(): parts = lax.all_to_all(tied(packed, own[:16, :width]), Z, 0, 0)  28.8 us
    pallas_call x1, Pallas kernels, attend(): pl.pallas_call(functools.partial(attend_kernel, per_group, unit, page, he...  22.9 us
    ppermute x5, starting transfers between devices, along(): return lax.ppermute(block, Z, [(i, (i + step) % nz) for i in range(nz)])  17.5 us
    ppermute x2, waiting for transfers between devices, on_device(): lax.ppermute(share[i], (Y,) + GRP, route).astype(jnp.float32)  10.6 us
    ppermute x5, starting transfers between devices, across(): return lax.ppermute(block, PLANE, [(e, e ^ step) for e in range(plane)])  8.14 us
    all_to_all x1, waiting for transfers between devices, on_device(): restored = lax.all_to_all(restored, Y, 0, 0)  8.12 us
    ppermute x2, starting transfers between devices, on_device(): lax.ppermute(share[i], (Y,) + GRP, route).astype(jnp.float32)  6.18 us
  transfers between devices with their start and end apart: 17, of which 9 were waited for; matrix products, arithmetic and copies ran while one was open for 4% of the time, Pallas kernels for 3%

profile of v5, /device:TPU:6, one launch (start us, length us, event | category | flops | bytes accessed | tf_op | source)
XLA Modules:
  0.0 192.4 jit_solution(18163198126157211855)
XLA Ops:
  6.5 3.7 %dequantize.1 = bf16[8,2048,128]{2,1,0:T(8,128)(2,1)} custom-call(s32[2,2,512,128]{3,2,1,0:T(8,128)} %codes_ref.1, f32[2,2,4,512]{3,2,1,0:T(4,128)} %scales_ref.1), custom_call_target="tpu_custom_call" | custom-call | tf_op jit(solution)/shard_map/dequantize/pallas_call | solution.py:52
  10.3 6.1 %all-to-all-start = ((bf16[8,2048,128]{2,1,0:T(8,128)(2,1)}), bf16[8,2048,128]{2,1,0:T(8,128)(2,1)}, u32[]{:S(2)}, u32[]{:S(2)}) async-start(bf16[8,2048,128]{2,1,0:T(8,128)(2,1)} %dequantize.1), calls=%async_computation | async-start | bytes 8388608 | tf_op jit(solution)/shard_map/all_to_all | solution.py:354
  16.3 0.7 select_convert_fusion.table_ref
  17.0 1.8 rotate.1
  18.8 7.2 %collective-permute-start.4 = (bf16[2,320,128]{2,1,0:T(8,128)(2,1)}, bf16[2,320,128]{2,1,0:T(8,128)(2,1)S(1)}, u32[]{:S(2)}, u32[]{:S(2)}) collective-permute-start(bf16[2,320,128]{2,1,0:T(8,128)(2,1)} %rotate.1), channel_id=1, source_target_pairs={{0,16},{4,20},{8,24},{12,28},{16,0},{20,4},{24,8},{28,12},{1,17},{... | collective-permute-start | bytes 491528 | tf_op jit(solution)/shard_map/ppermute | solution.py:349
  26.0 1.5 collective-permute-start.7
  27.5 2.7 %collective-permute-start.8 = (bf16[2,320,128]{2,1,0:T(8,128)(2,1)}, bf16[2,320,128]{2,1,0:T(8,128)(2,1)S(1)}, u32[]{:S(2)}, u32[]{:S(2)}) collective-permute-start(bf16[2,320,128]{2,1,0:T(8,128)(2,1)} %rotate.1), channel_id=1, source_target_pairs={{0,24},{4,28},{8,0},{12,4},{16,8},{20,12},{24,16},{28,20},{1,25},{... | collective-permute-start | bytes 491528 | tf_op jit(solution)/shard_map/ppermute | solution.py:349
  30.5 31.8 %collective-permute-done = s32[2,64,4]{1,2,0:T(4,128)S(1)} collective-permute-done((s32[2,64,4]{1,2,0:T(4,128)S(1)}, s32[2,64,4]{1,2,0:T(4,128)S(1)}, u32[]{:S(2)}, u32[]{:S(2)}) %collective-permute-start) | collective-permute-done | bytes 2080 | tf_op jit(solution)/shard_map/ppermute | solution.py:352
  62.4 1.5 collective-permute-start.1
  63.9 2.8 %collective-permute-start.2 = (s32[2,2,64,4]{2,3,1,0:T(4,128)S(1)}, s32[2,2,64,4]{2,3,1,0:T(4,128)S(1)}, u32[]{:S(2)}, u32[]{:S(2)}) collective-permute-start(s32[2,2,64,4]{2,3,1,0:T(4,128)S(1)} %pad_add_fusion), channel_id=1, source_target_pairs={{0,128},{32,160},{64,192},{96,224},{128,0},{160,32},{192,64},{224,... | collective-permute-start | bytes 12296 | tf_op jit(solution)/shard_map/ppermute | solution.py:352
  66.7 2.2 %collective-permute-start.3 = (s32[2,2,64,4]{2,3,1,0:T(4,128)S(1)}, s32[2,2,64,4]{2,3,1,0:T(4,128)S(1)}, u32[]{:S(2)}, u32[]{:S(2)}) collective-permute-start(s32[2,2,64,4]{2,3,1,0:T(4,128)S(1)} %pad_add_fusion), channel_id=1, source_target_pairs={{0,192},{32,224},{64,128},{96,160},{128,64},{160,96},{192,0},{224,... | collective-permute-start | bytes 12296 | tf_op jit(solution)/shard_map/ppermute | solution.py:352
  68.8 0.2 collective-permute-done.2
  69.0 2.5 %collective-permute-done.3 = s32[2,2,64,4]{2,3,1,0:T(4,128)S(1)} collective-permute-done((s32[2,2,64,4]{2,3,1,0:T(4,128)S(1)}, s32[2,2,64,4]{2,3,1,0:T(4,128)S(1)}, u32[]{:S(2)}, u32[]{:S(2)}) %collective-permute-start.3) | collective-permute-done | bytes 4128 | tf_op jit(solution)/shard_map/ppermute | solution.py:352
  71.6 0.1 select_add_fusion
  71.8 0.9 pad_maximum_fusion.refs_0_
  72.7 2.0 %collective-permute-start.5 = (bf16[2,2,320,128]{3,2,1,0:T(8,128)(2,1)S(1)}, bf16[2,2,320,128]{3,2,1,0:T(8,128)(2,1)S(1)}, u32[]{:S(2)}, u32[]{:S(2)}) collective-permute-start(bf16[2,2,320,128]{3,2,1,0:T(8,128)(2,1)S(1)} %pad_maximum_fusion.refs_0_), channel_id=1, source_target_pairs={{0,4},{4,8},{8,12},{12,16},{16,20},{20,24},{24,28},{28,0},{1,5},{5... | collective-permute-start | bytes 983048 | tf_op jit(solution)/shard_map/ppermute | solution.py:349
  74.7 4.2 %collective-permute-start.6 = (bf16[2,2,320,128]{3,2,1,0:T(8,128)(2,1)S(1)}, bf16[2,2,320,128]{3,2,1,0:T(8,128)(2,1)S(1)}, u32[]{:S(2)}, u32[]{:S(2)}) collective-permute-start(bf16[2,2,320,128]{3,2,1,0:T(8,128)(2,1)S(1)} %pad_maximum_fusion.refs_0_), channel_id=1, source_target_pairs={{0,28},{4,0},{8,4},{12,8},{16,12},{20,16},{24,20},{28,24},{1,29},{... | collective-permute-start | bytes 983048 | tf_op jit(solution)/shard_map/ppermute | solution.py:349
  78.9 0.2 fusion.10
  79.1 0.1 copy.30
  79.3 0.1 copy.28
  79.6 0.1 copy.26
  79.8 0.1 copy.24
  80.0 0.1 copy.22
  80.2 0.1 copy.20
  80.4 0.1 copy.18
  80.8 0.2 fusion
  81.1 0.7 reshape.111.reach_ref
  81.8 1.3 slice.84.after_ref
  83.1 0.8 collective-permute-done.5.refs_1_
  83.9 0.7 copy-done.7
  84.7 22.9 %attend.1.block_ref = bf16[8,2,352,128]{3,2,1,0:T(8,128)(2,1)} custom-call(s32[512]{0:T(512)} %reshape.111.reach_ref, s32[8]{0:T(128)} %copy-done.5, bf16[2,2,320,128]{3,2,1,0:T(8,128)(2,1)} %copy-done.3, bf16[2,2,320,128]{3,2,1,0:T(8,128)(2,1)} %copy-done.7, bf16[2,2,320,128]{3,2,1,0:T(8,128)(2,1)} %copy-done.8, bf16[1,2,320,128]{3,2,1,0:T(8,128)(2,1)} %bitcast.69, ...), custom_call_target="tpu_custom_call" | custom-call | flops 10737418240 | bytes 8388608 | tf_op jit(solution)/shard_map/attend/pallas_call | solution.py:237
  107.6 3.7 %all-to-all-start.1 = ((bf16[8,2,352,128]{3,2,1,0:T(8,128)(2,1)}), bf16[8,2,352,128]{3,2,1,0:T(8,128)(2,1)S(1)}, u32[]{:S(2)}, u32[]{:S(2)}) async-start(bf16[8,2,352,128]{3,2,1,0:T(8,128)(2,1)} %tie.1), calls=%async_computation.1 | async-start | bytes 2883584 | tf_op jit(solution)/shard_map/all_to_all | solution.py:382
  111.3 1.7 collective-permute-start.9
  113.0 28.8 %all-to-all-done.1.parts_ref = bf16[8,2,352,128]{3,2,1,0:T(8,128)(2,1)S(1)} async-done(((bf16[8,2,352,128]{3,2,1,0:T(8,128)(2,1)}), bf16[8,2,352,128]{3,2,1,0:T(8,128)(2,1)S(1)}, u32[]{:S(2)}, u32[]{:S(2)}) %all-to-all-start.1) | async-done | bytes 1441824 | tf_op jit(solution)/shard_map/all_to_all | solution.py:382
  141.8 1.1 copy-done
  142.9 3.4 %combine.1 = bf16[4,64,1280]{2,1,0:T(8,128)(2,1)} custom-call(bf16[8,2,352,128]{3,2,1,0:T(8,128)(2,1)} %copy-done, bf16[128,128]{1,0:T(8,128)(2,1)} %select_convert_fusion.table_ref), custom_call_target="tpu_custom_call" | custom-call | tf_op jit(solution)/shard_map/combine/pallas_call | solution.py:294
  146.3 5.0 %all-to-all-start.2 = ((bf16[4,64,1280]{2,1,0:T(8,128)(2,1)}), bf16[4,64,1280]{2,1,0:T(8,128)(2,1)S(1)}, u32[]{:S(2)}, u32[]{:S(2)}) async-start(bf16[4,64,1280]{2,1,0:T(8,128)(2,1)} %combine.1), calls=%async_computation.2 | async-start | bytes 1310720 | tf_op jit(solution)/shard_map/all_to_all | solution.py:384
  151.3 0.7 pad_add_fusion.1.place_ref
  152.0 8.1 %all-to-all-done.2.rows_ref = bf16[4,64,1280]{2,1,0:T(8,128)(2,1)S(1)} async-done(((bf16[4,64,1280]{2,1,0:T(8,128)(2,1)}), bf16[4,64,1280]{2,1,0:T(8,128)(2,1)S(1)}, u32[]{:S(2)}, u32[]{:S(2)}) %all-to-all-start.2) | async-done | bytes 655392 | tf_op jit(solution)/shard_map/all_to_all | solution.py:384
  160.1 0.8 copy-done.1
  160.9 4.1 %project.1 = (bf16[2,64,1280]{2,1,0:T(8,128)(2,1)}, bf16[2,64,1280]{2,1,0:T(8,128)(2,1)}) custom-call(s32[3]{0:T(128)} %pad_add_fusion.1.place_ref, bf16[4,64,1280]{2,1,0:T(8,128)(2,1)} %copy-done.1, bf16[640,1280]{1,0:T(8,128)(2,1)} %all-gather.2.cloned.1.call-done.own_ref, bf16[640,1280]{1,0:T(8,128)(2,1)} %collective-permute-done.9.other_ref), custom_call_target="tpu_custom_call" | custom-call | tf_op jit(solution)/shard_map/project/pallas_call | solution.py:322
  165.1 1.8 collective-permute-done.10
  166.9 1.1 add_convert_fusion
  168.0 4.3 %collective-permute-start.12 = (bf16[64,1280]{1,0:T(8,128)(2,1)S(1)}, bf16[64,1280]{1,0:T(8,128)(2,1)S(1)}, u32[]{:S(2)}, u32[]{:S(2)}) collective-permute-start(bf16[64,1280]{1,0:T(8,128)(2,1)S(1)} %get-tuple-element.12), channel_id=1, source_target_pairs={{0,128},{1,192},{2,0},{3,64},{64,129},{65,193},{66,1},{67,65},{128... | collective-permute-start | bytes 491528 | tf_op jit(solution)/shard_map/ppermute | solution.py:398
  172.3 1.9 collective-permute-start.11
  174.2 2.6 %collective-permute-done.12 = bf16[64,1280]{1,0:T(8,128)(2,1)S(1)} collective-permute-done((bf16[64,1280]{1,0:T(8,128)(2,1)S(1)}, bf16[64,1280]{1,0:T(8,128)(2,1)S(1)}, u32[]{:S(2)}, u32[]{:S(2)}) %collective-permute-start.12) | collective-permute-done | bytes 163872 | tf_op jit(solution)/shard_map/ppermute | solution.py:398
  176.8 8.0 %collective-permute-done.11 = bf16[64,1280]{1,0:T(8,128)(2,1)S(1)} collective-permute-done((bf16[64,1280]{1,0:T(8,128)(2,1)S(1)}, bf16[64,1280]{1,0:T(8,128)(2,1)S(1)}, u32[]{:S(2)}, u32[]{:S(2)}) %collective-permute-start.11) | collective-permute-done | bytes 163872 | tf_op jit(solution)/shard_map/ppermute | solution.py:398
  184.8 0.7 add_convert_fusion.1
  (60 shorter events, 1.4 us)
Async XLA Ops:
  10.3 19.9 %copy-start.4 = (s32[2,64,4]{1,2,0:T(4,128)S(1)}, s32[2,64,4]{1,2,0:T(4,128)}, u32[]{:S(2)}) copy-start(s32[2,64,4]{1,2,0:T(4,128)} %param.9) | copy-start | bytes 6148
  10.3 20.0 %copy-start.6 = (s32[8]{0:T(128)S(1)}, s32[8]{0:T(128)}, u32[]{:S(2)}) copy-start(s32[8]{0:T(128)} %constant.86) | copy-start | bytes 100
  10.3 73.5 %all-to-all-start = ((bf16[8,2048,128]{2,1,0:T(8,128)(2,1)}), bf16[8,2048,128]{2,1,0:T(8,128)(2,1)}, u32[]{:S(2)}, u32[]{:S(2)}) async-start(bf16[8,2048,128]{2,1,0:T(8,128)(2,1)} %dequantize.1), calls=%async_computation | async-start | bytes 8388608 | tf_op jit(solution)/shard_map/all_to_all | solution.py:354
  16.3 65.4 %all-gather.2.cloned.1.call-start = ((), (), s32[]{:S(2)}) async-start(), calls=%async_computation.3 | async-start | bytes 1843200 | tf_op jit(solution)/shard_map/all_gather | solution.py:378
  18.8 52.9 %collective-permute-start.4 = (bf16[2,320,128]{2,1,0:T(8,128)(2,1)}, bf16[2,320,128]{2,1,0:T(8,128)(2,1)S(1)}, u32[]{:S(2)}, u32[]{:S(2)}) collective-permute-start(bf16[2,320,128]{2,1,0:T(8,128)(2,1)} %rotate.1), channel_id=1, source_target_pairs={{0,16},{4,20},{8,24},{12,28},{16,0},{20,4},{24,8},{28,12},{1,17},{... | collective-permute-start | bytes 491528 | tf_op jit(solution)/shard_map/ppermute | solution.py:349
  26.0 57.0 %collective-permute-start.7 = (bf16[2,320,128]{2,1,0:T(8,128)(2,1)}, bf16[2,320,128]{2,1,0:T(8,128)(2,1)S(1)}, u32[]{:S(2)}, u32[]{:S(2)}) collective-permute-start(bf16[2,320,128]{2,1,0:T(8,128)(2,1)} %rotate.1), channel_id=1, source_target_pairs={{0,8},{4,12},{8,16},{12,20},{16,24},{20,28},{24,0},{28,4},{1,9},{5... | collective-permute-start | bytes 491528 | tf_op jit(solution)/shard_map/ppermute | solution.py:349
  27.5 55.6 %collective-permute-start.8 = (bf16[2,320,128]{2,1,0:T(8,128)(2,1)}, bf16[2,320,128]{2,1,0:T(8,128)(2,1)S(1)}, u32[]{:S(2)}, u32[]{:S(2)}) collective-permute-start(bf16[2,320,128]{2,1,0:T(8,128)(2,1)} %rotate.1), channel_id=1, source_target_pairs={{0,24},{4,28},{8,0},{12,4},{16,8},{20,12},{24,16},{28,20},{1,25},{... | collective-permute-start | bytes 491528 | tf_op jit(solution)/shard_map/ppermute | solution.py:349
  30.2 32.2 %collective-permute-start = (s32[2,64,4]{1,2,0:T(4,128)S(1)}, s32[2,64,4]{1,2,0:T(4,128)S(1)}, u32[]{:S(2)}, u32[]{:S(2)}) collective-permute-start(s32[2,64,4]{1,2,0:T(4,128)S(1)} %copy-done.4), channel_id=1, source_target_pairs={{0,32},{32,0},{64,96},{96,64},{128,160},{160,128},{192,224},{224,1... | collective-permute-start | bytes 6152 | tf_op jit(solution)/shard_map/ppermute | solution.py:352
  30.3 53.5 %copy-start.5 = (s32[8]{0:T(128)}, s32[8]{0:T(128)S(1)}, u32[]{:S(2)}) copy-start(s32[8]{0:T(128)S(1)} %get-tuple-element.10.order_ref) | copy-start | bytes 100
  62.4 4.3 %collective-permute-start.1 = (s32[2,2,64,4]{2,3,1,0:T(4,128)S(1)}, s32[2,2,64,4]{2,3,1,0:T(4,128)S(1)}, u32[]{:S(2)}, u32[]{:S(2)}) collective-permute-start(s32[2,2,64,4]{2,3,1,0:T(4,128)S(1)} %pad_add_fusion), channel_id=1, source_target_pairs={{0,64},{32,96},{64,0},{96,32},{128,192},{160,224},{192,128},{224,1... | collective-permute-start | bytes 12296 | tf_op jit(solution)/shard_map/ppermute | solution.py:352
  63.9 5.2 %collective-permute-start.2 = (s32[2,2,64,4]{2,3,1,0:T(4,128)S(1)}, s32[2,2,64,4]{2,3,1,0:T(4,128)S(1)}, u32[]{:S(2)}, u32[]{:S(2)}) collective-permute-start(s32[2,2,64,4]{2,3,1,0:T(4,128)S(1)} %pad_add_fusion), channel_id=1, source_target_pairs={{0,128},{32,160},{64,192},{96,224},{128,0},{160,32},{192,64},{224,... | collective-permute-start | bytes 12296 | tf_op jit(solution)/shard_map/ppermute | solution.py:352
  66.7 4.9 %collective-permute-start.3 = (s32[2,2,64,4]{2,3,1,0:T(4,128)S(1)}, s32[2,2,64,4]{2,3,1,0:T(4,128)S(1)}, u32[]{:S(2)}, u32[]{:S(2)}) collective-permute-start(s32[2,2,64,4]{2,3,1,0:T(4,128)S(1)} %pad_add_fusion), channel_id=1, source_target_pairs={{0,192},{32,224},{64,128},{96,160},{128,64},{160,96},{192,0},{224,... | collective-permute-start | bytes 12296 | tf_op jit(solution)/shard_map/ppermute | solution.py:352
  72.7 11.1 %copy-start.3 = (bf16[2,2,320,128]{3,2,1,0:T(8,128)(2,1)}, bf16[2,2,320,128]{3,2,1,0:T(8,128)(2,1)S(1)}, u32[]{:S(2)}) copy-start(bf16[2,2,320,128]{3,2,1,0:T(8,128)(2,1)S(1)} %pad_maximum_fusion.refs_0_) | copy-start | bytes 983044
  72.7 11.1 %collective-permute-start.5 = (bf16[2,2,320,128]{3,2,1,0:T(8,128)(2,1)S(1)}, bf16[2,2,320,128]{3,2,1,0:T(8,128)(2,1)S(1)}, u32[]{:S(2)}, u32[]{:S(2)}) collective-permute-start(bf16[2,2,320,128]{3,2,1,0:T(8,128)(2,1)S(1)} %pad_maximum_fusion.refs_0_), channel_id=1, source_target_pairs={{0,4},{4,8},{8,12},{12,16},{16,20},{20,24},{24,28},{28,0},{1,5},{5... | collective-permute-start | bytes 983048 | tf_op jit(solution)/shard_map/ppermute | solution.py:349
  74.7 9.1 %collective-permute-start.6 = (bf16[2,2,320,128]{3,2,1,0:T(8,128)(2,1)S(1)}, bf16[2,2,320,128]{3,2,1,0:T(8,128)(2,1)S(1)}, u32[]{:S(2)}, u32[]{:S(2)}) collective-permute-start(bf16[2,2,320,128]{3,2,1,0:T(8,128)(2,1)S(1)} %pad_maximum_fusion.refs_0_), channel_id=1, source_target_pairs={{0,28},{4,0},{8,4},{12,8},{16,12},{20,16},{24,20},{28,24},{1,29},{... | collective-permute-start | bytes 983048 | tf_op jit(solution)/shard_map/ppermute | solution.py:349
  83.0 0.8 copy-start.9
  83.0 0.8 copy-start.10
  83.8 0.7 copy-start.7
  83.8 0.8 copy-start.8
  107.6 3.7 %copy-start.2 = (bf16[640,1280]{1,0:T(8,128)(2,1)S(1)}, bf16[640,1280]{1,0:T(8,128)(2,1)}, u32[]{:S(2)}) copy-start(bf16[640,1280]{1,0:T(8,128)(2,1)} %all-gather.2.cloned.1.call-done.own_ref) | copy-start | bytes 4915204
  107.6 34.2 %all-to-all-start.1 = ((bf16[8,2,352,128]{3,2,1,0:T(8,128)(2,1)}), bf16[8,2,352,128]{3,2,1,0:T(8,128)(2,1)S(1)}, u32[]{:S(2)}, u32[]{:S(2)}) async-start(bf16[8,2,352,128]{3,2,1,0:T(8,128)(2,1)} %tie.1), calls=%async_computation.1 | async-start | bytes 2883584 | tf_op jit(solution)/shard_map/all_to_all | solution.py:382
  111.3 40.7 %collective-permute-start.9 = (bf16[640,1280]{1,0:T(8,128)(2,1)S(1)}, bf16[640,1280]{1,0:T(8,128)(2,1)}, u32[]{:S(2)}, u32[]{:S(2)}) collective-permute-start(bf16[640,1280]{1,0:T(8,128)(2,1)S(1)} %copy-done.2), channel_id=1, source_target_pairs={{0,32},{32,0},{64,96},{96,64},{128,160},{160,128},{192,224},{224,1... | collective-permute-start | bytes 4915208 | tf_op jit(solution)/shard_map/ppermute | solution.py:352
  141.8 1.1 copy-start
  146.3 13.8 %all-to-all-start.2 = ((bf16[4,64,1280]{2,1,0:T(8,128)(2,1)}), bf16[4,64,1280]{2,1,0:T(8,128)(2,1)S(1)}, u32[]{:S(2)}, u32[]{:S(2)}) async-start(bf16[4,64,1280]{2,1,0:T(8,128)(2,1)} %combine.1), calls=%async_computation.2 | async-start | bytes 1310720 | tf_op jit(solution)/shard_map/all_to_all | solution.py:384
  160.1 0.8 copy-start.1
  165.1 1.8 collective-permute-start.10
  168.0 8.8 %collective-permute-start.12 = (bf16[64,1280]{1,0:T(8,128)(2,1)S(1)}, bf16[64,1280]{1,0:T(8,128)(2,1)S(1)}, u32[]{:S(2)}, u32[]{:S(2)}) collective-permute-start(bf16[64,1280]{1,0:T(8,128)(2,1)S(1)} %get-tuple-element.12), channel_id=1, source_target_pairs={{0,128},{1,192},{2,0},{3,64},{64,129},{65,193},{66,1},{67,65},{128... | collective-permute-start | bytes 491528 | tf_op jit(solution)/shard_map/ppermute | solution.py:398
  172.3 12.6 %collective-permute-start.11 = (bf16[64,1280]{1,0:T(8,128)(2,1)S(1)}, bf16[64,1280]{1,0:T(8,128)(2,1)S(1)}, u32[]{:S(2)}, u32[]{:S(2)}) collective-permute-start(bf16[64,1280]{1,0:T(8,128)(2,1)S(1)} %get-tuple-element.11), channel_id=1, source_target_pairs={{0,0},{1,64},{2,128},{3,192},{64,1},{65,65},{66,129},{67,193},{128... | collective-permute-start | bytes 491528 | tf_op jit(solution)/shard_map/ppermute | solution.py:398
Sparse Core Ops, SparseCore 0:
  30.3 37.4 all-gather.1

commit v6 on v5

--- a/solution.py
+++ b/solution.py
@@ -27,7 +27,7 @@
     return jnp.where(parity == 1, -1.0, 1.0).astype(jnp.float32)
 
 
-def dequantize_kernel(codes_ref, scales_ref, out):
+def dequantize_kernel(codes_ref, scales_ref, marks_ref, out):
     kinds, groups, length, width = codes_ref.shape
     parts = scales_ref.shape[2]
     for g in range(groups):
@@ -44,33 +44,35 @@
             values = values.astype(jnp.bfloat16)
             for copy in range(out.shape[0]):
                 out[copy, pl.ds((g * kinds + kind) * length, length), :] = values
-
-
-def dequantize(codes, scales, copies):
+    marks = marks_ref[...].astype(jnp.float32)
+    marks = jnp.concatenate([marks, jnp.zeros((16 - marks.shape[0], width), jnp.float32)], axis=0)
+    for copy in range(out.shape[0]):
+        out[copy, pl.ds(kinds * groups * length, 16), :] = marks.astype(jnp.bfloat16)
+
+
+def dequantize(codes, scales, marks, copies):
     kinds, groups, length, width = codes.shape
-    shape = (copies, groups * kinds * length, width)
+    shape = (copies, groups * kinds * length + 16, width)
     return pl.pallas_call(
         dequantize_kernel,
         out_shape=jax.ShapeDtypeStruct(shape, jnp.bfloat16),
         compiler_params=pltpu.CompilerParams(vmem_limit_bytes=VMEM_LIMIT),
         name="dequantize",
-    )(codes, scales)
-
-
-def tie_kernel(block_ref, after_ref, out_ref):
-    pass
-
-
-def tied(block, after):
+    )(codes, scales, marks)
+
+
+def pass_kernel(block_ref, *refs):
+    refs[-1][...] = block_ref[...]
+
+
+def passed_after(block, *after):
     anywhere = pl.BlockSpec(memory_space=pl.ANY)
     return pl.pallas_call(
-        tie_kernel,
-        in_specs=[anywhere, anywhere],
-        out_specs=anywhere,
+        pass_kernel,
+        in_specs=[pl.BlockSpec(memory_space=pltpu.VMEM)] + [anywhere] * len(after),
         out_shape=jax.ShapeDtypeStruct(block.shape, block.dtype),
-        input_output_aliases={0: 0},
-        name="tie",
-    )(block, after)
+        name="pass",
+    )(block, *after)
 
 
 def rotate_kernel(queries_ref, table_ref, out_ref):
@@ -100,9 +102,9 @@
     )(queries, table)
 
 
-def attend_kernel(per_group, unit, page, held, reach_ref, order_ref, *refs):
-    q_refs, kv_ref, packed_ref = refs[: len(held)], *refs[len(held) : len(held) + 2]
-    pages_ref, s_ref, top_ref, sum_ref, acc_ref = refs[len(held) + 2 :]
+def attend_kernel(per_group, unit, page, held, starts, order_ref, *refs):
+    q_refs, kv_ref, marks_ref, packed_ref = refs[: len(held)], *refs[len(held) : len(held) + 3]
+    reach_ref, pages_ref, mask_ref, s_ref, top_ref, sum_ref, acc_ref = refs[len(held) + 3 :]
     queries = [ref.at[i, 0] for ref, n in zip(q_refs, held) for i in range(n)]
     blocks = len(queries)
     rows, width = queries[0].shape
@@ -112,11 +114,31 @@
     shard_pages = length // page
     all_pages = sources * shard_pages
     masked_at = all_pages + unit
-    group_at = pl.program_id(0) * all_pages
+    g = pl.program_id(0)
+    place, z = order_ref[blocks], order_ref[blocks + 1]
+
+    shape = (sources, marks_ref.shape[2])
+    in_row = shape[1] // shard_pages
+    row = g * 2 + place * blocks // in_row
+    kept = jnp.zeros(shape, jnp.float32)
+    for r in range(4):
+        kept = jnp.where(row == r, marks_ref[:, r, :].astype(jnp.float32), kept)
+    lane = lax.broadcasted_iota(jnp.int32, shape, 1)
+    source = lax.broadcasted_iota(jnp.int32, shape, 0)
+    first_query = starts + (place * blocks // in_row * in_row + lane // shard_pages) * tokens
+    first_key = (source * blocks + z) * length + lane % shard_pages * page
+    causal = jnp.clip(first_query - first_key, -2 * page, 2 * page)
+    mask_ref[...] = jnp.where(kept > 0.5, causal, -2 * page)
+    pltpu.sync_copy(mask_ref, reach_ref)
+    here = place * blocks % in_row
+
+    def reach_of(p, b):
+        return reach_ref[p // shard_pages, (here + order_ref[b]) * shard_pages + p % shard_pages]
+
 
     def place(p, counts):
         full, some = counts
-        reaches = [reach_ref[(group_at + p) * blocks + b] for b in range(blocks)]
+        reaches = [reach_of(p, b) for b in range(blocks)]
         low = functools.reduce(jnp.minimum, reaches)
         high = functools.reduce(jnp.maximum, reaches)
         pages_ref[full] = p
@@ -166,7 +188,7 @@
             for u in range(unit):
                 x = s[:, u * page : (u + 1) * page]
                 if masked:
-                    reach = jnp.where(ps[u] < 0, -2 * page, reach_ref[(group_at + pages_at[u]) * blocks + b])
+                    reach = jnp.where(ps[u] < 0, -2 * page, reach_of(pages_at[u], b))
                     x = x.reshape(per_group, tokens, page)
                     x = jnp.where((ahead <= reach)[None], x, NEG_FILL).reshape(rows, page)
                 s_ref[slot, at, u * page : (u + 1) * page] = x
@@ -223,27 +245,32 @@
         packed_ref[order_ref[b], 0, pl.ds(rows, 32), :] = tail
 
 
-def attend(queries, kv, per_group, reach, order):
+def attend(queries, kv, per_group, starts, order):
     held = [q.shape[0] for q in queries]
     blocks = sum(held)
     _, groups, rows, width = queries[0].shape
     sources, height, _ = kv.shape
-    height = height // groups
+    height = (height - 16) // groups
     page = 128
     pages = sources * (height // 2 // page)
     unit = 4
     packed = (blocks, groups, rows + 32, width)
     scores = blocks * groups * rows * pages * page // 2
     return pl.pallas_call(
-        functools.partial(attend_kernel, per_group, unit, page, held),
+        functools.partial(attend_kernel, per_group, unit, page, held, starts),
         grid_spec=pltpu.PrefetchScalarGridSpec(
-            num_scalar_prefetch=2,
+            num_scalar_prefetch=1,
             grid=(groups,),
             in_specs=[pl.BlockSpec((n, 1, rows, width), lambda g, *_: (0, g, 0, 0)) for n in held]
-            + [pl.BlockSpec((sources, height, width), lambda g, *_: (0, g, 0))],
+            + [
+                pl.BlockSpec((sources, height, width), lambda g, *_: (0, g, 0)),
+                pl.BlockSpec((sources, 16, width), lambda g, *_: (0, groups * height // 16, 0)),
+            ],
             out_specs=pl.BlockSpec((blocks, 1, rows + 32, width), lambda g, *_: (0, g, 0, 0)),
             scratch_shapes=[
+                pltpu.SMEM((sources, width), jnp.int32),
                 pltpu.SMEM((2 * (pages + unit),), jnp.int32),
+                pltpu.VMEM((sources, width), jnp.int32),
                 pltpu.VMEM((pages // unit + 1, blocks * rows, unit * page), jnp.float32),
                 pltpu.VMEM((blocks * rows, page), jnp.float32),
                 pltpu.VMEM((blocks * rows, page), jnp.float32),
@@ -256,7 +283,7 @@
             flops=8 * scores * width, bytes_accessed=8 * 1024 * 1024, transcendentals=scores
         ),
         name="attend",
-    )(reach, order, *queries, kv)
+    )(order, *queries, kv, kv)
 
 
 def combine_kernel(per_group, parts_ref, table_ref, out_ref):
@@ -338,8 +365,6 @@
     _, groups, shard_len, width = cache_codes.shape
     heads = queries.shape[1] // width
     per_group = heads // groups
-    pages = pattern.shape[2]
-    page = shard_len // pages
     blocks = pattern.shape[1]
     total_len = shard_len * blocks
     total_q = block_rows * blocks
@@ -351,7 +376,8 @@
     def across(block, step):
         return lax.ppermute(block, PLANE, [(e, e ^ step) for e in range(plane)])
 
-    kv = lax.all_to_all(dequantize(cache_codes, cache_scales, plane), PLANE, 0, 0)
+    marks = pattern.reshape(-1, width)
+    kv = lax.all_to_all(dequantize(cache_codes, cache_scales, marks, plane), PLANE, 0, 0)
 
     rotated = rotate(queries, table.astype(jnp.bfloat16), groups)
     pair = jnp.stack([rotated, along(rotated, nz // 2)])
@@ -359,27 +385,13 @@
     held += [along(rotated, 2)[None], along(rotated, -2)[None]]
     back = [s + far for s in (0, 1, -1) for far in (0, nz // 2)] + [2, -2]
     at = (z - jnp.array(back, jnp.int32)) % nz
-    first_query = total_len - total_q + (place * nz + at) * block_rows
-
-    kept = jnp.stack([pattern, across(pattern, 1)])
-    kept = jnp.concatenate([kept] + [across(kept, d) for d in range(2, plane, 2)])
-    kept = lax.dynamic_slice_in_dim(kept, place * nz, nz, axis=2)
-    shard = jnp.arange(plane, dtype=jnp.int32)
-    kept = sum(
-        jnp.where((shard ^ place == d)[:, None, None, None], kept[d][None], 0)
-        for d in range(plane)
-    )
-    kept = jnp.transpose(kept, (1, 0, 3, 2))
-    kept = sum(jnp.where(at == i, kept[..., i : i + 1], 0) for i in range(nz))
-    first_key = (shard * nz + z)[:, None] * shard_len + jnp.arange(pages, dtype=jnp.int32) * page
-    causal = jnp.clip(first_query[None, None, :] - first_key[:, :, None], -2 * page, 2 * page)
-    reach = jnp.where(kept == 1, causal[None], -2 * page).reshape(-1)
-
-    own = lax.all_gather(out_weight.T, Z, axis=0, tiled=True)
+    order = jnp.concatenate([at, jnp.stack([place, z])]).astype(jnp.int32)
+
+    own = lax.all_gather(passed_after(out_weight.T, *held[1:]), Z, axis=0, tiled=True)
     other = across(own, 1)
 
-    packed = attend(held, kv, per_group, reach, at)
-    parts = lax.all_to_all(tied(packed, own[:16, :width]), Z, 0, 0)
+    packed = attend(held, kv, per_group, total_len - total_q, order)
+    parts = lax.all_to_all(packed, Z, 0, 0)
     restored = combine(parts, table.astype(jnp.bfloat16), per_group, ny)
     restored = lax.all_to_all(restored, Y, 0, 0)
     here = jnp.stack([x, x_hi, core]).astype(jnp.int32)

time: 196 us -> 185 us (0.944)
  starting transfers between devices: 46.6 us -> 42.7 us
  waiting for transfers between devices: 84.7 us -> 81.2 us
  local copies, waits for them, and re-layouts: 6.74 us -> 4.36 us
    ppermute x5 -> x1, waiting for transfers between devices: 34.5 us -> 0.01 us  [across(): return lax.ppermute(block, PLANE, [(e, e ^ step) for e in range(plane)])]
    all_to_all x2, waiting for transfers between devices: 28.8 us -> 47.5 us  [the longest x1 37.1 us: on_device(): parts = lax.all_to_all(packed, Z, 0, 0)]
    ppermute x5, waiting for transfers between devices: 0.78 us -> 13.5 us  [along(): return lax.ppermute(block, Z, [(i, (i + step) % nz) for i in range(nz)])]
    ppermute x5 -> x1, starting transfers between devices: 8.14 us -> 0.89 us  [across(): return lax.ppermute(block, PLANE, [(e, e ^ step) for e in range(plane)])]
    all_to_all x2, starting transfers between devices: 9.77 us -> 13.5 us  [the longest x1 7.59 us: on_device(): parts = lax.all_to_all(packed, Z, 0, 0)]
    ppermute x2, waiting for transfers between devices: 10.6 us -> 7.29 us  [on_device(): lax.ppermute(share[i], (Y,) + GRP, route).astype(jnp.float32)]
    all_to_all x1, waiting for transfers between devices: 8.12 us -> 10.6 us  [on_device(): restored = lax.all_to_all(restored, Y, 0, 0)]
    slice x10 -> x0, local copies, waits for them, and re-layouts: 2.43 us -> none  [the longest x1 1.26 us: on_device(): parts = lax.all_to_all(tied(packed, own[:16, :width]), Z, 0, 0)]
  transfers between devices with their start and end apart: 17 -> 13, of which waited for: 9 -> 10; matrix products, arithmetic and copies ran while one was open for 4% -> 2% of each run, Pallas kernels for 3% -> 16%
where the time goes in v6:
time: 185 us; the launch traced here: 183 us
  waiting for transfers between devices  81.2 us (44%)
  starting transfers between devices  42.7 us (23%)
  Pallas kernels  36.4 us (20%)
  between operations  13.5 us (7%)
  other arithmetic  4.63 us (3%)
  local copies, waits for them, and re-layouts  4.36 us (2%)
    all_to_all x1, waiting for transfers between devices, on_device(): parts = lax.all_to_all(packed, Z, 0, 0)  37.1 us
    pallas_call x1, Pallas kernels, attend(): pl.pallas_call(functools.partial(attend_kernel, per_group, unit, page, he...  21.7 us
    ppermute x5, starting transfers between devices, along(): return lax.ppermute(block, Z, [(i, (i + step) % nz) for i in range(nz)])  18.2 us
    ppermute x5, waiting for transfers between devices, along(): return lax.ppermute(block, Z, [(i, (i + step) % nz) for i in range(nz)])  13.5 us
    all_to_all x1, waiting for transfers between devices, on_device(): restored = lax.all_to_all(restored, Y, 0, 0)  10.6 us
    all_to_all x1, waiting for transfers between devices, on_device(): lax.all_to_all(dequantize(cache_codes, cache_scales, marks, plane), PLANE...  10.4 us
    all_to_all x1, starting transfers between devices, on_device(): parts = lax.all_to_all(packed, Z, 0, 0)  7.59 us
    ppermute x2, waiting for transfers between devices, on_device(): lax.ppermute(share[i], (Y,) + GRP, route).astype(jnp.float32)  7.29 us
  transfers between devices with their start and end apart: 13, of which 10 were waited for; matrix products, arithmetic and copies ran while one was open for 2% of the time, Pallas kernels for 16%

profile of v6, /device:TPU:6, one launch (start us, length us, event | category | flops | bytes accessed | tf_op | source)
XLA Modules:
  0.0 182.7 jit_solution(18436784100832617472)
XLA Ops:
  6.5 0.8 copy.8
  7.3 0.7 reshape.3.marks_ref
  8.0 3.6 %dequantize.1 = bf16[8,2064,128]{2,1,0:T(8,128)(2,1)} custom-call(s32[2,2,512,128]{3,2,1,0:T(8,128)} %codes_ref.1, f32[2,2,4,512]{3,2,1,0:T(4,128)} %scales_ref.1, s32[4,128]{1,0:T(4,128)} %reshape.3.marks_ref), custom_call_target="tpu_custom_call" | custom-call | tf_op jit(solution)/shard_map/dequantize/pallas_call | solution.py:56
  11.6 5.9 %all-to-all-start = ((bf16[8,2064,128]{2,1,0:T(8,128)(2,1)}), bf16[8,2064,128]{2,1,0:T(8,128)(2,1)}, u32[]{:S(2)}, u32[]{:S(2)}) async-start(bf16[8,2064,128]{2,1,0:T(8,128)(2,1)} %dequantize.1), calls=%async_computation | async-start | bytes 8454144 | tf_op jit(solution)/shard_map/all_to_all | solution.py:380
  17.6 0.0 all-gather.2.cloned.1.call-start
  17.6 0.7 select_convert_fusion.table_ref
  18.2 1.8 rotate.1
  20.0 7.2 %collective-permute-start = (bf16[2,320,128]{2,1,0:T(8,128)(2,1)}, bf16[2,320,128]{2,1,0:T(8,128)(2,1)S(1)}, u32[]{:S(2)}, u32[]{:S(2)}) collective-permute-start(bf16[2,320,128]{2,1,0:T(8,128)(2,1)} %rotate.1), channel_id=1, source_target_pairs={{0,16},{4,20},{8,24},{12,28},{16,0},{20,4},{24,8},{28,12},{1,17},{... | collective-permute-start | bytes 491528 | tf_op jit(solution)/shard_map/ppermute | solution.py:374
  27.2 3.9 %collective-permute-done = bf16[2,320,128]{2,1,0:T(8,128)(2,1)S(1)} collective-permute-done((bf16[2,320,128]{2,1,0:T(8,128)(2,1)}, bf16[2,320,128]{2,1,0:T(8,128)(2,1)S(1)}, u32[]{:S(2)}, u32[]{:S(2)}) %collective-permute-start) | collective-permute-done | bytes 163872 | tf_op jit(solution)/shard_map/ppermute | solution.py:374
  31.2 0.9 pad_maximum_fusion.refs_0_
  32.1 4.3 %collective-permute-start.1 = (bf16[2,2,320,128]{3,2,1,0:T(8,128)(2,1)S(1)}, bf16[2,2,320,128]{3,2,1,0:T(8,128)(2,1)S(1)}, u32[]{:S(2)}, u32[]{:S(2)}) collective-permute-start(bf16[2,2,320,128]{3,2,1,0:T(8,128)(2,1)S(1)} %pad_maximum_fusion.refs_0_), channel_id=1, source_target_pairs={{0,4},{4,8},{8,12},{12,16},{16,20},{20,24},{24,28},{28,0},{1,5},{5... | collective-permute-start | bytes 983048 | tf_op jit(solution)/shard_map/ppermute | solution.py:374
  36.4 2.6 %collective-permute-start.2 = (bf16[2,2,320,128]{3,2,1,0:T(8,128)(2,1)S(1)}, bf16[2,2,320,128]{3,2,1,0:T(8,128)(2,1)S(1)}, u32[]{:S(2)}, u32[]{:S(2)}) collective-permute-start(bf16[2,2,320,128]{3,2,1,0:T(8,128)(2,1)S(1)} %pad_maximum_fusion.refs_0_), channel_id=1, source_target_pairs={{0,28},{4,0},{8,4},{12,8},{16,12},{20,16},{24,20},{28,24},{1,29},{... | collective-permute-start | bytes 983048 | tf_op jit(solution)/shard_map/ppermute | solution.py:374
  39.0 0.5 collective-permute-start.3
  39.5 3.6 %collective-permute-start.4 = (bf16[2,320,128]{2,1,0:T(8,128)(2,1)}, bf16[2,320,128]{2,1,0:T(8,128)(2,1)S(1)}, u32[]{:S(2)}, u32[]{:S(2)}) collective-permute-start(bf16[2,320,128]{2,1,0:T(8,128)(2,1)} %rotate.1), channel_id=1, source_target_pairs={{0,24},{4,28},{8,0},{12,4},{16,8},{20,12},{24,16},{28,20},{1,25},{... | collective-permute-start | bytes 491528 | tf_op jit(solution)/shard_map/ppermute | solution.py:374
  43.1 9.1 %collective-permute-done.3 = bf16[2,320,128]{2,1,0:T(8,128)(2,1)S(1)} collective-permute-done((bf16[2,320,128]{2,1,0:T(8,128)(2,1)}, bf16[2,320,128]{2,1,0:T(8,128)(2,1)S(1)}, u32[]{:S(2)}, u32[]{:S(2)}) %collective-permute-start.3) | collective-permute-done | bytes 163872 | tf_op jit(solution)/shard_map/ppermute | solution.py:374
  52.2 0.5 collective-permute-done.4
  52.6 0.0 collective-permute-done.1.refs_1_.refs_0_
  52.7 0.0 collective-permute-done.2.refs_2_.refs_1_
  52.7 0.2 copy-done.6
  52.8 0.5 copy-done.7
  53.3 0.1 copy-done.4
  53.4 0.1 copy-done.5
  53.5 1.6 pass.1
  55.1 0.0 all-gather.2.cloned.1.call-update
  55.2 0.7 pad_add_fusion.1.order_ref
  55.9 10.4 %all-to-all-done.refs_5_.refs_6_ = bf16[8,2064,128]{2,1,0:T(8,128)(2,1)} async-done(((bf16[8,2064,128]{2,1,0:T(8,128)(2,1)}), bf16[8,2064,128]{2,1,0:T(8,128)(2,1)}, u32[]{:S(2)}, u32[]{:S(2)}) %all-to-all-start) | async-done | bytes 4227104 | tf_op jit(solution)/shard_map/all_to_all | solution.py:380
  66.3 0.0 copy-done.3
  66.3 21.7 %attend.1 = bf16[8,2,352,128]{3,2,1,0:T(8,128)(2,1)} custom-call(s32[10]{0:T(128)} %pad_add_fusion.1.order_ref, bf16[2,2,320,128]{3,2,1,0:T(8,128)(2,1)} %copy-done.3, bf16[2,2,320,128]{3,2,1,0:T(8,128)(2,1)} %copy-done.4, bf16[2,2,320,128]{3,2,1,0:T(8,128)(2,1)} %copy-done.5, bf16[1,2,320,128]{3,2,1,0:T(8,128)(2,1)} %bitcast.18, ...), custom_call_target="tpu_custom_call" | custom-call | flops 10737418240 | bytes 8388608 | tf_op jit(solution)/shard_map/attend/pallas_call | solution.py:259
  88.0 7.6 %all-to-all-start.1 = ((bf16[8,2,352,128]{3,2,1,0:T(8,128)(2,1)}), bf16[8,2,352,128]{3,2,1,0:T(8,128)(2,1)S(1)}, u32[]{:S(2)}, u32[]{:S(2)}) async-start(bf16[8,2,352,128]{3,2,1,0:T(8,128)(2,1)} %attend.1), calls=%async_computation.1 | async-start | bytes 2883584 | tf_op jit(solution)/shard_map/all_to_all | solution.py:394
  95.6 0.4 all-gather.2.cloned.1.call-done.own_ref
  96.0 0.9 collective-permute-start.5
  96.9 37.1 %all-to-all-done.1.parts_ref = bf16[8,2,352,128]{3,2,1,0:T(8,128)(2,1)S(1)} async-done(((bf16[8,2,352,128]{3,2,1,0:T(8,128)(2,1)}), bf16[8,2,352,128]{3,2,1,0:T(8,128)(2,1)S(1)}, u32[]{:S(2)}, u32[]{:S(2)}) %all-to-all-start.1) | async-done | bytes 1441824 | tf_op jit(solution)/shard_map/all_to_all | solution.py:394
  134.0 1.1 copy-done
  135.2 3.5 %combine.1 = bf16[4,64,1280]{2,1,0:T(8,128)(2,1)} custom-call(bf16[8,2,352,128]{3,2,1,0:T(8,128)(2,1)} %copy-done, bf16[128,128]{1,0:T(8,128)(2,1)} %select_convert_fusion.table_ref), custom_call_target="tpu_custom_call" | custom-call | tf_op jit(solution)/shard_map/combine/pallas_call | solution.py:321
  138.6 4.7 %all-to-all-start.2 = ((bf16[4,64,1280]{2,1,0:T(8,128)(2,1)}), bf16[4,64,1280]{2,1,0:T(8,128)(2,1)S(1)}, u32[]{:S(2)}, u32[]{:S(2)}) async-start(bf16[4,64,1280]{2,1,0:T(8,128)(2,1)} %combine.1), calls=%async_computation.2 | async-start | bytes 1310720 | tf_op jit(solution)/shard_map/all_to_all | solution.py:396
  143.3 0.6 pad_add_fusion.place_ref
  143.9 0.0 collective-permute-done.5.other_ref
  143.9 10.6 %all-to-all-done.2.rows_ref = bf16[4,64,1280]{2,1,0:T(8,128)(2,1)S(1)} async-done(((bf16[4,64,1280]{2,1,0:T(8,128)(2,1)}), bf16[4,64,1280]{2,1,0:T(8,128)(2,1)S(1)}, u32[]{:S(2)}, u32[]{:S(2)}) %all-to-all-start.2) | async-done | bytes 655392 | tf_op jit(solution)/shard_map/all_to_all | solution.py:396
  154.4 0.9 copy-done.1
  155.3 4.2 %project.1 = (bf16[2,64,1280]{2,1,0:T(8,128)(2,1)}, bf16[2,64,1280]{2,1,0:T(8,128)(2,1)}) custom-call(s32[3]{0:T(128)} %pad_add_fusion.place_ref, bf16[4,64,1280]{2,1,0:T(8,128)(2,1)} %copy-done.1, bf16[640,1280]{1,0:T(8,128)(2,1)} %all-gather.2.cloned.1.call-done.own_ref, bf16[640,1280]{1,0:T(8,128)(2,1)} %copy-done.2), custom_call_target="tpu_custom_call" | custom-call | tf_op jit(solution)/shard_map/project/pallas_call | solution.py:349
  159.4 0.0 collective-permute-start.6
  159.4 1.8 %collective-permute-done.6 = bf16[2,64,1280]{2,1,0:T(8,128)(2,1)S(1)} collective-permute-done((bf16[2,64,1280]{2,1,0:T(8,128)(2,1)}, bf16[2,64,1280]{2,1,0:T(8,128)(2,1)S(1)}, u32[]{:S(2)}, u32[]{:S(2)}) %collective-permute-start.6) | collective-permute-done | bytes 327712 | tf_op jit(solution)/shard_map/ppermute | solution.py:400
  161.3 1.1 add_convert_fusion
  162.4 0.1 collective-permute-start.8
  162.5 5.4 %collective-permute-start.7 = (bf16[64,1280]{1,0:T(8,128)(2,1)S(1)}, bf16[64,1280]{1,0:T(8,128)(2,1)S(1)}, u32[]{:S(2)}, u32[]{:S(2)}) collective-permute-start(bf16[64,1280]{1,0:T(8,128)(2,1)S(1)} %get-tuple-element.9), channel_id=1, source_target_pairs={{0,0},{1,64},{2,128},{3,192},{64,1},{65,65},{66,129},{67,193},{128... | collective-permute-start | bytes 491528 | tf_op jit(solution)/shard_map/ppermute | solution.py:410
  167.9 3.3 %collective-permute-done.8 = bf16[64,1280]{1,0:T(8,128)(2,1)S(1)} collective-permute-done((bf16[64,1280]{1,0:T(8,128)(2,1)S(1)}, bf16[64,1280]{1,0:T(8,128)(2,1)S(1)}, u32[]{:S(2)}, u32[]{:S(2)}) %collective-permute-start.8) | collective-permute-done | bytes 163872 | tf_op jit(solution)/shard_map/ppermute | solution.py:410
  171.2 4.0 %collective-permute-done.7 = bf16[64,1280]{1,0:T(8,128)(2,1)S(1)} collective-permute-done((bf16[64,1280]{1,0:T(8,128)(2,1)S(1)}, bf16[64,1280]{1,0:T(8,128)(2,1)S(1)}, u32[]{:S(2)}, u32[]{:S(2)}) %collective-permute-start.7) | collective-permute-done | bytes 163872 | tf_op jit(solution)/shard_map/ppermute | solution.py:410
  175.2 0.7 add_convert_fusion.1
  (13 shorter events, 0.1 us)
Async XLA Ops:
  11.6 54.6 %all-to-all-start = ((bf16[8,2064,128]{2,1,0:T(8,128)(2,1)}), bf16[8,2064,128]{2,1,0:T(8,128)(2,1)}, u32[]{:S(2)}, u32[]{:S(2)}) async-start(bf16[8,2064,128]{2,1,0:T(8,128)(2,1)} %dequantize.1), calls=%async_computation | async-start | bytes 8454144 | tf_op jit(solution)/shard_map/all_to_all | solution.py:380
  17.6 37.6 %copy-start.8 = (s32[8]{0:T(128)S(1)}, s32[8]{0:T(128)}, u32[]{:S(2)}) copy-start(s32[8]{0:T(128)} %constant.62) | copy-start | bytes 100
  17.6 78.5 %all-gather.2.cloned.1.call-start = ((), (), s32[]{:S(2)}) async-start(), calls=%async_computation.3 | async-start | bytes 1843200 | tf_op jit(solution)/shard_map/all_gather | solution.py:390
  20.0 11.1 %collective-permute-start = (bf16[2,320,128]{2,1,0:T(8,128)(2,1)}, bf16[2,320,128]{2,1,0:T(8,128)(2,1)S(1)}, u32[]{:S(2)}, u32[]{:S(2)}) collective-permute-start(bf16[2,320,128]{2,1,0:T(8,128)(2,1)} %rotate.1), channel_id=1, source_target_pairs={{0,16},{4,20},{8,24},{12,28},{16,0},{20,4},{24,8},{28,12},{1,17},{... | collective-permute-start | bytes 491528 | tf_op jit(solution)/shard_map/ppermute | solution.py:374
  32.1 34.1 %copy-start.3 = (bf16[2,2,320,128]{3,2,1,0:T(8,128)(2,1)}, bf16[2,2,320,128]{3,2,1,0:T(8,128)(2,1)S(1)}, u32[]{:S(2)}) copy-start(bf16[2,2,320,128]{3,2,1,0:T(8,128)(2,1)S(1)} %pad_maximum_fusion.refs_0_) | copy-start | bytes 983044
  32.1 20.5 %collective-permute-start.1 = (bf16[2,2,320,128]{3,2,1,0:T(8,128)(2,1)S(1)}, bf16[2,2,320,128]{3,2,1,0:T(8,128)(2,1)S(1)}, u32[]{:S(2)}, u32[]{:S(2)}) collective-permute-start(bf16[2,2,320,128]{3,2,1,0:T(8,128)(2,1)S(1)} %pad_maximum_fusion.refs_0_), channel_id=1, source_target_pairs={{0,4},{4,8},{8,12},{12,16},{16,20},{20,24},{24,28},{28,0},{1,5},{5... | collective-permute-start | bytes 983048 | tf_op jit(solution)/shard_map/ppermute | solution.py:374
  36.4 16.3 %collective-permute-start.2 = (bf16[2,2,320,128]{3,2,1,0:T(8,128)(2,1)S(1)}, bf16[2,2,320,128]{3,2,1,0:T(8,128)(2,1)S(1)}, u32[]{:S(2)}, u32[]{:S(2)}) collective-permute-start(bf16[2,2,320,128]{3,2,1,0:T(8,128)(2,1)S(1)} %pad_maximum_fusion.refs_0_), channel_id=1, source_target_pairs={{0,28},{4,0},{8,4},{12,8},{16,12},{20,16},{24,20},{28,24},{1,29},{... | collective-permute-start | bytes 983048 | tf_op jit(solution)/shard_map/ppermute | solution.py:374
  39.0 13.2 %collective-permute-start.3 = (bf16[2,320,128]{2,1,0:T(8,128)(2,1)}, bf16[2,320,128]{2,1,0:T(8,128)(2,1)S(1)}, u32[]{:S(2)}, u32[]{:S(2)}) collective-permute-start(bf16[2,320,128]{2,1,0:T(8,128)(2,1)} %rotate.1), channel_id=1, source_target_pairs={{0,8},{4,12},{8,16},{12,20},{16,24},{20,28},{24,0},{28,4},{1,9},{5... | collective-permute-start | bytes 491528 | tf_op jit(solution)/shard_map/ppermute | solution.py:374
  39.5 13.1 %collective-permute-start.4 = (bf16[2,320,128]{2,1,0:T(8,128)(2,1)}, bf16[2,320,128]{2,1,0:T(8,128)(2,1)S(1)}, u32[]{:S(2)}, u32[]{:S(2)}) collective-permute-start(bf16[2,320,128]{2,1,0:T(8,128)(2,1)} %rotate.1), channel_id=1, source_target_pairs={{0,24},{4,28},{8,0},{12,4},{16,8},{20,12},{24,16},{28,20},{1,25},{... | collective-permute-start | bytes 491528 | tf_op jit(solution)/shard_map/ppermute | solution.py:374
  52.2 0.7 copy-start.6
  52.6 0.7 copy-start.7
  52.6 0.8 copy-start.4
  52.7 0.9 copy-start.5
  88.0 46.1 %all-to-all-start.1 = ((bf16[8,2,352,128]{3,2,1,0:T(8,128)(2,1)}), bf16[8,2,352,128]{3,2,1,0:T(8,128)(2,1)S(1)}, u32[]{:S(2)}, u32[]{:S(2)}) async-start(bf16[8,2,352,128]{3,2,1,0:T(8,128)(2,1)} %attend.1), calls=%async_computation.1 | async-start | bytes 2883584 | tf_op jit(solution)/shard_map/all_to_all | solution.py:394
  96.0 47.9 %collective-permute-start.5 = (bf16[640,1280]{1,0:T(8,128)(2,1)}, bf16[640,1280]{1,0:T(8,128)(2,1)S(1)}, u32[]{:S(2)}, u32[]{:S(2)}) collective-permute-start(bf16[640,1280]{1,0:T(8,128)(2,1)} %all-gather.2.cloned.1.call-done.own_ref), channel_id=1, source_target_pairs={{0,32},{32,0},{64,96},{96,64},{128,160},{160,128},{192,224},{224,1... | collective-permute-start | bytes 4915208 | tf_op jit(solution)/shard_map/ppermute | solution.py:377
  134.0 1.1 copy-start
  138.6 15.8 %all-to-all-start.2 = ((bf16[4,64,1280]{2,1,0:T(8,128)(2,1)}), bf16[4,64,1280]{2,1,0:T(8,128)(2,1)S(1)}, u32[]{:S(2)}, u32[]{:S(2)}) async-start(bf16[4,64,1280]{2,1,0:T(8,128)(2,1)} %combine.1), calls=%async_computation.2 | async-start | bytes 1310720 | tf_op jit(solution)/shard_map/all_to_all | solution.py:396
  143.9 10.6 %copy-start.2 = (bf16[640,1280]{1,0:T(8,128)(2,1)}, bf16[640,1280]{1,0:T(8,128)(2,1)S(1)}, u32[]{:S(2)}) copy-start(bf16[640,1280]{1,0:T(8,128)(2,1)S(1)} %collective-permute-done.5.other_ref) | copy-start | bytes 4915204
  154.4 0.9 copy-start.1
  159.4 1.8 %collective-permute-start.6 = (bf16[2,64,1280]{2,1,0:T(8,128)(2,1)}, bf16[2,64,1280]{2,1,0:T(8,128)(2,1)S(1)}, u32[]{:S(2)}, u32[]{:S(2)}) collective-permute-start(bf16[2,64,1280]{2,1,0:T(8,128)(2,1)} %get-tuple-element.8), channel_id=1, source_target_pairs={{0,1},{1,0},{2,3},{3,2},{4,5},{5,4},{6,7},{7,6},{8,9},{9,8},{10,11... | collective-permute-start | bytes 983048 | tf_op jit(solution)/shard_map/ppermute | solution.py:400
  162.4 8.8 %collective-permute-start.8 = (bf16[64,1280]{1,0:T(8,128)(2,1)S(1)}, bf16[64,1280]{1,0:T(8,128)(2,1)S(1)}, u32[]{:S(2)}, u32[]{:S(2)}) collective-permute-start(bf16[64,1280]{1,0:T(8,128)(2,1)S(1)} %get-tuple-element.10), channel_id=1, source_target_pairs={{0,128},{1,192},{2,0},{3,64},{64,129},{65,193},{66,1},{67,65},{128... | collective-permute-start | bytes 491528 | tf_op jit(solution)/shard_map/ppermute | solution.py:410
  162.5 12.7 %collective-permute-start.7 = (bf16[64,1280]{1,0:T(8,128)(2,1)S(1)}, bf16[64,1280]{1,0:T(8,128)(2,1)S(1)}, u32[]{:S(2)}, u32[]{:S(2)}) collective-permute-start(bf16[64,1280]{1,0:T(8,128)(2,1)S(1)} %get-tuple-element.9), channel_id=1, source_target_pairs={{0,0},{1,64},{2,128},{3,192},{64,1},{65,65},{66,129},{67,193},{128... | collective-permute-start | bytes 491528 | tf_op jit(solution)/shard_map/ppermute | solution.py:410
Sparse Core Ops, SparseCore 0:
  55.3 40.6 all-gather.1

commit v7 on v6

--- a/solution.py
+++ b/solution.py
@@ -27,38 +27,74 @@
     return jnp.where(parity == 1, -1.0, 1.0).astype(jnp.float32)
 
 
-def dequantize_kernel(codes_ref, scales_ref, marks_ref, out):
-    kinds, groups, length, width = codes_ref.shape
+def dequantize_kernel(codes_ref, scales_ref, *refs):
+    out = refs[-1]
+    kinds, _, length, width = codes_ref.shape
     parts = scales_ref.shape[2]
-    for g in range(groups):
-        for kind in range(kinds):
-            scales = scales_ref[kind, g]
-            spread = jnp.concatenate(
-                [
-                    jnp.broadcast_to(scales[i : i + 1], (width // parts, length))
-                    for i in range(parts)
-                ],
-                axis=0,
-            )
-            values = (codes_ref[kind, g].astype(jnp.float32) - 7.5) * spread.T
-            values = values.astype(jnp.bfloat16)
-            for copy in range(out.shape[0]):
-                out[copy, pl.ds((g * kinds + kind) * length, length), :] = values
-    marks = marks_ref[...].astype(jnp.float32)
-    marks = jnp.concatenate([marks, jnp.zeros((16 - marks.shape[0], width), jnp.float32)], axis=0)
-    for copy in range(out.shape[0]):
-        out[copy, pl.ds(kinds * groups * length, 16), :] = marks.astype(jnp.bfloat16)
-
-
-def dequantize(codes, scales, marks, copies):
-    kinds, groups, length, width = codes.shape
-    shape = (copies, groups * kinds * length + 16, width)
+    for kind in range(kinds):
+        scales = scales_ref[kind, 0]
+        spread = jnp.concatenate(
+            [
+                jnp.broadcast_to(scales[i : i + 1], (width // parts, length))
+                for i in range(parts)
+            ],
+            axis=0,
+        )
+        values = (codes_ref[kind, 0].astype(jnp.float32) - 7.5) * spread.T
+        values = values.astype(jnp.bfloat16)
+        for copy in range(out.shape[0]):
+            out[copy, pl.ds(kind * length, length), :] = values
+    if len(refs) == 2:
+        groups, blocks, pages = refs[0].shape
+        in_row = width // pages
+        lane = lax.broadcasted_iota(jnp.int32, (in_row, width), 1)
+        first = lax.broadcasted_iota(jnp.int32, (in_row, width), 0) * pages
+        marks = []
+        for g in range(groups):
+            for start in range(0, blocks, in_row):
+                part = refs[0][g, start : start + in_row, :].astype(jnp.float32)
+                row = jnp.zeros((in_row, width), jnp.float32)
+                for p in range(pages):
+                    row = jnp.where(lane == first + p, part[:, p : p + 1], row)
+                marks.append(jnp.sum(row, axis=0, keepdims=True))
+        marks.append(jnp.zeros((16 - len(marks), width), jnp.float32))
+        marks = jnp.concatenate(marks, axis=0)
+        for copy in range(out.shape[0]):
+            out[copy, pl.ds(kinds * length, 16), :] = marks.astype(jnp.bfloat16)
+
+
+def dequantize(codes, scales, g, copies, *marks):
+    kinds, _, length, width = codes.shape
+    shape = (copies, kinds * length + 16 * len(marks), width)
     return pl.pallas_call(
         dequantize_kernel,
+        grid=(1,),
+        in_specs=[
+            pl.BlockSpec((kinds, 1, length, width), lambda i: (0, g, 0, 0)),
+            pl.BlockSpec((kinds, 1) + scales.shape[2:], lambda i: (0, g, 0, 0)),
+        ]
+        + [pl.BlockSpec(m.shape, lambda i: (0, 0, 0)) for m in marks],
+        out_specs=pl.BlockSpec(shape, lambda i: (0, 0, 0)),
         out_shape=jax.ShapeDtypeStruct(shape, jnp.bfloat16),
         compiler_params=pltpu.CompilerParams(vmem_limit_bytes=VMEM_LIMIT),
         name="dequantize",
-    )(codes, scales, marks)
+    )(codes, scales, *marks)
+
+
+def tie_kernel(*refs):
+    pass
+
+
+def tied(block, *after):
+    anywhere = pl.BlockSpec(memory_space=pl.ANY)
+    return pl.pallas_call(
+        tie_kernel,
+        in_specs=[anywhere] * (1 + len(after)),
+        out_specs=anywhere,
+        out_shape=jax.ShapeDtypeStruct(block.shape, block.dtype),
+        input_output_aliases={0: 0},
+        name="tie",
+    )(block, *after)
 
 
 def pass_kernel(block_ref, *refs):
@@ -102,19 +138,37 @@
     )(queries, table)
 
 
-def attend_kernel(per_group, unit, page, held, starts, order_ref, *refs):
-    q_refs, kv_ref, marks_ref, packed_ref = refs[: len(held)], *refs[len(held) : len(held) + 3]
-    reach_ref, pages_ref, mask_ref, s_ref, top_ref, sum_ref, acc_ref = refs[len(held) + 3 :]
-    queries = [ref.at[i, 0] for ref, n in zip(q_refs, held) for i in range(n)]
+def attend_kernel(per_group, units, page, held, starts, g, order_ref, *refs):
+    q_from, kv_from, marks_from = refs[: len(held)], *refs[len(held) : len(held) + 2]
+    packed_ref, reach_ref, mask_ref, s_ref, top_ref, acc_ref = refs[-11:-5]
+    marks_ref, kv_ref, q_ref, kv_sems, q_sems = refs[-5:]
+    marks_at = marks_from.shape[1] // page * page
+    half = kv_ref.shape[1] // 2
+    halves = [pl.ds(0, half), pl.ds(half, half)]
+    marks_copy = pltpu.make_async_copy(
+        marks_from.at[:, pl.ds(marks_at, 16)], marks_ref, kv_sems.at[0]
+    )
+    kv_copies = [
+        pltpu.make_async_copy(kv_from.at[:, at], kv_ref.at[:, at], kv_sems.at[1 + i])
+        for i, at in enumerate(halves)
+    ]
+    q_copies = [
+        pltpu.make_async_copy(
+            ref.at[:, g], q_ref.at[pl.ds(sum(held[:i]), held[i])], q_sems.at[i]
+        )
+        for i, ref in enumerate(q_from)
+    ]
+    for copy in (marks_copy, kv_copies[0], *q_copies, kv_copies[1]):
+        copy.start()
+    queries = [q_ref.at[i] for i in range(sum(held))]
+    marks_copy.wait()
     blocks = len(queries)
     rows, width = queries[0].shape
     tokens = rows // per_group
     sources, height, _ = kv_ref.shape
-    length = height // 2
+    length = height // 2 // page * page
     shard_pages = length // page
-    all_pages = sources * shard_pages
-    masked_at = all_pages + unit
-    g = pl.program_id(0)
+    unit, masked_unit = units
     place, z = order_ref[blocks], order_ref[blocks + 1]
 
     shape = (sources, marks_ref.shape[2])
@@ -128,55 +182,74 @@
     first_query = starts + (place * blocks // in_row * in_row + lane // shard_pages) * tokens
     first_key = (source * blocks + z) * length + lane % shard_pages * page
     causal = jnp.clip(first_query - first_key, -2 * page, 2 * page)
-    mask_ref[...] = jnp.where(kept > 0.5, causal, -2 * page)
+    reach = jnp.where(kept > 0.5, causal, -2 * page)
+    here = place * blocks % in_row
+    mine = jnp.logical_and(lane >= here * shard_pages, lane < (here + blocks) * shard_pages)
+    low = jnp.where(mine, reach, 2 * page)
+    high = jnp.where(mine, reach, -2 * page)
+    step = shard_pages
+    while step < shape[1]:
+        low = jnp.minimum(low, pltpu.roll(low, step, 1))
+        high = jnp.maximum(high, pltpu.roll(high, step, 1))
+        step *= 2
+    first_lanes = lane < shard_pages
+    whole_page = jnp.logical_and(first_lanes, low >= page - 1).astype(jnp.int32)
+    some_page = jnp.logical_and(first_lanes, jnp.logical_and(high > -tokens, low < page - 1))
+    some_page = some_page.astype(jnp.int32)
+
+    def counted(flags):
+        before = jnp.zeros_like(flags)
+        for i in range(1, shard_pages):
+            before = before + jnp.where(lane >= i, pltpu.roll(flags, i, 1), 0)
+        row = jnp.sum(flags, axis=1, keepdims=True)
+        above = jnp.zeros_like(row)
+        for i in range(sources - 1):
+            above = above + jnp.where(source[:, :1] > i, row[i : i + 1], 0)
+        return before + above, jnp.sum(row, axis=0, keepdims=True)
+
+    whole_rank, whole_total = counted(whole_page)
+    some_rank, some_total = counted(some_page)
+    grouped = whole_total // unit * unit
+    spare = whole_total - grouped
+    whole_list = jnp.zeros(shape, jnp.int32)
+    some_list = jnp.full(shape, 0, jnp.int32)
+    for p in range(shard_pages):
+        number = source * shard_pages + p + 1
+        at = slice(p, p + 1)
+        in_whole = jnp.logical_and(whole_page[:, at] == 1, whole_rank[:, at] < grouped)
+        spared = jnp.logical_and(whole_page[:, at] == 1, whole_rank[:, at] >= grouped)
+        to_whole = jnp.where(in_whole, whole_rank[:, at], -1)
+        to_some = jnp.where(spared, whole_rank[:, at] - grouped, -1)
+        to_some = jnp.where(some_page[:, at] == 1, spare + some_rank[:, at], to_some)
+        whole_list = whole_list + jnp.where(lane == to_whole, number, 0)
+        some_list = some_list + jnp.where(lane == to_some, number, 0)
+    whole_list = jnp.sum(whole_list, axis=0, keepdims=True) - 1
+    some_list = jnp.sum(some_list, axis=0, keepdims=True) - 1
+    mask_ref[0] = reach
+    counts = jnp.broadcast_to(grouped, whole_list.shape), jnp.broadcast_to(
+        spare + some_total, whole_list.shape
+    )
+    rest = jnp.zeros((sources - 4, shape[1]), jnp.int32)
+    mask_ref[1] = jnp.concatenate([whole_list, some_list, *counts, rest], axis=0)
     pltpu.sync_copy(mask_ref, reach_ref)
-    here = place * blocks % in_row
+    whole = reach_ref[1, 2, 0] // unit
+    rounds = (reach_ref[1, 3, 0] + masked_unit - 1) // masked_unit
 
     def reach_of(p, b):
-        return reach_ref[p // shard_pages, (here + order_ref[b]) * shard_pages + p % shard_pages]
-
-
-    def place(p, counts):
-        full, some = counts
-        reaches = [reach_of(p, b) for b in range(blocks)]
-        low = functools.reduce(jnp.minimum, reaches)
-        high = functools.reduce(jnp.maximum, reaches)
-        pages_ref[full] = p
-        pages_ref[masked_at + some] = p
-        whole = low >= page - 1
-        part = jnp.logical_and(high > -tokens, low < page - 1)
-        return full + whole.astype(jnp.int32), some + part.astype(jnp.int32)
-
-    start = (jnp.int32(0), jnp.int32(0))
-    full, some = lax.fori_loop(0, all_pages, place, start, unroll=4)
-    whole = full // unit
-
-    def leftover(i, some):
-        pages_ref[masked_at + some] = pages_ref[whole * unit + i]
-        return some + 1
-
-    some = lax.fori_loop(0, full - whole * unit, leftover, some)
-    rounds = (some + unit - 1) // unit
-
-    def pad(i, _):
-        pages_ref[masked_at + some + i] = -1
-        return 0
-
-    lax.fori_loop(0, rounds * unit - some, pad, 0)
+        return reach_ref[0, p // shard_pages, (here + order_ref[b]) * shard_pages + p % shard_pages]
 
     ahead = lax.broadcasted_iota(jnp.int32, (tokens, page), 1) - lax.broadcasted_iota(
         jnp.int32, (tokens, page), 0
     )
     top_ref[...] = jnp.full(top_ref.shape, NEG_FILL, jnp.float32)
-    sum_ref[...] = jnp.zeros(sum_ref.shape, jnp.float32)
     acc_ref[...] = jnp.zeros(acc_ref.shape, jnp.float32)
 
     def fetch(p, at):
         first = pl.multiple_of(at + p % shard_pages * page, page)
         return kv_ref[p // shard_pages, pl.ds(first, page), :]
 
-    def first_pass(i, base, slot, masked):
-        ps = [pages_ref[base + i * unit + u] for u in range(unit)]
+    def first_pass(i, base, plane, size, masked):
+        ps = [reach_ref[1, base, i * size + u] for u in range(size)]
         pages_at = [jnp.maximum(p, 0) for p in ps]
         k = jnp.concatenate([fetch(p, 0) for p in pages_at], axis=0)
         for b in range(blocks):
@@ -185,46 +258,55 @@
                 queries[b][...], k, (((1,), (1,)), ((), ())), preferred_element_type=jnp.float32
             )
             top = top_ref[at, :]
-            for u in range(unit):
+            for u in range(size):
                 x = s[:, u * page : (u + 1) * page]
                 if masked:
                     reach = jnp.where(ps[u] < 0, -2 * page, reach_of(pages_at[u], b))
-                    x = x.reshape(per_group, tokens, page)
-                    x = jnp.where((ahead <= reach)[None], x, NEG_FILL).reshape(rows, page)
-                s_ref[slot, at, u * page : (u + 1) * page] = x
+                    bias = jnp.where(ahead <= reach, 0.0, -jnp.inf)
+                    x = (x.reshape(per_group, tokens, page) + bias[None]).reshape(rows, page)
+                s_ref[plane + i * size + u, at, :] = x
                 top = jnp.maximum(top, x)
             top_ref[at, :] = top
         return 0
 
-    def second_pass(i, base, slot):
-        pages_at = [jnp.maximum(pages_ref[base + i * unit + u], 0) for u in range(unit)]
+    def second_pass(i, base, plane, size):
+        pages_at = [jnp.maximum(reach_ref[1, base, i * size + u], 0) for u in range(size)]
         v = jnp.concatenate([fetch(p, length) for p in pages_at], axis=0)
+        v = jnp.concatenate([v, jnp.ones((size * page, width), jnp.bfloat16)], axis=1)
         for b in range(blocks):
             at = pl.ds(b * rows, rows)
             top = top_ref[at, :]
-            weights = [
-                jnp.exp2(s_ref[slot, at, u * page : (u + 1) * page] - top) for u in range(unit)
-            ]
-            sum_ref[at, :] = sum_ref[at, :] + functools.reduce(jnp.add, weights)
-            weights = jnp.concatenate([w.astype(jnp.bfloat16) for w in weights], axis=1)
+            weights = jnp.concatenate(
+                [
+                    jnp.exp2(s_ref[plane + i * size + u, at, :] - top).astype(jnp.bfloat16)
+                    for u in range(size)
+                ],
+                axis=1,
+            )
             acc_ref[at, :] = acc_ref[at, :] + jnp.dot(
                 weights, v, preferred_element_type=jnp.float32
             )
         return 0
 
-    lax.fori_loop(0, whole, lambda i, _: first_pass(i, 0, i, False), 0)
-    lax.fori_loop(0, rounds, lambda i, _: first_pass(i, masked_at, whole + i, True), 0)
+    for copy in (kv_copies[0], *q_copies):
+        copy.wait()
+    masked_plane = whole * unit
+    lax.fori_loop(0, whole, lambda i, _: first_pass(i, 0, 0, unit, False), 0)
+    lax.fori_loop(
+        0, rounds, lambda i, _: first_pass(i, 1, masked_plane, masked_unit, True), 0
+    )
     for b in range(blocks):
         at = pl.ds(b * rows, rows)
         top = jnp.max(top_ref[at, :], axis=1, keepdims=True)
         top_ref[at, :] = jnp.broadcast_to(top, (rows, page))
-    lax.fori_loop(0, whole, lambda i, _: second_pass(i, 0, i), 0)
-    lax.fori_loop(0, rounds, lambda i, _: second_pass(i, masked_at, whole + i), 0)
+    kv_copies[1].wait()
+    lax.fori_loop(0, whole, lambda i, _: second_pass(i, 0, 0, unit), 0)
+    lax.fori_loop(0, rounds, lambda i, _: second_pass(i, 1, masked_plane, masked_unit), 0)
     for b in range(blocks):
         at = pl.ds(b * rows, rows)
-        total = jnp.sum(sum_ref[at, :], axis=1, keepdims=True)
+        total = acc_ref[at, width:]
         total = jnp.maximum(total, 1e-30)
-        out = (acc_ref[at, :] / total).astype(jnp.bfloat16)
+        out = (acc_ref[at, :width] / total).astype(jnp.bfloat16)
         lse = top_ref[at, :] + jnp.log2(total)
         across = [
             jnp.sum(
@@ -239,60 +321,61 @@
         high = across.astype(jnp.bfloat16).astype(jnp.float32)
         middle = (across - high).astype(jnp.bfloat16).astype(jnp.float32)
         low = across - high - middle
-        tail = jnp.concatenate([high, middle, low, jnp.zeros_like(low)], axis=0)
+        tail = jnp.concatenate([high + pltpu.roll(middle, page // 2, 1), low], axis=0)
         tail = tail.astype(jnp.bfloat16)
         packed_ref[order_ref[b], 0, pl.ds(0, rows), :] = out
-        packed_ref[order_ref[b], 0, pl.ds(rows, 32), :] = tail
-
-
-def attend(queries, kv, per_group, starts, order):
+        packed_ref[order_ref[b], 0, pl.ds(rows, 16), :] = tail
+
+
+def attend(queries, kv, marks, g, per_group, starts, order, *others):
     held = [q.shape[0] for q in queries]
     blocks = sum(held)
     _, groups, rows, width = queries[0].shape
     sources, height, _ = kv.shape
-    height = (height - 16) // groups
     page = 128
+    height = height // page * page
     pages = sources * (height // 2 // page)
-    unit = 4
-    packed = (blocks, groups, rows + 32, width)
-    scores = blocks * groups * rows * pages * page // 2
-    return pl.pallas_call(
-        functools.partial(attend_kernel, per_group, unit, page, held, starts),
+    units = (4, 2)
+    packed = (blocks, groups, rows + 16, width)
+    scores = blocks * rows * pages * page // 2
+    return pl.pallas_call(
+        functools.partial(attend_kernel, per_group, units, page, held, starts, g),
         grid_spec=pltpu.PrefetchScalarGridSpec(
             num_scalar_prefetch=1,
-            grid=(groups,),
-            in_specs=[pl.BlockSpec((n, 1, rows, width), lambda g, *_: (0, g, 0, 0)) for n in held]
-            + [
-                pl.BlockSpec((sources, height, width), lambda g, *_: (0, g, 0)),
-                pl.BlockSpec((sources, 16, width), lambda g, *_: (0, groups * height // 16, 0)),
-            ],
-            out_specs=pl.BlockSpec((blocks, 1, rows + 32, width), lambda g, *_: (0, g, 0, 0)),
+            grid=(1,),
+            in_specs=[pl.BlockSpec(memory_space=pl.ANY)] * (len(held) + 2 + len(others)),
+            out_specs=pl.BlockSpec((blocks, 1, rows + 16, width), lambda i, *_: (0, g, 0, 0)),
             scratch_shapes=[
-                pltpu.SMEM((sources, width), jnp.int32),
-                pltpu.SMEM((2 * (pages + unit),), jnp.int32),
-                pltpu.VMEM((sources, width), jnp.int32),
-                pltpu.VMEM((pages // unit + 1, blocks * rows, unit * page), jnp.float32),
+                pltpu.SMEM((2, sources, width), jnp.int32),
+                pltpu.VMEM((2, sources, width), jnp.int32),
+                pltpu.VMEM((pages + units[1], blocks * rows, page), jnp.float32),
                 pltpu.VMEM((blocks * rows, page), jnp.float32),
-                pltpu.VMEM((blocks * rows, page), jnp.float32),
-                pltpu.VMEM((blocks * rows, width), jnp.float32),
+                pltpu.VMEM((blocks * rows, 2 * width), jnp.float32),
+                pltpu.VMEM((sources, 16, width), jnp.bfloat16),
+                pltpu.VMEM((sources, height, width), jnp.bfloat16),
+                pltpu.VMEM((blocks, rows, width), jnp.bfloat16),
+                pltpu.SemaphoreType.DMA((3,)),
+                pltpu.SemaphoreType.DMA((len(held),)),
             ],
         ),
         out_shape=jax.ShapeDtypeStruct(packed, jnp.bfloat16),
+        input_output_aliases={len(held) + 3: 0} if others else {},
         compiler_params=pltpu.CompilerParams(vmem_limit_bytes=VMEM_LIMIT),
         cost_estimate=pl.CostEstimate(
             flops=8 * scores * width, bytes_accessed=8 * 1024 * 1024, transcendentals=scores
         ),
         name="attend",
-    )(order, *queries, kv, kv)
+    )(order, *queries, kv, marks, *others)
 
 
 def combine_kernel(per_group, parts_ref, table_ref, out_ref):
     sources, groups, height, width = parts_ref.shape
-    rows = height - 32
+    rows = height - 16
     tokens = rows // per_group
     for g in range(groups):
-        tails = parts_ref[:, g, pl.ds(rows, 32), :].astype(jnp.float32)
-        lse = tails[:, 0:8] + tails[:, 8:16] + tails[:, 16:24]
+        tails = parts_ref[:, g, pl.ds(rows, 16), :].astype(jnp.float32)
+        middle = pltpu.roll(tails[:, 0:8].reshape(sources * 8, width), width // 2, 1)
+        lse = tails[:, 0:8] + middle.reshape(sources, 8, width) + tails[:, 8:16]
         weights = jnp.exp2(lse - jnp.max(lse, axis=0, keepdims=True))
         weights = weights / jnp.sum(weights, axis=0, keepdims=True)
         weights = weights.reshape(sources * 8, width).T
@@ -317,7 +400,7 @@
 
 def combine(parts, table, per_group, copies):
     _, groups, height, width = parts.shape
-    tokens = (height - 32) // per_group
+    tokens = (height - 16) // per_group
     return pl.pallas_call(
         functools.partial(combine_kernel, per_group),
         out_shape=jax.ShapeDtypeStruct((copies, tokens, groups * per_group * width), jnp.bfloat16),
@@ -376,8 +459,9 @@
     def across(block, step):
         return lax.ppermute(block, PLANE, [(e, e ^ step) for e in range(plane)])
 
-    marks = pattern.reshape(-1, width)
-    kv = lax.all_to_all(dequantize(cache_codes, cache_scales, marks, plane), PLANE, 0, 0)
+    first = dequantize(cache_codes, cache_scales, 0, plane, pattern)
+    second = dequantize(cache_codes, cache_scales, 1, plane)
+    first = lax.all_to_all(first, PLANE, 0, 0)
 
     rotated = rotate(queries, table.astype(jnp.bfloat16), groups)
     pair = jnp.stack([rotated, along(rotated, nz // 2)])
@@ -385,12 +469,16 @@
     held += [along(rotated, 2)[None], along(rotated, -2)[None]]
     back = [s + far for s in (0, 1, -1) for far in (0, nz // 2)] + [2, -2]
     at = (z - jnp.array(back, jnp.int32)) % nz
+    second = tied(second, first[0, :16], *(h[-1, 0, :16] for h in (held[0], held[3], held[4])))
+    second = lax.all_to_all(second, PLANE, 0, 0)
     order = jnp.concatenate([at, jnp.stack([place, z])]).astype(jnp.int32)
 
     own = lax.all_gather(passed_after(out_weight.T, *held[1:]), Z, axis=0, tiled=True)
     other = across(own, 1)
 
-    packed = attend(held, kv, per_group, total_len - total_q, order)
+    starts = total_len - total_q
+    packed = attend(held, first, first, 0, per_group, starts, order)
+    packed = attend(held, second, first, 1, per_group, starts, order, packed)
     parts = lax.all_to_all(packed, Z, 0, 0)
     restored = combine(parts, table.astype(jnp.bfloat16), per_group, ny)
     restored = lax.all_to_all(restored, Y, 0, 0)

time: 185 us -> 181 us (0.978)
  waiting for transfers between devices: 81.2 us -> 69 us
  Pallas kernels: 36.4 us -> 41.8 us
  local copies, waits for them, and re-layouts: 4.36 us -> 8.8 us
    all_to_all x1, waiting for transfers between devices: 37.1 us -> 17.4 us  [on_device(): parts = lax.all_to_all(packed, Z, 0, 0)]
    all_gather x1, waiting for transfers between devices: 0.44 us -> 18 us  [on_device(): lax.all_gather(passed_after(out_weight.T, *held[1:]), Z, axis=0, tiled=True)]
    all_to_all x1 -> x2, waiting for transfers between devices: 10.4 us -> 0.86 us  [the longest x1 0.85 us: on_device(): first = lax.all_to_all(first, PLANE, 0, 0)]
    pallas_call x2 -> x5, Pallas kernels: 25.3 us -> 30.4 us  [the longest x2 25 us: attend(): pl.pallas_call(functools.partial(attend_kernel, per_group, units, page, h...]
    all_to_all x1 -> x2, starting transfers between devices: 5.93 us -> 10.9 us  [the longest x1 5.93 us: on_device(): first = lax.all_to_all(first, PLANE, 0, 0)]
    all_to_all x1, starting transfers between devices: 7.59 us -> 3.59 us  [on_device(): parts = lax.all_to_all(packed, Z, 0, 0)]
    unnamed x19 -> x25, local copies, waits for them, and re-layouts: 3.65 us -> 6.33 us
    squeeze x0 -> x4, local copies, waits for them, and re-layouts: none -> 2.45 us  [the longest x3 1.82 us: on_device(): h[-1, 0, :16]]
  transfers between devices with their start and end apart: 13 -> 14, of which waited for: 10 -> 11; matrix products, arithmetic and copies ran while one was open for 2% -> 2% of each run, Pallas kernels for 16% -> 19%
where the time goes in v7:
time: 181 us; the launch traced here: 180 us
  waiting for transfers between devices  69 us (38%)
  starting transfers between devices  42.9 us (24%)
  Pallas kernels  41.8 us (23%)
  between operations  13.5 us (7%)
  local copies, waits for them, and re-layouts  8.8 us (5%)
  other arithmetic  3.8 us (2%)
    pallas_call x2, Pallas kernels, attend(): pl.pallas_call(functools.partial(attend_kernel, per_group, units, page, h...  25 us
    all_gather x1, waiting for transfers between devices, on_device(): lax.all_gather(passed_after(out_weight.T, *held[1:]), Z, axis=0, tiled=True)  18 us
    all_to_all x1, waiting for transfers between devices, on_device(): parts = lax.all_to_all(packed, Z, 0, 0)  17.4 us
    ppermute x5, starting transfers between devices, along(): return lax.ppermute(block, Z, [(i, (i + step) % nz) for i in range(nz)])  17.2 us
    ppermute x5, waiting for transfers between devices, along(): return lax.ppermute(block, Z, [(i, (i + step) % nz) for i in range(nz)])  13.4 us
    all_to_all x1, waiting for transfers between devices, on_device(): restored = lax.all_to_all(restored, Y, 0, 0)  9.45 us
    ppermute x2, waiting for transfers between devices, on_device(): lax.ppermute(share[i], (Y,) + GRP, route).astype(jnp.float32)  8.03 us
    unnamed x25, local copies, waits for them, and re-layouts  6.33 us
  transfers between devices with their start and end apart: 14, of which 11 were waited for; matrix products, arithmetic and copies ran while one was open for 2% of the time, Pallas kernels for 19%

profile of v7, /device:TPU:6, one launch (start us, length us, event | category | flops | bytes accessed | tf_op | source)
XLA Modules:
  0.0 179.9 jit_solution(1463033482762923939)
XLA Ops:
  6.5 1.4 copy.9.refs_0_
  8.0 2.7 %dequantize.3 = bf16[8,1040,128]{2,1,0:T(8,128)(2,1)} custom-call(s32[2,2,512,128]{3,2,1,0:T(8,128)} %codes_ref.3, f32[2,2,4,512]{3,2,1,0:T(4,128)} %scales_ref.3, s32[2,64,4]{2,1,0:T(8,128)} %copy.9.refs_0_), custom_call_target="tpu_custom_call" | custom-call | tf_op jit(solution)/shard_map/dequantize/pallas_call | solution.py:69
  10.7 5.9 %all-to-all-start = ((bf16[8,1040,128]{2,1,0:T(8,128)(2,1)}), bf16[8,1040,128]{2,1,0:T(8,128)(2,1)S(1)}, u32[]{:S(2)}, u32[]{:S(2)}) async-start(bf16[8,1040,128]{2,1,0:T(8,128)(2,1)} %dequantize.3), calls=%async_computation | async-start | bytes 4259840 | tf_op jit(solution)/shard_map/all_to_all | solution.py:464
  16.6 0.7 select_convert_fusion.table_ref
  17.3 1.8 %rotate.1 = bf16[2,320,128]{2,1,0:T(8,128)(2,1)} custom-call(bf16[64,1280]{1,0:T(8,128)(2,1)} %queries_ref.1, bf16[128,128]{1,0:T(8,128)(2,1)} %select_convert_fusion.table_ref), custom_call_target="tpu_custom_call" | custom-call | tf_op jit(solution)/shard_map/rotate/pallas_call | solution.py:133
  19.1 7.2 %collective-permute-start = (bf16[2,320,128]{2,1,0:T(8,128)(2,1)}, bf16[2,320,128]{2,1,0:T(8,128)(2,1)S(1)}, u32[]{:S(2)}, u32[]{:S(2)}) collective-permute-start(bf16[2,320,128]{2,1,0:T(8,128)(2,1)} %rotate.1), channel_id=1, source_target_pairs={{0,16},{4,20},{8,24},{12,28},{16,0},{20,4},{24,8},{28,12},{1,17},{... | collective-permute-start | bytes 491528 | tf_op jit(solution)/shard_map/ppermute | solution.py:457
  26.3 1.5 collective-permute-start.3
  27.8 2.7 %collective-permute-start.4 = (bf16[2,320,128]{2,1,0:T(8,128)(2,1)}, bf16[2,320,128]{2,1,0:T(8,128)(2,1)S(1)}, u32[]{:S(2)}, u32[]{:S(2)}) collective-permute-start(bf16[2,320,128]{2,1,0:T(8,128)(2,1)} %rotate.1), channel_id=1, source_target_pairs={{0,24},{4,28},{8,0},{12,4},{16,8},{20,12},{24,16},{28,20},{1,25},{... | collective-permute-start | bytes 491528 | tf_op jit(solution)/shard_map/ppermute | solution.py:457
  30.4 2.6 %dequantize.2.refs_0_ = bf16[8,1024,128]{2,1,0:T(8,128)(2,1)} custom-call(s32[2,2,512,128]{3,2,1,0:T(8,128)} %codes_ref.3, f32[2,2,4,512]{3,2,1,0:T(4,128)} %scales_ref.3), custom_call_target="tpu_custom_call" | custom-call | tf_op jit(solution)/shard_map/dequantize/pallas_call | solution.py:69
  33.1 1.7 collective-permute-done
  34.7 0.6 slice_bitcast_fusion.4.refs_2_
  35.3 2.2 %collective-permute-done.3 = bf16[2,320,128]{2,1,0:T(8,128)(2,1)S(1)} collective-permute-done((bf16[2,320,128]{2,1,0:T(8,128)(2,1)}, bf16[2,320,128]{2,1,0:T(8,128)(2,1)S(1)}, u32[]{:S(2)}, u32[]{:S(2)}) %collective-permute-start.3) | collective-permute-done | bytes 163872 | tf_op jit(solution)/shard_map/ppermute | solution.py:457
  37.5 0.6 slice_bitcast_fusion.3.refs_3_
  38.1 3.1 %collective-permute-done.4 = bf16[2,320,128]{2,1,0:T(8,128)(2,1)S(1)} collective-permute-done((bf16[2,320,128]{2,1,0:T(8,128)(2,1)}, bf16[2,320,128]{2,1,0:T(8,128)(2,1)S(1)}, u32[]{:S(2)}, u32[]{:S(2)}) %collective-permute-start.4) | collective-permute-done | bytes 163872 | tf_op jit(solution)/shard_map/ppermute | solution.py:457
  41.3 0.6 slice_bitcast_fusion.2.refs_4_
  41.9 0.9 all-to-all-done.refs_5_.refs_6_
  42.7 0.6 slice_bitcast_fusion.5.refs_1_
  43.4 0.7 copy-done.2
  44.1 5.0 %all-to-all-start.1 = ((bf16[8,1024,128]{2,1,0:T(8,128)(2,1)}), bf16[8,1024,128]{2,1,0:T(8,128)(2,1)S(1)}, u32[]{:S(2)}, u32[]{:S(2)}) async-start(bf16[8,1024,128]{2,1,0:T(8,128)(2,1)} %tie.1), calls=%async_computation.1 | async-start | bytes 4194304 | tf_op jit(solution)/shard_map/all_to_all | solution.py:473
  49.1 1.9 %collective-permute-start.1 = (bf16[2,2,320,128]{3,2,1,0:T(8,128)(2,1)S(1)}, bf16[2,2,320,128]{3,2,1,0:T(8,128)(2,1)S(1)}, u32[]{:S(2)}, u32[]{:S(2)}) collective-permute-start(bf16[2,2,320,128]{3,2,1,0:T(8,128)(2,1)S(1)} %pad_maximum_fusion.refs_0_), channel_id=1, source_target_pairs={{0,4},{4,8},{8,12},{12,16},{16,20},{20,24},{24,28},{28,0},{1,5},{5... | collective-permute-start | bytes 983048 | tf_op jit(solution)/shard_map/ppermute | solution.py:457
  51.0 4.0 %collective-permute-start.2 = (bf16[2,2,320,128]{3,2,1,0:T(8,128)(2,1)S(1)}, bf16[2,2,320,128]{3,2,1,0:T(8,128)(2,1)S(1)}, u32[]{:S(2)}, u32[]{:S(2)}) collective-permute-start(bf16[2,2,320,128]{3,2,1,0:T(8,128)(2,1)S(1)} %pad_maximum_fusion.refs_0_), channel_id=1, source_target_pairs={{0,28},{4,0},{8,4},{12,8},{16,12},{20,16},{24,20},{28,24},{1,29},{... | collective-permute-start | bytes 983048 | tf_op jit(solution)/shard_map/ppermute | solution.py:457
  55.0 6.4 %collective-permute-done.1.refs_1_.refs_0_ = bf16[2,2,320,128]{3,2,1,0:T(8,128)(2,1)S(1)} collective-permute-done((bf16[2,2,320,128]{3,2,1,0:T(8,128)(2,1)S(1)}, bf16[2,2,320,128]{3,2,1,0:T(8,128)(2,1)S(1)}, u32[]{:S(2)}, u32[]{:S(2)}) %collective-permute-start.1) | collective-permute-done | bytes 327712 | tf_op jit(solution)/shard_map/ppermute | solution.py:457
  61.5 0.8 copy-done.7
  62.2 0.1 copy-done.8
  62.3 1.6 pass.1
  64.0 0.0 all-gather.2.cloned.1.call-update
  64.0 0.7 pad_add_fusion.1.order_ref
  64.7 10.9 %attend.2.refs_7_ = bf16[8,2,336,128]{3,2,1,0:T(8,128)(2,1)} custom-call(s32[10]{0:T(128)} %pad_add_fusion.1.order_ref, bf16[2,2,320,128]{3,2,1,0:T(8,128)(2,1)} %copy-done.6, bf16[2,2,320,128]{3,2,1,0:T(8,128)(2,1)} %copy-done.7, bf16[2,2,320,128]{3,2,1,0:T(8,128)(2,1)} %copy-done.8, bf16[1,2,320,128]{3,2,1,0:T(8,128)(2,1)} %bitcast.28, ...), custom_call_target="tpu_custom_call" | custom-call | flops 5368709120 | bytes 8388608 | tf_op jit(solution)/shard_map/attend/pallas_call | solution.py:341
  75.6 1.3 copy-done.3
  76.9 14.1 %attend.3 = bf16[8,2,336,128]{3,2,1,0:T(8,128)(2,1)} custom-call(s32[10]{0:T(128)} %pad_add_fusion.1.order_ref, bf16[2,2,320,128]{3,2,1,0:T(8,128)(2,1)} %copy-done.6, bf16[2,2,320,128]{3,2,1,0:T(8,128)(2,1)} %copy-done.7, bf16[2,2,320,128]{3,2,1,0:T(8,128)(2,1)} %copy-done.8, bf16[1,2,320,128]{3,2,1,0:T(8,128)(2,1)} %bitcast.29, ...), custom_call_target="tpu_custom_call", output_to_operand_aliasing={{}: (8, {})} | custom-call | flops 5368709120 | bytes 8388608 | tf_op jit(solution)/shard_map/attend/pallas_call | solution.py:341
  91.1 3.6 %all-to-all-start.2 = ((bf16[8,2,336,128]{3,2,1,0:T(8,128)(2,1)}), bf16[8,2,336,128]{3,2,1,0:T(8,128)(2,1)S(1)}, u32[]{:S(2)}, u32[]{:S(2)}) async-start(bf16[8,2,336,128]{3,2,1,0:T(8,128)(2,1)} %attend.3), calls=%async_computation.2 | async-start | bytes 2752512 | tf_op jit(solution)/shard_map/all_to_all | solution.py:482
  94.7 18.0 %all-gather.2.cloned.1.call-done.own_ref = bf16[640,1280]{1,0:T(8,128)(2,1)} async-done(((bf16[80,1280]{1,0:T(8,128)(2,1)}), bf16[640,1280]{1,0:T(8,128)(2,1)}) %all-gather.2.cloned.1.call-update) | async-done | bytes 1638416 | tf_op jit(solution)/shard_map/all_gather | solution.py:476
  112.7 17.4 %all-to-all-done.2.parts_ref = bf16[8,2,336,128]{3,2,1,0:T(8,128)(2,1)S(1)} async-done(((bf16[8,2,336,128]{3,2,1,0:T(8,128)(2,1)}), bf16[8,2,336,128]{3,2,1,0:T(8,128)(2,1)S(1)}, u32[]{:S(2)}, u32[]{:S(2)}) %all-to-all-start.2) | async-done | bytes 1376288 | tf_op jit(solution)/shard_map/all_to_all | solution.py:482
  130.1 1.1 copy-done
  131.2 3.9 %combine.1 = bf16[4,64,1280]{2,1,0:T(8,128)(2,1)} custom-call(bf16[8,2,336,128]{3,2,1,0:T(8,128)(2,1)} %copy-done, bf16[128,128]{1,0:T(8,128)(2,1)} %select_convert_fusion.table_ref), custom_call_target="tpu_custom_call" | custom-call | tf_op jit(solution)/shard_map/combine/pallas_call | solution.py:404
  135.0 5.7 %all-to-all-start.3 = ((bf16[4,64,1280]{2,1,0:T(8,128)(2,1)}), bf16[4,64,1280]{2,1,0:T(8,128)(2,1)S(1)}, u32[]{:S(2)}, u32[]{:S(2)}) async-start(bf16[4,64,1280]{2,1,0:T(8,128)(2,1)} %combine.1), calls=%async_computation.3 | async-start | bytes 1310720 | tf_op jit(solution)/shard_map/all_to_all | solution.py:484
  140.8 0.7 pad_add_fusion.place_ref
  141.4 0.0 collective-permute-done.5.other_ref
  141.4 9.5 %all-to-all-done.3.rows_ref = bf16[4,64,1280]{2,1,0:T(8,128)(2,1)S(1)} async-done(((bf16[4,64,1280]{2,1,0:T(8,128)(2,1)}), bf16[4,64,1280]{2,1,0:T(8,128)(2,1)S(1)}, u32[]{:S(2)}, u32[]{:S(2)}) %all-to-all-start.3) | async-done | bytes 655392 | tf_op jit(solution)/shard_map/all_to_all | solution.py:484
  150.9 0.9 copy-done.1
  151.7 4.1 %project.1 = (bf16[2,64,1280]{2,1,0:T(8,128)(2,1)}, bf16[2,64,1280]{2,1,0:T(8,128)(2,1)}) custom-call(s32[3]{0:T(128)} %pad_add_fusion.place_ref, bf16[4,64,1280]{2,1,0:T(8,128)(2,1)} %copy-done.1, bf16[640,1280]{1,0:T(8,128)(2,1)} %all-gather.2.cloned.1.call-done.own_ref, bf16[640,1280]{1,0:T(8,128)(2,1)} %copy-done.4), custom_call_target="tpu_custom_call" | custom-call | tf_op jit(solution)/shard_map/project/pallas_call | solution.py:432
  155.9 1.8 %collective-permute-done.6 = bf16[2,64,1280]{2,1,0:T(8,128)(2,1)S(1)} collective-permute-done((bf16[2,64,1280]{2,1,0:T(8,128)(2,1)}, bf16[2,64,1280]{2,1,0:T(8,128)(2,1)S(1)}, u32[]{:S(2)}, u32[]{:S(2)}) %collective-permute-start.6) | collective-permute-done | bytes 327712 | tf_op jit(solution)/shard_map/ppermute | solution.py:488
  157.7 1.1 add_convert_fusion
  158.8 0.9 collective-permute-start.8
  159.7 4.6 %collective-permute-start.7 = (bf16[64,1280]{1,0:T(8,128)(2,1)S(1)}, bf16[64,1280]{1,0:T(8,128)(2,1)S(1)}, u32[]{:S(2)}, u32[]{:S(2)}) collective-permute-start(bf16[64,1280]{1,0:T(8,128)(2,1)S(1)} %get-tuple-element.9), channel_id=1, source_target_pairs={{0,0},{1,64},{2,128},{3,192},{64,1},{65,65},{66,129},{67,193},{128... | collective-permute-start | bytes 491528 | tf_op jit(solution)/shard_map/ppermute | solution.py:498
  164.3 3.3 %collective-permute-done.8 = bf16[64,1280]{1,0:T(8,128)(2,1)S(1)} collective-permute-done((bf16[64,1280]{1,0:T(8,128)(2,1)S(1)}, bf16[64,1280]{1,0:T(8,128)(2,1)S(1)}, u32[]{:S(2)}, u32[]{:S(2)}) %collective-permute-start.8) | collective-permute-done | bytes 163872 | tf_op jit(solution)/shard_map/ppermute | solution.py:498
  167.6 4.8 %collective-permute-done.7 = bf16[64,1280]{1,0:T(8,128)(2,1)S(1)} collective-permute-done((bf16[64,1280]{1,0:T(8,128)(2,1)S(1)}, bf16[64,1280]{1,0:T(8,128)(2,1)S(1)}, u32[]{:S(2)}, u32[]{:S(2)}) %collective-permute-start.7) | collective-permute-done | bytes 163872 | tf_op jit(solution)/shard_map/ppermute | solution.py:498
  172.3 0.7 add_convert_fusion.1
  (27 shorter events, 0.1 us)
Async XLA Ops:
  10.7 32.0 %all-to-all-start = ((bf16[8,1040,128]{2,1,0:T(8,128)(2,1)}), bf16[8,1040,128]{2,1,0:T(8,128)(2,1)S(1)}, u32[]{:S(2)}, u32[]{:S(2)}) async-start(bf16[8,1040,128]{2,1,0:T(8,128)(2,1)} %dequantize.3), calls=%async_computation | async-start | bytes 4259840 | tf_op jit(solution)/shard_map/all_to_all | solution.py:464
  19.1 15.6 %collective-permute-start = (bf16[2,320,128]{2,1,0:T(8,128)(2,1)}, bf16[2,320,128]{2,1,0:T(8,128)(2,1)S(1)}, u32[]{:S(2)}, u32[]{:S(2)}) collective-permute-start(bf16[2,320,128]{2,1,0:T(8,128)(2,1)} %rotate.1), channel_id=1, source_target_pairs={{0,16},{4,20},{8,24},{12,28},{16,0},{20,4},{24,8},{28,12},{1,17},{... | collective-permute-start | bytes 491528 | tf_op jit(solution)/shard_map/ppermute | solution.py:457
  26.3 11.2 %collective-permute-start.3 = (bf16[2,320,128]{2,1,0:T(8,128)(2,1)}, bf16[2,320,128]{2,1,0:T(8,128)(2,1)S(1)}, u32[]{:S(2)}, u32[]{:S(2)}) collective-permute-start(bf16[2,320,128]{2,1,0:T(8,128)(2,1)} %rotate.1), channel_id=1, source_target_pairs={{0,8},{4,12},{8,16},{12,20},{16,24},{20,28},{24,0},{28,4},{1,9},{5... | collective-permute-start | bytes 491528 | tf_op jit(solution)/shard_map/ppermute | solution.py:457
  27.8 13.5 %collective-permute-start.4 = (bf16[2,320,128]{2,1,0:T(8,128)(2,1)}, bf16[2,320,128]{2,1,0:T(8,128)(2,1)S(1)}, u32[]{:S(2)}, u32[]{:S(2)}) collective-permute-start(bf16[2,320,128]{2,1,0:T(8,128)(2,1)} %rotate.1), channel_id=1, source_target_pairs={{0,24},{4,28},{8,0},{12,4},{16,8},{20,12},{24,16},{28,20},{1,25},{... | collective-permute-start | bytes 491528 | tf_op jit(solution)/shard_map/ppermute | solution.py:457
  37.5 5.8 %copy-start.9 = (bf16[2,320,128]{2,1,0:T(8,128)(2,1)}, bf16[2,320,128]{2,1,0:T(8,128)(2,1)S(1)}, u32[]{:S(2)}) copy-start(bf16[2,320,128]{2,1,0:T(8,128)(2,1)S(1)} %collective-permute-done.3) | copy-start | bytes 491524
  41.3 2.1 %copy-start.10 = (bf16[2,320,128]{2,1,0:T(8,128)(2,1)}, bf16[2,320,128]{2,1,0:T(8,128)(2,1)S(1)}, u32[]{:S(2)}) copy-start(bf16[2,320,128]{2,1,0:T(8,128)(2,1)S(1)} %collective-permute-done.4) | copy-start | bytes 491524
  42.7 1.4 copy-start.2
  44.1 5.0 %copy-start.5 = (bf16[2,320,128]{2,1,0:T(8,128)(2,1)S(1)}, bf16[2,320,128]{2,1,0:T(8,128)(2,1)}, u32[]{:S(2)}) copy-start(bf16[2,320,128]{2,1,0:T(8,128)(2,1)} %rotate.1) | copy-start | bytes 491524
  44.1 31.5 %all-to-all-start.1 = ((bf16[8,1024,128]{2,1,0:T(8,128)(2,1)}), bf16[8,1024,128]{2,1,0:T(8,128)(2,1)S(1)}, u32[]{:S(2)}, u32[]{:S(2)}) async-start(bf16[8,1024,128]{2,1,0:T(8,128)(2,1)} %tie.1), calls=%async_computation.1 | async-start | bytes 4194304 | tf_op jit(solution)/shard_map/all_to_all | solution.py:473
  49.1 14.9 %copy-start.11 = (s32[8]{0:T(128)S(1)}, s32[8]{0:T(128)}, u32[]{:S(2)}) copy-start(s32[8]{0:T(128)} %constant.62) | copy-start | bytes 100
  49.1 63.6 %all-gather.2.cloned.1.call-start = ((), (), s32[]{:S(2)}) async-start(), calls=%async_computation.4 | async-start | bytes 1843200 | tf_op jit(solution)/shard_map/all_gather | solution.py:476
  49.1 15.6 %copy-start.6 = (bf16[2,2,320,128]{3,2,1,0:T(8,128)(2,1)}, bf16[2,2,320,128]{3,2,1,0:T(8,128)(2,1)S(1)}, u32[]{:S(2)}) copy-start(bf16[2,2,320,128]{3,2,1,0:T(8,128)(2,1)S(1)} %pad_maximum_fusion.refs_0_) | copy-start | bytes 983044
  49.1 12.3 %collective-permute-start.1 = (bf16[2,2,320,128]{3,2,1,0:T(8,128)(2,1)S(1)}, bf16[2,2,320,128]{3,2,1,0:T(8,128)(2,1)S(1)}, u32[]{:S(2)}, u32[]{:S(2)}) collective-permute-start(bf16[2,2,320,128]{3,2,1,0:T(8,128)(2,1)S(1)} %pad_maximum_fusion.refs_0_), channel_id=1, source_target_pairs={{0,4},{4,8},{8,12},{12,16},{16,20},{20,24},{24,28},{28,0},{1,5},{5... | collective-permute-start | bytes 983048 | tf_op jit(solution)/shard_map/ppermute | solution.py:457
  51.0 10.5 %collective-permute-start.2 = (bf16[2,2,320,128]{3,2,1,0:T(8,128)(2,1)S(1)}, bf16[2,2,320,128]{3,2,1,0:T(8,128)(2,1)S(1)}, u32[]{:S(2)}, u32[]{:S(2)}) collective-permute-start(bf16[2,2,320,128]{3,2,1,0:T(8,128)(2,1)S(1)} %pad_maximum_fusion.refs_0_), channel_id=1, source_target_pairs={{0,28},{4,0},{8,4},{12,8},{16,12},{20,16},{24,20},{28,24},{1,29},{... | collective-permute-start | bytes 983048 | tf_op jit(solution)/shard_map/ppermute | solution.py:457
  61.4 0.8 copy-start.7
  61.5 0.9 copy-start.8
  75.6 1.3 copy-start.3
  91.1 39.0 %all-to-all-start.2 = ((bf16[8,2,336,128]{3,2,1,0:T(8,128)(2,1)}), bf16[8,2,336,128]{3,2,1,0:T(8,128)(2,1)S(1)}, u32[]{:S(2)}, u32[]{:S(2)}) async-start(bf16[8,2,336,128]{3,2,1,0:T(8,128)(2,1)} %attend.3), calls=%async_computation.2 | async-start | bytes 2752512 | tf_op jit(solution)/shard_map/all_to_all | solution.py:482
  112.6 28.8 %collective-permute-start.5 = (bf16[640,1280]{1,0:T(8,128)(2,1)}, bf16[640,1280]{1,0:T(8,128)(2,1)S(1)}, u32[]{:S(2)}, u32[]{:S(2)}) collective-permute-start(bf16[640,1280]{1,0:T(8,128)(2,1)} %all-gather.2.cloned.1.call-done.own_ref), channel_id=1, source_target_pairs={{0,32},{32,0},{64,96},{96,64},{128,160},{160,128},{192,224},{224,1... | collective-permute-start | bytes 4915208 | tf_op jit(solution)/shard_map/ppermute | solution.py:460
  130.1 1.1 copy-start
  135.0 15.8 %all-to-all-start.3 = ((bf16[4,64,1280]{2,1,0:T(8,128)(2,1)}), bf16[4,64,1280]{2,1,0:T(8,128)(2,1)S(1)}, u32[]{:S(2)}, u32[]{:S(2)}) async-start(bf16[4,64,1280]{2,1,0:T(8,128)(2,1)} %combine.1), calls=%async_computation.3 | async-start | bytes 1310720 | tf_op jit(solution)/shard_map/all_to_all | solution.py:484
  141.4 9.5 %copy-start.4 = (bf16[640,1280]{1,0:T(8,128)(2,1)}, bf16[640,1280]{1,0:T(8,128)(2,1)S(1)}, u32[]{:S(2)}) copy-start(bf16[640,1280]{1,0:T(8,128)(2,1)S(1)} %collective-permute-done.5.other_ref) | copy-start | bytes 4915204
  150.9 0.9 copy-start.1
  155.9 1.8 %collective-permute-start.6 = (bf16[2,64,1280]{2,1,0:T(8,128)(2,1)}, bf16[2,64,1280]{2,1,0:T(8,128)(2,1)S(1)}, u32[]{:S(2)}, u32[]{:S(2)}) collective-permute-start(bf16[2,64,1280]{2,1,0:T(8,128)(2,1)} %get-tuple-element.8), channel_id=1, source_target_pairs={{0,1},{1,0},{2,3},{3,2},{4,5},{5,4},{6,7},{7,6},{8,9},{9,8},{10,11... | collective-permute-start | bytes 983048 | tf_op jit(solution)/shard_map/ppermute | solution.py:488
  158.8 8.8 %collective-permute-start.8 = (bf16[64,1280]{1,0:T(8,128)(2,1)S(1)}, bf16[64,1280]{1,0:T(8,128)(2,1)S(1)}, u32[]{:S(2)}, u32[]{:S(2)}) collective-permute-start(bf16[64,1280]{1,0:T(8,128)(2,1)S(1)} %get-tuple-element.10), channel_id=1, source_target_pairs={{0,128},{1,192},{2,0},{3,64},{64,129},{65,193},{66,1},{67,65},{128... | collective-permute-start | bytes 491528 | tf_op jit(solution)/shard_map/ppermute | solution.py:498
  159.7 12.6 %collective-permute-start.7 = (bf16[64,1280]{1,0:T(8,128)(2,1)S(1)}, bf16[64,1280]{1,0:T(8,128)(2,1)S(1)}, u32[]{:S(2)}, u32[]{:S(2)}) collective-permute-start(bf16[64,1280]{1,0:T(8,128)(2,1)S(1)} %get-tuple-element.9), channel_id=1, source_target_pairs={{0,0},{1,64},{2,128},{3,192},{64,1},{65,65},{66,129},{67,193},{128... | collective-permute-start | bytes 491528 | tf_op jit(solution)/shard_map/ppermute | solution.py:498
Sparse Core Ops, SparseCore 0:
  64.1 48.4 all-gather.1

commit v8 on v6

v8 whole, which is shorter than its diff:
```python
import functools
import math

import jax
import jax.numpy as jnp
from jax import lax
from jax.experimental import pallas as pl
from jax.experimental.pallas import tpu as pltpu
from jax.sharding import Mesh
from jax.sharding import PartitionSpec as P

NEG_FILL = -1e30
LOG2E = math.log2(math.e)
VMEM_LIMIT = 60 * 1024 * 1024

Y, X, Z = "y", "x_lo", "z"
PLANE = (Y, X)
GRP = ("x_hi", "core")


def hadamard(order):
    index = jnp.arange(order, dtype=jnp.int32)
    common = index[:, None] & index[None, :]
    parity = jnp.zeros((order, order), jnp.int32)
    for shift_bit in range(int(order).bit_length()):
        parity = parity ^ common >> shift_bit & 1
    return jnp.where(parity == 1, -1.0, 1.0).astype(jnp.float32)


def dequantize_kernel(codes_ref, scales_ref, pattern_ref, out):
    kinds, groups, length, width = codes_ref.shape
    parts = scales_ref.shape[2]
    for g in range(groups):
        for kind in range(kinds):
            scales = scales_ref[kind, g]
            spread = jnp.concatenate(
                [
                    jnp.broadcast_to(scales[i : i + 1], (width // parts, length))
                    for i in range(parts)
                ],
                axis=0,
            )
            values = (codes_ref[kind, g].astype(jnp.float32) - 7.5) * spread.T
            values = values.astype(jnp.bfloat16)
            for copy in range(out.shape[0]):
                out[copy, pl.ds((g * kinds + kind) * length, length), :] = values
    groups, pages, blocks = pattern_ref.shape
    in_row = width // pages
    lane = lax.broadcasted_iota(jnp.int32, (in_row, width), 1)
    first = lax.broadcasted_iota(jnp.int32, (in_row, width), 0) * pages
    marks = []
    for g in range(groups):
        kept = pattern_ref[g].astype(jnp.float32)
        kept = jnp.concatenate([kept, jnp.zeros((pages, width - blocks), jnp.float32)], axis=1)
        kept = jnp.concatenate([kept, jnp.zeros((width - pages, width), jnp.float32)], axis=0).T
        for start in range(0, blocks, in_row):
            part = kept[start : start + in_row]
            row = jnp.zeros((in_row, width), jnp.float32)
            for p in range(pages):
                row = jnp.where(lane == first + p, part[:, p : p + 1], row)
            marks.append(jnp.sum(row, axis=0, keepdims=True))
    marks.append(jnp.zeros((16 - len(marks), width), jnp.float32))
    marks = jnp.concatenate(marks, axis=0).astype(jnp.bfloat16)
    for copy in range(out.shape[0]):
        out[copy, pl.ds(kinds * groups * length, 16), :] = marks


def dequantize(codes, scales, pattern, copies):
    kinds, groups, length, width = codes.shape
    return pl.pallas_call(
        dequantize_kernel,
        out_shape=jax.ShapeDtypeStruct(
            (copies, kinds * groups * length + 16, width), jnp.bfloat16
        ),
        compiler_params=pltpu.CompilerParams(vmem_limit_bytes=VMEM_LIMIT),
        name="dequantize",
    )(codes, scales, pattern)


def pass_kernel(block_ref, *refs):
    refs[-1][...] = block_ref[...]


def passed_after(block, *after):
    anywhere = pl.BlockSpec(memory_space=pl.ANY)
    return pl.pallas_call(
        pass_kernel,
        in_specs=[pl.BlockSpec(memory_space=pltpu.VMEM)] + [anywhere] * len(after),
        out_shape=jax.ShapeDtypeStruct(block.shape, block.dtype),
        name="pass",
    )(block, *after)


def rotate_kernel(queries_ref, table_ref, out_ref):
    groups, rows, width = out_ref.shape
    tokens = queries_ref.shape[0]
    per_group = rows // tokens
    scale = LOG2E / width
    for h in range(groups * per_group):
        turned = jnp.dot(
            queries_ref[:, h * width : (h + 1) * width],
            table_ref[...],
            preferred_element_type=jnp.float32,
        )
        at = pl.ds(h % per_group * tokens, tokens)
        out_ref[h // per_group, at, :] = (turned * scale).astype(jnp.bfloat16)


def rotate(queries, table, groups):
    tokens, columns = queries.shape
    width = table.shape[0]
    rows = columns // width // groups * tokens
    return pl.pallas_call(
        rotate_kernel,
        out_shape=jax.ShapeDtypeStruct((groups, rows, width), jnp.bfloat16),
        compiler_params=pltpu.CompilerParams(vmem_limit_bytes=VMEM_LIMIT),
        name="rotate",
    )(queries, table)


def attend_kernel(per_group, units, page, held, starts, order_ref, *refs):
    q_from, kv_from, marks_from = refs[: len(held)], *refs[len(held) : len(held) + 2]
    out_ref, reach_ref, mask_ref, s_ref, top_ref, acc_ref = refs[-13:-7]
    marks_ref, kv_ref, q_ref, packed_ref, kv_sems, q_sems, out_sems = refs[-7:]
    groups = q_ref.shape[1]
    half = kv_ref.shape[1] // groups // 2
    marks_copy = pltpu.make_async_copy(
        marks_from.at[:, pl.ds(marks_from.shape[1] - 16, 16)], marks_ref, kv_sems.at[2 * groups]
    )
    q_copies = [
        pltpu.make_async_copy(ref, q_ref.at[pl.ds(sum(held[:i]), held[i])], q_sems.at[i])
        for i, ref in enumerate(q_from)
    ]

    def kv_copy(i):
        at = pl.ds(pl.multiple_of(i * half, half), half)
        return pltpu.make_async_copy(kv_from.at[:, at], kv_ref.at[:, at], kv_sems.at[i])

    def out_copy(g):
        return pltpu.make_async_copy(packed_ref.at[:, g], out_ref.at[:, g], out_sems.at[g])

    marks_copy.start()
    kv_copy(0).start()
    for copy in q_copies:
        copy.start()
    for i in range(1, 2 * groups):
        kv_copy(i).start()
    marks_copy.wait()
    blocks, _, rows, width = q_ref.shape
    tokens = rows // per_group
    sources, height, _ = kv_ref.shape
    length = half
    shard_pages = length // page
    big_unit, unit, masked_unit = units
    place, z = order_ref[blocks], order_ref[blocks + 1]

    shape = (sources, marks_ref.shape[2])
    in_row = shape[1] // shard_pages
    here = place * blocks % in_row

    def list_pages(g):
        row = g * 2 + place * blocks // in_row
        kept = jnp.zeros(shape, jnp.float32)
        for r in range(4):
            kept = jnp.where(row == r, marks_ref[:, r, :].astype(jnp.float32), kept)
        lane = lax.broadcasted_iota(jnp.int32, shape, 1)
        source = lax.broadcasted_iota(jnp.int32, shape, 0)
        first_query = starts + (place * blocks // in_row * in_row + lane // shard_pages) * tokens
        first_key = (source * blocks + z) * length + lane % shard_pages * page
        causal = jnp.clip(first_query - first_key, -2 * page, 2 * page)
        reach = jnp.where(kept > 0.5, causal, -2 * page)
        mine = jnp.logical_and(lane >= here * shard_pages, lane < (here + blocks) * shard_pages)
        low = jnp.where(mine, reach, 2 * page)
        high = jnp.where(mine, reach, -2 * page)
        step = shard_pages
        while step < shape[1]:
            low = jnp.minimum(low, pltpu.roll(low, step, 1))
            high = jnp.maximum(high, pltpu.roll(high, step, 1))
            step *= 2
        first_lanes = lane < shard_pages
        whole_page = jnp.logical_and(first_lanes, low >= page - 1).astype(jnp.int32)
        some_page = jnp.logical_and(first_lanes, jnp.logical_and(high > -tokens, low < page - 1))
        some_page = some_page.astype(jnp.int32)

        def counted(flags):
            before = jnp.zeros_like(flags)
            for i in range(1, shard_pages):
                before = before + jnp.where(lane >= i, pltpu.roll(flags, i, 1), 0)
            row = jnp.sum(flags, axis=1, keepdims=True)
            above = jnp.zeros_like(row)
            for i in range(sources - 1):
                above = above + jnp.where(source[:, :1] > i, row[i : i + 1], 0)
            return before + above, jnp.sum(row, axis=0, keepdims=True)

        whole_rank, whole_total = counted(whole_page)
        some_rank, some_total = counted(some_page)
        grouped = whole_total // unit * unit
        spare = whole_total - grouped
        whole_list = jnp.zeros(shape, jnp.int32)
        some_list = jnp.full(shape, 0, jnp.int32)
        for p in range(shard_pages):
            number = source * shard_pages + p + 1
            at = slice(p, p + 1)
            in_whole = jnp.logical_and(whole_page[:, at] == 1, whole_rank[:, at] < grouped)
            spared = jnp.logical_and(whole_page[:, at] == 1, whole_rank[:, at] >= grouped)
            to_whole = jnp.where(in_whole, whole_rank[:, at], -1)
            to_some = jnp.where(spared, whole_rank[:, at] - grouped, -1)
            to_some = jnp.where(some_page[:, at] == 1, spare + some_rank[:, at], to_some)
            whole_list = whole_list + jnp.where(lane == to_whole, number, 0)
            some_list = some_list + jnp.where(lane == to_some, number, 0)
        whole_list = jnp.sum(whole_list, axis=0, keepdims=True) - 1
        some_list = jnp.sum(some_list, axis=0, keepdims=True) - 1
        mask_ref[g, 0] = reach
        counts = jnp.broadcast_to(grouped, whole_list.shape), jnp.broadcast_to(
            spare + some_total, whole_list.shape
        )
        rest = jnp.zeros((sources - 4, shape[1]), jnp.int32)
        mask_ref[g, 1] = jnp.concatenate([whole_list, some_list, *counts, rest], axis=0)

    for g in range(groups):
        list_pages(g)
    pltpu.sync_copy(mask_ref, reach_ref)
    for copy in q_copies:
        copy.wait()

    ahead = lax.broadcasted_iota(jnp.int32, (tokens, page), 1) - lax.broadcasted_iota(
        jnp.int32, (tokens, page), 0
    )
    def one_group(g, _):
        whole = reach_ref[g, 1, 2, 0] // unit
        rounds = (reach_ref[g, 1, 3, 0] + masked_unit - 1) // masked_unit
        kv_at = g * 2 * half

        def reach_of(p, b):
            lane_at = (here + order_ref[b]) * shard_pages + p % shard_pages
            return reach_ref[g, 0, p // shard_pages, lane_at]

        top_ref[...] = jnp.full(top_ref.shape, NEG_FILL, jnp.float32)
        acc_ref[...] = jnp.zeros(acc_ref.shape, jnp.float32)

        def fetch(p, at):
            first = pl.multiple_of(kv_at + at + p % shard_pages * page, page)
            return kv_ref[p // shard_pages, pl.ds(first, page), :]

        def first_pass(i, base, start, plane, size, masked):
            ps = [reach_ref[g, 1, base, start + i * size + u] for u in range(size)]
            pages_at = [jnp.maximum(p, 0) for p in ps]
            k = jnp.concatenate([fetch(p, 0) for p in pages_at], axis=0)
            for b in range(blocks):
                at = pl.ds(b * rows, rows)
                s = lax.dot_general(
                    q_ref[b, g], k, (((1,), (1,)), ((), ())), preferred_element_type=jnp.float32
                )
                top = top_ref[at, :]
                for u in range(size):
                    x = s[:, u * page : (u + 1) * page]
                    if masked:
                        reach = jnp.where(ps[u] < 0, -2 * page, reach_of(pages_at[u], b))
                        bias = jnp.where(ahead <= reach, 0.0, -jnp.inf)
                        x = (x.reshape(per_group, tokens, page) + bias[None]).reshape(rows, page)
                    s_ref[plane + i * size + u, at, :] = x
                    top = jnp.maximum(top, x)
                top_ref[at, :] = top
            return 0

        def second_pass(i, base, start, plane, size):
            pages_at = [jnp.maximum(reach_ref[g, 1, base, start + i * size + u], 0) for u in range(size)]
            v = jnp.concatenate([fetch(p, length) for p in pages_at], axis=0)
            v = jnp.concatenate([v, jnp.ones((size * page, width), jnp.bfloat16)], axis=1)
            for b in range(blocks):
                at = pl.ds(b * rows, rows)
                top = top_ref[at, :]
                weights = jnp.concatenate(
                    [
                        jnp.exp2(s_ref[plane + i * size + u, at, :] - top).astype(jnp.bfloat16)
                        for u in range(size)
                    ],
                    axis=1,
                )
                acc_ref[at, :] = acc_ref[at, :] + jnp.dot(
                    weights, v, preferred_element_type=jnp.float32
                )
            return 0

        kv_copy(2 * g).wait()
        masked_plane = whole * unit
        big = whole * unit // big_unit
        small_at = big * big_unit
        small = whole - small_at // unit
        lax.fori_loop(0, big, lambda i, _: first_pass(i, 0, 0, 0, big_unit, False), 0)
        lax.fori_loop(
            0, small, lambda i, _: first_pass(i, 0, small_at, small_at, unit, False), 0
        )
        lax.fori_loop(
            0, rounds, lambda i, _: first_pass(i, 1, 0, masked_plane, masked_unit, True), 0
        )
        for b in range(blocks):
            at = pl.ds(b * rows, rows)
            top = jnp.max(top_ref[at, :], axis=1, keepdims=True)
            top_ref[at, :] = jnp.broadcast_to(top, (rows, page))
        kv_copy(2 * g + 1).wait()
        lax.fori_loop(0, big, lambda i, _: second_pass(i, 0, 0, 0, big_unit), 0)
        lax.fori_loop(0, small, lambda i, _: second_pass(i, 0, small_at, small_at, unit), 0)
        lax.fori_loop(0, rounds, lambda i, _: second_pass(i, 1, 0, masked_plane, masked_unit), 0)
        for b in range(blocks):
            at = pl.ds(b * rows, rows)
            total = acc_ref[at, width:]
            total = jnp.maximum(total, 1e-30)
            out = (acc_ref[at, :width] / total).astype(jnp.bfloat16)
            lse = top_ref[at, :] + jnp.log2(total)
            across = [
                jnp.sum(
                    jnp.where(ahead == 0, lse[h * tokens : (h + 1) * tokens], 0.0),
                    axis=0,
                    keepdims=True,
                )
                for h in range(per_group)
            ]
            across.append(jnp.zeros((8 - per_group, page), jnp.float32))
            across = jnp.concatenate(across, axis=0)
            high = across.astype(jnp.bfloat16).astype(jnp.float32)
            middle = (across - high).astype(jnp.bfloat16).astype(jnp.float32)
            low = across - high - middle
            tail = jnp.concatenate([high + pltpu.roll(middle, page // 2, 1), low], axis=0)
            tail = tail.astype(jnp.bfloat16)
            packed_ref[order_ref[b], g, pl.ds(0, rows), :] = out
            packed_ref[order_ref[b], g, pl.ds(rows, 16), :] = tail
        out_copy(g).start()
        return 0

    lax.fori_loop(0, groups, one_group, 0)
    for g in range(groups):
        out_copy(g).wait()


def attend(queries, kv, per_group, starts, order):
    held = [q.shape[0] for q in queries]
    blocks = sum(held)
    _, groups, rows, width = queries[0].shape
    sources, height, _ = kv.shape
    page = 128
    height = height // page * page
    pages = sources * (height // groups // 2 // page)
    units = (8, 4, 2)
    packed = (blocks, groups, rows + 16, width)
    scores = blocks * groups * rows * pages * page // 2
    anywhere = pl.BlockSpec(memory_space=pl.ANY)
    return pl.pallas_call(
        functools.partial(attend_kernel, per_group, units, page, held, starts),
        in_specs=[pl.BlockSpec(memory_space=pltpu.SMEM)] + [anywhere] * (len(held) + 2),
        out_specs=anywhere,
        scratch_shapes=[
            pltpu.SMEM((groups, 2, sources, width), jnp.int32),
            pltpu.VMEM((groups, 2, sources, width), jnp.int32),
            pltpu.VMEM((pages + units[-1], blocks * rows, page), jnp.float32),
            pltpu.VMEM((blocks * rows, page), jnp.float32),
            pltpu.VMEM((blocks * rows, 2 * width), jnp.float32),
            pltpu.VMEM((sources, 16, width), jnp.bfloat16),
            pltpu.VMEM((sources, height, width), jnp.bfloat16),
            pltpu.VMEM((blocks, groups, rows, width), jnp.bfloat16),
            pltpu.VMEM(packed, jnp.bfloat16),
            pltpu.SemaphoreType.DMA((2 * groups + 1,)),
            pltpu.SemaphoreType.DMA((len(held),)),
            pltpu.SemaphoreType.DMA((groups,)),
        ],
        out_shape=jax.ShapeDtypeStruct(packed, jnp.bfloat16),
        compiler_params=pltpu.CompilerParams(vmem_limit_bytes=VMEM_LIMIT),
        cost_estimate=pl.CostEstimate(
            flops=8 * scores * width, bytes_accessed=8 * 1024 * 1024, transcendentals=scores
        ),
        name="attend",
    )(order, *queries, kv, kv)


def combine_kernel(per_group, parts_ref, table_ref, out_ref):
    sources, groups, height, width = parts_ref.shape
    rows = height - 16
    tokens = rows // per_group
    for g in range(groups):
        tails = parts_ref[:, g, pl.ds(rows, 16), :].astype(jnp.float32)
        middle = pltpu.roll(tails[:, 0:8].reshape(sources * 8, width), width // 2, 1)
        lse = tails[:, 0:8] + middle.reshape(sources, 8, width) + tails[:, 8:16]
        weights = jnp.exp2(lse - jnp.max(lse, axis=0, keepdims=True))
        weights = weights / jnp.sum(weights, axis=0, keepdims=True)
        weights = weights.reshape(sources * 8, width).T
        attended = []
        for h in range(per_group):
            one = jnp.zeros((tokens, width), jnp.float32)
            for e in range(sources):
                value = parts_ref[e, g, pl.ds(h * tokens, tokens), :].astype(jnp.float32)
                one = one + value * weights[:tokens, e * 8 + h : e * 8 + h + 1]
            attended.append(one)
        attended = jnp.concatenate(attended, axis=0)
        high = attended.astype(jnp.bfloat16)
        low = (attended - high.astype(jnp.float32)).astype(jnp.bfloat16)
        restored = jnp.dot(high, table_ref[...], preferred_element_type=jnp.float32)
        restored = restored + jnp.dot(low, table_ref[...], preferred_element_type=jnp.float32)
        restored = (restored * (1.0 / math.sqrt(width))).astype(jnp.bfloat16)
        for copy in range(out_ref.shape[0]):
            for h in range(per_group):
                at = (g * per_group + h) * width
                out_ref[copy, :, at : at + width] = restored[h * tokens : (h + 1) * tokens]


def combine(parts, table, per_group, copies):
    _, groups, height, width = parts.shape
    tokens = (height - 16) // per_group
    return pl.pallas_call(
        functools.partial(combine_kernel, per_group),
        out_shape=jax.ShapeDtypeStruct((copies, tokens, groups * per_group * width), jnp.bfloat16),
        compiler_params=pltpu.CompilerParams(vmem_limit_bytes=VMEM_LIMIT),
        name="combine",
    )(parts, table)


def project_kernel(place_ref, rows_ref, own_ref, other_ref, keep_ref, send_ref):
    _, tokens, _ = rows_ref.shape
    columns = own_ref.shape[0]
    x, x_hi, core = place_ref[0], place_ref[1], place_ref[2]
    wanted = [2 * hi + c for c in (core, 1 - core) for hi in (x_hi, 1 - x_hi)]
    rows = jnp.concatenate([rows_ref[i] for i in wanted], axis=0)
    for side, weights_ref in ((x, own_ref), (1 - x, other_ref)):
        at = pl.ds(pl.multiple_of(side * columns, columns), columns)
        terms = lax.dot_general(
            rows, weights_ref[...], (((1,), (1,)), ((), ())), preferred_element_type=jnp.float32
        ).astype(jnp.bfloat16)
        for i in range(2):
            keep_ref[i, :, at] = terms[i * tokens : (i + 1) * tokens]
            send_ref[i, :, at] = terms[(2 + i) * tokens : (3 + i) * tokens]


def project(rows, own, other, place):
    _, tokens, _ = rows.shape
    columns = own.shape[0]
    whole = pl.BlockSpec(memory_space=pltpu.VMEM)
    return pl.pallas_call(
        project_kernel,
        in_specs=[pl.BlockSpec(memory_space=pltpu.SMEM), whole, whole, whole],
        out_shape=[jax.ShapeDtypeStruct((2, tokens, 2 * columns), jnp.bfloat16)] * 2,
        compiler_params=pltpu.CompilerParams(vmem_limit_bytes=VMEM_LIMIT),
        name="project",
    )(place, rows, own, other)


def on_device(queries, cache_codes, cache_scales, pattern, out_weight):
    ny, nx, nz = (lax.axis_size(a) for a in (Y, X, Z))
    y, x, z = (lax.axis_index(a) for a in (Y, X, Z))
    x_hi, core = (lax.axis_index(a) for a in GRP)
    plane = ny * nx
    place = y * nx + x
    block_rows = queries.shape[0]
    _, groups, shard_len, width = cache_codes.shape
    heads = queries.shape[1] // width
    per_group = heads // groups
    blocks = pattern.shape[1]
    total_len = shard_len * blocks
    total_q = block_rows * blocks
    table = hadamard(width)

    def along(block, step):
        return lax.ppermute(block, Z, [(i, (i + step) % nz) for i in range(nz)])

    def across(block, step):
        return lax.ppermute(block, PLANE, [(e, e ^ step) for e in range(plane)])

    kv = lax.all_to_all(dequantize(cache_codes, cache_scales, jnp.transpose(pattern, (0, 2, 1)), plane), PLANE, 0, 0)

    rotated = rotate(queries, table.astype(jnp.bfloat16), groups)
    pair = jnp.stack([rotated, along(rotated, nz // 2)])
    held = [pair, along(pair, 1), along(pair, -1)]
    held += [along(rotated, 2)[None], along(rotated, -2)[None]]
    back = [s + far for s in (0, 1, -1) for far in (0, nz // 2)] + [2, -2]
    at = (z - jnp.array(back, jnp.int32)) % nz
    order = jnp.concatenate([at, jnp.stack([place, z])]).astype(jnp.int32)

    own = lax.all_gather(passed_after(out_weight.T, *held[1:]), Z, axis=0, tiled=True)
    other = across(own, 1)

    packed = attend(held, kv, per_group, total_len - total_q, order)
    parts = lax.all_to_all(packed, Z, 0, 0)
    restored = combine(parts, table.astype(jnp.bfloat16), per_group, ny)
    restored = lax.all_to_all(restored, Y, 0, 0)
    here = jnp.stack([x, x_hi, core]).astype(jnp.int32)
    keep, send = project(restored, own, other, here)

    send = lax.ppermute(send, GRP[1], [(0, 1), (1, 0)])
    share = (keep.astype(jnp.float32) + send.astype(jnp.float32)).astype(jnp.bfloat16)
    cores = ny // 2
    where = [(a, b, c) for a in range(ny) for b in range(cores) for c in range(2)]
    mixed = jnp.zeros(share.shape[1:], jnp.float32)
    for i in range(2):
        route = [
            ((a * cores + b) * 2 + c, ((2 * (b ^ i) + c) * cores + a // 2) * 2 + a % 2)
            for a, b, c in where
        ]
        mixed = mixed + lax.ppermute(share[i], (Y,) + GRP, route).astype(jnp.float32)
    return mixed.astype(jnp.bfloat16)


def solution(mesh):
    parts = Mesh(mesh.devices.reshape(4, 2, 8, 2, 2), (Y, X, Z) + GRP)
    ctx = (Y, X, Z)
    placed = (
        P(ctx, GRP),
        P(None, GRP, ctx, None),
        P(None, GRP, None, ctx),
        P(GRP, None, ctx),
        P(GRP, ctx),
    )
    return jax.shard_map(
        on_device, mesh=parts, in_specs=placed, out_specs=P(ctx, GRP), check_vma=False
    )
```

time: 185 us -> 175 us (0.946)
  waiting for transfers between devices: 81.2 us -> 76.6 us
    all_to_all x1, waiting for transfers between devices: 37.1 us -> 23.9 us  [on_device(): parts = lax.all_to_all(packed, Z, 0, 0)]
    all_gather x1, waiting for transfers between devices: 0.44 us -> 9.12 us  [on_device(): lax.all_gather(passed_after(out_weight.T, *held[1:]), Z, axis=0, tiled=True)]
    all_to_all x1, starting transfers between devices: 4.65 us -> 7.02 us  [on_device(): restored = lax.all_to_all(restored, Y, 0, 0)]
    all_to_all x1, starting transfers between devices: 7.59 us -> 5.34 us  [on_device(): parts = lax.all_to_all(packed, Z, 0, 0)]
    pallas_call x2, Pallas kernels: 25.3 us -> 23.1 us  [the longest x1 19.3 us: attend(): pl.pallas_call(functools.partial(attend_kernel, per_group, units, page, h...]
  transfers between devices with their start and end apart: 13 -> 13, of which waited for: 10 -> 10; matrix products, arithmetic and copies ran while one was open for 2% -> 2% of each run, Pallas kernels for 16% -> 15%
where the time goes in v8:
time: 175 us; the launch traced here: 174 us
  waiting for transfers between devices  76.6 us (44%)
  starting transfers between devices  42 us (24%)
  Pallas kernels  34.6 us (20%)
  between operations  13.5 us (8%)
  other arithmetic  4.63 us (3%)
  local copies, waits for them, and re-layouts  2.87 us (2%)
    all_to_all x1, waiting for transfers between devices, on_device(): parts = lax.all_to_all(packed, Z, 0, 0)  23.9 us
    pallas_call x1, Pallas kernels, attend(): pl.pallas_call(functools.partial(attend_kernel, per_group, units, page, h...  19.3 us
    ppermute x5, starting transfers between devices, along(): return lax.ppermute(block, Z, [(i, (i + step) % nz) for i in range(nz)])  18.2 us
    ppermute x5, waiting for transfers between devices, along(): return lax.ppermute(block, Z, [(i, (i + step) % nz) for i in range(nz)])  13.5 us
    all_to_all x1, waiting for transfers between devices, on_device(): restored = lax.all_to_all(restored, Y, 0, 0)  10.6 us
    all_to_all x1, waiting for transfers between devices, on_device(): lax.all_to_all(dequantize(cache_codes, cache_scales, jnp.transpose(patter...  10.4 us
    all_gather x1, waiting for transfers between devices, on_device(): lax.all_gather(passed_after(out_weight.T, *held[1:]), Z, axis=0, tiled=True)  9.12 us
    ppermute x2, waiting for transfers between devices, on_device(): lax.ppermute(share[i], (Y,) + GRP, route).astype(jnp.float32)  7.25 us
  transfers between devices with their start and end apart: 13, of which 10 were waited for; matrix products, arithmetic and copies ran while one was open for 2% of the time, Pallas kernels for 15%

profile of v8, /device:TPU:6, one launch (start us, length us, event | category | flops | bytes accessed | tf_op | source)
XLA Modules:
  0.0 174.1 jit_solution(6126544984848230688)
XLA Ops:
  6.5 3.8 %dequantize.1 = bf16[8,2064,128]{2,1,0:T(8,128)(2,1)} custom-call(s32[2,2,512,128]{3,2,1,0:T(8,128)} %codes_ref.1, f32[2,2,4,512]{3,2,1,0:T(4,128)} %scales_ref.1, s32[2,4,64]{2,1,0:T(4,128)} %bitcast.22), custom_call_target="tpu_custom_call" | custom-call | tf_op jit(solution)/shard_map/dequantize/pallas_call | solution.py:70
  10.4 5.9 %all-to-all-start = ((bf16[8,2064,128]{2,1,0:T(8,128)(2,1)}), bf16[8,2064,128]{2,1,0:T(8,128)(2,1)}, u32[]{:S(2)}, u32[]{:S(2)}) async-start(bf16[8,2064,128]{2,1,0:T(8,128)(2,1)} %dequantize.1), calls=%async_computation | async-start | bytes 8454144 | tf_op jit(solution)/shard_map/all_to_all | solution.py:466
  16.3 0.0 all-gather.2.cloned.1.call-start
  16.3 0.7 select_convert_fusion.table_ref
  17.0 1.8 %rotate.1 = bf16[2,320,128]{2,1,0:T(8,128)(2,1)} custom-call(bf16[64,1280]{1,0:T(8,128)(2,1)} %queries_ref.1, bf16[128,128]{1,0:T(8,128)(2,1)} %select_convert_fusion.table_ref), custom_call_target="tpu_custom_call" | custom-call | tf_op jit(solution)/shard_map/rotate/pallas_call | solution.py:113
  18.8 7.2 %collective-permute-start = (bf16[2,320,128]{2,1,0:T(8,128)(2,1)}, bf16[2,320,128]{2,1,0:T(8,128)(2,1)S(1)}, u32[]{:S(2)}, u32[]{:S(2)}) collective-permute-start(bf16[2,320,128]{2,1,0:T(8,128)(2,1)} %rotate.1), channel_id=1, source_target_pairs={{0,16},{4,20},{8,24},{12,28},{16,0},{20,4},{24,8},{28,12},{1,17},{... | collective-permute-start | bytes 491528 | tf_op jit(solution)/shard_map/ppermute | solution.py:461
  26.0 3.9 %collective-permute-done = bf16[2,320,128]{2,1,0:T(8,128)(2,1)S(1)} collective-permute-done((bf16[2,320,128]{2,1,0:T(8,128)(2,1)}, bf16[2,320,128]{2,1,0:T(8,128)(2,1)S(1)}, u32[]{:S(2)}, u32[]{:S(2)}) %collective-permute-start) | collective-permute-done | bytes 163872 | tf_op jit(solution)/shard_map/ppermute | solution.py:461
  29.9 0.9 pad_maximum_fusion.refs_0_
  30.9 0.0 copy-start.3
  30.9 4.2 %collective-permute-start.1 = (bf16[2,2,320,128]{3,2,1,0:T(8,128)(2,1)S(1)}, bf16[2,2,320,128]{3,2,1,0:T(8,128)(2,1)S(1)}, u32[]{:S(2)}, u32[]{:S(2)}) collective-permute-start(bf16[2,2,320,128]{3,2,1,0:T(8,128)(2,1)S(1)} %pad_maximum_fusion.refs_0_), channel_id=1, source_target_pairs={{0,4},{4,8},{8,12},{12,16},{16,20},{20,24},{24,28},{28,0},{1,5},{5... | collective-permute-start | bytes 983048 | tf_op jit(solution)/shard_map/ppermute | solution.py:461
  35.1 2.6 %collective-permute-start.2 = (bf16[2,2,320,128]{3,2,1,0:T(8,128)(2,1)S(1)}, bf16[2,2,320,128]{3,2,1,0:T(8,128)(2,1)S(1)}, u32[]{:S(2)}, u32[]{:S(2)}) collective-permute-start(bf16[2,2,320,128]{3,2,1,0:T(8,128)(2,1)S(1)} %pad_maximum_fusion.refs_0_), channel_id=1, source_target_pairs={{0,28},{4,0},{8,4},{12,8},{16,12},{20,16},{24,20},{28,24},{1,29},{... | collective-permute-start | bytes 983048 | tf_op jit(solution)/shard_map/ppermute | solution.py:461
  37.7 0.5 collective-permute-start.3
  38.3 3.6 %collective-permute-start.4 = (bf16[2,320,128]{2,1,0:T(8,128)(2,1)}, bf16[2,320,128]{2,1,0:T(8,128)(2,1)S(1)}, u32[]{:S(2)}, u32[]{:S(2)}) collective-permute-start(bf16[2,320,128]{2,1,0:T(8,128)(2,1)} %rotate.1), channel_id=1, source_target_pairs={{0,24},{4,28},{8,0},{12,4},{16,8},{20,12},{24,16},{28,20},{1,25},{... | collective-permute-start | bytes 491528 | tf_op jit(solution)/shard_map/ppermute | solution.py:461
  41.8 9.1 %collective-permute-done.3 = bf16[2,320,128]{2,1,0:T(8,128)(2,1)S(1)} collective-permute-done((bf16[2,320,128]{2,1,0:T(8,128)(2,1)}, bf16[2,320,128]{2,1,0:T(8,128)(2,1)S(1)}, u32[]{:S(2)}, u32[]{:S(2)}) %collective-permute-start.3) | collective-permute-done | bytes 163872 | tf_op jit(solution)/shard_map/ppermute | solution.py:461
  50.9 0.5 collective-permute-done.4
  51.4 0.0 collective-permute-done.1.refs_1_.refs_0_
  51.4 0.0 collective-permute-done.2.refs_2_.refs_1_
  51.4 0.0 copy-start.5
  51.4 0.2 copy-done.6
  51.6 0.5 copy-done.7
  52.0 0.1 copy-done.4
  52.2 0.1 copy-done.5
  52.2 1.6 pass.1
  53.9 0.0 all-gather.2.cloned.1.call-update
  53.9 0.0 copy-done.8
  53.9 0.7 pad_add_fusion.1.order_ref
  54.6 10.4 %all-to-all-done.refs_5_.refs_6_ = bf16[8,2064,128]{2,1,0:T(8,128)(2,1)} async-done(((bf16[8,2064,128]{2,1,0:T(8,128)(2,1)}), bf16[8,2064,128]{2,1,0:T(8,128)(2,1)}, u32[]{:S(2)}, u32[]{:S(2)}) %all-to-all-start) | async-done | bytes 4227104 | tf_op jit(solution)/shard_map/all_to_all | solution.py:466
  65.0 19.3 %attend.1 = bf16[8,2,336,128]{3,2,1,0:T(8,128)(2,1)} custom-call(s32[10]{0:T(128)} %pad_add_fusion.1.order_ref, bf16[2,2,320,128]{3,2,1,0:T(8,128)(2,1)} %copy-done.3, bf16[2,2,320,128]{3,2,1,0:T(8,128)(2,1)} %copy-done.4, bf16[2,2,320,128]{3,2,1,0:T(8,128)(2,1)} %copy-done.5, bf16[1,2,320,128]{3,2,1,0:T(8,128)(2,1)} %bitcast.19, ...), custom_call_target="tpu_custom_call" | custom-call | flops 10737418240 | bytes 8388608 | tf_op jit(solution)/shard_map/attend/pallas_call | solution.py:348
  84.3 5.3 %all-to-all-start.1 = ((bf16[8,2,336,128]{3,2,1,0:T(8,128)(2,1)}), bf16[8,2,336,128]{3,2,1,0:T(8,128)(2,1)S(1)}, u32[]{:S(2)}, u32[]{:S(2)}) async-start(bf16[8,2,336,128]{3,2,1,0:T(8,128)(2,1)} %attend.1), calls=%async_computation.1 | async-start | bytes 2752512 | tf_op jit(solution)/shard_map/all_to_all | solution.py:480
  89.6 9.1 %all-gather.2.cloned.1.call-done.own_ref = bf16[640,1280]{1,0:T(8,128)(2,1)} async-done(((bf16[80,1280]{1,0:T(8,128)(2,1)}), bf16[640,1280]{1,0:T(8,128)(2,1)}) %all-gather.2.cloned.1.call-update) | async-done | bytes 1638416 | tf_op jit(solution)/shard_map/all_gather | solution.py:476
  98.7 0.0 collective-permute-start.5
  98.7 23.9 %all-to-all-done.1.parts_ref = bf16[8,2,336,128]{3,2,1,0:T(8,128)(2,1)S(1)} async-done(((bf16[8,2,336,128]{3,2,1,0:T(8,128)(2,1)}), bf16[8,2,336,128]{3,2,1,0:T(8,128)(2,1)S(1)}, u32[]{:S(2)}, u32[]{:S(2)}) %all-to-all-start.1) | async-done | bytes 1376288 | tf_op jit(solution)/shard_map/all_to_all | solution.py:480
  122.7 1.1 copy-done
  123.8 3.9 %combine.1 = bf16[4,64,1280]{2,1,0:T(8,128)(2,1)} custom-call(bf16[8,2,336,128]{3,2,1,0:T(8,128)(2,1)} %copy-done, bf16[128,128]{1,0:T(8,128)(2,1)} %select_convert_fusion.table_ref), custom_call_target="tpu_custom_call" | custom-call | tf_op jit(solution)/shard_map/combine/pallas_call | solution.py:408
  127.6 7.0 %all-to-all-start.2 = ((bf16[4,64,1280]{2,1,0:T(8,128)(2,1)}), bf16[4,64,1280]{2,1,0:T(8,128)(2,1)S(1)}, u32[]{:S(2)}, u32[]{:S(2)}) async-start(bf16[4,64,1280]{2,1,0:T(8,128)(2,1)} %combine.1), calls=%async_computation.2 | async-start | bytes 1310720 | tf_op jit(solution)/shard_map/all_to_all | solution.py:482
  134.7 0.6 pad_add_fusion.place_ref
  135.2 0.0 collective-permute-done.5.other_ref
  135.2 10.6 %all-to-all-done.2.rows_ref = bf16[4,64,1280]{2,1,0:T(8,128)(2,1)S(1)} async-done(((bf16[4,64,1280]{2,1,0:T(8,128)(2,1)}), bf16[4,64,1280]{2,1,0:T(8,128)(2,1)S(1)}, u32[]{:S(2)}, u32[]{:S(2)}) %all-to-all-start.2) | async-done | bytes 655392 | tf_op jit(solution)/shard_map/all_to_all | solution.py:482
  145.8 0.9 copy-done.1
  146.7 4.2 %project.1 = (bf16[2,64,1280]{2,1,0:T(8,128)(2,1)}, bf16[2,64,1280]{2,1,0:T(8,128)(2,1)}) custom-call(s32[3]{0:T(128)} %pad_add_fusion.place_ref, bf16[4,64,1280]{2,1,0:T(8,128)(2,1)} %copy-done.1, bf16[640,1280]{1,0:T(8,128)(2,1)} %all-gather.2.cloned.1.call-done.own_ref, bf16[640,1280]{1,0:T(8,128)(2,1)} %copy-done.2), custom_call_target="tpu_custom_call" | custom-call | tf_op jit(solution)/shard_map/project/pallas_call | solution.py:436
  150.8 0.0 collective-permute-start.6
  150.8 1.8 %collective-permute-done.6 = bf16[2,64,1280]{2,1,0:T(8,128)(2,1)S(1)} collective-permute-done((bf16[2,64,1280]{2,1,0:T(8,128)(2,1)}, bf16[2,64,1280]{2,1,0:T(8,128)(2,1)S(1)}, u32[]{:S(2)}, u32[]{:S(2)}) %collective-permute-start.6) | collective-permute-done | bytes 327712 | tf_op jit(solution)/shard_map/ppermute | solution.py:486
  152.7 1.1 add_convert_fusion
  153.8 0.1 collective-permute-start.8
  153.9 5.4 %collective-permute-start.7 = (bf16[64,1280]{1,0:T(8,128)(2,1)S(1)}, bf16[64,1280]{1,0:T(8,128)(2,1)S(1)}, u32[]{:S(2)}, u32[]{:S(2)}) collective-permute-start(bf16[64,1280]{1,0:T(8,128)(2,1)S(1)} %get-tuple-element.9), channel_id=1, source_target_pairs={{0,0},{1,64},{2,128},{3,192},{64,1},{65,65},{66,129},{67,193},{128... | collective-permute-start | bytes 491528 | tf_op jit(solution)/shard_map/ppermute | solution.py:496
  159.3 3.3 %collective-permute-done.8 = bf16[64,1280]{1,0:T(8,128)(2,1)S(1)} collective-permute-done((bf16[64,1280]{1,0:T(8,128)(2,1)S(1)}, bf16[64,1280]{1,0:T(8,128)(2,1)S(1)}, u32[]{:S(2)}, u32[]{:S(2)}) %collective-permute-start.8) | collective-permute-done | bytes 163872 | tf_op jit(solution)/shard_map/ppermute | solution.py:496
  162.5 4.0 %collective-permute-done.7 = bf16[64,1280]{1,0:T(8,128)(2,1)S(1)} collective-permute-done((bf16[64,1280]{1,0:T(8,128)(2,1)S(1)}, bf16[64,1280]{1,0:T(8,128)(2,1)S(1)}, u32[]{:S(2)}, u32[]{:S(2)}) %collective-permute-start.7) | collective-permute-done | bytes 163872 | tf_op jit(solution)/shard_map/ppermute | solution.py:496
  166.5 0.7 add_convert_fusion.1
  (11 shorter events, 0.1 us)
Async XLA Ops:
  10.4 54.6 %all-to-all-start = ((bf16[8,2064,128]{2,1,0:T(8,128)(2,1)}), bf16[8,2064,128]{2,1,0:T(8,128)(2,1)}, u32[]{:S(2)}, u32[]{:S(2)}) async-start(bf16[8,2064,128]{2,1,0:T(8,128)(2,1)} %dequantize.1), calls=%async_computation | async-start | bytes 8454144 | tf_op jit(solution)/shard_map/all_to_all | solution.py:466
  16.3 37.6 %copy-start.8 = (s32[8]{0:T(128)S(1)}, s32[8]{0:T(128)}, u32[]{:S(2)}) copy-start(s32[8]{0:T(128)} %constant.62) | copy-start | bytes 100
  16.3 82.4 %all-gather.2.cloned.1.call-start = ((), (), s32[]{:S(2)}) async-start(), calls=%async_computation.3 | async-start | bytes 1843200 | tf_op jit(solution)/shard_map/all_gather | solution.py:476
  18.8 11.1 %collective-permute-start = (bf16[2,320,128]{2,1,0:T(8,128)(2,1)}, bf16[2,320,128]{2,1,0:T(8,128)(2,1)S(1)}, u32[]{:S(2)}, u32[]{:S(2)}) collective-permute-start(bf16[2,320,128]{2,1,0:T(8,128)(2,1)} %rotate.1), channel_id=1, source_target_pairs={{0,16},{4,20},{8,24},{12,28},{16,0},{20,4},{24,8},{28,12},{1,17},{... | collective-permute-start | bytes 491528 | tf_op jit(solution)/shard_map/ppermute | solution.py:461
  30.9 34.1 %copy-start.3 = (bf16[2,2,320,128]{3,2,1,0:T(8,128)(2,1)}, bf16[2,2,320,128]{3,2,1,0:T(8,128)(2,1)S(1)}, u32[]{:S(2)}) copy-start(bf16[2,2,320,128]{3,2,1,0:T(8,128)(2,1)S(1)} %pad_maximum_fusion.refs_0_) | copy-start | bytes 983044
  30.9 20.5 %collective-permute-start.1 = (bf16[2,2,320,128]{3,2,1,0:T(8,128)(2,1)S(1)}, bf16[2,2,320,128]{3,2,1,0:T(8,128)(2,1)S(1)}, u32[]{:S(2)}, u32[]{:S(2)}) collective-permute-start(bf16[2,2,320,128]{3,2,1,0:T(8,128)(2,1)S(1)} %pad_maximum_fusion.refs_0_), channel_id=1, source_target_pairs={{0,4},{4,8},{8,12},{12,16},{16,20},{20,24},{24,28},{28,0},{1,5},{5... | collective-permute-start | bytes 983048 | tf_op jit(solution)/shard_map/ppermute | solution.py:461
  35.1 16.3 %collective-permute-start.2 = (bf16[2,2,320,128]{3,2,1,0:T(8,128)(2,1)S(1)}, bf16[2,2,320,128]{3,2,1,0:T(8,128)(2,1)S(1)}, u32[]{:S(2)}, u32[]{:S(2)}) collective-permute-start(bf16[2,2,320,128]{3,2,1,0:T(8,128)(2,1)S(1)} %pad_maximum_fusion.refs_0_), channel_id=1, source_target_pairs={{0,28},{4,0},{8,4},{12,8},{16,12},{20,16},{24,20},{28,24},{1,29},{... | collective-permute-start | bytes 983048 | tf_op jit(solution)/shard_map/ppermute | solution.py:461
  37.7 13.2 %collective-permute-start.3 = (bf16[2,320,128]{2,1,0:T(8,128)(2,1)}, bf16[2,320,128]{2,1,0:T(8,128)(2,1)S(1)}, u32[]{:S(2)}, u32[]{:S(2)}) collective-permute-start(bf16[2,320,128]{2,1,0:T(8,128)(2,1)} %rotate.1), channel_id=1, source_target_pairs={{0,8},{4,12},{8,16},{12,20},{16,24},{20,28},{24,0},{28,4},{1,9},{5... | collective-permute-start | bytes 491528 | tf_op jit(solution)/shard_map/ppermute | solution.py:461
  38.3 13.1 %collective-permute-start.4 = (bf16[2,320,128]{2,1,0:T(8,128)(2,1)}, bf16[2,320,128]{2,1,0:T(8,128)(2,1)S(1)}, u32[]{:S(2)}, u32[]{:S(2)}) collective-permute-start(bf16[2,320,128]{2,1,0:T(8,128)(2,1)} %rotate.1), channel_id=1, source_target_pairs={{0,24},{4,28},{8,0},{12,4},{16,8},{20,12},{24,16},{28,20},{1,25},{... | collective-permute-start | bytes 491528 | tf_op jit(solution)/shard_map/ppermute | solution.py:461
  50.9 0.7 copy-start.6
  51.4 0.7 copy-start.7
  51.4 0.8 copy-start.4
  51.4 0.9 copy-start.5
  84.3 38.4 %all-to-all-start.1 = ((bf16[8,2,336,128]{3,2,1,0:T(8,128)(2,1)}), bf16[8,2,336,128]{3,2,1,0:T(8,128)(2,1)S(1)}, u32[]{:S(2)}, u32[]{:S(2)}) async-start(bf16[8,2,336,128]{3,2,1,0:T(8,128)(2,1)} %attend.1), calls=%async_computation.1 | async-start | bytes 2752512 | tf_op jit(solution)/shard_map/all_to_all | solution.py:480
  98.7 36.5 %collective-permute-start.5 = (bf16[640,1280]{1,0:T(8,128)(2,1)}, bf16[640,1280]{1,0:T(8,128)(2,1)S(1)}, u32[]{:S(2)}, u32[]{:S(2)}) collective-permute-start(bf16[640,1280]{1,0:T(8,128)(2,1)} %all-gather.2.cloned.1.call-done.own_ref), channel_id=1, source_target_pairs={{0,32},{32,0},{64,96},{96,64},{128,160},{160,128},{192,224},{224,1... | collective-permute-start | bytes 4915208 | tf_op jit(solution)/shard_map/ppermute | solution.py:464
  122.6 1.1 copy-start
  127.6 18.2 %all-to-all-start.2 = ((bf16[4,64,1280]{2,1,0:T(8,128)(2,1)}), bf16[4,64,1280]{2,1,0:T(8,128)(2,1)S(1)}, u32[]{:S(2)}, u32[]{:S(2)}) async-start(bf16[4,64,1280]{2,1,0:T(8,128)(2,1)} %combine.1), calls=%async_computation.2 | async-start | bytes 1310720 | tf_op jit(solution)/shard_map/all_to_all | solution.py:482
  135.2 10.6 %copy-start.2 = (bf16[640,1280]{1,0:T(8,128)(2,1)}, bf16[640,1280]{1,0:T(8,128)(2,1)S(1)}, u32[]{:S(2)}) copy-start(bf16[640,1280]{1,0:T(8,128)(2,1)S(1)} %collective-permute-done.5.other_ref) | copy-start | bytes 4915204
  145.8 0.9 copy-start.1
  150.8 1.8 %collective-permute-start.6 = (bf16[2,64,1280]{2,1,0:T(8,128)(2,1)}, bf16[2,64,1280]{2,1,0:T(8,128)(2,1)S(1)}, u32[]{:S(2)}, u32[]{:S(2)}) collective-permute-start(bf16[2,64,1280]{2,1,0:T(8,128)(2,1)} %get-tuple-element.8), channel_id=1, source_target_pairs={{0,1},{1,0},{2,3},{3,2},{4,5},{5,4},{6,7},{7,6},{8,9},{9,8},{10,11... | collective-permute-start | bytes 983048 | tf_op jit(solution)/shard_map/ppermute | solution.py:486
  153.8 8.8 %collective-permute-start.8 = (bf16[64,1280]{1,0:T(8,128)(2,1)S(1)}, bf16[64,1280]{1,0:T(8,128)(2,1)S(1)}, u32[]{:S(2)}, u32[]{:S(2)}) collective-permute-start(bf16[64,1280]{1,0:T(8,128)(2,1)S(1)} %get-tuple-element.10), channel_id=1, source_target_pairs={{0,128},{1,192},{2,0},{3,64},{64,129},{65,193},{66,1},{67,65},{128... | collective-permute-start | bytes 491528 | tf_op jit(solution)/shard_map/ppermute | solution.py:496
  153.9 12.7 %collective-permute-start.7 = (bf16[64,1280]{1,0:T(8,128)(2,1)S(1)}, bf16[64,1280]{1,0:T(8,128)(2,1)S(1)}, u32[]{:S(2)}, u32[]{:S(2)}) collective-permute-start(bf16[64,1280]{1,0:T(8,128)(2,1)S(1)} %get-tuple-element.9), channel_id=1, source_target_pairs={{0,0},{1,64},{2,128},{3,192},{64,1},{65,65},{66,129},{67,193},{128... | collective-permute-start | bytes 491528 | tf_op jit(solution)/shard_map/ppermute | solution.py:496
Sparse Core Ops, SparseCore 0:
  54.0 44.6 all-gather.1

commit v9 on v8

--- a/solution.py
+++ b/solution.py
@@ -27,9 +27,20 @@
     return jnp.where(parity == 1, -1.0, 1.0).astype(jnp.float32)
 
 
-def dequantize_kernel(codes_ref, scales_ref, pattern_ref, out):
+def dequantize_kernel(codes_ref, scales_ref, pattern_ref, out_ref, block_ref, sems):
     kinds, groups, length, width = codes_ref.shape
     parts = scales_ref.shape[2]
+    copies = out_ref.shape[0]
+    started = []
+
+    def send(section, rows):
+        for i in range(copies):
+            copy = pltpu.make_async_copy(
+                block_ref.at[rows], out_ref.at[i, rows], sems.at[section, i]
+            )
+            copy.start()
+            started.append(copy)
+
     for g in range(groups):
         for kind in range(kinds):
             scales = scales_ref[kind, g]
@@ -42,8 +53,9 @@
             )
             values = (codes_ref[kind, g].astype(jnp.float32) - 7.5) * spread.T
             values = values.astype(jnp.bfloat16)
-            for copy in range(out.shape[0]):
-                out[copy, pl.ds((g * kinds + kind) * length, length), :] = values
+            rows = pl.ds((g * kinds + kind) * length, length)
+            block_ref[rows, :] = values
+            send(g * kinds + kind, rows)
     groups, pages, blocks = pattern_ref.shape
     in_row = width // pages
     lane = lax.broadcasted_iota(jnp.int32, (in_row, width), 1)
@@ -61,17 +73,25 @@
             marks.append(jnp.sum(row, axis=0, keepdims=True))
     marks.append(jnp.zeros((16 - len(marks), width), jnp.float32))
     marks = jnp.concatenate(marks, axis=0).astype(jnp.bfloat16)
-    for copy in range(out.shape[0]):
-        out[copy, pl.ds(kinds * groups * length, 16), :] = marks
+    rows = pl.ds(kinds * groups * length, 16)
+    block_ref[rows, :] = marks
+    send(kinds * groups, rows)
+    for copy in started:
+        copy.wait()
 
 
 def dequantize(codes, scales, pattern, copies):
     kinds, groups, length, width = codes.shape
+    shape = (kinds * groups * length + 16, width)
     return pl.pallas_call(
         dequantize_kernel,
-        out_shape=jax.ShapeDtypeStruct(
-            (copies, kinds * groups * length + 16, width), jnp.bfloat16
-        ),
+        in_specs=[pl.BlockSpec(memory_space=pltpu.VMEM)] * 3,
+        out_specs=pl.BlockSpec(memory_space=pl.ANY),
+        out_shape=jax.ShapeDtypeStruct((copies,) + shape, jnp.bfloat16),
+        scratch_shapes=[
+            pltpu.VMEM(shape, jnp.bfloat16),
+            pltpu.SemaphoreType.DMA((kinds * groups + 1, copies)),
+        ],
         compiler_params=pltpu.CompilerParams(vmem_limit_bytes=VMEM_LIMIT),
         name="dequantize",
     )(codes, scales, pattern)

time: 175 us -> 176 us (level); the launches traced: 174 us -> 177 us
  starting transfers between devices: 42 us -> 46.5 us
  Pallas kernels: 34.6 us -> 31.1 us
  waiting for transfers between devices: 76.6 us -> 78.6 us
    all_to_all x1, waiting for transfers between devices: 23.9 us -> 30.2 us  [on_device(): parts = lax.all_to_all(packed, Z, 0, 0)]
    all_gather x1, waiting for transfers between devices: 9.12 us -> 4.95 us  [on_device(): lax.all_gather(passed_after(out_weight.T, *held[1:]), Z, axis=0, tiled=True)]
    all_to_all x1, starting transfers between devices: 5.34 us -> 8.93 us  [on_device(): parts = lax.all_to_all(packed, Z, 0, 0)]
    pallas_call x1, Pallas kernels: 19.3 us -> 15.9 us  [attend(): pl.pallas_call(functools.partial(attend_kernel, per_group, units, page, h...]
  transfers between devices with their start and end apart: 13 -> 13, of which waited for: 10 -> 10; matrix products, arithmetic and copies ran while one was open for 2% -> 2% of each run, Pallas kernels for 15% -> 13%
where the time goes in v9:
time: 176 us; the launch traced here: 177 us
  waiting for transfers between devices  78.6 us (45%)
  starting transfers between devices  46.5 us (26%)
  Pallas kernels  31.1 us (18%)
  between operations  13.5 us (8%)
  other arithmetic  4.63 us (3%)
  local copies, waits for them, and re-layouts  2.87 us (2%)
    all_to_all x1, waiting for transfers between devices, on_device(): parts = lax.all_to_all(packed, Z, 0, 0)  30.2 us
    ppermute x5, starting transfers between devices, along(): return lax.ppermute(block, Z, [(i, (i + step) % nz) for i in range(nz)])  18.2 us
    pallas_call x1, Pallas kernels, attend(): pl.pallas_call(functools.partial(attend_kernel, per_group, units, page, h...  15.9 us
    ppermute x5, waiting for transfers between devices, along(): return lax.ppermute(block, Z, [(i, (i + step) % nz) for i in range(nz)])  13.5 us
    all_to_all x1, waiting for transfers between devices, on_device(): restored = lax.all_to_all(restored, Y, 0, 0)  10.5 us
    all_to_all x1, waiting for transfers between devices, on_device(): lax.all_to_all(dequantize(cache_codes, cache_scales, jnp.transpose(patter...  10.4 us
    all_to_all x1, starting transfers between devices, on_device(): parts = lax.all_to_all(packed, Z, 0, 0)  8.93 us
    ppermute x2, waiting for transfers between devices, on_device(): lax.ppermute(share[i], (Y,) + GRP, route).astype(jnp.float32)  7.25 us
  transfers between devices with their start and end apart: 13, of which 10 were waited for; matrix products, arithmetic and copies ran while one was open for 2% of the time, Pallas kernels for 13%

profile of v9, /device:TPU:6, one launch (start us, length us, event | category | flops | bytes accessed | tf_op | source)
XLA Modules:
  0.0 177.2 jit_solution(12620164951387421222)
XLA Ops:
  6.5 3.8 %dequantize.1 = bf16[8,2064,128]{2,1,0:T(8,128)(2,1)} custom-call(s32[2,2,512,128]{3,2,1,0:T(8,128)} %codes_ref.1, f32[2,2,4,512]{3,2,1,0:T(4,128)} %scales_ref.1, s32[2,4,64]{2,1,0:T(4,128)} %bitcast.22), custom_call_target="tpu_custom_call" | custom-call | tf_op jit(solution)/shard_map/dequantize/pallas_call | solution.py:86
  10.3 5.9 %all-to-all-start = ((bf16[8,2064,128]{2,1,0:T(8,128)(2,1)}), bf16[8,2064,128]{2,1,0:T(8,128)(2,1)}, u32[]{:S(2)}, u32[]{:S(2)}) async-start(bf16[8,2064,128]{2,1,0:T(8,128)(2,1)} %dequantize.1), calls=%async_computation | async-start | bytes 8454144 | tf_op jit(solution)/shard_map/all_to_all | solution.py:486
  16.2 0.0 all-gather.2.cloned.1.call-start
  16.3 0.7 select_convert_fusion.table_ref
  16.9 1.8 %rotate.1 = bf16[2,320,128]{2,1,0:T(8,128)(2,1)} custom-call(bf16[64,1280]{1,0:T(8,128)(2,1)} %queries_ref.1, bf16[128,128]{1,0:T(8,128)(2,1)} %select_convert_fusion.table_ref), custom_call_target="tpu_custom_call" | custom-call | tf_op jit(solution)/shard_map/rotate/pallas_call | solution.py:133
  18.7 7.2 %collective-permute-start = (bf16[2,320,128]{2,1,0:T(8,128)(2,1)}, bf16[2,320,128]{2,1,0:T(8,128)(2,1)S(1)}, u32[]{:S(2)}, u32[]{:S(2)}) collective-permute-start(bf16[2,320,128]{2,1,0:T(8,128)(2,1)} %rotate.1), channel_id=1, source_target_pairs={{0,16},{4,20},{8,24},{12,28},{16,0},{20,4},{24,8},{28,12},{1,17},{... | collective-permute-start | bytes 491528 | tf_op jit(solution)/shard_map/ppermute | solution.py:481
  25.9 3.9 %collective-permute-done = bf16[2,320,128]{2,1,0:T(8,128)(2,1)S(1)} collective-permute-done((bf16[2,320,128]{2,1,0:T(8,128)(2,1)}, bf16[2,320,128]{2,1,0:T(8,128)(2,1)S(1)}, u32[]{:S(2)}, u32[]{:S(2)}) %collective-permute-start) | collective-permute-done | bytes 163872 | tf_op jit(solution)/shard_map/ppermute | solution.py:481
  29.9 0.9 pad_maximum_fusion.refs_0_
  30.8 0.0 copy-start.3
  30.8 4.3 %collective-permute-start.1 = (bf16[2,2,320,128]{3,2,1,0:T(8,128)(2,1)S(1)}, bf16[2,2,320,128]{3,2,1,0:T(8,128)(2,1)S(1)}, u32[]{:S(2)}, u32[]{:S(2)}) collective-permute-start(bf16[2,2,320,128]{3,2,1,0:T(8,128)(2,1)S(1)} %pad_maximum_fusion.refs_0_), channel_id=1, source_target_pairs={{0,4},{4,8},{8,12},{12,16},{16,20},{20,24},{24,28},{28,0},{1,5},{5... | collective-permute-start | bytes 983048 | tf_op jit(solution)/shard_map/ppermute | solution.py:481
  35.1 2.6 %collective-permute-start.2 = (bf16[2,2,320,128]{3,2,1,0:T(8,128)(2,1)S(1)}, bf16[2,2,320,128]{3,2,1,0:T(8,128)(2,1)S(1)}, u32[]{:S(2)}, u32[]{:S(2)}) collective-permute-start(bf16[2,2,320,128]{3,2,1,0:T(8,128)(2,1)S(1)} %pad_maximum_fusion.refs_0_), channel_id=1, source_target_pairs={{0,28},{4,0},{8,4},{12,8},{16,12},{20,16},{24,20},{28,24},{1,29},{... | collective-permute-start | bytes 983048 | tf_op jit(solution)/shard_map/ppermute | solution.py:481
  37.7 0.5 collective-permute-start.3
  38.2 3.6 %collective-permute-start.4 = (bf16[2,320,128]{2,1,0:T(8,128)(2,1)}, bf16[2,320,128]{2,1,0:T(8,128)(2,1)S(1)}, u32[]{:S(2)}, u32[]{:S(2)}) collective-permute-start(bf16[2,320,128]{2,1,0:T(8,128)(2,1)} %rotate.1), channel_id=1, source_target_pairs={{0,24},{4,28},{8,0},{12,4},{16,8},{20,12},{24,16},{28,20},{1,25},{... | collective-permute-start | bytes 491528 | tf_op jit(solution)/shard_map/ppermute | solution.py:481
  41.8 9.1 %collective-permute-done.3 = bf16[2,320,128]{2,1,0:T(8,128)(2,1)S(1)} collective-permute-done((bf16[2,320,128]{2,1,0:T(8,128)(2,1)}, bf16[2,320,128]{2,1,0:T(8,128)(2,1)S(1)}, u32[]{:S(2)}, u32[]{:S(2)}) %collective-permute-start.3) | collective-permute-done | bytes 163872 | tf_op jit(solution)/shard_map/ppermute | solution.py:481
  50.9 0.5 collective-permute-done.4
  51.3 0.0 collective-permute-done.1.refs_1_.refs_0_
  51.3 0.0 collective-permute-done.2.refs_2_.refs_1_
  51.4 0.0 copy-start.5
  51.4 0.2 copy-done.6
  51.5 0.5 copy-done.7
  52.0 0.1 copy-done.4
  52.1 0.1 copy-done.5
  52.2 1.6 pass.1
  53.8 0.0 all-gather.2.cloned.1.call-update
  53.9 0.0 copy-done.8
  53.9 0.7 pad_add_fusion.1.order_ref
  54.6 10.4 %all-to-all-done.refs_5_.refs_6_ = bf16[8,2064,128]{2,1,0:T(8,128)(2,1)} async-done(((bf16[8,2064,128]{2,1,0:T(8,128)(2,1)}), bf16[8,2064,128]{2,1,0:T(8,128)(2,1)}, u32[]{:S(2)}, u32[]{:S(2)}) %all-to-all-start) | async-done | bytes 4227104 | tf_op jit(solution)/shard_map/all_to_all | solution.py:486
  64.9 15.9 %attend.1 = bf16[8,2,336,128]{3,2,1,0:T(8,128)(2,1)} custom-call(s32[10]{0:T(128)} %pad_add_fusion.1.order_ref, bf16[2,2,320,128]{3,2,1,0:T(8,128)(2,1)} %copy-done.3, bf16[2,2,320,128]{3,2,1,0:T(8,128)(2,1)} %copy-done.4, bf16[2,2,320,128]{3,2,1,0:T(8,128)(2,1)} %copy-done.5, bf16[1,2,320,128]{3,2,1,0:T(8,128)(2,1)} %bitcast.19, ...), custom_call_target="tpu_custom_call" | custom-call | flops 10737418240 | bytes 8388608 | tf_op jit(solution)/shard_map/attend/pallas_call | solution.py:368
  80.8 8.9 %all-to-all-start.1 = ((bf16[8,2,336,128]{3,2,1,0:T(8,128)(2,1)}), bf16[8,2,336,128]{3,2,1,0:T(8,128)(2,1)S(1)}, u32[]{:S(2)}, u32[]{:S(2)}) async-start(bf16[8,2,336,128]{3,2,1,0:T(8,128)(2,1)} %attend.1), calls=%async_computation.1 | async-start | bytes 2752512 | tf_op jit(solution)/shard_map/all_to_all | solution.py:500
  89.8 5.0 %all-gather.2.cloned.1.call-done.own_ref = bf16[640,1280]{1,0:T(8,128)(2,1)} async-done(((bf16[80,1280]{1,0:T(8,128)(2,1)}), bf16[640,1280]{1,0:T(8,128)(2,1)}) %all-gather.2.cloned.1.call-update) | async-done | bytes 1638416 | tf_op jit(solution)/shard_map/all_gather | solution.py:496
  94.7 0.8 collective-permute-start.5
  95.6 30.2 %all-to-all-done.1.parts_ref = bf16[8,2,336,128]{3,2,1,0:T(8,128)(2,1)S(1)} async-done(((bf16[8,2,336,128]{3,2,1,0:T(8,128)(2,1)}), bf16[8,2,336,128]{3,2,1,0:T(8,128)(2,1)S(1)}, u32[]{:S(2)}, u32[]{:S(2)}) %all-to-all-start.1) | async-done | bytes 1376288 | tf_op jit(solution)/shard_map/all_to_all | solution.py:500
  125.7 1.1 copy-done
  126.8 3.9 %combine.1 = bf16[4,64,1280]{2,1,0:T(8,128)(2,1)} custom-call(bf16[8,2,336,128]{3,2,1,0:T(8,128)(2,1)} %copy-done, bf16[128,128]{1,0:T(8,128)(2,1)} %select_convert_fusion.table_ref), custom_call_target="tpu_custom_call" | custom-call | tf_op jit(solution)/shard_map/combine/pallas_call | solution.py:428
  130.7 7.2 %all-to-all-start.2 = ((bf16[4,64,1280]{2,1,0:T(8,128)(2,1)}), bf16[4,64,1280]{2,1,0:T(8,128)(2,1)S(1)}, u32[]{:S(2)}, u32[]{:S(2)}) async-start(bf16[4,64,1280]{2,1,0:T(8,128)(2,1)} %combine.1), calls=%async_computation.2 | async-start | bytes 1310720 | tf_op jit(solution)/shard_map/all_to_all | solution.py:502
  137.8 0.6 pad_add_fusion.place_ref
  138.4 0.0 collective-permute-done.5.other_ref
  138.4 10.5 %all-to-all-done.2.rows_ref = bf16[4,64,1280]{2,1,0:T(8,128)(2,1)S(1)} async-done(((bf16[4,64,1280]{2,1,0:T(8,128)(2,1)}), bf16[4,64,1280]{2,1,0:T(8,128)(2,1)S(1)}, u32[]{:S(2)}, u32[]{:S(2)}) %all-to-all-start.2) | async-done | bytes 655392 | tf_op jit(solution)/shard_map/all_to_all | solution.py:502
  149.0 0.9 copy-done.1
  149.8 4.2 %project.1 = (bf16[2,64,1280]{2,1,0:T(8,128)(2,1)}, bf16[2,64,1280]{2,1,0:T(8,128)(2,1)}) custom-call(s32[3]{0:T(128)} %pad_add_fusion.place_ref, bf16[4,64,1280]{2,1,0:T(8,128)(2,1)} %copy-done.1, bf16[640,1280]{1,0:T(8,128)(2,1)} %all-gather.2.cloned.1.call-done.own_ref, bf16[640,1280]{1,0:T(8,128)(2,1)} %copy-done.2), custom_call_target="tpu_custom_call" | custom-call | tf_op jit(solution)/shard_map/project/pallas_call | solution.py:456
  154.0 0.0 collective-permute-start.6
  154.0 1.8 %collective-permute-done.6 = bf16[2,64,1280]{2,1,0:T(8,128)(2,1)S(1)} collective-permute-done((bf16[2,64,1280]{2,1,0:T(8,128)(2,1)}, bf16[2,64,1280]{2,1,0:T(8,128)(2,1)S(1)}, u32[]{:S(2)}, u32[]{:S(2)}) %collective-permute-start.6) | collective-permute-done | bytes 327712 | tf_op jit(solution)/shard_map/ppermute | solution.py:506
  155.8 1.1 add_convert_fusion
  156.9 0.1 collective-permute-start.8
  157.0 5.4 %collective-permute-start.7 = (bf16[64,1280]{1,0:T(8,128)(2,1)S(1)}, bf16[64,1280]{1,0:T(8,128)(2,1)S(1)}, u32[]{:S(2)}, u32[]{:S(2)}) collective-permute-start(bf16[64,1280]{1,0:T(8,128)(2,1)S(1)} %get-tuple-element.9), channel_id=1, source_target_pairs={{0,0},{1,64},{2,128},{3,192},{64,1},{65,65},{66,129},{67,193},{128... | collective-permute-start | bytes 491528 | tf_op jit(solution)/shard_map/ppermute | solution.py:516
  162.4 3.3 %collective-permute-done.8 = bf16[64,1280]{1,0:T(8,128)(2,1)S(1)} collective-permute-done((bf16[64,1280]{1,0:T(8,128)(2,1)S(1)}, bf16[64,1280]{1,0:T(8,128)(2,1)S(1)}, u32[]{:S(2)}, u32[]{:S(2)}) %collective-permute-start.8) | collective-permute-done | bytes 163872 | tf_op jit(solution)/shard_map/ppermute | solution.py:516
  165.7 4.0 %collective-permute-done.7 = bf16[64,1280]{1,0:T(8,128)(2,1)S(1)} collective-permute-done((bf16[64,1280]{1,0:T(8,128)(2,1)S(1)}, bf16[64,1280]{1,0:T(8,128)(2,1)S(1)}, u32[]{:S(2)}, u32[]{:S(2)}) %collective-permute-start.7) | collective-permute-done | bytes 163872 | tf_op jit(solution)/shard_map/ppermute | solution.py:516
  169.7 0.7 add_convert_fusion.1
  (11 shorter events, 0.0 us)
Async XLA Ops:
  10.3 54.6 %all-to-all-start = ((bf16[8,2064,128]{2,1,0:T(8,128)(2,1)}), bf16[8,2064,128]{2,1,0:T(8,128)(2,1)}, u32[]{:S(2)}, u32[]{:S(2)}) async-start(bf16[8,2064,128]{2,1,0:T(8,128)(2,1)} %dequantize.1), calls=%async_computation | async-start | bytes 8454144 | tf_op jit(solution)/shard_map/all_to_all | solution.py:486
  16.2 37.6 %copy-start.8 = (s32[8]{0:T(128)S(1)}, s32[8]{0:T(128)}, u32[]{:S(2)}) copy-start(s32[8]{0:T(128)} %constant.62) | copy-start | bytes 100
  16.2 78.5 %all-gather.2.cloned.1.call-start = ((), (), s32[]{:S(2)}) async-start(), calls=%async_computation.3 | async-start | bytes 1843200 | tf_op jit(solution)/shard_map/all_gather | solution.py:496
  18.7 11.1 %collective-permute-start = (bf16[2,320,128]{2,1,0:T(8,128)(2,1)}, bf16[2,320,128]{2,1,0:T(8,128)(2,1)S(1)}, u32[]{:S(2)}, u32[]{:S(2)}) collective-permute-start(bf16[2,320,128]{2,1,0:T(8,128)(2,1)} %rotate.1), channel_id=1, source_target_pairs={{0,16},{4,20},{8,24},{12,28},{16,0},{20,4},{24,8},{28,12},{1,17},{... | collective-permute-start | bytes 491528 | tf_op jit(solution)/shard_map/ppermute | solution.py:481
  30.8 34.1 %copy-start.3 = (bf16[2,2,320,128]{3,2,1,0:T(8,128)(2,1)}, bf16[2,2,320,128]{3,2,1,0:T(8,128)(2,1)S(1)}, u32[]{:S(2)}) copy-start(bf16[2,2,320,128]{3,2,1,0:T(8,128)(2,1)S(1)} %pad_maximum_fusion.refs_0_) | copy-start | bytes 983044
  30.8 20.5 %collective-permute-start.1 = (bf16[2,2,320,128]{3,2,1,0:T(8,128)(2,1)S(1)}, bf16[2,2,320,128]{3,2,1,0:T(8,128)(2,1)S(1)}, u32[]{:S(2)}, u32[]{:S(2)}) collective-permute-start(bf16[2,2,320,128]{3,2,1,0:T(8,128)(2,1)S(1)} %pad_maximum_fusion.refs_0_), channel_id=1, source_target_pairs={{0,4},{4,8},{8,12},{12,16},{16,20},{20,24},{24,28},{28,0},{1,5},{5... | collective-permute-start | bytes 983048 | tf_op jit(solution)/shard_map/ppermute | solution.py:481
  35.1 16.3 %collective-permute-start.2 = (bf16[2,2,320,128]{3,2,1,0:T(8,128)(2,1)S(1)}, bf16[2,2,320,128]{3,2,1,0:T(8,128)(2,1)S(1)}, u32[]{:S(2)}, u32[]{:S(2)}) collective-permute-start(bf16[2,2,320,128]{3,2,1,0:T(8,128)(2,1)S(1)} %pad_maximum_fusion.refs_0_), channel_id=1, source_target_pairs={{0,28},{4,0},{8,4},{12,8},{16,12},{20,16},{24,20},{28,24},{1,29},{... | collective-permute-start | bytes 983048 | tf_op jit(solution)/shard_map/ppermute | solution.py:481
  37.7 13.2 %collective-permute-start.3 = (bf16[2,320,128]{2,1,0:T(8,128)(2,1)}, bf16[2,320,128]{2,1,0:T(8,128)(2,1)S(1)}, u32[]{:S(2)}, u32[]{:S(2)}) collective-permute-start(bf16[2,320,128]{2,1,0:T(8,128)(2,1)} %rotate.1), channel_id=1, source_target_pairs={{0,8},{4,12},{8,16},{12,20},{16,24},{20,28},{24,0},{28,4},{1,9},{5... | collective-permute-start | bytes 491528 | tf_op jit(solution)/shard_map/ppermute | solution.py:481
  38.2 13.1 %collective-permute-start.4 = (bf16[2,320,128]{2,1,0:T(8,128)(2,1)}, bf16[2,320,128]{2,1,0:T(8,128)(2,1)S(1)}, u32[]{:S(2)}, u32[]{:S(2)}) collective-permute-start(bf16[2,320,128]{2,1,0:T(8,128)(2,1)} %rotate.1), channel_id=1, source_target_pairs={{0,24},{4,28},{8,0},{12,4},{16,8},{20,12},{24,16},{28,20},{1,25},{... | collective-permute-start | bytes 491528 | tf_op jit(solution)/shard_map/ppermute | solution.py:481
  50.9 0.7 copy-start.6
  51.3 0.7 copy-start.7
  51.3 0.8 copy-start.4
  51.4 0.9 copy-start.5
  80.8 44.9 %all-to-all-start.1 = ((bf16[8,2,336,128]{3,2,1,0:T(8,128)(2,1)}), bf16[8,2,336,128]{3,2,1,0:T(8,128)(2,1)S(1)}, u32[]{:S(2)}, u32[]{:S(2)}) async-start(bf16[8,2,336,128]{3,2,1,0:T(8,128)(2,1)} %attend.1), calls=%async_computation.1 | async-start | bytes 2752512 | tf_op jit(solution)/shard_map/all_to_all | solution.py:500
  94.7 43.7 %collective-permute-start.5 = (bf16[640,1280]{1,0:T(8,128)(2,1)}, bf16[640,1280]{1,0:T(8,128)(2,1)S(1)}, u32[]{:S(2)}, u32[]{:S(2)}) collective-permute-start(bf16[640,1280]{1,0:T(8,128)(2,1)} %all-gather.2.cloned.1.call-done.own_ref), channel_id=1, source_target_pairs={{0,32},{32,0},{64,96},{96,64},{128,160},{160,128},{192,224},{224,1... | collective-permute-start | bytes 4915208 | tf_op jit(solution)/shard_map/ppermute | solution.py:484
  125.7 1.1 copy-start
  130.7 18.3 %all-to-all-start.2 = ((bf16[4,64,1280]{2,1,0:T(8,128)(2,1)}), bf16[4,64,1280]{2,1,0:T(8,128)(2,1)S(1)}, u32[]{:S(2)}, u32[]{:S(2)}) async-start(bf16[4,64,1280]{2,1,0:T(8,128)(2,1)} %combine.1), calls=%async_computation.2 | async-start | bytes 1310720 | tf_op jit(solution)/shard_map/all_to_all | solution.py:502
  138.4 10.5 %copy-start.2 = (bf16[640,1280]{1,0:T(8,128)(2,1)}, bf16[640,1280]{1,0:T(8,128)(2,1)S(1)}, u32[]{:S(2)}) copy-start(bf16[640,1280]{1,0:T(8,128)(2,1)S(1)} %collective-permute-done.5.other_ref) | copy-start | bytes 4915204
  149.0 0.9 copy-start.1
  154.0 1.8 %collective-permute-start.6 = (bf16[2,64,1280]{2,1,0:T(8,128)(2,1)}, bf16[2,64,1280]{2,1,0:T(8,128)(2,1)S(1)}, u32[]{:S(2)}, u32[]{:S(2)}) collective-permute-start(bf16[2,64,1280]{2,1,0:T(8,128)(2,1)} %get-tuple-element.8), channel_id=1, source_target_pairs={{0,1},{1,0},{2,3},{3,2},{4,5},{5,4},{6,7},{7,6},{8,9},{9,8},{10,11... | collective-permute-start | bytes 983048 | tf_op jit(solution)/shard_map/ppermute | solution.py:506
  156.9 8.8 %collective-permute-start.8 = (bf16[64,1280]{1,0:T(8,128)(2,1)S(1)}, bf16[64,1280]{1,0:T(8,128)(2,1)S(1)}, u32[]{:S(2)}, u32[]{:S(2)}) collective-permute-start(bf16[64,1280]{1,0:T(8,128)(2,1)S(1)} %get-tuple-element.10), channel_id=1, source_target_pairs={{0,128},{1,192},{2,0},{3,64},{64,129},{65,193},{66,1},{67,65},{128... | collective-permute-start | bytes 491528 | tf_op jit(solution)/shard_map/ppermute | solution.py:516
  157.0 12.7 %collective-permute-start.7 = (bf16[64,1280]{1,0:T(8,128)(2,1)S(1)}, bf16[64,1280]{1,0:T(8,128)(2,1)S(1)}, u32[]{:S(2)}, u32[]{:S(2)}) collective-permute-start(bf16[64,1280]{1,0:T(8,128)(2,1)S(1)} %get-tuple-element.9), channel_id=1, source_target_pairs={{0,0},{1,64},{2,128},{3,192},{64,1},{65,65},{66,129},{67,193},{128... | collective-permute-start | bytes 491528 | tf_op jit(solution)/shard_map/ppermute | solution.py:516
Sparse Core Ops, SparseCore 0:
  54.0 40.6 all-gather.1
